TPU v7x, 32 devices: a whole 2x2x4 slice. The times are simulated.
32 devices in a mesh: parts: 2 (over x), space: 8 (over z, y), dp: 2 (over core).
Axes of the slice: x: 2, y: 2, z: 4, core: 2. Of those that a mesh axis runs over, the one named last changes fastest.
Arguments:
- fields: bfloat16 [16, 16, 180, 768], P(('parts', 'dp'), 'space'), parts along dimension 0, may hold values from -6 to 6
- cotangent: bfloat16 [16, 16, 180, 768], P(('parts', 'dp'), 'space'), parts along dimension 0, may hold values from -6 to 6
- w_first: bfloat16 [2, 8, 96, 96], replicated, may hold values from -0.4375 to 0.4375
- b_first: float32 [2, 8, 96], replicated, may hold values from -4 to 4
- w_second: bfloat16 [2, 8, 96, 96], replicated, may hold values from -0.4375 to 0.4375
- b_second: float32 [2, 8, 96], replicated, may hold values from -3 to 3
Outputs:
- output: bfloat16 [16, 16, 180, 768], P(('parts', 'dp'), 'space'), parts along dimension 0
- grad_fields: bfloat16 [16, 16, 180, 768], P(('parts', 'dp'), 'space'), parts along dimension 0
- grad_w_first: float32 [4, 8, 96, 96], P('parts'), parts along dimension 0
- grad_b_first: float32 [4, 8, 96], P('parts'), parts along dimension 0
- grad_w_second: float32 [4, 8, 96, 96], P('parts'), parts along dimension 0
- grad_b_second: float32 [4, 8, 96], P('parts'), parts along dimension 0
There are 2 independent parts, one for each index of `parts`. A program takes and returns all parts, laid end to end along the dimension named above; an argument that names none is the same for every part. Nothing has to cross between parts.
All inputs are finite; a program needn't handle non-finite values.
Results may differ from a plain program's by a relative error of at most 0.012.
The roundings to bfloat16 on the way count: a program that leaves them out, or rounds other values in their place, can miss the bound.
Values may be sent and summed in bfloat16 or wider, within the bound.
No kernel may reach another device: no remote copies, remote signals or barrier semaphores. Data moves between devices by JAX's collectives and lax.ppermute only.
A program may use at most 128 MiB of HBM per device.

v0:
```python
import math

import jax
import jax.numpy as jnp
from jax import lax
from jax.sharding import PartitionSpec as P

KW = 64


shrink_level = 0.05


def product_of(pattern, former, latter):
    return jnp.einsum(pattern, former, latter, preferred_element_type=jnp.float32)


def lon_tables(mode_count, cell_count):
    wavenums = jnp.arange(mode_count, dtype=jnp.int32)
    columns = jnp.arange(cell_count, dtype=jnp.int32)
    phase_index = (wavenums[:, None] * columns[None, :] % cell_count).astype(jnp.float32)
    phases = phase_index * (2.0 * math.pi / cell_count)
    factor = 1.0 / math.sqrt(cell_count)
    forward = jnp.concatenate([jnp.cos(phases) * factor, -jnp.sin(phases) * factor], axis=0)
    doubling = jnp.where(wavenums == 0, 1.0, 2.0).astype(jnp.float32)
    doubling = jnp.concatenate([doubling, doubling])
    inverse = jnp.transpose(forward * doubling[:, None])
    return (forward.astype(jnp.bfloat16), inverse.astype(jnp.bfloat16))


def lat_table(row_count):
    indices = jnp.arange(row_count, dtype=jnp.int32)
    phase_index = (indices[:, None] * indices[None, :] % row_count).astype(jnp.float32)
    phases = phase_index * (2.0 * math.pi / row_count)
    factor = 1.0 / math.sqrt(row_count)
    cosine = jnp.cos(phases) * factor
    sine_part = jnp.sin(phases) * factor
    blocks = jnp.stack(
        [jnp.stack([cosine, sine_part], axis=-1), jnp.stack([-sine_part, cosine], axis=-1)], axis=1
    )
    return blocks.reshape(2 * row_count, 2 * row_count).astype(jnp.bfloat16)


def to_modes(matrix, pattern, values):
    spectrum = product_of(pattern, matrix, values).astype(jnp.bfloat16)
    return spectrum.reshape(values.shape[0], values.shape[1], 2, -1, values.shape[3])


def to_cells(matrix, pattern, spectrum):
    flattened = spectrum.reshape(spectrum.shape[0], spectrum.shape[1], -1, spectrum.shape[4])
    return product_of(pattern, matrix, flattened)


def finish(base, matrix, pattern, spectrum):
    return (base.astype(jnp.float32) + to_cells(matrix, pattern, spectrum)).astype(jnp.bfloat16)


def lat_apply(matrix, spectrum):
    samples, lat_rows, parts_count, mode_count, channels = spectrum.shape
    flattened = spectrum.reshape(samples, lat_rows * parts_count, mode_count, channels)
    mixed = product_of("pq,bqkd->bpkd", matrix, flattened).astype(jnp.bfloat16)
    return mixed.reshape(samples, lat_rows, parts_count, mode_count, channels)


def split_parts(spectrum, block_count):
    samples, lat_rows, parts_count, mode_count, channels = spectrum.shape
    shape_out = (samples, lat_rows, mode_count, block_count, channels // block_count)
    return (spectrum[:, :, 0].reshape(shape_out), spectrum[:, :, 1].reshape(shape_out))


def join_parts(real_part, imag_part):
    samples, lat_rows, mode_count, block_count, block_size = real_part.shape
    merged = (samples, lat_rows, mode_count, block_count * block_size)
    return jnp.stack([real_part.reshape(merged), imag_part.reshape(merged)], axis=2)


def soft_shrink(values):
    return values - shrink_level * jnp.tanh(values / shrink_level)


def shrink_slope(values):
    bent = jnp.tanh(values / shrink_level)
    return bent * bent


def silu_slope(values):
    logistic = jax.nn.sigmoid(values)
    return logistic * (1.0 + values * (1.0 - logistic))


def complex_mix(real_part, imag_part, weight):
    pattern = "bhknj,nji->bhkni"
    real_out = product_of(pattern, real_part, weight[0]) - product_of(pattern, imag_part, weight[1])
    imag_out = product_of(pattern, real_part, weight[1]) + product_of(pattern, imag_part, weight[0])
    return (real_out, imag_out)


def complex_back(real_part, imag_part, weight):
    pattern = "bhkni,nji->bhknj"
    real_out = product_of(pattern, real_part, weight[0]) + product_of(pattern, imag_part, weight[1])
    imag_out = product_of(pattern, imag_part, weight[0]) - product_of(pattern, real_part, weight[1])
    return (real_out, imag_out)


def complex_grad(act_real, act_imag, grad_real, grad_imag):
    pattern = "bhknj,bhkni->nji"
    real_out = product_of(pattern, act_real, grad_real) + product_of(pattern, act_imag, grad_imag)
    imag_out = product_of(pattern, act_real, grad_imag) - product_of(pattern, act_imag, grad_real)
    return jnp.stack([real_out, imag_out])


def summed_over(values):
    return jnp.sum(values, axis=(0, 1, 2), dtype=jnp.float32)


def mlp_forward(mixed_in, w_first, b_first, w_second, b_second):
    real_in, imag_in = split_parts(mixed_in, w_first.shape[1])
    pre_real, pre_imag = complex_mix(real_in, imag_in, w_first)
    pre_real = pre_real + b_first[0]
    pre_imag = pre_imag + b_first[1]
    act_real = jax.nn.silu(pre_real).astype(jnp.bfloat16)
    act_imag = jax.nn.silu(pre_imag).astype(jnp.bfloat16)
    out_real, out_imag = complex_mix(act_real, act_imag, w_second)
    out_real = out_real + b_second[0]
    out_imag = out_imag + b_second[1]
    shrunk = join_parts(
        soft_shrink(out_real).astype(jnp.bfloat16), soft_shrink(out_imag).astype(jnp.bfloat16)
    )
    return (shrunk, (real_in, imag_in, pre_real, pre_imag, act_real, act_imag, out_real, out_imag))


def shrink_back(cot_lat, forward_state, w_second):
    real_in, imag_in, pre_real, pre_imag, act_real, act_imag, out_real, out_imag = forward_state
    grad_real, grad_imag = split_parts(cot_lat, w_second.shape[1])
    kept_real = (grad_real.astype(jnp.float32) * shrink_slope(out_real)).astype(jnp.bfloat16)
    kept_imag = (grad_imag.astype(jnp.float32) * shrink_slope(out_imag)).astype(jnp.bfloat16)
    sum_w_second = complex_grad(act_real, act_imag, kept_real, kept_imag)
    sum_b_second = jnp.stack([summed_over(kept_real), summed_over(kept_imag)])
    return (kept_real, kept_imag, sum_w_second, sum_b_second)


def act_back(kept_real, kept_imag, forward_state, w_first, w_second):
    real_in, imag_in, pre_real, pre_imag, act_real, act_imag, out_real, out_imag = forward_state
    back_real, back_imag = complex_back(kept_real, kept_imag, w_second)
    gated_real = (back_real * silu_slope(pre_real)).astype(jnp.bfloat16)
    gated_imag = (back_imag * silu_slope(pre_imag)).astype(jnp.bfloat16)
    sum_w_first = complex_grad(real_in, imag_in, gated_real, gated_imag)
    sum_b_first = jnp.stack([summed_over(gated_real), summed_over(gated_imag)])
    into_real, into_imag = complex_back(gated_real, gated_imag, w_first)
    grad_mixed = join_parts(into_real.astype(jnp.bfloat16), into_imag.astype(jnp.bfloat16))
    return (grad_mixed, sum_w_first, sum_b_first)


def body(fields, cotangent, w_first, b_first, w_second, b_second):
    lat_total = fields.shape[1] * lax.axis_size("space")
    forward_lon, inverse_lon = lon_tables(KW, fields.shape[2])
    lat_matrix = lat_table(lat_total)
    lat_inverse = jnp.transpose(lat_matrix)
    spectrum = to_modes(forward_lon, "kw,blwd->blkd", fields)
    gathered = lax.all_to_all(spectrum, "space", split_axis=3, concat_axis=1, tiled=True)
    mixed_in = lat_apply(lat_matrix, gathered)
    shrunk, forward_state = mlp_forward(mixed_in, w_first, b_first, w_second, b_second)
    lat_image = lat_apply(lat_inverse, shrunk)
    image_band = lax.all_to_all(lat_image, "space", split_axis=1, concat_axis=3, tiled=True)
    output = finish(fields, inverse_lon, "wk,blkd->blwd", image_band)
    cot_spec = to_modes(inverse_lon, "wk,blwd->blkd", cotangent)
    cot_gathered = lax.all_to_all(cot_spec, "space", split_axis=3, concat_axis=1, tiled=True)
    cot_lat = lat_apply(lat_matrix, cot_gathered)
    kept_real, kept_imag, sum_w_second, sum_b_second = shrink_back(cot_lat, forward_state, w_second)
    grad_mixed, sum_w_first, sum_b_first = act_back(
        kept_real, kept_imag, forward_state, w_first, w_second
    )
    grad_spec = lat_apply(lat_inverse, grad_mixed)
    grad_band = lax.all_to_all(grad_spec, "space", split_axis=1, concat_axis=3, tiled=True)
    grad_fields = finish(cotangent, forward_lon, "kw,blkd->blwd", grad_band)
    sum_w_first, sum_b_first, sum_w_second, sum_b_second = lax.psum(
        (sum_w_first, sum_b_first, sum_w_second, sum_b_second), ("space", "dp")
    )
    positions = fields.shape[0] * lax.axis_size("dp") * lat_total * KW
    factor = 1.0 / math.sqrt(positions)
    return (
        output,
        grad_fields,
        sum_w_first * factor,
        sum_b_first * factor,
        sum_w_second * factor,
        sum_b_second * factor,
    )


def solution(mesh):
    in_specs = (
        P(("parts", "dp"), "space", None, None),
        P(("parts", "dp"), "space", None, None),
        P(),
        P(),
        P(),
        P(),
    )
    out_specs = (
        P(("parts", "dp"), "space", None, None),
        P(("parts", "dp"), "space", None, None),
        P("parts", None, None, None),
        P("parts", None, None),
        P("parts", None, None, None),
        P("parts", None, None),
    )
    return jax.shard_map(body, mesh=mesh, in_specs=in_specs, out_specs=out_specs, check_vma=False)
```

profile of v0, /device:TPU:0, one launch (start us, length us, event | category | flops | bytes accessed | tf_op | source)
XLA Modules:
  0.0 374.5 jit_solution(8051468724019115680)
XLA Ops:
  12.7 7.4 %all-to-all-start = ((bf16[4,2,2,64,768]{4,2,1,0,3:T(2,128)(2,1)}), bf16[4,2,2,64,768]{4,2,1,0,3:T(2,128)(2,1)}, u32[]{:S(2)}, u32[]{:S(2)}) async-start(bf16[4,2,2,64,768]{4,2,1,0,3:T(2,128)(2,1)} %copy.60), calls=%async_computation | async-start | bytes 3145728 | tf_op jit(solution)/shard_map/all_to_all | solution.py:160
  23.9 33.3 %all-to-all-done = bf16[4,2,2,64,768]{4,2,1,0,3:T(2,128)(2,1)} async-done(((bf16[4,2,2,64,768]{4,2,1,0,3:T(2,128)(2,1)}), bf16[4,2,2,64,768]{4,2,1,0,3:T(2,128)(2,1)}, u32[]{:S(2)}, u32[]{:S(2)}) %all-to-all-start) | async-done | bytes 1572896 | tf_op jit(solution)/shard_map/all_to_all | solution.py:160
  57.2 4.6 %all-to-all-start.2 = ((bf16[4,2,2,64,768]{4,2,1,0,3:T(2,128)(2,1)}), bf16[4,2,2,64,768]{4,2,1,0,3:T(2,128)(2,1)}, u32[]{:S(2)}, u32[]{:S(2)}) async-start(bf16[4,2,2,64,768]{4,2,1,0,3:T(2,128)(2,1)} %copy.77), calls=%async_computation.2 | async-start | bytes 3145728 | tf_op jit(solution)/shard_map/all_to_all | solution.py:167
  62.5 4.2 %copy.189 = bf16[4,2,2,8,8,768]{5,2,1,3,4,0:T(2,128)(2,1)} copy(bf16[4,2,2,8,8,768]{5,2,1,0,4,3:T(2,128)(2,1)} %bitcast.4) | data formatting | bytes 3145728 | tf_op jit(solution)/shard_map/all_to_all | solution.py:160
  66.6 4.6 %reshape.166 = bf16[4,32,8,768]{3,1,2,0:T(8,128)(2,1)} reshape(bf16[4,8,2,2,8,768]{5,3,2,1,4,0:T(2,128)(2,1)} %bitcast.354) | data formatting | bytes 3145728 | tf_op jit(solution)/shard_map/reshape | solution.py:60
  74.4 4.5 %reshape.167 = bf16[4,16,2,8,768]{4,2,1,3,0:T(2,128)(2,1)} reshape(bf16[4,32,8,768]{3,1,2,0:T(8,128)(2,1)} %fusion.34) | data formatting | bytes 3145728 | tf_op jit(solution)/shard_map/reshape | solution.py:62
  78.9 9.4 %slice_reduce_fusion = (bf16[4,16,8,768]{3,1,2,0:T(8,128)(2,1)}, bf16[4,16,8,768]{3,1,2,0:T(8,128)(2,1)}) fusion(bf16[4,16,2,8,768]{4,2,1,3,0:T(2,128)(2,1)} %reshape.167), kind=kLoop, calls=%fused_computation.58 | loop fusion | bytes 3145728 | tf_op jit(solution)/shard_map/slice | solution.py:68
  90.5 3.6 reshape.198
  102.9 4.2 %copy.188 = bf16[4,2,2,8,8,768]{5,2,1,3,4,0:T(2,128)(2,1)} copy(bf16[4,2,2,8,8,768]{5,2,1,0,4,3:T(2,128)(2,1)} %bitcast.49) | data formatting | bytes 3145728 | tf_op jit(solution)/shard_map/all_to_all | solution.py:167
  107.1 4.6 %reshape.172 = bf16[4,32,8,768]{3,1,2,0:T(8,128)(2,1)} reshape(bf16[4,8,2,2,8,768]{5,3,2,1,4,0:T(2,128)(2,1)} %bitcast.355) | data formatting | bytes 3145728 | tf_op jit(solution)/shard_map/reshape | solution.py:60
  114.9 4.5 %reshape.173 = bf16[4,16,2,8,768]{4,2,1,3,0:T(2,128)(2,1)} reshape(bf16[4,32,8,768]{3,1,2,0:T(8,128)(2,1)} %fusion.35) | data formatting | bytes 3145728 | tf_op jit(solution)/shard_map/reshape | solution.py:62
  119.4 5.7 %fusion.124 = (bf16[4,16,1,8,768]{4,2,1,3,0:T(2,128)(2,1)}, bf16[4,16,1,8,768]{4,2,1,3,0:T(2,128)(2,1)S(1)}) fusion(bf16[4,16,2,8,768]{4,2,1,3,0:T(2,128)(2,1)} %reshape.173), kind=kLoop, calls=%fused_computation.193 | loop fusion | bytes 3145728 | tf_op jit(solution)/shard_map/slice | solution.py:68
  130.4 4.2 %fusion.11 = (bf16[4,16,8,8,96]{4,1,2,0,3:T(8,128)(2,1)S(1)}, f32[8,4,16,8,96]{4,2,3,1,0:T(8,128)}) fusion(f32[8,96]{1,0:T(8,128)S(1)} %get-tuple-element.40, f32[8,4,16,8,96]{4,2,3,1,0:T(8,128)} %fusion.60, bf16[2,8,96,96]{3,2,1,0:T(8,128)(2,1)} %param.8, bf16[4,16,8,8,96]{4,3,1,2,0:T(8,128)(2,1)} %reshape.198), kind=kOutput, calls=%fused_computation.22 | convolution fusion | flops 78249984 | bytes 5704704 | tf_op jit(solution)/shard_map/bhknj,nji->bhkni/dot_general | solution.py:15
  148.4 5.3 %convert_reduce_fusion.1 = (f32[8,96]{1,0:T(8,128)S(1)}, bf16[4,16,8,8,96]{4,1,2,0,3:T(8,128)(2,1)}, bf16[4,16,8,8,96]{4,1,2,0,3:T(8,128)(2,1)S(1)}) fusion(f32[4,16,8,8,96]{4,3,2,1,0:T(8,128)} %reshape.177, f32[8,96]{1,0:T(8,128)S(1)} %get-tuple-element.38, f32[8,4,16,8,96]{4,2,3,1,0:T(8,128)} %fusion.69, bf16[4,16,8,8,96]{4,1,2,0,3:T(8,128)(2,1)} %copy-done.16, ...), kind=kOutput, calls=%fused_computation.39 | convolution fusion | flops 79822080 | bytes 7018496 | tf_op jit(solution)/shard_map/bhknj,nji->bhkni/dot_general | solution.py:15
  162.4 4.7 %reshape.168 = bf16[4,32,8,768]{3,1,2,0:T(8,128)(2,1)} reshape(bf16[4,16,2,8,768]{4,2,1,3,0:T(2,128)(2,1)} %copy.71) | data formatting | bytes 3145728 | tf_op jit(solution)/shard_map/reshape | solution.py:60
  170.2 4.5 %reshape.169 = bf16[4,16,2,8,768]{4,2,1,3,0:T(2,128)(2,1)} reshape(bf16[4,32,8,768]{3,1,2,0:T(8,128)(2,1)} %fusion.32) | data formatting | bytes 3145728 | tf_op jit(solution)/shard_map/reshape | solution.py:62
  174.8 4.0 %copy.73 = bf16[4,16,2,8,768]{4,2,3,0,1:T(2,128)(2,1)} copy(bf16[4,16,2,8,768]{4,2,1,3,0:T(2,128)(2,1)} %reshape.169) | data formatting | bytes 3145728 | tf_op jit(solution)/shard_map/reshape | solution.py:62
  178.8 6.3 %all-to-all-start.1 = ((bf16[4,16,2,8,768]{4,2,3,0,1:T(2,128)(2,1)}), bf16[4,16,2,8,768]{4,2,3,0,1:T(2,128)(2,1)}, u32[]{:S(2)}, u32[]{:S(2)}) async-start(bf16[4,16,2,8,768]{4,2,3,0,1:T(2,128)(2,1)} %copy.73), calls=%async_computation.1 | async-start | bytes 3145728 | tf_op jit(solution)/shard_map/all_to_all | solution.py:164
  209.3 4.6 %reshape.174 = bf16[4,32,8,768]{3,1,2,0:T(8,128)(2,1)} reshape(bf16[4,16,2,8,768]{4,2,1,3,0:T(2,128)(2,1)} %copy.85) | data formatting | bytes 3145728 | tf_op jit(solution)/shard_map/reshape | solution.py:60
  217.1 4.9 %reshape.175 = bf16[4,16,2,8,768]{4,2,1,3,0:T(2,128)(2,1)} reshape(bf16[4,32,8,768]{3,1,2,0:T(8,128)(2,1)} %fusion.33) | data formatting | bytes 3145728 | tf_op jit(solution)/shard_map/reshape | solution.py:62
  222.1 4.2 %copy.87 = bf16[4,16,2,8,768]{4,2,3,0,1:T(2,128)(2,1)} copy(bf16[4,16,2,8,768]{4,2,1,3,0:T(2,128)(2,1)} %reshape.175) | data formatting | bytes 3145728 | tf_op jit(solution)/shard_map/reshape | solution.py:62
  232.7 6.1 %all-to-all-start.3 = ((bf16[4,16,2,8,768]{4,2,3,0,1:T(2,128)(2,1)}), bf16[4,16,2,8,768]{4,2,3,0,1:T(2,128)(2,1)}, u32[]{:S(2)}, u32[]{:S(2)}) async-start(bf16[4,16,2,8,768]{4,2,3,0,1:T(2,128)(2,1)} %copy.87), calls=%async_computation.3 | async-start | bytes 3145728 | tf_op jit(solution)/shard_map/all_to_all | solution.py:174
  245.5 77.7 %all-reduce = (f32[2,8,96]{2,1,0:T(8,128)S(1)}, f32[2,8,96]{2,1,0:T(8,128)S(1)}) all-reduce(f32[2,8,96]{2,1,0:T(8,128)S(1)} %pad_maximum_fusion.6, f32[2,8,96]{2,1,0:T(8,128)S(1)} %pad_maximum_fusion.7), channel_id=1, replica_groups=mesh['parts'=2,'space'=8,'dp'=2] {'space','dp'}, use_global_device_ids=true, to_apply=%region_3.4 | all-reduce | flops 3072 | bytes 24576 | tf_op jit(solution)/shard_map/psum | solution.py:176
  324.4 28.8 %all-reduce.4.cloned.1.call-done = (f32[2,8,96,96]{3,2,1,0:T(8,128)}, f32[2,8,96,96]{3,2,1,0:T(8,128)}) async-done(((f32[2,8,96,96]{3,2,1,0:T(8,128)}, f32[2,8,96,96]{3,2,1,0:T(8,128)}), (f32[2,8,96,96]{3,2,1,0:T(8,128)}, f32[2,8,96,96]{3,2,1,0:T(8,128)})) %all-reduce.4.cloned.1.call-update) | async-done | bytes 1179664 | tf_op jit(solution)/shard_map/psum | solution.py:176
  (144 shorter events, 113.8 us)
Async XLA Ops:
  12.7 7.6 %copy-start.1 = (bf16[4,2,180,768]{3,1,2,0:T(2,128)(2,1)S(1)}, bf16[4,2,180,768]{3,1,2,0:T(2,128)(2,1)}, u32[]{:S(2)}) copy-start(bf16[4,2,180,768]{3,1,2,0:T(2,128)(2,1)} %param.7) | copy-start | bytes 6635524
  12.7 44.5 %all-to-all-start = ((bf16[4,2,2,64,768]{4,2,1,0,3:T(2,128)(2,1)}), bf16[4,2,2,64,768]{4,2,1,0,3:T(2,128)(2,1)}, u32[]{:S(2)}, u32[]{:S(2)}) async-start(bf16[4,2,2,64,768]{4,2,1,0,3:T(2,128)(2,1)} %copy.60), calls=%async_computation | async-start | bytes 3145728 | tf_op jit(solution)/shard_map/all_to_all | solution.py:160
  20.9 2.9 copy-start.27
  20.9 2.9 copy-start.28
  57.2 45.7 %all-to-all-start.2 = ((bf16[4,2,2,64,768]{4,2,1,0,3:T(2,128)(2,1)}), bf16[4,2,2,64,768]{4,2,1,0,3:T(2,128)(2,1)}, u32[]{:S(2)}, u32[]{:S(2)}) async-start(bf16[4,2,2,64,768]{4,2,1,0,3:T(2,128)(2,1)} %copy.77), calls=%async_computation.2 | async-start | bytes 3145728 | tf_op jit(solution)/shard_map/all_to_all | solution.py:167
  97.3 2.1 copy-start.21
  130.4 4.3 %copy-start.2 = (f32[4,16,8,8,96]{4,3,2,1,0:T(8,128)S(1)}, f32[4,16,8,8,96]{4,3,2,1,0:T(8,128)}, u32[]{:S(2)}) copy-start(f32[4,16,8,8,96]{4,3,2,1,0:T(8,128)} %reshape.178) | copy-start | bytes 4718596
  130.4 4.3 %copy-start.3 = (f32[8,4,16,8,96]{4,2,3,1,0:T(8,128)S(1)}, f32[8,4,16,8,96]{4,2,3,1,0:T(8,128)}, u32[]{:S(2)}) copy-start(f32[8,4,16,8,96]{4,2,3,1,0:T(8,128)} %fusion.73) | copy-start | bytes 4718596
  130.4 4.3 %copy-start.22 = (bf16[2,8,96,96]{3,2,1,0:T(8,128)(2,1)S(1)}, bf16[2,8,96,96]{3,2,1,0:T(8,128)(2,1)}, u32[]{:S(2)}) copy-start(bf16[2,8,96,96]{3,2,1,0:T(8,128)(2,1)} %param.10) | copy-start | bytes 884740
  134.7 2.7 copy-start.16
  178.8 53.9 %all-to-all-start.1 = ((bf16[4,16,2,8,768]{4,2,3,0,1:T(2,128)(2,1)}), bf16[4,16,2,8,768]{4,2,3,0,1:T(2,128)(2,1)}, u32[]{:S(2)}, u32[]{:S(2)}) async-start(bf16[4,16,2,8,768]{4,2,3,0,1:T(2,128)(2,1)} %copy.73), calls=%async_computation.1 | async-start | bytes 3145728 | tf_op jit(solution)/shard_map/all_to_all | solution.py:164
  185.0 1.8 copy-start.8
  185.1 1.8 copy-start.23
  189.6 3.4 copy-start.11
  189.6 2.3 copy-start.29
  222.0 4.2 %copy-start.15 = (bf16[4,16,8,8,96]{4,1,2,0,3:T(8,128)(2,1)S(1)}, bf16[4,16,8,8,96]{4,1,2,0,3:T(8,128)(2,1)}, u32[]{:S(2)}) copy-start(bf16[4,16,8,8,96]{4,1,2,0,3:T(8,128)(2,1)} %copy-done.14) | copy-start | bytes 2359300
  222.0 4.2 %copy-start.25 = (bf16[4,16,8,8,96]{4,3,1,2,0:T(8,128)(2,1)S(1)}, bf16[4,16,8,8,96]{4,3,1,2,0:T(8,128)(2,1)}, u32[]{:S(2)}) copy-start(bf16[4,16,8,8,96]{4,3,1,2,0:T(8,128)(2,1)} %reshape.198) | copy-start | bytes 2359300
  232.7 8.2 %copy-start.7 = (bf16[4,16,8,8,96]{4,1,2,0,3:T(8,128)(2,1)S(1)}, bf16[4,16,8,8,96]{4,1,2,0,3:T(8,128)(2,1)}, u32[]{:S(2)}) copy-start(bf16[4,16,8,8,96]{4,1,2,0,3:T(8,128)(2,1)} %get-tuple-element.33) | copy-start | bytes 2359300
  232.7 129.2 %all-to-all-start.3 = ((bf16[4,16,2,8,768]{4,2,3,0,1:T(2,128)(2,1)}), bf16[4,16,2,8,768]{4,2,3,0,1:T(2,128)(2,1)}, u32[]{:S(2)}, u32[]{:S(2)}) async-start(bf16[4,16,2,8,768]{4,2,3,0,1:T(2,128)(2,1)} %copy.87), calls=%async_computation.3 | async-start | bytes 3145728 | tf_op jit(solution)/shard_map/all_to_all | solution.py:174
  238.9 114.4 %all-reduce.4.cloned.1.call-start = ((), (), s32[]{:S(2)}) async-start(), calls=%async_computation.4 | async-start | bytes 3145728 | tf_op jit(solution)/shard_map/psum | solution.py:176
  241.0 1.8 copy-start.5
  241.0 1.8 copy-start.31
  353.3 2.2 copy-start.26
  355.4 2.6 copy-start
  (13 other events, 19.1 us)
Sparse Core Ops, SparseCore 0:
  245.6 107.5 all-reduce.3
where the time goes:
time: 381 us; the launch traced here: 374 us
  local copies, waits for them, and re-layouts  126 us (33%)
  blocking collectives  77.7 us (20%)
  waiting for transfers between devices  62.2 us (16%)
  matrix products  53.1 us (14%)
  starting transfers between devices  24.4 us (6%)
  other arithmetic  16.8 us (4%)
  between operations  14.7 us (4%)
    psum x1, blocking collectives, body(): lax.psum((sum_w_first, sum_b_first, sum_w_second, sum_b_second), ('space'...  77.7 us
    dot_general x32, matrix products, product_of(): jnp.einsum(pattern, former, latter, preferred_element_type=jnp.float32)  53.1 us
    all_to_all x1, waiting for transfers between devices, body(): lax.all_to_all(spectrum, 'space', split_axis=3, concat_axis=1, tiled=True)  33.3 us
    psum x1, waiting for transfers between devices, body(): lax.psum((sum_w_first, sum_b_first, sum_w_second, sum_b_second), ('space'...  28.8 us
    reshape x6, local copies, waits for them, and re-layouts, lat_apply(): return mixed.reshape(samples, lat_rows, parts_count, mode_count, channels)  26.6 us
    reshape x4, local copies, waits for them, and re-layouts, lat_apply(): spectrum.reshape(samples, lat_rows * parts_count, mode_count, channels)  18.6 us
    another operation x6, local copies, waits for them, and re-layouts, join_parts(): jnp.stack([real_part.reshape(merged), imag_part.reshape(merged)], axis=2)  16.5 us
    unnamed x66, local copies, waits for them, and re-layouts  12.2 us
  transfers between devices with their start and end apart: 5, of which 2 were waited for; matrix products, arithmetic and copies ran while one was open for 27% of the time, Pallas kernels for 0%

commit v1 on v0

v1 whole, which is shorter than its diff:
```python
import functools
import math

import jax
import jax.numpy as jnp
from jax import lax
from jax.experimental import pallas as pl
from jax.experimental.pallas import tpu as pltpu
from jax.sharding import PartitionSpec as P

KW = 64
shrink_level = 0.05
VMEM_BYTES = 48 * 1024 * 1024


def product_of(former, latter):
    return jnp.dot(former, latter, preferred_element_type=jnp.float32)


def lon_tables(mode_count, cell_count):
    wavenums = jnp.arange(mode_count, dtype=jnp.int32)
    columns = jnp.arange(cell_count, dtype=jnp.int32)
    phase_index = (wavenums[:, None] * columns[None, :] % cell_count).astype(jnp.float32)
    phases = phase_index * (2.0 * math.pi / cell_count)
    factor = 1.0 / math.sqrt(cell_count)
    forward = jnp.concatenate([jnp.cos(phases) * factor, -jnp.sin(phases) * factor], axis=0)
    doubling = jnp.where(wavenums == 0, 1.0, 2.0).astype(jnp.float32)
    doubling = jnp.concatenate([doubling, doubling])
    scaled = forward * doubling[:, None]
    return (forward.astype(jnp.bfloat16), scaled.astype(jnp.bfloat16))


def by_owner(table, owners):
    cells = table.shape[1]
    split = table.reshape(2, owners, -1, cells)
    return jnp.transpose(split, (1, 0, 2, 3)).reshape(-1, cells)


def lat_table(row_count):
    indices = jnp.arange(row_count, dtype=jnp.int32)
    phase_index = (indices[:, None] * indices[None, :] % row_count).astype(jnp.float32)
    phases = phase_index * (2.0 * math.pi / row_count)
    factor = 1.0 / math.sqrt(row_count)
    cosine = jnp.cos(phases) * factor
    sine_part = jnp.sin(phases) * factor
    blocks = jnp.stack(
        [jnp.stack([cosine, sine_part], axis=-1), jnp.stack([-sine_part, cosine], axis=-1)], axis=0
    )
    return blocks.astype(jnp.bfloat16)


def lat_spread(row_count, modes):
    table = lat_table(row_count)
    same = jnp.eye(modes, dtype=jnp.bfloat16)
    spread = table[:, :, None, :, :, None] * same[None, None, :, None, None, :]
    size = 2 * row_count * modes
    return spread.reshape(size, size)


def block_weights(weight, groups):
    _, count, size, _ = weight.shape
    per = count // groups
    parts = weight.reshape(2, groups, per, size, size)
    same = jnp.eye(per, dtype=weight.dtype)
    spread = parts[:, :, :, :, None, :] * same[None, None, :, None, :, None]
    joined = spread.reshape(2, groups, per * size, per * size)
    real, imag = joined[0], joined[1]
    upper = jnp.concatenate([real, imag], axis=-1)
    lower = jnp.concatenate([-imag, real], axis=-1)
    return jnp.concatenate([upper, lower], axis=-2)


def block_bias(bias, groups):
    return jnp.transpose(bias.reshape(2, groups, 1, -1), (1, 2, 0, 3)).reshape(groups, 1, -1)


def params(*semantics):
    return pltpu.CompilerParams(vmem_limit_bytes=VMEM_BYTES, dimension_semantics=semantics)


def to_modes_kernel(table_ref, cells_ref, modes_ref):
    owners, _, rows, _, channels = modes_ref.shape
    for row in range(cells_ref.shape[1]):
        spectrum = product_of(table_ref[...], cells_ref[0, row]).astype(jnp.bfloat16)
        modes_ref[:, 0, row] = spectrum.reshape(owners, -1, channels)


def to_modes(table, cells, owners):
    samples, rows, width, channels = cells.shape
    size = table.shape[0]
    shape = (owners, samples, rows, size // owners, channels)
    return pl.pallas_call(
        to_modes_kernel,
        grid=(samples,),
        out_shape=jax.ShapeDtypeStruct(shape, jnp.bfloat16),
        in_specs=[
            pl.BlockSpec((size, width), lambda b: (0, 0)),
            pl.BlockSpec((1, rows, width, channels), lambda b: (b, 0, 0, 0)),
        ],
        out_specs=pl.BlockSpec((owners, 1) + shape[2:], lambda b: (0, b, 0, 0, 0)),
        compiler_params=params("arbitrary"),
        cost_estimate=pl.CostEstimate(
            flops=2 * samples * rows * size * width * channels,
            bytes_accessed=2 * samples * rows * channels * (width + size),
            transcendentals=0,
        ),
        name="to_modes",
    )(table, cells)


def to_cells_kernel(table_ref, modes_ref, base_ref, out_ref):
    channels = modes_ref.shape[-1]
    for row in range(base_ref.shape[1]):
        spectrum = modes_ref[:, 0, row].reshape(-1, channels)
        image = product_of(table_ref[...], spectrum)
        out_ref[0, row] = (base_ref[0, row].astype(jnp.float32) + image).astype(jnp.bfloat16)


def to_cells(table, modes, base):
    samples, rows, width, channels = base.shape
    size = table.shape[1]
    block = pl.BlockSpec((1, rows, width, channels), lambda b: (b, 0, 0, 0))
    return pl.pallas_call(
        to_cells_kernel,
        grid=(samples,),
        out_shape=jax.ShapeDtypeStruct(base.shape, jnp.bfloat16),
        in_specs=[
            pl.BlockSpec((width, size), lambda b: (0, 0)),
            pl.BlockSpec((modes.shape[0], 1) + modes.shape[2:], lambda b: (0, b, 0, 0, 0)),
            block,
        ],
        out_specs=block,
        compiler_params=params("arbitrary"),
        cost_estimate=pl.CostEstimate(
            flops=2 * samples * rows * size * width * channels,
            bytes_accessed=2 * samples * rows * channels * (2 * width + size),
            transcendentals=0,
        ),
        name="to_cells",
    )(table, modes, base)


def sigmoid_of(values):
    return 0.5 + 0.5 * jnp.tanh(0.5 * values)


def mix_lat(table_ref, bands_ref, mixed_ref):
    samples, width = bands_ref.shape[1], bands_ref.shape[-1]
    half = table_ref.shape[0] // 2
    for sample in range(samples):
        bands = bands_ref[:, sample].reshape(-1, width)
        mixed = product_of(table_ref[...], bands).astype(jnp.bfloat16)
        rows = pl.ds(sample * half, half)
        mixed_ref[rows, 0:width] = mixed[:half]
        mixed_ref[rows, width : 2 * width] = mixed[half:]


def unmix_lat(table_ref, mixed_ref, bands_ref):
    samples, width = bands_ref.shape[1], bands_ref.shape[-1]
    half = table_ref.shape[0] // 2
    for sample in range(samples):
        rows = pl.ds(sample * half, half)
        joined = jnp.concatenate(
            [mixed_ref[rows, 0:width], mixed_ref[rows, width : 2 * width]], axis=0
        )
        bands = product_of(table_ref[...], joined).astype(jnp.bfloat16)
        bands_ref[:, sample] = bands.reshape(
            bands_ref.shape[0], bands_ref.shape[2], bands_ref.shape[3], width
        )


def forward_kernel(
    lat_ref, unlat_ref, bands_ref, w1_ref, b1_ref, w2_ref, b2_ref,
    image_ref, mixed_ref, act_ref, gate_ref, bend_ref, shrunk_ref,
):
    mix_lat(lat_ref, bands_ref, mixed_ref.at[0])
    pre = product_of(mixed_ref[0], w1_ref[0]) + b1_ref[0]
    logistic = sigmoid_of(pre)
    act = pre * logistic
    act_ref[0] = act.astype(jnp.bfloat16)
    gate_ref[0] = logistic + act * (1.0 - logistic)
    out = product_of(act_ref[0], w2_ref[0]) + b2_ref[0]
    bent = jnp.tanh(out * (1.0 / shrink_level))
    bend_ref[0] = bent * bent
    shrunk_ref[...] = (out - shrink_level * bent).astype(jnp.bfloat16)
    unmix_lat(unlat_ref, shrunk_ref, image_ref)


def backward_kernel(
    lat_ref, unlat_ref, bands_ref, w1_ref, w2_ref, mixed_ref, act_ref, gate_ref, bend_ref,
    image_ref, g1_ref, g2_ref, gb1_ref, gb2_ref, cot_ref, kept_ref,
):
    transposed = (((1,), (1,)), ((), ()))
    summed = (((0,), (0,)), ((), ()))

    def times(former, latter, dims):
        return lax.dot_general(former, latter, dims, preferred_element_type=jnp.float32)

    def weight_sums(acts, grads, grad_ref):
        width = acts.shape[1] // 2
        size = grad_ref.shape[-1]
        full = times(acts, grads, summed)
        real = full[:width, :width] + full[width:, width:]
        imag = full[:width, width:] - full[width:, :width]
        for block in range(grad_ref.shape[2]):
            spot = slice(block * size, (block + 1) * size)
            grad_ref[0, 0, block] = real[spot, spot]
            grad_ref[1, 0, block] = imag[spot, spot]

    mix_lat(lat_ref, bands_ref, cot_ref)
    kept_ref[...] = (cot_ref[...].astype(jnp.float32) * bend_ref[0]).astype(jnp.bfloat16)
    gb2_ref[0] = jnp.sum(kept_ref[...].astype(jnp.float32), axis=0, keepdims=True)
    back = times(kept_ref[...], w2_ref[0], transposed)
    cot_ref[...] = (back * gate_ref[0]).astype(jnp.bfloat16)
    weight_sums(act_ref[0], kept_ref[...], g2_ref)
    gb1_ref[0] = jnp.sum(cot_ref[...].astype(jnp.float32), axis=0, keepdims=True)
    kept_ref[...] = times(cot_ref[...], w1_ref[0], transposed).astype(jnp.bfloat16)
    weight_sums(mixed_ref[0], cot_ref[...], g1_ref)
    unmix_lat(unlat_ref, kept_ref, image_ref)


def group_spec(*shape):
    return pl.BlockSpec((1,) + shape, lambda g: (g,) + (0,) * len(shape))


def bands_spec(bands, groups):
    return pl.BlockSpec(bands.shape[:-1] + (bands.shape[-1] // groups,), lambda g: (0, 0, 0, 0, g))


def forward_mid(lat, unlat, bands, w1, b1, w2, b2):
    groups, lanes, _ = w1.shape
    size = lat.shape[0]
    positions = bands.shape[1] * size // 2
    table = pl.BlockSpec((size, size), lambda g: (0, 0))
    state = (groups, positions, lanes)
    state_spec = group_spec(positions, lanes)
    return pl.pallas_call(
        forward_kernel,
        grid=(groups,),
        out_shape=(
            jax.ShapeDtypeStruct(bands.shape, jnp.bfloat16),
            jax.ShapeDtypeStruct(state, jnp.bfloat16),
            jax.ShapeDtypeStruct(state, jnp.bfloat16),
            jax.ShapeDtypeStruct(state, jnp.float32),
            jax.ShapeDtypeStruct(state, jnp.float32),
        ),
        in_specs=[
            table, table, bands_spec(bands, groups),
            group_spec(lanes, lanes), group_spec(1, lanes),
            group_spec(lanes, lanes), group_spec(1, lanes),
        ],
        out_specs=(bands_spec(bands, groups),) + (state_spec,) * 4,
        scratch_shapes=[pltpu.VMEM((positions, lanes), jnp.bfloat16)],
        compiler_params=params("arbitrary"),
        cost_estimate=pl.CostEstimate(
            flops=4 * groups * positions * lanes * lanes,
            bytes_accessed=16 * groups * positions * lanes + 4 * groups * lanes * lanes,
            transcendentals=2 * groups * positions * lanes,
        ),
        name="mix_forward",
    )(lat, unlat, bands, w1, b1, w2, b2)


def backward_mid(lat, unlat, bands, w1, w2, state, count):
    groups, lanes, _ = w1.shape
    size = lat.shape[0]
    positions = bands.shape[1] * size // 2
    table = pl.BlockSpec((size, size), lambda g: (0, 0))
    state_spec = group_spec(positions, lanes)
    per = count // groups
    edge = lanes // 2 // per
    grad = jax.ShapeDtypeStruct((2, groups, per, edge, edge), jnp.float32)
    grad_spec = pl.BlockSpec((2, 1, per, edge, edge), lambda g: (0, g, 0, 0, 0))
    bias = jax.ShapeDtypeStruct((groups, 1, lanes), jnp.float32)
    return pl.pallas_call(
        backward_kernel,
        grid=(groups,),
        out_shape=(
            jax.ShapeDtypeStruct(bands.shape, jnp.bfloat16), grad, grad, bias, bias,
        ),
        in_specs=[
            table, table, bands_spec(bands, groups),
            group_spec(lanes, lanes), group_spec(lanes, lanes),
        ] + [state_spec] * 4,
        out_specs=(
            bands_spec(bands, groups), grad_spec, grad_spec,
            group_spec(1, lanes), group_spec(1, lanes),
        ),
        scratch_shapes=[pltpu.VMEM((positions, lanes), jnp.bfloat16)] * 2,
        compiler_params=params("arbitrary"),
        cost_estimate=pl.CostEstimate(
            flops=8 * groups * positions * lanes * lanes,
            bytes_accessed=16 * groups * positions * lanes + 4 * groups * lanes * lanes,
            transcendentals=0,
        ),
        name="mix_backward",
    )(lat, unlat, bands, w1, w2, *state)


def body(fields, cotangent, w_first, b_first, w_second, b_second):
    samples, rows, width, channels = fields.shape
    owners = lax.axis_size("space")
    lat_total = rows * owners
    modes = KW // owners
    count = w_first.shape[1]
    groups = 2
    direct = 2 * modes % 16 == 0
    lead = owners if direct else 1
    share = (owners, samples, rows, 2 * modes, channels)

    def send_out(spectrum):
        if not direct:
            spectrum = spectrum.reshape(samples, rows, owners, 2 * modes, channels)
            spectrum = jnp.transpose(spectrum, (2, 0, 1, 3, 4))
        arrived = lax.all_to_all(spectrum, "space", split_axis=0, concat_axis=0, tiled=True)
        if not direct:
            arrived = jnp.transpose(arrived, (1, 0, 2, 3, 4)).reshape(1, samples, 1, -1, channels)
        return arrived

    def send_back(bands):
        if not direct:
            bands = bands.reshape(samples, owners, rows, 2 * modes, channels)
            bands = jnp.transpose(bands, (1, 0, 2, 3, 4))
        arrived = lax.all_to_all(bands, "space", split_axis=0, concat_axis=0, tiled=True)
        if not direct:
            arrived = jnp.transpose(arrived, (1, 2, 0, 3, 4)).reshape(1, samples, rows, -1, channels)
        return arrived

    plain, scaled = lon_tables(KW, width)
    plain, scaled = by_owner(plain, owners), by_owner(scaled, owners)
    spectrum = to_modes(plain, fields, lead)
    spectrum, cotangent, scaled, w_first, w_second = lax.optimization_barrier(
        (spectrum, cotangent, scaled, w_first, w_second)
    )
    gathered = send_out(spectrum)
    cot_spec = to_modes(scaled, cotangent, lead)
    cot_gathered = send_out(cot_spec)

    lat = lat_spread(lat_total, modes)
    unlat = jnp.transpose(lat)
    w1, w2 = block_weights(w_first, groups), block_weights(w_second, groups)
    b1, b2 = block_bias(b_first, groups), block_bias(b_second, groups)
    image, *state = forward_mid(lat, unlat, gathered, w1, b1, w2, b2)
    image_band = send_back(image)
    grad_image, sum_w_first, sum_w_second, sum_b_first, sum_b_second = backward_mid(
        lat, unlat, cot_gathered, w1, w2, state, count
    )
    grad_band = send_back(grad_image)
    output = to_cells(jnp.transpose(scaled), image_band, fields)
    grad_fields = to_cells(jnp.transpose(plain), grad_band, cotangent)

    def bias_of(sums):
        split = sums.reshape(groups, 2, count // groups, -1)
        return jnp.transpose(split, (1, 0, 2, 3)).reshape(b_first.shape)

    sums = lax.psum(
        (
            sum_w_first.reshape(w_first.shape), bias_of(sum_b_first),
            sum_w_second.reshape(w_first.shape), bias_of(sum_b_second),
        ),
        ("space", "dp"),
    )
    positions = samples * lax.axis_size("dp") * lat_total * KW
    factor = 1.0 / math.sqrt(positions)
    return (output, grad_fields) + tuple(value * factor for value in sums)


def solution(mesh):
    split = P(("parts", "dp"), "space", None, None)
    in_specs = (split, split, P(), P(), P(), P())
    out_specs = (
        split,
        split,
        P("parts", None, None, None),
        P("parts", None, None),
        P("parts", None, None, None),
        P("parts", None, None),
    )
    return jax.shard_map(body, mesh=mesh, in_specs=in_specs, out_specs=out_specs, check_vma=False)
```

time: 381 us -> 288 us (0.76); the launches traced: 374 us -> 287 us
  local copies, waits for them, and re-layouts: 126 us -> 36 us
  matrix products: 53.1 us -> 0 us
  Pallas kernels: 0 us -> 27.4 us
  waiting for transfers between devices: 62.2 us -> 84.7 us
  blocking collectives: 77.7 us -> 84.7 us
    dot_general x32 -> x0, matrix products: 53.1 us -> none  [product_of(): jnp.einsum(pattern, former, latter, preferred_element_type=jnp.float32)]
    reshape x12 -> x9, local copies, waits for them, and re-layouts: 50.7 us -> 0.48 us  [the longest x2 0.17 us: bias_of(): split = sums.reshape(groups, 2, count // groups, -1)]
    pallas_call x0 -> x6, Pallas kernels: none -> 27.4 us  [the longest x1 10.8 us: backward_mid(): pl.pallas_call(backward_kernel, grid=(groups,), out_shape=(jax.ShapeDtype...]
    all_to_all x4, waiting for transfers between devices: 33.3 us -> 57.2 us  [the longest x2 32.9 us: send_out(): lax.all_to_all(spectrum, 'space', split_axis=0, concat_axis=0, tiled=True)]
    another operation x8 -> x0, local copies, waits for them, and re-layouts: 22.3 us -> none  [the longest x6 16.5 us: join_parts(): jnp.stack([real_part.reshape(merged), imag_part.reshape(merged)], axis=2)]
    convert_element_type x8 -> x0, local copies, waits for them, and re-layouts: 13.2 us -> none  [the longest x1 3.22 us: shrink_back(): grad_imag.astype(jnp.float32) * shrink_slope(out_imag)]
    all_to_all x4 -> x0, local copies, waits for them, and re-layouts: 11.7 us -> none  [the longest x1 4.19 us: body(): lax.all_to_all(spectrum, 'space', split_axis=3, concat_axis=1, tiled=True)]
    slice x2, local copies, waits for them, and re-layouts: 15.1 us -> 4.68 us  [block_weights(): real, imag = (joined[0], joined[1])]
  transfers between devices with their start and end apart: 5 -> 5, of which waited for: 2 -> 3; matrix products, arithmetic and copies ran while one was open for 27% -> 14% of each run, Pallas kernels for 0% -> 8%
where the time goes in v1:
time: 288 us; the launch traced here: 287 us
  waiting for transfers between devices  84.7 us (29%)
  blocking collectives  84.7 us (29%)
  local copies, waits for them, and re-layouts  36 us (12%)
  Pallas kernels  27.4 us (10%)
  starting transfers between devices  21.8 us (8%)
  other arithmetic  18.1 us (6%)
  between operations  14.3 us (5%)
    psum x1, blocking collectives, body(): lax.psum((sum_w_first.reshape(w_first.shape), bias_of(sum_b_first), sum_w...  84.7 us
    all_to_all x2, waiting for transfers between devices, send_out(): lax.all_to_all(spectrum, 'space', split_axis=0, concat_axis=0, tiled=True)  32.9 us
    psum x1, waiting for transfers between devices, body(): lax.psum((sum_w_first.reshape(w_first.shape), bias_of(sum_b_first), sum_w...  26.9 us
    all_to_all x2, waiting for transfers between devices, send_back(): lax.all_to_all(bands, 'space', split_axis=0, concat_axis=0, tiled=True)  24.3 us
    unnamed x33, local copies, waits for them, and re-layouts  16.4 us
    all_to_all x2, starting transfers between devices, send_out(): lax.all_to_all(spectrum, 'space', split_axis=0, concat_axis=0, tiled=True)  11.6 us
    pallas_call x1, Pallas kernels, backward_mid(): pl.pallas_call(backward_kernel, grid=(groups,), out_shape=(jax.ShapeDtype...  10.8 us
    all_to_all x2, starting transfers between devices, send_back(): lax.all_to_all(bands, 'space', split_axis=0, concat_axis=0, tiled=True)  10.2 us
  transfers between devices with their start and end apart: 5, of which 3 were waited for; matrix products, arithmetic and copies ran while one was open for 14% of the time, Pallas kernels for 8%

profile of v1, /device:TPU:0, one launch (start us, length us, event | category | flops | bytes accessed | tf_op | source)
XLA Modules:
  0.0 287.0 jit_solution(12001623802573297912)
XLA Ops:
  7.6 1.9 copy.29.cells_ref.base_ref
  13.3 7.3 %all-to-all-start = ((bf16[8,4,2,16,768]{4,3,2,1,0:T(8,128)(2,1)}), bf16[8,4,2,16,768]{4,3,2,1,0:T(8,128)(2,1)}, u32[]{:S(2)}, u32[]{:S(2)}) async-start(bf16[8,4,2,16,768]{4,3,2,1,0:T(8,128)(2,1)} %copy-done.3), calls=%async_computation | async-start | bytes 3145728 | tf_op jit(solution)/shard_map/all_to_all | solution.py:315
  24.8 32.9 %all-to-all-done.bands_ref = bf16[8,4,2,16,768]{4,3,2,1,0:T(8,128)(2,1)} async-done(((bf16[8,4,2,16,768]{4,3,2,1,0:T(8,128)(2,1)}), bf16[8,4,2,16,768]{4,3,2,1,0:T(8,128)(2,1)}, u32[]{:S(2)}, u32[]{:S(2)}) %all-to-all-start) | async-done | bytes 1572896 | tf_op jit(solution)/shard_map/all_to_all | solution.py:315
  57.7 4.3 %all-to-all-start.2 = ((bf16[8,4,2,16,768]{4,3,2,1,0:T(8,128)(2,1)}), bf16[8,4,2,16,768]{4,3,2,1,0:T(8,128)(2,1)}, u32[]{:S(2)}, u32[]{:S(2)}) async-start(bf16[8,4,2,16,768]{4,3,2,1,0:T(8,128)(2,1)} %copy-done.2), calls=%async_computation.2 | async-start | bytes 3145728 | tf_op jit(solution)/shard_map/all_to_all | solution.py:315
  63.8 4.1 %mul.221 = bf16[256,256]{0,1:T(8,128)(2,1)S(1)} reshape(bf16[2,16,8,16,2,8]{2,1,0,5,4,3:T(8,128)(2,1)} %broadcast_multiply_fusion) | data formatting | bytes 262144 | tf_op jit(solution)/shard_map/mul | solution.py:55
  68.0 2.6 broadcast_multiply_fusion.1
  76.5 3.1 %fusion.16 = (bf16[1,2,4,96,4,96]{5,4,3,2,1,0:T(4,128)(2,1)}, bf16[1,2,4,96,4,96]{5,4,3,2,1,0:T(4,128)(2,1)}) fusion(bf16[2,2,4,96,4,96]{5,4,3,2,1,0:T(4,128)(2,1)} %get-tuple-element.60), kind=kLoop, calls=%fused_computation.47 | loop fusion | bytes 2359296 | tf_op jit(solution)/shard_map/slice | solution.py:67
  79.6 2.5 squeeze.14
  82.0 2.5 squeeze.15
  84.5 2.0 neg.22
  86.6 3.2 %maximum_maximum_fusion.w1_ref = bf16[2,768,768]{2,1,0:T(8,128)(2,1)} fusion(bf16[2,384,384]{2,1,0:T(8,128)(2,1)} %squeeze.12, bf16[2,384,384]{2,1,0:T(8,128)(2,1)} %neg.21, bf16[2,384,384]{2,1,0:T(8,128)(2,1)S(1)} %squeeze.13), kind=kLoop, calls=%fused_computation | loop fusion | flops 9437184 | bytes 4128768 | tf_op jit(solution)/shard_map/concatenate | solution.py:70
  91.5 8.4 %mix_forward.1 = (bf16[8,4,2,16,768]{4,3,2,1,0:T(8,128)(2,1)S(1)}, bf16[2,512,768]{2,1,0:T(8,128)(2,1)S(1)}, bf16[2,512,768]{2,1,0:T(8,128)(2,1)S(1)}, f32[2,512,768]{2,1,0:T(8,128)}, f32[2,512,768]{2,1,0:T(8,128)}) custom-call(bf16[256,256]{1,0:T(8,128)(2,1)S(1)} %copy.34.lat_ref, bf16[256,256]{1,0:T(8,128)(2,1)S(1)} %bitcast.40, ...), custom_call_target="tpu_custom_call" | custom-call | flops 2415919104 | bytes 17301504 | tf_op jit(solution)/shard_map/mix_forward/pallas_call | solution.py:237
  103.3 5.9 %all-to-all-start.1 = ((bf16[8,4,2,16,768]{4,3,2,1,0:T(8,128)(2,1)}), bf16[8,4,2,16,768]{4,3,2,1,0:T(8,128)(2,1)}, u32[]{:S(2)}, u32[]{:S(2)}) async-start(bf16[8,4,2,16,768]{4,3,2,1,0:T(8,128)(2,1)} %copy-done.5), calls=%async_computation.1 | async-start | bytes 3145728 | tf_op jit(solution)/shard_map/all_to_all | solution.py:324
  109.2 10.8 %mix_backward.1 = (bf16[8,4,2,16,768]{4,3,2,1,0:T(8,128)(2,1)S(1)}, f32[2,2,4,96,96]{4,3,2,1,0:T(8,128)}, f32[2,2,4,96,96]{4,3,2,1,0:T(8,128)}, f32[2,1,768]{2,1,0:T(1,128)S(1)}, f32[2,1,768]{2,1,0:T(1,128)S(1)}) custom-call(bf16[256,256]{1,0:T(8,128)(2,1)S(1)} %copy.34.lat_ref, bf16[256,256]{1,0:T(8,128)(2,1)S(1)} %bitcast.41, ...), custom_call_target="tpu_custom_call" | custom-call | flops 4831838208 | bytes 17301504 | tf_op jit(solution)/shard_map/mix_backward/pallas_call | solution.py:275
  121.2 24.3 %all-to-all-done.1.modes_ref = bf16[8,4,2,16,768]{4,3,2,1,0:T(8,128)(2,1)} async-done(((bf16[8,4,2,16,768]{4,3,2,1,0:T(8,128)(2,1)}), bf16[8,4,2,16,768]{4,3,2,1,0:T(8,128)(2,1)}, u32[]{:S(2)}, u32[]{:S(2)}) %all-to-all-start.1) | async-done | bytes 1572896 | tf_op jit(solution)/shard_map/all_to_all | solution.py:324
  145.5 4.3 %all-to-all-start.3 = ((bf16[8,4,2,16,768]{4,3,2,1,0:T(8,128)(2,1)}), bf16[8,4,2,16,768]{4,3,2,1,0:T(8,128)(2,1)}, u32[]{:S(2)}, u32[]{:S(2)}) async-start(bf16[8,4,2,16,768]{4,3,2,1,0:T(8,128)(2,1)} %copy-done.4), calls=%async_computation.3 | async-start | bytes 3145728 | tf_op jit(solution)/shard_map/all_to_all | solution.py:324
  151.0 84.7 %all-reduce = (f32[2,8,96]{2,1,0:T(8,128)S(1)}, f32[2,8,96]{2,1,0:T(8,128)S(1)}) all-reduce(f32[2,8,96]{2,1,0:T(8,128)S(1)} %bitcast.48, f32[2,8,96]{2,1,0:T(8,128)S(1)} %bitcast.49), channel_id=1, replica_groups=mesh['parts'=2,'space'=8,'dp'=2] {'space','dp'}, use_global_device_ids=true, to_apply=%region_1.2 | all-reduce | flops 3072 | bytes 24576 | tf_op jit(solution)/shard_map/psum | solution.py:356
  236.9 26.9 %all-reduce.4.cloned.1.call-done = (f32[2,8,96,96]{3,2,1,0:T(8,128)}, f32[2,8,96,96]{3,2,1,0:T(8,128)}) async-done(((f32[2,8,96,96]{3,2,1,0:T(8,128)}, f32[2,8,96,96]{3,2,1,0:T(8,128)}), (f32[2,8,96,96]{3,2,1,0:T(8,128)}, f32[2,8,96,96]{3,2,1,0:T(8,128)})) %all-reduce.4.cloned.1.call-update) | async-done | bytes 1179664 | tf_op jit(solution)/shard_map/psum | solution.py:356
  263.8 2.2 broadcast_multiply_fusion.4
  266.0 2.1 broadcast_multiply_fusion.3
  268.1 3.0 %to_cells.2 = bf16[4,2,180,768]{3,2,1,0:T(8,128)(2,1)S(1)} custom-call(bf16[180,128]{1,0:T(8,128)(2,1)S(1)} %copy.35.table_ref, bf16[8,4,2,16,768]{4,3,2,1,0:T(8,128)(2,1)} %all-to-all-done.1.modes_ref, bf16[4,2,180,768]{3,2,1,0:T(8,128)(2,1)S(1)} %copy-done.1), custom_call_target="tpu_custom_call" | custom-call | flops 283115520 | bytes 5996544 | tf_op jit(solution)/shard_map/to_cells/pallas_call | solution.py:123
  271.1 3.1 %copy.43 = bf16[4,2,180,768]{3,1,2,0:T(2,128)(2,1)} copy(bf16[4,2,180,768]{3,2,1,0:T(8,128)(2,1)S(1)} %to_cells.2) | data formatting | bytes 4423680
  274.1 3.0 %to_cells.3 = bf16[4,2,180,768]{3,2,1,0:T(8,128)(2,1)S(1)} custom-call(bf16[180,128]{1,0:T(8,128)(2,1)S(1)} %bitcast.42, bf16[8,4,2,16,768]{4,3,2,1,0:T(8,128)(2,1)} %all-to-all-done.3.modes_ref, bf16[4,2,180,768]{3,2,1,0:T(8,128)(2,1)S(1)} %copy.38.cells_ref.base_ref), custom_call_target="tpu_custom_call" | custom-call | flops 283115520 | bytes 5996544 | tf_op jit(solution)/shard_map/to_cells/pallas_call | solution.py:123
  277.1 3.1 %copy.44 = bf16[4,2,180,768]{3,1,2,0:T(2,128)(2,1)} copy(bf16[4,2,180,768]{3,2,1,0:T(8,128)(2,1)S(1)} %to_cells.3) | data formatting | bytes 4423680
  (74 shorter events, 24.8 us)
Async XLA Ops:
  10.7 1.5 copy-start
  12.2 1.1 copy-start.3
  13.3 44.4 %all-to-all-start = ((bf16[8,4,2,16,768]{4,3,2,1,0:T(8,128)(2,1)}), bf16[8,4,2,16,768]{4,3,2,1,0:T(8,128)(2,1)}, u32[]{:S(2)}, u32[]{:S(2)}) async-start(bf16[8,4,2,16,768]{4,3,2,1,0:T(8,128)(2,1)} %copy-done.3), calls=%async_computation | async-start | bytes 3145728 | tf_op jit(solution)/shard_map/all_to_all | solution.py:315
  23.7 1.1 copy-start.2
  57.7 45.6 %all-to-all-start.2 = ((bf16[8,4,2,16,768]{4,3,2,1,0:T(8,128)(2,1)}), bf16[8,4,2,16,768]{4,3,2,1,0:T(8,128)(2,1)}, u32[]{:S(2)}, u32[]{:S(2)}) async-start(bf16[8,4,2,16,768]{4,3,2,1,0:T(8,128)(2,1)} %copy-done.2), calls=%async_computation.2 | async-start | bytes 3145728 | tf_op jit(solution)/shard_map/all_to_all | solution.py:315
  62.3 5.7 %copy-start.11 = (bf16[2,8,96,96]{3,2,1,0:T(8,128)(2,1)S(1)}, bf16[2,8,96,96]{3,2,1,0:T(8,128)(2,1)}, u32[]{:S(2)}) copy-start(bf16[2,8,96,96]{3,2,1,0:T(8,128)(2,1)} %param.10) | copy-start | bytes 884740
  62.3 5.7 %copy-start.12 = (bf16[2,8,96,96]{3,2,1,0:T(8,128)(2,1)S(1)}, bf16[2,8,96,96]{3,2,1,0:T(8,128)(2,1)}, u32[]{:S(2)}) copy-start(bf16[2,8,96,96]{3,2,1,0:T(8,128)(2,1)} %param.8) | copy-start | bytes 884740
  72.2 4.1 %copy-start.13 = (f32[2,8,96]{2,1,0:T(8,128)S(1)}, f32[2,8,96]{2,1,0:T(8,128)}, u32[]{:S(2)}) copy-start(f32[2,8,96]{2,1,0:T(8,128)} %param.9) | copy-start | bytes 18436
  79.6 6.9 %copy-start.14 = (f32[2,8,96]{2,1,0:T(8,128)S(1)}, f32[2,8,96]{2,1,0:T(8,128)}, u32[]{:S(2)}) copy-start(f32[2,8,96]{2,1,0:T(8,128)} %param.11) | copy-start | bytes 18436
  86.6 3.3 %copy-start.8 = (bf16[2,384,384]{2,1,0:T(8,128)(2,1)S(1)}, bf16[2,384,384]{2,1,0:T(8,128)(2,1)}, u32[]{:S(2)}) copy-start(bf16[2,384,384]{2,1,0:T(8,128)(2,1)} %squeeze.15) | copy-start | bytes 1769476
  86.6 3.3 %copy-start.9 = (bf16[2,384,384]{2,1,0:T(8,128)(2,1)S(1)}, bf16[2,384,384]{2,1,0:T(8,128)(2,1)}, u32[]{:S(2)}) copy-start(bf16[2,384,384]{2,1,0:T(8,128)(2,1)} %neg.22) | copy-start | bytes 1769476
  86.6 3.2 %copy-start.10 = (bf16[2,384,384]{2,1,0:T(8,128)(2,1)S(1)}, bf16[2,384,384]{2,1,0:T(8,128)(2,1)}, u32[]{:S(2)}) copy-start(bf16[2,384,384]{2,1,0:T(8,128)(2,1)} %squeeze.14) | copy-start | bytes 1769476
  99.9 1.1 copy-start.5
  101.0 1.2 copy-start.6
  102.2 1.2 copy-start.7
  103.3 42.2 %all-to-all-start.1 = ((bf16[8,4,2,16,768]{4,3,2,1,0:T(8,128)(2,1)}), bf16[8,4,2,16,768]{4,3,2,1,0:T(8,128)(2,1)}, u32[]{:S(2)}, u32[]{:S(2)}) async-start(bf16[8,4,2,16,768]{4,3,2,1,0:T(8,128)(2,1)} %copy-done.5), calls=%async_computation.1 | async-start | bytes 3145728 | tf_op jit(solution)/shard_map/all_to_all | solution.py:324
  120.1 1.1 copy-start.4
  145.5 128.6 %all-to-all-start.3 = ((bf16[8,4,2,16,768]{4,3,2,1,0:T(8,128)(2,1)}), bf16[8,4,2,16,768]{4,3,2,1,0:T(8,128)(2,1)}, u32[]{:S(2)}, u32[]{:S(2)}) async-start(bf16[8,4,2,16,768]{4,3,2,1,0:T(8,128)(2,1)} %copy-done.4), calls=%async_computation.3 | async-start | bytes 3145728 | tf_op jit(solution)/shard_map/all_to_all | solution.py:324
  149.8 114.0 %all-reduce.4.cloned.1.call-start = ((), (), s32[]{:S(2)}) async-start(), calls=%async_computation.4 | async-start | bytes 3145728 | tf_op jit(solution)/shard_map/psum | solution.py:356
  263.8 4.3 %copy-start.1 = (bf16[4,2,180,768]{3,2,1,0:T(8,128)(2,1)S(1)}, bf16[4,2,180,768]{3,2,1,0:T(8,128)(2,1)}, u32[]{:S(2)}) copy-start(bf16[4,2,180,768]{3,2,1,0:T(8,128)(2,1)} %copy-done) | copy-start | bytes 6635524
Sparse Core Ops, SparseCore 0:
  154.8 108.9 all-reduce.3

commit v2 on v1

--- a/solution.py
+++ b/solution.py
@@ -7,6 +7,8 @@
 from jax.experimental import pallas as pl
 from jax.experimental.pallas import tpu as pltpu
 from jax.sharding import PartitionSpec as P
+import ml_dtypes
+import numpy as np
 
 KW = 64
 shrink_level = 0.05
@@ -17,61 +19,78 @@
     return jnp.dot(former, latter, preferred_element_type=jnp.float32)
 
 
-def lon_tables(mode_count, cell_count):
-    wavenums = jnp.arange(mode_count, dtype=jnp.int32)
-    columns = jnp.arange(cell_count, dtype=jnp.int32)
-    phase_index = (wavenums[:, None] * columns[None, :] % cell_count).astype(jnp.float32)
-    phases = phase_index * (2.0 * math.pi / cell_count)
-    factor = 1.0 / math.sqrt(cell_count)
-    forward = jnp.concatenate([jnp.cos(phases) * factor, -jnp.sin(phases) * factor], axis=0)
-    doubling = jnp.where(wavenums == 0, 1.0, 2.0).astype(jnp.float32)
-    doubling = jnp.concatenate([doubling, doubling])
-    scaled = forward * doubling[:, None]
-    return (forward.astype(jnp.bfloat16), scaled.astype(jnp.bfloat16))
-
-
-def by_owner(table, owners):
-    cells = table.shape[1]
-    split = table.reshape(2, owners, -1, cells)
-    return jnp.transpose(split, (1, 0, 2, 3)).reshape(-1, cells)
-
-
-def lat_table(row_count):
-    indices = jnp.arange(row_count, dtype=jnp.int32)
-    phase_index = (indices[:, None] * indices[None, :] % row_count).astype(jnp.float32)
-    phases = phase_index * (2.0 * math.pi / row_count)
-    factor = 1.0 / math.sqrt(row_count)
-    cosine = jnp.cos(phases) * factor
-    sine_part = jnp.sin(phases) * factor
-    blocks = jnp.stack(
-        [jnp.stack([cosine, sine_part], axis=-1), jnp.stack([-sine_part, cosine], axis=-1)], axis=0
-    )
-    return blocks.astype(jnp.bfloat16)
+def lon_tables(mode_count, cell_count, owners):
+    wavenums = np.arange(mode_count, dtype=np.int32)
+    columns = np.arange(cell_count, dtype=np.int32)
+    phase_index = (wavenums[:, None] * columns[None, :] % cell_count).astype(np.float32)
+    phases = phase_index * np.float32(2.0 * math.pi / cell_count)
+    factor = np.float32(1.0 / math.sqrt(cell_count))
+    forward = np.stack([np.cos(phases) * factor, -np.sin(phases) * factor])
+    scaled = forward * np.where(wavenums == 0, 1.0, 2.0).astype(np.float32)[:, None]
+
+    def ordered(table):
+        split = table.reshape(2, owners, -1, cell_count).transpose(1, 0, 2, 3)
+        return split.reshape(-1, cell_count).astype(ml_dtypes.bfloat16)
+
+    return ordered(forward), ordered(scaled)
 
 
 def lat_spread(row_count, modes):
-    table = lat_table(row_count)
-    same = jnp.eye(modes, dtype=jnp.bfloat16)
+    indices = np.arange(row_count, dtype=np.int32)
+    phase_index = (indices[:, None] * indices[None, :] % row_count).astype(np.float32)
+    phases = phase_index * np.float32(2.0 * math.pi / row_count)
+    factor = np.float32(1.0 / math.sqrt(row_count))
+    cosine = np.cos(phases) * factor
+    sine_part = np.sin(phases) * factor
+    table = np.stack([np.stack([cosine, sine_part], -1), np.stack([-sine_part, cosine], -1)])
+    same = np.eye(modes, dtype=np.float32)
     spread = table[:, :, None, :, :, None] * same[None, None, :, None, None, :]
     size = 2 * row_count * modes
-    return spread.reshape(size, size)
-
-
-def block_weights(weight, groups):
-    _, count, size, _ = weight.shape
-    per = count // groups
-    parts = weight.reshape(2, groups, per, size, size)
-    same = jnp.eye(per, dtype=weight.dtype)
-    spread = parts[:, :, :, :, None, :] * same[None, None, :, None, :, None]
-    joined = spread.reshape(2, groups, per * size, per * size)
-    real, imag = joined[0], joined[1]
-    upper = jnp.concatenate([real, imag], axis=-1)
-    lower = jnp.concatenate([-imag, real], axis=-1)
-    return jnp.concatenate([upper, lower], axis=-2)
+    return spread.reshape(size, size).astype(ml_dtypes.bfloat16)
 
 
 def block_bias(bias, groups):
     return jnp.transpose(bias.reshape(2, groups, 1, -1), (1, 2, 0, 3)).reshape(groups, 1, -1)
+
+
+def spread_kernel(*refs):
+    half_way = len(refs) // 2
+    for blocks_ref, joined_ref in zip(refs[:half_way], refs[half_way:]):
+        _, per, size, _ = blocks_ref.shape
+        width = per * size
+        row = lax.broadcasted_iota(jnp.int32, (size, width), 0)
+        lane = lax.broadcasted_iota(jnp.int32, (size, width), 1)
+        for block in range(per):
+            place = (row + block * size == lane).astype(jnp.bfloat16)
+            real = product_of(blocks_ref[0, block], place).astype(jnp.bfloat16)
+            imag = product_of(blocks_ref[1, block], place)
+            upper = pl.ds(block * size, size)
+            lower = pl.ds(width + block * size, size)
+            joined_ref[0, upper, 0:width] = real
+            joined_ref[0, upper, width : 2 * width] = imag.astype(jnp.bfloat16)
+            joined_ref[0, lower, 0:width] = (-imag).astype(jnp.bfloat16)
+            joined_ref[0, lower, width : 2 * width] = real
+
+
+def spread_weights(groups, *weights):
+    _, count, size, _ = weights[0].shape
+    per = count // groups
+    lanes = 2 * per * size
+    shape = jax.ShapeDtypeStruct((groups, lanes, lanes), jnp.bfloat16)
+    return pl.pallas_call(
+        spread_kernel,
+        grid=(groups,),
+        out_shape=(shape,) * len(weights),
+        in_specs=[pl.BlockSpec((2, per, size, size), lambda g: (0, g, 0, 0))] * len(weights),
+        out_specs=(group_spec(lanes, lanes),) * len(weights),
+        compiler_params=params("arbitrary"),
+        cost_estimate=pl.CostEstimate(
+            flops=len(weights) * 2 * count * size * size * lanes,
+            bytes_accessed=len(weights) * 2 * groups * lanes * lanes,
+            transcendentals=0,
+        ),
+        name="spread_weights",
+    )(*weights)
 
 
 def params(*semantics):
@@ -187,8 +206,8 @@
 
 
 def backward_kernel(
-    lat_ref, unlat_ref, bands_ref, w1_ref, w2_ref, mixed_ref, act_ref, gate_ref, bend_ref,
-    image_ref, g1_ref, g2_ref, gb1_ref, gb2_ref, cot_ref, kept_ref,
+    block_size, lat_ref, unlat_ref, bands_ref, w1_ref, w2_ref, mixed_ref, act_ref, gate_ref, bend_ref,
+    image_ref, sums_ref, cot_ref, kept_ref,
 ):
     transposed = (((1,), (1,)), ((), ()))
     summed = (((0,), (0,)), ((), ()))
@@ -196,26 +215,31 @@
     def times(former, latter, dims):
         return lax.dot_general(former, latter, dims, preferred_element_type=jnp.float32)
 
-    def weight_sums(acts, grads, grad_ref):
+    def weight_sums(acts, grads, slot):
         width = acts.shape[1] // 2
-        size = grad_ref.shape[-1]
         full = times(acts, grads, summed)
         real = full[:width, :width] + full[width:, width:]
         imag = full[:width, width:] - full[width:, :width]
-        for block in range(grad_ref.shape[2]):
-            spot = slice(block * size, (block + 1) * size)
-            grad_ref[0, 0, block] = real[spot, spot]
-            grad_ref[1, 0, block] = imag[spot, spot]
+        bias = jnp.sum(grads.astype(jnp.float32), axis=0, keepdims=True)
+        size = block_size
+        owner = lax.broadcasted_iota(jnp.int32, (size, width), 1) // size
+        extra = sums_ref.shape[3] - size
+        first = lax.broadcasted_iota(jnp.int32, (extra, width), 0) == 0
+        for part, values in enumerate((real, imag)):
+            joined = values[:size]
+            for block in range(1, width // size):
+                joined = jnp.where(owner == block, values[block * size : (block + 1) * size], joined)
+            sums_ref[slot, part, 0, 0:size] = joined
+            row = bias[:, part * width : (part + 1) * width]
+            sums_ref[slot, part, 0, size:] = jnp.where(first, row, 0.0)
 
     mix_lat(lat_ref, bands_ref, cot_ref)
     kept_ref[...] = (cot_ref[...].astype(jnp.float32) * bend_ref[0]).astype(jnp.bfloat16)
-    gb2_ref[0] = jnp.sum(kept_ref[...].astype(jnp.float32), axis=0, keepdims=True)
     back = times(kept_ref[...], w2_ref[0], transposed)
     cot_ref[...] = (back * gate_ref[0]).astype(jnp.bfloat16)
-    weight_sums(act_ref[0], kept_ref[...], g2_ref)
-    gb1_ref[0] = jnp.sum(cot_ref[...].astype(jnp.float32), axis=0, keepdims=True)
+    weight_sums(act_ref[0], kept_ref[...], 1)
     kept_ref[...] = times(cot_ref[...], w1_ref[0], transposed).astype(jnp.bfloat16)
-    weight_sums(mixed_ref[0], cot_ref[...], g1_ref)
+    weight_sums(mixed_ref[0], cot_ref[...], 0)
     unmix_lat(unlat_ref, kept_ref, image_ref)
 
 
@@ -267,24 +291,22 @@
     positions = bands.shape[1] * size // 2
     table = pl.BlockSpec((size, size), lambda g: (0, 0))
     state_spec = group_spec(positions, lanes)
-    per = count // groups
-    edge = lanes // 2 // per
-    grad = jax.ShapeDtypeStruct((2, groups, per, edge, edge), jnp.float32)
-    grad_spec = pl.BlockSpec((2, 1, per, edge, edge), lambda g: (0, g, 0, 0, 0))
-    bias = jax.ShapeDtypeStruct((groups, 1, lanes), jnp.float32)
+    size_of_block = lanes // 2 // (count // groups)
+    rows = size_of_block + 16
     return pl.pallas_call(
-        backward_kernel,
+        functools.partial(backward_kernel, size_of_block),
         grid=(groups,),
         out_shape=(
-            jax.ShapeDtypeStruct(bands.shape, jnp.bfloat16), grad, grad, bias, bias,
+            jax.ShapeDtypeStruct(bands.shape, jnp.bfloat16),
+            jax.ShapeDtypeStruct((2, 2, groups, rows, lanes // 2), jnp.float32),
         ),
         in_specs=[
             table, table, bands_spec(bands, groups),
             group_spec(lanes, lanes), group_spec(lanes, lanes),
         ] + [state_spec] * 4,
         out_specs=(
-            bands_spec(bands, groups), grad_spec, grad_spec,
-            group_spec(1, lanes), group_spec(1, lanes),
+            bands_spec(bands, groups),
+            pl.BlockSpec((2, 2, 1, rows, lanes // 2), lambda g: (0, 0, g, 0, 0)),
         ),
         scratch_shapes=[pltpu.VMEM((positions, lanes), jnp.bfloat16)] * 2,
         compiler_params=params("arbitrary"),
@@ -297,16 +319,44 @@
     )(lat, unlat, bands, w1, w2, *state)
 
 
+def swap_with(values, axis, distance):
+    size = lax.axis_size(axis)
+    return lax.ppermute(values, axis, [(i, i ^ distance) for i in range(size)])
+
+
+def summed_over_group(sums):
+    lanes = sums.shape[-1]
+    held = sums.reshape(-1, lanes)
+    steps = [("dp", 1, jnp.float32)]
+    distance = 1
+    while distance < lax.axis_size("space"):
+        steps.append(("space", distance, jnp.float32 if distance == 1 else jnp.bfloat16))
+        distance *= 2
+    for axis, distance, kind in steps:
+        side = lax.axis_index(axis) // distance % 2
+        pair = held.reshape(2, -1, lanes)
+        given = lax.dynamic_index_in_dim(pair, 1 - side, 0, keepdims=False).astype(kind)
+        taken = swap_with(given, axis, distance)
+        held = lax.dynamic_index_in_dim(pair, side, 0, keepdims=False) + taken.astype(jnp.float32)
+    held = held.astype(jnp.bfloat16)
+    for axis, distance, _ in reversed(steps):
+        side = lax.axis_index(axis) // distance % 2
+        taken = swap_with(held, axis, distance)
+        held = jnp.where(
+            side == 0, jnp.concatenate([held, taken]), jnp.concatenate([taken, held])
+        )
+    return held.reshape(sums.shape)
+
+
 def body(fields, cotangent, w_first, b_first, w_second, b_second):
     samples, rows, width, channels = fields.shape
     owners = lax.axis_size("space")
     lat_total = rows * owners
     modes = KW // owners
-    count = w_first.shape[1]
+    count, edge = w_first.shape[1:3]
     groups = 2
     direct = 2 * modes % 16 == 0
     lead = owners if direct else 1
-    share = (owners, samples, rows, 2 * modes, channels)
 
     def send_out(spectrum):
         if not direct:
@@ -326,43 +376,36 @@
             arrived = jnp.transpose(arrived, (1, 2, 0, 3, 4)).reshape(1, samples, rows, -1, channels)
         return arrived
 
-    plain, scaled = lon_tables(KW, width)
-    plain, scaled = by_owner(plain, owners), by_owner(scaled, owners)
+    plain, scaled = lon_tables(KW, width, owners)
+    lat = lat_spread(lat_total, modes)
+
     spectrum = to_modes(plain, fields, lead)
-    spectrum, cotangent, scaled, w_first, w_second = lax.optimization_barrier(
-        (spectrum, cotangent, scaled, w_first, w_second)
+    spectrum, cotangent, w_first, w_second = lax.optimization_barrier(
+        (spectrum, cotangent, w_first, w_second)
     )
     gathered = send_out(spectrum)
     cot_spec = to_modes(scaled, cotangent, lead)
+    w1, w2 = spread_weights(groups, w_first, w_second)
+    b1, b2 = block_bias(b_first, groups), block_bias(b_second, groups)
+    cot_spec, w1, w2, b1, b2 = lax.optimization_barrier((cot_spec, w1, w2, b1, b2))
     cot_gathered = send_out(cot_spec)
 
-    lat = lat_spread(lat_total, modes)
-    unlat = jnp.transpose(lat)
-    w1, w2 = block_weights(w_first, groups), block_weights(w_second, groups)
-    b1, b2 = block_bias(b_first, groups), block_bias(b_second, groups)
-    image, *state = forward_mid(lat, unlat, gathered, w1, b1, w2, b2)
+    image, *state = forward_mid(lat, lat.T, gathered, w1, b1, w2, b2)
     image_band = send_back(image)
-    grad_image, sum_w_first, sum_w_second, sum_b_first, sum_b_second = backward_mid(
-        lat, unlat, cot_gathered, w1, w2, state, count
-    )
+    grad_image, sums = backward_mid(lat, lat.T, cot_gathered, w1, w2, state, count)
     grad_band = send_back(grad_image)
-    output = to_cells(jnp.transpose(scaled), image_band, fields)
-    grad_fields = to_cells(jnp.transpose(plain), grad_band, cotangent)
-
-    def bias_of(sums):
-        split = sums.reshape(groups, 2, count // groups, -1)
-        return jnp.transpose(split, (1, 0, 2, 3)).reshape(b_first.shape)
-
-    sums = lax.psum(
-        (
-            sum_w_first.reshape(w_first.shape), bias_of(sum_b_first),
-            sum_w_second.reshape(w_first.shape), bias_of(sum_b_second),
-        ),
-        ("space", "dp"),
-    )
+    output = to_cells(scaled.T, image_band, fields)
+    grad_fields = to_cells(plain.T, grad_band, cotangent)
+
     positions = samples * lax.axis_size("dp") * lat_total * KW
     factor = 1.0 / math.sqrt(positions)
-    return (output, grad_fields) + tuple(value * factor for value in sums)
+    sums = summed_over_group(sums).astype(jnp.float32) * factor
+    grads = []
+    for which in range(2):
+        blocks = sums[which, :, :, :edge].reshape(2, groups, edge, count // groups, edge)
+        grads.append(jnp.transpose(blocks, (0, 1, 3, 2, 4)).reshape(w_first.shape))
+        grads.append(sums[which, :, :, edge].reshape(b_first.shape))
+    return (output, grad_fields) + tuple(grads)
 
 
 def solution(mesh):

time: 288 us -> 217 us (0.75)
  blocking collectives: 84.7 us -> 0 us
  waiting for transfers between devices: 84.7 us -> 121 us
  other arithmetic: 18.1 us -> 2.77 us
  between operations: 14.3 us -> 1.09 us
  starting transfers between devices: 21.8 us -> 30.4 us
  local copies, waits for them, and re-layouts: 36 us -> 31.5 us
    psum x1 -> x0, blocking collectives: 84.7 us -> none  [body(): lax.psum((sum_w_first.reshape(w_first.shape), bias_of(sum_b_first), sum_w...]
    ppermute x0 -> x8, waiting for transfers between devices: none -> 48.1 us  [swap_with(): return lax.ppermute(values, axis, [(i, i ^ distance) for i in range(size)])]
    psum x1 -> x0, waiting for transfers between devices: 26.9 us -> none  [body(): lax.psum((sum_w_first.reshape(w_first.shape), bias_of(sum_b_first), sum_w...]
    all_to_all x2, waiting for transfers between devices: 32.9 us -> 54.6 us  [send_out(): lax.all_to_all(spectrum, 'space', split_axis=0, concat_axis=0, tiled=True)]
    ppermute x0 -> x8, starting transfers between devices: none -> 9.99 us  [swap_with(): return lax.ppermute(values, axis, [(i, i ^ distance) for i in range(size)])]
    mul x7 -> x1, other arithmetic: 9.95 us -> 0.18 us  [body(): sums = summed_over_group(sums).astype(jnp.float32) * factor]
    squeeze x4 -> x2, local copies, waits for them, and re-layouts: 8.13 us -> 0.08 us  [summed_over_group(): lax.dynamic_index_in_dim(pair, 1 - side, 0, keepdims=False).astype(kind)]
    all_to_all x2, waiting for transfers between devices: 24.3 us -> 18.6 us  [send_back(): lax.all_to_all(bands, 'space', split_axis=0, concat_axis=0, tiled=True)]
  transfers between devices with their start and end apart: 5 -> 12, of which waited for: 3 -> 10; matrix products, arithmetic and copies ran while one was open for 14% -> 8% of each run, Pallas kernels for 8% -> 11%
where the time goes in v2:
time: 217 us; the launch traced here: 216 us
  waiting for transfers between devices  121 us (56%)
  local copies, waits for them, and re-layouts  31.5 us (15%)
  starting transfers between devices  30.4 us (14%)
  Pallas kernels  28.8 us (13%)
  other arithmetic  2.77 us (1%)
    all_to_all x2, waiting for transfers between devices, send_out(): lax.all_to_all(spectrum, 'space', split_axis=0, concat_axis=0, tiled=True)  54.6 us
    ppermute x8, waiting for transfers between devices, swap_with(): return lax.ppermute(values, axis, [(i, i ^ distance) for i in range(size)])  48.1 us
    unnamed x45, local copies, waits for them, and re-layouts  20.9 us
    all_to_all x2, waiting for transfers between devices, send_back(): lax.all_to_all(bands, 'space', split_axis=0, concat_axis=0, tiled=True)  18.6 us
    all_to_all x2, starting transfers between devices, send_out(): lax.all_to_all(spectrum, 'space', split_axis=0, concat_axis=0, tiled=True)  11.6 us
    pallas_call x1, Pallas kernels, backward_mid(): pl.pallas_call(functools.partial(backward_kernel, size_of_block), grid=(g...  10.1 us
    ppermute x8, starting transfers between devices, swap_with(): return lax.ppermute(values, axis, [(i, i ^ distance) for i in range(size)])  9.99 us
    all_to_all x2, starting transfers between devices, send_back(): lax.all_to_all(bands, 'space', split_axis=0, concat_axis=0, tiled=True)  8.78 us
  transfers between devices with their start and end apart: 12, of which 10 were waited for; matrix products, arithmetic and copies ran while one was open for 8% of the time, Pallas kernels for 11%

profile of v2, /device:TPU:0, one launch (start us, length us, event | category | flops | bytes accessed | tf_op | source)
XLA Modules:
  0.0 215.8 jit_solution(15103631666260909553)
XLA Ops:
  0.6 1.9 copy.29.cells_ref.base_ref
  2.6 2.3 %to_modes.2 = bf16[8,4,2,16,768]{4,3,2,1,0:T(8,128)(2,1)} custom-call(bf16[128,180]{1,0:T(8,128)(2,1)S(1)} %copy-done.7, bf16[4,2,180,768]{3,2,1,0:T(8,128)(2,1)S(1)} %copy.29.cells_ref.base_ref), custom_call_target="tpu_custom_call" | custom-call | flops 283115520 | bytes 3784704 | tf_op jit(solution)/shard_map/to_modes/pallas_call | solution.py:111
  6.4 7.3 %all-to-all-start = ((bf16[8,4,2,16,768]{4,3,2,1,0:T(8,128)(2,1)}), bf16[8,4,2,16,768]{4,3,2,1,0:T(8,128)(2,1)}, u32[]{:S(2)}, u32[]{:S(2)}) async-start(bf16[8,4,2,16,768]{4,3,2,1,0:T(8,128)(2,1)} %to_modes.2), calls=%async_computation | async-start | bytes 3145728 | tf_op jit(solution)/shard_map/all_to_all | solution.py:365
  13.8 2.0 copy.30.cells_ref.base_ref
  21.0 29.9 %all-to-all-done.bands_ref = bf16[8,4,2,16,768]{4,3,2,1,0:T(8,128)(2,1)} async-done(((bf16[8,4,2,16,768]{4,3,2,1,0:T(8,128)(2,1)}), bf16[8,4,2,16,768]{4,3,2,1,0:T(8,128)(2,1)}, u32[]{:S(2)}, u32[]{:S(2)}) %all-to-all-start) | async-done | bytes 1572896 | tf_op jit(solution)/shard_map/all_to_all | solution.py:365
  50.8 4.3 %all-to-all-start.2 = ((bf16[8,4,2,16,768]{4,3,2,1,0:T(8,128)(2,1)}), bf16[8,4,2,16,768]{4,3,2,1,0:T(8,128)(2,1)}, u32[]{:S(2)}, u32[]{:S(2)}) async-start(bf16[8,4,2,16,768]{4,3,2,1,0:T(8,128)(2,1)} %copy-done.2), calls=%async_computation.2 | async-start | bytes 3145728 | tf_op jit(solution)/shard_map/all_to_all | solution.py:365
  55.2 8.4 %mix_forward.1 = (bf16[8,4,2,16,768]{4,3,2,1,0:T(8,128)(2,1)S(1)}, bf16[2,512,768]{2,1,0:T(8,128)(2,1)S(1)}, bf16[2,512,768]{2,1,0:T(8,128)(2,1)S(1)}, f32[2,512,768]{2,1,0:T(8,128)}, f32[2,512,768]{2,1,0:T(8,128)}) custom-call(bf16[256,256]{1,0:T(8,128)(2,1)S(1)} %copy-done.12, bf16[256,256]{1,0:T(8,128)(2,1)S(1)} %copy-done.13, ...), custom_call_target="tpu_custom_call" | custom-call | flops 2415919104 | bytes 17301504 | tf_op jit(solution)/shard_map/mix_forward/pallas_call | solution.py:261
  67.0 24.8 %all-to-all-done.2.bands_ref = bf16[8,4,2,16,768]{4,3,2,1,0:T(8,128)(2,1)} async-done(((bf16[8,4,2,16,768]{4,3,2,1,0:T(8,128)(2,1)}), bf16[8,4,2,16,768]{4,3,2,1,0:T(8,128)(2,1)}, u32[]{:S(2)}, u32[]{:S(2)}) %all-to-all-start.2) | async-done | bytes 1572896 | tf_op jit(solution)/shard_map/all_to_all | solution.py:365
  91.8 4.3 %all-to-all-start.1 = ((bf16[8,4,2,16,768]{4,3,2,1,0:T(8,128)(2,1)}), bf16[8,4,2,16,768]{4,3,2,1,0:T(8,128)(2,1)}, u32[]{:S(2)}, u32[]{:S(2)}) async-start(bf16[8,4,2,16,768]{4,3,2,1,0:T(8,128)(2,1)} %copy-done.4), calls=%async_computation.1 | async-start | bytes 3145728 | tf_op jit(solution)/shard_map/all_to_all | solution.py:374
  96.1 10.1 %mix_backward.1 = (bf16[8,4,2,16,768]{4,3,2,1,0:T(8,128)(2,1)S(1)}, f32[2,2,2,112,384]{4,3,2,1,0:T(8,128)S(1)}) custom-call(bf16[256,256]{1,0:T(8,128)(2,1)S(1)} %copy-done.12, bf16[256,256]{1,0:T(8,128)(2,1)S(1)} %copy-done.13, bf16[8,4,2,16,768]{4,3,2,1,0:T(8,128)(2,1)} %all-to-all-done.2.bands_ref, bf16[2,768,768]{2,1,0:T(8,128)(2,1)} %copy-done.14, ...), custom_call_target="tpu_custom_call" | custom-call | flops 4831838208 | bytes 17301504 | tf_op jit(solution)/shard_map/mix_backward/pallas_call | solution.py:296
  108.6 2.2 %collective-permute-done = f32[448,384]{1,0:T(8,128)} collective-permute-done((f32[448,384]{1,0:T(8,128)S(1)}, f32[448,384]{1,0:T(8,128)}, u32[]{:S(2)}, u32[]{:S(2)}) %collective-permute-start) | collective-permute-done | bytes 688160 | tf_op jit(solution)/shard_map/ppermute | solution.py:324
  112.2 1.9 collective-permute-start.1
  114.1 18.5 %all-to-all-done.1.modes_ref = bf16[8,4,2,16,768]{4,3,2,1,0:T(8,128)(2,1)} async-done(((bf16[8,4,2,16,768]{4,3,2,1,0:T(8,128)(2,1)}), bf16[8,4,2,16,768]{4,3,2,1,0:T(8,128)(2,1)}, u32[]{:S(2)}, u32[]{:S(2)}) %all-to-all-start.1) | async-done | bytes 1572896 | tf_op jit(solution)/shard_map/all_to_all | solution.py:374
  132.7 4.5 %all-to-all-start.3 = ((bf16[8,4,2,16,768]{4,3,2,1,0:T(8,128)(2,1)}), bf16[8,4,2,16,768]{4,3,2,1,0:T(8,128)(2,1)}, u32[]{:S(2)}, u32[]{:S(2)}) async-start(bf16[8,4,2,16,768]{4,3,2,1,0:T(8,128)(2,1)} %copy-done.3), calls=%async_computation.3 | async-start | bytes 3145728 | tf_op jit(solution)/shard_map/all_to_all | solution.py:374
  140.0 23.9 %collective-permute-done.2 = bf16[112,384]{1,0:T(8,128)(2,1)S(1)} collective-permute-done((bf16[112,384]{1,0:T(8,128)(2,1)S(1)}, bf16[112,384]{1,0:T(8,128)(2,1)S(1)}, u32[]{:S(2)}, u32[]{:S(2)}) %collective-permute-start.2) | collective-permute-done | bytes 86048 | tf_op jit(solution)/shard_map/ppermute | solution.py:324
  164.0 4.7 %collective-permute-start.3 = (bf16[56,384]{1,0:T(8,128)(2,1)S(1)}, bf16[56,384]{1,0:T(8,128)(2,1)S(1)}, u32[]{:S(2)}, u32[]{:S(2)}) collective-permute-start(bf16[56,384]{1,0:T(8,128)(2,1)S(1)} %fusion.2), channel_id=1, source_target_pairs={{0,8},{2,10},{4,12},{6,14},{8,0},{10,2},{12,4},{14,6},{1,9},{3,11}... | collective-permute-start | bytes 129032 | tf_op jit(solution)/shard_map/ppermute | solution.py:324
  168.7 6.8 %collective-permute-done.3 = bf16[56,384]{1,0:T(8,128)(2,1)S(1)} collective-permute-done((bf16[56,384]{1,0:T(8,128)(2,1)S(1)}, bf16[56,384]{1,0:T(8,128)(2,1)S(1)}, u32[]{:S(2)}, u32[]{:S(2)}) %collective-permute-start.3) | collective-permute-done | bytes 43040 | tf_op jit(solution)/shard_map/ppermute | solution.py:324
  175.6 4.9 %collective-permute-done.4 = bf16[56,384]{1,0:T(8,128)(2,1)S(1)} collective-permute-done((bf16[56,384]{1,0:T(8,128)(2,1)S(1)}, bf16[56,384]{1,0:T(8,128)(2,1)S(1)}, u32[]{:S(2)}, u32[]{:S(2)}) %collective-permute-start.4) | collective-permute-done | bytes 43040 | tf_op jit(solution)/shard_map/ppermute | solution.py:324
  180.6 4.5 %collective-permute-done.5 = bf16[112,384]{1,0:T(8,128)(2,1)S(1)} collective-permute-done((bf16[112,384]{1,0:T(8,128)(2,1)S(1)}, bf16[112,384]{1,0:T(8,128)(2,1)S(1)}, u32[]{:S(2)}, u32[]{:S(2)}) %collective-permute-start.5) | collective-permute-done | bytes 86048 | tf_op jit(solution)/shard_map/ppermute | solution.py:324
  186.5 4.1 %collective-permute-done.6 = bf16[224,384]{1,0:T(8,128)(2,1)S(1)} collective-permute-done((bf16[224,384]{1,0:T(8,128)(2,1)S(1)}, bf16[224,384]{1,0:T(8,128)(2,1)S(1)}, u32[]{:S(2)}, u32[]{:S(2)}) %collective-permute-start.6) | collective-permute-done | bytes 172064 | tf_op jit(solution)/shard_map/ppermute | solution.py:324
  203.7 3.0 %to_cells.2 = bf16[4,2,180,768]{3,2,1,0:T(8,128)(2,1)S(1)} custom-call(bf16[180,128]{1,0:T(8,128)(2,1)S(1)} %copy-done.9, bf16[8,4,2,16,768]{4,3,2,1,0:T(8,128)(2,1)} %all-to-all-done.1.modes_ref, bf16[4,2,180,768]{3,2,1,0:T(8,128)(2,1)S(1)} %copy-done.1), custom_call_target="tpu_custom_call" | custom-call | flops 283115520 | bytes 5996544 | tf_op jit(solution)/shard_map/to_cells/pallas_call | solution.py:142
  206.7 3.1 %copy.37 = bf16[4,2,180,768]{3,1,2,0:T(2,128)(2,1)} copy(bf16[4,2,180,768]{3,2,1,0:T(8,128)(2,1)S(1)} %to_cells.2) | data formatting | bytes 4423680
  209.7 3.0 %to_cells.3 = bf16[4,2,180,768]{3,2,1,0:T(8,128)(2,1)S(1)} custom-call(bf16[180,128]{1,0:T(8,128)(2,1)S(1)} %copy-done.8, bf16[8,4,2,16,768]{4,3,2,1,0:T(8,128)(2,1)} %all-to-all-done.3.modes_ref, bf16[4,2,180,768]{3,2,1,0:T(8,128)(2,1)S(1)} %copy.30.cells_ref.base_ref), custom_call_target="tpu_custom_call" | custom-call | flops 283115520 | bytes 5996544 | tf_op jit(solution)/shard_map/to_cells/pallas_call | solution.py:142
  212.7 3.1 %copy.38 = bf16[4,2,180,768]{3,1,2,0:T(2,128)(2,1)} copy(bf16[4,2,180,768]{3,2,1,0:T(8,128)(2,1)S(1)} %to_cells.3) | data formatting | bytes 4423680
  (79 shorter events, 31.3 us)
Async XLA Ops:
  0.6 2.0 copy-start.7
  4.9 1.5 copy-start
  6.4 44.4 %all-to-all-start = ((bf16[8,4,2,16,768]{4,3,2,1,0:T(8,128)(2,1)}), bf16[8,4,2,16,768]{4,3,2,1,0:T(8,128)(2,1)}, u32[]{:S(2)}, u32[]{:S(2)}) async-start(bf16[8,4,2,16,768]{4,3,2,1,0:T(8,128)(2,1)} %to_modes.2), calls=%async_computation | async-start | bytes 3145728 | tf_op jit(solution)/shard_map/all_to_all | solution.py:365
  13.7 2.0 copy-start.19
  13.7 2.2 copy-start.20
  13.7 2.3 %copy-start.10 = (bf16[2,8,96,96]{3,2,1,0:T(8,128)(2,1)S(1)}, bf16[2,8,96,96]{3,2,1,0:T(8,128)(2,1)}, u32[]{:S(2)}) copy-start(bf16[2,8,96,96]{3,2,1,0:T(8,128)(2,1)} %refs_0_) | copy-start | bytes 884740
  13.7 2.3 %copy-start.11 = (bf16[2,8,96,96]{3,2,1,0:T(8,128)(2,1)S(1)}, bf16[2,8,96,96]{3,2,1,0:T(8,128)(2,1)}, u32[]{:S(2)}) copy-start(bf16[2,8,96,96]{3,2,1,0:T(8,128)(2,1)} %refs_1_) | copy-start | bytes 884740
  13.8 4.7 %copy-start.6 = (bf16[128,180]{1,0:T(8,128)(2,1)S(1)}, bf16[128,180]{1,0:T(8,128)(2,1)}, u32[]{:S(2)}) copy-start(bf16[128,180]{1,0:T(8,128)(2,1)} %constant.130.clone.table_ref) | copy-start | bytes 138244
  20.9 34.2 %copy-start.12 = (bf16[256,256]{1,0:T(8,128)(2,1)S(1)}, bf16[256,256]{1,0:T(8,128)(2,1)}, u32[]{:S(2)}) copy-start(bf16[256,256]{1,0:T(8,128)(2,1)} %constant.131.clone.lat_ref) | copy-start | bytes 393220
  20.9 34.2 %copy-start.13 = (bf16[256,256]{1,0:T(8,128)(2,1)S(1)}, bf16[256,256]{1,0:T(8,128)(2,1)}, u32[]{:S(2)}) copy-start(bf16[256,256]{1,0:T(8,128)(2,1)} %constant.132.clone.unlat_ref) | copy-start | bytes 393220
  50.8 40.9 %all-to-all-start.2 = ((bf16[8,4,2,16,768]{4,3,2,1,0:T(8,128)(2,1)}), bf16[8,4,2,16,768]{4,3,2,1,0:T(8,128)(2,1)}, u32[]{:S(2)}, u32[]{:S(2)}) async-start(bf16[8,4,2,16,768]{4,3,2,1,0:T(8,128)(2,1)} %copy-done.2), calls=%async_computation.2 | async-start | bytes 3145728 | tf_op jit(solution)/shard_map/all_to_all | solution.py:365
  91.8 40.9 %all-to-all-start.1 = ((bf16[8,4,2,16,768]{4,3,2,1,0:T(8,128)(2,1)}), bf16[8,4,2,16,768]{4,3,2,1,0:T(8,128)(2,1)}, u32[]{:S(2)}, u32[]{:S(2)}) async-start(bf16[8,4,2,16,768]{4,3,2,1,0:T(8,128)(2,1)} %copy-done.4), calls=%async_computation.1 | async-start | bytes 3145728 | tf_op jit(solution)/shard_map/all_to_all | solution.py:374
  108.4 2.3 %collective-permute-start = (f32[448,384]{1,0:T(8,128)S(1)}, f32[448,384]{1,0:T(8,128)}, u32[]{:S(2)}, u32[]{:S(2)}) collective-permute-start(f32[448,384]{1,0:T(8,128)S(1)} %dynamic-slice_bitcast_fusion), channel_id=1, source_target_pairs={{0,1},{1,0},{2,3},{3,2},{4,5},{5,4},{6,7},{7,6},{8,9},{9,8},{10,11... | collective-permute-start | bytes 2064392 | tf_op jit(solution)/shard_map/ppermute | solution.py:324
  112.2 25.0 %collective-permute-start.1 = (f32[224,384]{1,0:T(8,128)S(1)}, f32[224,384]{1,0:T(8,128)}, u32[]{:S(2)}, u32[]{:S(2)}) collective-permute-start(f32[224,384]{1,0:T(8,128)S(1)} %dynamic-slice_bitcast_fusion.1), channel_id=1, source_target_pairs={{0,2},{2,0},{4,6},{6,4},{8,10},{10,8},{12,14},{14,12},{1,3},{3,1},... | collective-permute-start | bytes 1032200 | tf_op jit(solution)/shard_map/ppermute | solution.py:324
  132.7 77.0 %all-to-all-start.3 = ((bf16[8,4,2,16,768]{4,3,2,1,0:T(8,128)(2,1)}), bf16[8,4,2,16,768]{4,3,2,1,0:T(8,128)(2,1)}, u32[]{:S(2)}, u32[]{:S(2)}) async-start(bf16[8,4,2,16,768]{4,3,2,1,0:T(8,128)(2,1)} %copy-done.3), calls=%async_computation.3 | async-start | bytes 3145728 | tf_op jit(solution)/shard_map/all_to_all | solution.py:374
  138.3 25.6 %collective-permute-start.2 = (bf16[112,384]{1,0:T(8,128)(2,1)S(1)}, bf16[112,384]{1,0:T(8,128)(2,1)S(1)}, u32[]{:S(2)}, u32[]{:S(2)}) collective-permute-start(bf16[112,384]{1,0:T(8,128)(2,1)S(1)} %fusion), channel_id=1, source_target_pairs={{0,4},{2,6},{4,0},{6,2},{8,12},{10,14},{12,8},{14,10},{1,5},{3,7},... | collective-permute-start | bytes 258056 | tf_op jit(solution)/shard_map/ppermute | solution.py:324
  164.0 11.5 %collective-permute-start.3 = (bf16[56,384]{1,0:T(8,128)(2,1)S(1)}, bf16[56,384]{1,0:T(8,128)(2,1)S(1)}, u32[]{:S(2)}, u32[]{:S(2)}) collective-permute-start(bf16[56,384]{1,0:T(8,128)(2,1)S(1)} %fusion.2), channel_id=1, source_target_pairs={{0,8},{2,10},{4,12},{6,14},{8,0},{10,2},{12,4},{14,6},{1,9},{3,11}... | collective-permute-start | bytes 129032 | tf_op jit(solution)/shard_map/ppermute | solution.py:324
  175.5 5.0 %collective-permute-start.4 = (bf16[56,384]{1,0:T(8,128)(2,1)S(1)}, bf16[56,384]{1,0:T(8,128)(2,1)S(1)}, u32[]{:S(2)}, u32[]{:S(2)}) collective-permute-start(bf16[56,384]{1,0:T(8,128)(2,1)S(1)} %fusion.1), channel_id=1, source_target_pairs={{0,8},{2,10},{4,12},{6,14},{8,0},{10,2},{12,4},{14,6},{1,9},{3,11}... | collective-permute-start | bytes 129032 | tf_op jit(solution)/shard_map/ppermute | solution.py:324
  180.5 4.6 %collective-permute-start.5 = (bf16[112,384]{1,0:T(8,128)(2,1)S(1)}, bf16[112,384]{1,0:T(8,128)(2,1)S(1)}, u32[]{:S(2)}, u32[]{:S(2)}) collective-permute-start(bf16[112,384]{1,0:T(8,128)(2,1)S(1)} %maximum_select_fusion.3), channel_id=1, source_target_pairs={{0,4},{2,6},{4,0},{6,2},{8,12},{10,14},{12,8},{14,10},{1,5},{3,7},... | collective-permute-start | bytes 258056 | tf_op jit(solution)/shard_map/ppermute | solution.py:324
  185.1 5.5 %collective-permute-start.6 = (bf16[224,384]{1,0:T(8,128)(2,1)S(1)}, bf16[224,384]{1,0:T(8,128)(2,1)S(1)}, u32[]{:S(2)}, u32[]{:S(2)}) collective-permute-start(bf16[224,384]{1,0:T(8,128)(2,1)S(1)} %maximum_select_fusion.2), channel_id=1, source_target_pairs={{0,2},{2,0},{4,6},{6,4},{8,10},{10,8},{12,14},{14,12},{1,3},{3,1},... | collective-permute-start | bytes 516104 | tf_op jit(solution)/shard_map/ppermute | solution.py:324
  190.7 1.7 collective-permute-start.7
  197.3 4.7 %copy-start.9 = (bf16[180,128]{1,0:T(8,128)(2,1)S(1)}, bf16[180,128]{1,0:T(8,128)(2,1)}, u32[]{:S(2)}) copy-start(bf16[180,128]{1,0:T(8,128)(2,1)} %constant.133.clone.table_ref) | copy-start | bytes 138244
  202.0 1.6 copy-start.1
  206.7 3.1 %copy-start.8 = (bf16[180,128]{1,0:T(8,128)(2,1)S(1)}, bf16[180,128]{1,0:T(8,128)(2,1)}, u32[]{:S(2)}) copy-start(bf16[180,128]{1,0:T(8,128)(2,1)} %constant.134.clone.table_ref) | copy-start | bytes 138244
  (9 other events, 10.8 us)

commit v3 on v2

v3 whole, which is shorter than its diff:
```python
import functools
import math

import jax
import jax.numpy as jnp
from jax import lax
from jax.experimental import pallas as pl
from jax.experimental.pallas import tpu as pltpu
from jax.sharding import PartitionSpec as P
import ml_dtypes
import numpy as np

KW = 64
shrink_level = 0.05
VMEM_BYTES = 48 * 1024 * 1024


def product_of(former, latter):
    return jnp.dot(former, latter, preferred_element_type=jnp.float32)


def lon_tables(mode_count, cell_count, owners):
    wavenums = np.arange(mode_count, dtype=np.int32)
    columns = np.arange(cell_count, dtype=np.int32)
    phase_index = (wavenums[:, None] * columns[None, :] % cell_count).astype(np.float32)
    phases = phase_index * np.float32(2.0 * math.pi / cell_count)
    factor = np.float32(1.0 / math.sqrt(cell_count))
    forward = np.stack([np.cos(phases) * factor, -np.sin(phases) * factor])
    scaled = forward * np.where(wavenums == 0, 1.0, 2.0).astype(np.float32)[:, None]

    def ordered(table):
        split = table.reshape(2, owners, -1, cell_count).transpose(1, 0, 2, 3)
        return split.reshape(-1, cell_count).astype(ml_dtypes.bfloat16)

    return ordered(forward), ordered(scaled)


def lat_spread(row_count, modes):
    indices = np.arange(row_count, dtype=np.int32)
    phase_index = (indices[:, None] * indices[None, :] % row_count).astype(np.float32)
    phases = phase_index * np.float32(2.0 * math.pi / row_count)
    factor = np.float32(1.0 / math.sqrt(row_count))
    cosine = np.cos(phases) * factor
    sine_part = np.sin(phases) * factor
    table = np.stack([np.stack([cosine, sine_part], -1), np.stack([-sine_part, cosine], -1)])
    same = np.eye(modes, dtype=np.float32)
    spread = table[:, :, None, :, :, None] * same[None, None, :, None, None, :]
    size = 2 * row_count * modes
    return spread.reshape(size, size).astype(ml_dtypes.bfloat16)


def block_bias(bias, groups):
    return jnp.transpose(bias.reshape(2, groups, 1, -1), (1, 2, 0, 3)).reshape(groups, 1, -1)


def spread_kernel(*refs):
    half_way = len(refs) // 2
    for blocks_ref, joined_ref in zip(refs[:half_way], refs[half_way:]):
        _, per, size, _ = blocks_ref.shape
        width = per * size
        row = lax.broadcasted_iota(jnp.int32, (size, width), 0)
        lane = lax.broadcasted_iota(jnp.int32, (size, width), 1)
        for block in range(per):
            place = (row + block * size == lane).astype(jnp.bfloat16)
            real = product_of(blocks_ref[0, block], place).astype(jnp.bfloat16)
            imag = product_of(blocks_ref[1, block], place)
            upper = pl.ds(block * size, size)
            lower = pl.ds(width + block * size, size)
            joined_ref[0, upper, 0:width] = real
            joined_ref[0, upper, width : 2 * width] = imag.astype(jnp.bfloat16)
            joined_ref[0, lower, 0:width] = (-imag).astype(jnp.bfloat16)
            joined_ref[0, lower, width : 2 * width] = real


def spread_weights(groups, *weights):
    _, count, size, _ = weights[0].shape
    per = count // groups
    lanes = 2 * per * size
    shape = jax.ShapeDtypeStruct((groups, lanes, lanes), jnp.bfloat16)
    return pl.pallas_call(
        spread_kernel,
        grid=(groups,),
        out_shape=(shape,) * len(weights),
        in_specs=[pl.BlockSpec((2, per, size, size), lambda g: (0, g, 0, 0))] * len(weights),
        out_specs=(group_spec(lanes, lanes),) * len(weights),
        compiler_params=params("arbitrary"),
        cost_estimate=pl.CostEstimate(
            flops=len(weights) * 2 * count * size * size * lanes,
            bytes_accessed=len(weights) * 2 * groups * lanes * lanes,
            transcendentals=0,
        ),
        name="spread_weights",
    )(*weights)


def params(*semantics):
    return pltpu.CompilerParams(vmem_limit_bytes=VMEM_BYTES, dimension_semantics=semantics)


def place_of(me_ref, offset, rows):
    return pl.ds(pl.multiple_of((me_ref[0] ^ offset) * rows, rows), rows)


def to_modes_kernel(me_ref, table_ref, cells_ref, *refs):
    modes_refs, held_ref = refs[:-1], refs[-1]
    share = modes_refs[0].shape[2]
    for row in range(cells_ref.shape[1]):
        spectrum = product_of(table_ref[...], cells_ref[0, row])
        held_ref[row] = spectrum.astype(jnp.bfloat16)
        for offset, modes_ref in enumerate(modes_refs):
            modes_ref[0, row] = held_ref[row, place_of(me_ref, offset, share)]


def to_modes(me, table, cells, owners):
    samples, rows, width, channels = cells.shape
    size = table.shape[0]
    share = (rows, size // owners, channels)
    return pl.pallas_call(
        to_modes_kernel,
        grid_spec=pltpu.PrefetchScalarGridSpec(
            num_scalar_prefetch=1,
            grid=(samples,),
            in_specs=[
                pl.BlockSpec((size, width), lambda b, _: (0, 0)),
                pl.BlockSpec((1, rows, width, channels), lambda b, _: (b, 0, 0, 0)),
            ],
            out_specs=(pl.BlockSpec((1,) + share, lambda b, _: (b, 0, 0, 0)),) * owners,
            scratch_shapes=[pltpu.VMEM((rows, size, channels), jnp.bfloat16)],
        ),
        out_shape=(jax.ShapeDtypeStruct((samples,) + share, jnp.bfloat16),) * owners,
        compiler_params=params("arbitrary"),
        cost_estimate=pl.CostEstimate(
            flops=2 * samples * rows * size * width * channels,
            bytes_accessed=2 * samples * rows * channels * (width + size),
            transcendentals=0,
        ),
        name="to_modes",
    )(me, table, cells)


def to_cells_kernel(me_ref, table_ref, base_ref, *refs):
    modes_refs, out_ref, held_ref = refs[:-2], refs[-2], refs[-1]
    share = modes_refs[0].shape[2]
    for row in range(base_ref.shape[1]):
        for offset, modes_ref in enumerate(modes_refs):
            held_ref[row, place_of(me_ref, offset, share)] = modes_ref[0, row]
        image = product_of(table_ref[...], held_ref[row])
        out_ref[0, row] = (base_ref[0, row].astype(jnp.float32) + image).astype(jnp.bfloat16)


def to_cells(me, table, modes, base):
    samples, rows, width, channels = base.shape
    size = table.shape[1]
    share = modes[0].shape[1:]
    block = pl.BlockSpec((1, rows, width, channels), lambda b, _: (b, 0, 0, 0))
    return pl.pallas_call(
        to_cells_kernel,
        grid_spec=pltpu.PrefetchScalarGridSpec(
            num_scalar_prefetch=1,
            grid=(samples,),
            in_specs=[pl.BlockSpec((width, size), lambda b, _: (0, 0)), block]
            + [pl.BlockSpec((1,) + share, lambda b, _: (b, 0, 0, 0))] * len(modes),
            out_specs=block,
            scratch_shapes=[pltpu.VMEM((rows, size, channels), jnp.bfloat16)],
        ),
        out_shape=jax.ShapeDtypeStruct(base.shape, jnp.bfloat16),
        compiler_params=params("arbitrary"),
        cost_estimate=pl.CostEstimate(
            flops=2 * samples * rows * size * width * channels,
            bytes_accessed=2 * samples * rows * channels * (2 * width + size),
            transcendentals=0,
        ),
        name="to_cells",
    )(me, table, base, *modes)


def sigmoid_of(values):
    return 0.5 + 0.5 * jnp.tanh(0.5 * values)


def mix_lat(me_ref, table_ref, bands_refs, band_ref, mixed_ref):
    samples, rows, share, width = bands_refs[0].shape
    half = table_ref.shape[0] // 2
    for sample in range(samples):
        for offset, bands_ref in enumerate(bands_refs):
            place = place_of(me_ref, offset, rows * share)
            band_ref[sample, place] = bands_ref[sample].reshape(rows * share, width)
        mixed = product_of(table_ref[...], band_ref[sample]).astype(jnp.bfloat16)
        spot = pl.ds(sample * half, half)
        mixed_ref[spot, 0:width] = mixed[:half]
        mixed_ref[spot, width : 2 * width] = mixed[half:]


def unmix_lat(me_ref, table_ref, mixed_ref, band_ref, bands_refs):
    samples, rows, share, width = bands_refs[0].shape
    half = table_ref.shape[0] // 2
    for sample in range(samples):
        spot = pl.ds(sample * half, half)
        joined = jnp.concatenate(
            [mixed_ref[spot, 0:width], mixed_ref[spot, width : 2 * width]], axis=0
        )
        band_ref[sample] = product_of(table_ref[...], joined).astype(jnp.bfloat16)
        for offset, bands_ref in enumerate(bands_refs):
            place = place_of(me_ref, offset, rows * share)
            bands_ref[sample] = band_ref[sample, place].reshape(rows, share, width)


def forward_kernel(owners, me_ref, lat_ref, unlat_ref, w1_ref, b1_ref, w2_ref, b2_ref, *refs):
    bands_refs, image_refs = refs[:owners], refs[owners : 2 * owners]
    mixed_ref, act_ref, gate_ref, bend_ref, shrunk_ref, band_ref = refs[2 * owners :]
    mix_lat(me_ref, lat_ref, bands_refs, band_ref, mixed_ref.at[0])
    pre = product_of(mixed_ref[0], w1_ref[0]) + b1_ref[0]
    logistic = sigmoid_of(pre)
    act = pre * logistic
    act_ref[0] = act.astype(jnp.bfloat16)
    gate_ref[0] = logistic + act * (1.0 - logistic)
    out = product_of(act_ref[0], w2_ref[0]) + b2_ref[0]
    bent = jnp.tanh(out * (1.0 / shrink_level))
    bend_ref[0] = bent * bent
    shrunk_ref[...] = (out - shrink_level * bent).astype(jnp.bfloat16)
    unmix_lat(me_ref, unlat_ref, shrunk_ref, band_ref, image_refs)


def backward_kernel(
    block_size, owners, me_ref, lat_ref, unlat_ref, w1_ref, w2_ref,
    mixed_ref, act_ref, gate_ref, bend_ref, *refs
):
    bands_refs, image_refs = refs[:owners], refs[owners : 2 * owners]
    sums_ref, cot_ref, kept_ref, band_ref = refs[2 * owners :]
    transposed = (((1,), (1,)), ((), ()))
    summed = (((0,), (0,)), ((), ()))

    def times(former, latter, dims):
        return lax.dot_general(former, latter, dims, preferred_element_type=jnp.float32)

    def weight_sums(acts, grads, slot):
        width = acts.shape[1] // 2
        full = times(acts, grads, summed)
        real = full[:width, :width] + full[width:, width:]
        imag = full[:width, width:] - full[width:, :width]
        bias = jnp.sum(grads.astype(jnp.float32), axis=0, keepdims=True)
        size = block_size
        owner = lax.broadcasted_iota(jnp.int32, (size, width), 1) // size
        extra = sums_ref.shape[3] - size
        first = lax.broadcasted_iota(jnp.int32, (extra, width), 0) == 0
        for part, values in enumerate((real, imag)):
            joined = values[:size]
            for block in range(1, width // size):
                joined = jnp.where(owner == block, values[block * size : (block + 1) * size], joined)
            sums_ref[slot, part, 0, 0:size] = joined
            row = bias[:, part * width : (part + 1) * width]
            sums_ref[slot, part, 0, size:] = jnp.where(first, row, 0.0)

    mix_lat(me_ref, lat_ref, bands_refs, band_ref, cot_ref)
    kept_ref[...] = (cot_ref[...].astype(jnp.float32) * bend_ref[0]).astype(jnp.bfloat16)
    back = times(kept_ref[...], w2_ref[0], transposed)
    cot_ref[...] = (back * gate_ref[0]).astype(jnp.bfloat16)
    weight_sums(act_ref[0], kept_ref[...], 1)
    kept_ref[...] = times(cot_ref[...], w1_ref[0], transposed).astype(jnp.bfloat16)
    weight_sums(mixed_ref[0], cot_ref[...], 0)
    unmix_lat(me_ref, unlat_ref, kept_ref, band_ref, image_refs)


def group_spec(*shape):
    return pl.BlockSpec((1,) + shape, lambda g, *_: (g,) + (0,) * len(shape))


def bands_specs(bands, groups):
    shape = bands[0].shape
    block = shape[:-1] + (shape[-1] // groups,)
    return (pl.BlockSpec(block, lambda g, *_: (0, 0, 0, g)),) * len(bands)


def shapes_of(bands):
    return tuple(jax.ShapeDtypeStruct(band.shape, band.dtype) for band in bands)


def forward_mid(me, lat, unlat, bands, w1, b1, w2, b2):
    groups, lanes, _ = w1.shape
    size = lat.shape[0]
    samples = bands[0].shape[0]
    positions = samples * size // 2
    table = pl.BlockSpec((size, size), lambda g, _: (0, 0))
    state = (groups, positions, lanes)
    state_spec = group_spec(positions, lanes)
    specs = bands_specs(bands, groups)
    results = pl.pallas_call(
        functools.partial(forward_kernel, len(bands)),
        grid_spec=pltpu.PrefetchScalarGridSpec(
            num_scalar_prefetch=1,
            grid=(groups,),
            in_specs=[
                table, table,
                group_spec(lanes, lanes), group_spec(1, lanes),
                group_spec(lanes, lanes), group_spec(1, lanes),
                *specs,
            ],
            out_specs=specs + (state_spec,) * 4,
            scratch_shapes=[
                pltpu.VMEM((positions, lanes), jnp.bfloat16),
                pltpu.VMEM((samples, size, lanes // 2), jnp.bfloat16),
            ],
        ),
        out_shape=shapes_of(bands) + (
            jax.ShapeDtypeStruct(state, jnp.bfloat16),
            jax.ShapeDtypeStruct(state, jnp.bfloat16),
            jax.ShapeDtypeStruct(state, jnp.float32),
            jax.ShapeDtypeStruct(state, jnp.float32),
        ),
        compiler_params=params("arbitrary"),
        cost_estimate=pl.CostEstimate(
            flops=4 * groups * positions * lanes * lanes,
            bytes_accessed=16 * groups * positions * lanes + 4 * groups * lanes * lanes,
            transcendentals=2 * groups * positions * lanes,
        ),
        name="mix_forward",
    )(me, lat, unlat, w1, b1, w2, b2, *bands)
    return results[: len(bands)], results[len(bands) :]


def backward_mid(me, lat, unlat, bands, w1, w2, state, count):
    groups, lanes, _ = w1.shape
    size = lat.shape[0]
    samples = bands[0].shape[0]
    positions = samples * size // 2
    table = pl.BlockSpec((size, size), lambda g, _: (0, 0))
    state_spec = group_spec(positions, lanes)
    specs = bands_specs(bands, groups)
    size_of_block = lanes // 2 // (count // groups)
    rows = size_of_block + 16
    results = pl.pallas_call(
        functools.partial(backward_kernel, size_of_block, len(bands)),
        grid_spec=pltpu.PrefetchScalarGridSpec(
            num_scalar_prefetch=1,
            grid=(groups,),
            in_specs=[
                table, table, group_spec(lanes, lanes), group_spec(lanes, lanes),
                *([state_spec] * 4), *specs,
            ],
            out_specs=specs + (
                pl.BlockSpec((2, 2, 1, rows, lanes // 2), lambda g, _: (0, 0, g, 0, 0)),
            ),
            scratch_shapes=[
                pltpu.VMEM((positions, lanes), jnp.bfloat16),
                pltpu.VMEM((positions, lanes), jnp.bfloat16),
                pltpu.VMEM((samples, size, lanes // 2), jnp.bfloat16),
            ],
        ),
        out_shape=shapes_of(bands)
        + (jax.ShapeDtypeStruct((2, 2, groups, rows, lanes // 2), jnp.float32),),
        compiler_params=params("arbitrary"),
        cost_estimate=pl.CostEstimate(
            flops=8 * groups * positions * lanes * lanes,
            bytes_accessed=16 * groups * positions * lanes + 4 * groups * lanes * lanes,
            transcendentals=0,
        ),
        name="mix_backward",
    )(me, lat, unlat, w1, w2, *state, *bands)
    return results[: len(bands)], results[len(bands)]


def swap_with(values, axis, distance):
    size = lax.axis_size(axis)
    return lax.ppermute(values, axis, [(i, i ^ distance) for i in range(size)])


def far_first(size):
    return sorted(range(1, size), key=lambda offset: (-(offset >> 2), offset))


def summed_over_group(sums):
    lanes = sums.shape[-1]
    size = lax.axis_size("space")
    me, side = lax.axis_index("space"), lax.axis_index("dp")
    halves = sums.reshape(2, -1, lanes)
    given = lax.dynamic_index_in_dim(halves, 1 - side, 0, keepdims=False)
    held = lax.dynamic_index_in_dim(halves, side, 0, keepdims=False) + swap_with(given, "dp", 1)
    shares = held.reshape(size, -1, lanes)
    total = lax.dynamic_index_in_dim(shares, me, 0, keepdims=False)
    for offset in far_first(size):
        given = lax.dynamic_index_in_dim(shares, me ^ offset, 0, keepdims=False)
        taken = swap_with(given.astype(jnp.bfloat16), "space", offset)
        total = total + taken.astype(jnp.float32)
    total = total.astype(jnp.bfloat16)
    parts = jnp.zeros((size,) + total.shape, total.dtype)
    parts = lax.dynamic_update_index_in_dim(parts, total, me, 0)
    for offset in far_first(size):
        taken = swap_with(total, "space", offset)
        parts = lax.dynamic_update_index_in_dim(parts, taken, me ^ offset, 0)
    other = swap_with(parts, "dp", 1)
    both = jnp.where(side == 0, jnp.stack([parts, other]), jnp.stack([other, parts]))
    return both.reshape(sums.shape)


def body(fields, cotangent, w_first, b_first, w_second, b_second):
    samples, rows, width, channels = fields.shape
    owners = lax.axis_size("space")
    lat_total = rows * owners
    modes = KW // owners
    count, edge = w_first.shape[1:3]
    groups = 2
    direct = 2 * modes % 16 == 0
    lead = owners if direct else 1

    def swapped(blocks):
        taken = {0: blocks[0]}
        for offset in far_first(owners):
            taken[offset] = swap_with(blocks[offset], "space", offset)
        return [taken[offset] for offset in range(owners)]

    def send_out(blocks):
        if direct:
            return swapped(blocks)
        spectrum = blocks[0].reshape(samples, rows, owners, 2 * modes, channels)
        spectrum = jnp.transpose(spectrum, (2, 0, 1, 3, 4))
        arrived = lax.all_to_all(spectrum, "space", split_axis=0, concat_axis=0, tiled=True)
        return [jnp.transpose(arrived, (1, 0, 2, 3, 4)).reshape(samples, 1, -1, channels)]

    def send_back(blocks):
        if direct:
            return swapped(blocks)
        bands = blocks[0].reshape(samples, owners, rows, 2 * modes, channels)
        bands = jnp.transpose(bands, (1, 0, 2, 3, 4))
        arrived = lax.all_to_all(bands, "space", split_axis=0, concat_axis=0, tiled=True)
        return [jnp.transpose(arrived, (1, 2, 0, 3, 4)).reshape(samples, rows, -1, channels)]

    me = lax.axis_index("space") if direct else 0
    me = jnp.full((1,), me, jnp.int32)
    plain, scaled = lon_tables(KW, width, owners)
    lat = lat_spread(lat_total, modes)

    spectrum = to_modes(me, plain, fields, lead)
    spectrum, cotangent, w_first, w_second = lax.optimization_barrier(
        (spectrum, cotangent, w_first, w_second)
    )
    gathered = send_out(spectrum)
    cot_gathered = send_out(to_modes(me, scaled, cotangent, lead))
    w1, w2 = spread_weights(groups, w_first, w_second)
    b1, b2 = block_bias(b_first, groups), block_bias(b_second, groups)

    image, state = forward_mid(me, lat, lat.T, gathered, w1, b1, w2, b2)
    image_band = send_back(image)
    grad_image, sums = backward_mid(me, lat, lat.T, cot_gathered, w1, w2, state, count)
    grad_band = send_back(grad_image)
    output = to_cells(me, scaled.T, image_band, fields)
    grad_fields = to_cells(me, plain.T, grad_band, cotangent)

    positions = samples * lax.axis_size("dp") * lat_total * KW
    factor = 1.0 / math.sqrt(positions)
    sums = summed_over_group(sums).astype(jnp.float32) * factor
    grads = []
    for which in range(2):
        blocks = sums[which, :, :, :edge].reshape(2, groups, edge, count // groups, edge)
        grads.append(jnp.transpose(blocks, (0, 1, 3, 2, 4)).reshape(w_first.shape))
        grads.append(sums[which, :, :, edge].reshape(b_first.shape))
    return (output, grad_fields) + tuple(grads)


def solution(mesh):
    split = P(("parts", "dp"), "space", None, None)
    in_specs = (split, split, P(), P(), P(), P())
    out_specs = (
        split,
        split,
        P("parts", None, None, None),
        P("parts", None, None),
        P("parts", None, None, None),
        P("parts", None, None),
    )
    return jax.shard_map(body, mesh=mesh, in_specs=in_specs, out_specs=out_specs, check_vma=False)
```

time: 217 us -> 225 us (1.037)
  the two profiles are of different devices: /device:TPU:0 before, /device:TPU:13 now
where the time goes in v3:
time: 225 us; the launch traced here: 224 us
  waiting for transfers between devices  79.4 us (35%)
  starting transfers between devices  61.3 us (27%)
  local copies, waits for them, and re-layouts  49.8 us (22%)
  Pallas kernels  28.3 us (13%)
  other arithmetic  4.37 us (2%)
    ppermute x44, waiting for transfers between devices, swap_with(): return lax.ppermute(values, axis, [(i, i ^ distance) for i in range(size)])  79.4 us
    ppermute x44, starting transfers between devices, swap_with(): return lax.ppermute(values, axis, [(i, i ^ distance) for i in range(size)])  61.3 us
    unnamed x125, local copies, waits for them, and re-layouts  39.1 us
    pallas_call x1, Pallas kernels, backward_mid(): pl.pallas_call(functools.partial(backward_kernel, size_of_block, len(band...  10 us
    pallas_call x1, Pallas kernels, forward_mid(): pl.pallas_call(functools.partial(forward_kernel, len(bands)), grid_spec=p...  8.71 us
  transfers between devices with their start and end apart: 44, of which 17 were waited for; matrix products, arithmetic and copies ran while one was open for 5% of the time, Pallas kernels for 7%

profile of v3, /device:TPU:13, one launch (start us, length us, event | category | flops | bytes accessed | tf_op | source)
XLA Modules:
  0.0 224.2 jit_solution(9574712525872915229)
XLA Ops:
  5.7 2.4 %collective-permute-start.2 = (bf16[4,2,16,768]{3,2,1,0:T(8,128)(2,1)S(1)}, bf16[4,2,16,768]{3,2,1,0:T(8,128)(2,1)S(1)}, u32[]{:S(2)}, u32[]{:S(2)}) collective-permute-start(bf16[4,2,16,768]{3,2,1,0:T(8,128)(2,1)S(1)} %get-tuple-element.71), channel_id=1, source_target_pairs={{0,6},{2,4},{4,2},{6,0},{8,14},{10,12},{12,10},{14,8},{1,7},{3,5},... | collective-permute-start | bytes 589832 | tf_op jit(solution)/shard_map/ppermute | solution.py:364
  30.3 3.9 %collective-permute-done.4.refs_5_ = bf16[4,2,16,768]{3,2,1,0:T(8,128)(2,1)} collective-permute-done((bf16[4,2,16,768]{3,2,1,0:T(8,128)(2,1)}, bf16[4,2,16,768]{3,2,1,0:T(8,128)(2,1)}, u32[]{:S(2)}, u32[]{:S(2)}) %collective-permute-start.4) | collective-permute-done | bytes 196640 | tf_op jit(solution)/shard_map/ppermute | solution.py:364
  34.2 5.0 %collective-permute-done.5.refs_6_ = bf16[4,2,16,768]{3,2,1,0:T(8,128)(2,1)} collective-permute-done((bf16[4,2,16,768]{3,2,1,0:T(8,128)(2,1)}, bf16[4,2,16,768]{3,2,1,0:T(8,128)(2,1)}, u32[]{:S(2)}, u32[]{:S(2)}) %collective-permute-start.5) | collective-permute-done | bytes 196640 | tf_op jit(solution)/shard_map/ppermute | solution.py:364
  39.2 8.2 %collective-permute-done.6.refs_7_ = bf16[4,2,16,768]{3,2,1,0:T(8,128)(2,1)} collective-permute-done((bf16[4,2,16,768]{3,2,1,0:T(8,128)(2,1)}, bf16[4,2,16,768]{3,2,1,0:T(8,128)(2,1)}, u32[]{:S(2)}, u32[]{:S(2)}) %collective-permute-start.6) | collective-permute-done | bytes 196640 | tf_op jit(solution)/shard_map/ppermute | solution.py:364
  55.1 8.7 %mix_forward.1 = (bf16[4,2,16,768]{3,2,1,0:T(8,128)(2,1)S(1)}, bf16[4,2,16,768]{3,2,1,0:T(8,128)(2,1)}, bf16[4,2,16,768]{3,2,1,0:T(8,128)(2,1)}, bf16[4,2,16,768...) custom-call(s32[1]{0:T(128)} %bitcast.me_ref, ...), custom_call_target="tpu_custom_call" | custom-call | flops 2415919104 | bytes 17301504 | tf_op jit(solution)/shard_map/mix_forward/pallas_call | solution.py:287
  67.7 5.2 %collective-permute-done.19.refs_6_ = bf16[4,2,16,768]{3,2,1,0:T(8,128)(2,1)S(1)} collective-permute-done((bf16[4,2,16,768]{3,2,1,0:T(8,128)(2,1)}, bf16[4,2,16,768]{3,2,1,0:T(8,128)(2,1)S(1)}, u32[]{:S(2)}, u32[]{:S(2)}) %collective-permute-start.19) | collective-permute-done | bytes 196640 | tf_op jit(solution)/shard_map/ppermute | solution.py:364
  72.8 3.8 %collective-permute-done.20.refs_7_ = bf16[4,2,16,768]{3,2,1,0:T(8,128)(2,1)S(1)} collective-permute-done((bf16[4,2,16,768]{3,2,1,0:T(8,128)(2,1)}, bf16[4,2,16,768]{3,2,1,0:T(8,128)(2,1)S(1)}, u32[]{:S(2)}, u32[]{:S(2)}) %collective-permute-start.20) | collective-permute-done | bytes 196640 | tf_op jit(solution)/shard_map/ppermute | solution.py:364
  76.6 10.0 %mix_backward.1 = (bf16[4,2,16,768]{3,2,1,0:T(8,128)(2,1)S(1)}, bf16[4,2,16,768]{3,2,1,0:T(8,128)(2,1)S(1)}, bf16[4,2,16,768]{3,2,1,0:T(8,128)(2,1)S(1)}, bf16[4...) custom-call(s32[1]{0:T(128)} %bitcast.me_ref, ...), custom_call_target="tpu_custom_call" | custom-call | flops 4831838208 | bytes 17301504 | tf_op jit(solution)/shard_map/mix_backward/pallas_call | solution.py:331
  88.2 4.4 %collective-permute-start.28 = (f32[448,384]{1,0:T(8,128)S(1)}, f32[448,384]{1,0:T(8,128)}, u32[]{:S(2)}, u32[]{:S(2)}) collective-permute-start(f32[448,384]{1,0:T(8,128)S(1)} %dynamic-slice_bitcast_fusion), channel_id=1, source_target_pairs={{0,1},{1,0},{2,3},{3,2},{4,5},{5,4},{6,7},{7,6},{8,9},{9,8},{10,11... | collective-permute-start | bytes 2064392 | tf_op jit(solution)/shard_map/ppermute | solution.py:364
  96.6 5.9 %collective-permute-start.35 = (bf16[56,384]{1,0:T(8,128)(2,1)S(1)}, bf16[56,384]{1,0:T(8,128)(2,1)S(1)}, u32[]{:S(2)}, u32[]{:S(2)}) collective-permute-start(bf16[56,384]{1,0:T(8,128)(2,1)S(1)} %get-tuple-element.125), channel_id=1, source_target_pairs={{0,6},{2,4},{4,2},{6,0},{8,14},{10,12},{12,10},{14,8},{1,7},{3,5},... | collective-permute-start | bytes 129032 | tf_op jit(solution)/shard_map/ppermute | solution.py:364
  107.5 3.0 %collective-permute-done.30 = bf16[56,384]{1,0:T(8,128)(2,1)} collective-permute-done((bf16[56,384]{1,0:T(8,128)(2,1)}, bf16[56,384]{1,0:T(8,128)(2,1)}, u32[]{:S(2)}, u32[]{:S(2)}) %collective-permute-start.30) | collective-permute-done | bytes 43040 | tf_op jit(solution)/shard_map/ppermute | solution.py:364
  122.5 9.8 %collective-permute-done.37 = bf16[56,384]{1,0:T(8,128)(2,1)S(1)} collective-permute-done((bf16[56,384]{1,0:T(8,128)(2,1)S(1)}, bf16[56,384]{1,0:T(8,128)(2,1)S(1)}, u32[]{:S(2)}, u32[]{:S(2)}) %collective-permute-start.37) | collective-permute-done | bytes 43040 | tf_op jit(solution)/shard_map/ppermute | solution.py:364
  132.9 3.1 %collective-permute-done.38 = bf16[56,384]{1,0:T(8,128)(2,1)S(1)} collective-permute-done((bf16[56,384]{1,0:T(8,128)(2,1)S(1)}, bf16[56,384]{1,0:T(8,128)(2,1)S(1)}, u32[]{:S(2)}, u32[]{:S(2)}) %collective-permute-start.38) | collective-permute-done | bytes 43040 | tf_op jit(solution)/shard_map/ppermute | solution.py:364
  137.0 3.6 %collective-permute-done.39 = bf16[56,384]{1,0:T(8,128)(2,1)S(1)} collective-permute-done((bf16[56,384]{1,0:T(8,128)(2,1)S(1)}, bf16[56,384]{1,0:T(8,128)(2,1)S(1)}, u32[]{:S(2)}, u32[]{:S(2)}) %collective-permute-start.39) | collective-permute-done | bytes 43040 | tf_op jit(solution)/shard_map/ppermute | solution.py:364
  151.9 5.0 %collective-permute-start.22 = (bf16[4,2,16,768]{3,2,1,0:T(8,128)(2,1)}, bf16[4,2,16,768]{3,2,1,0:T(8,128)(2,1)S(1)}, u32[]{:S(2)}, u32[]{:S(2)}) collective-permute-start(bf16[4,2,16,768]{3,2,1,0:T(8,128)(2,1)} %copy-done.28), channel_id=1, source_target_pairs={{0,4},{2,6},{4,0},{6,2},{8,12},{10,14},{12,8},{14,10},{1,5},{3,7},... | collective-permute-start | bytes 589832 | tf_op jit(solution)/shard_map/ppermute | solution.py:364
  158.3 3.7 %collective-permute-done.12.refs_6_ = bf16[4,2,16,768]{3,2,1,0:T(8,128)(2,1)S(1)} collective-permute-done((bf16[4,2,16,768]{3,2,1,0:T(8,128)(2,1)}, bf16[4,2,16,768]{3,2,1,0:T(8,128)(2,1)S(1)}, u32[]{:S(2)}, u32[]{:S(2)}) %collective-permute-start.12) | collective-permute-done | bytes 196640 | tf_op jit(solution)/shard_map/ppermute | solution.py:364
  162.7 10.6 %collective-permute-start.43 = (bf16[8,56,384]{2,1,0:T(8,128)(2,1)}, bf16[8,56,384]{2,1,0:T(8,128)(2,1)}, u32[]{:S(2)}, u32[]{:S(2)}) collective-permute-start(bf16[8,56,384]{2,1,0:T(8,128)(2,1)} %bitcast_dynamic-update-slice_fusion), channel_id=1, source_target_pairs={{0,1},{1,0},{2,3},{3,2},{4,5},{5,4},{6,7},{7,6},{8,9},{9,8},{10,11... | collective-permute-start | bytes 1032200 | tf_op jit(solution)/shard_map/ppermute | solution.py:364
  174.7 3.3 %collective-permute-start.25 = (bf16[4,2,16,768]{3,2,1,0:T(8,128)(2,1)}, bf16[4,2,16,768]{3,2,1,0:T(8,128)(2,1)}, u32[]{:S(2)}, u32[]{:S(2)}) collective-permute-start(bf16[4,2,16,768]{3,2,1,0:T(8,128)(2,1)} %copy-done.23), channel_id=1, source_target_pairs={{0,10},{2,8},{4,14},{6,12},{8,2},{10,0},{12,6},{14,4},{1,11},{3,9}... | collective-permute-start | bytes 589832 | tf_op jit(solution)/shard_map/ppermute | solution.py:364
  185.1 3.1 %copy.37 = bf16[4,2,180,768]{3,1,2,0:T(2,128)(2,1)} copy(bf16[4,2,180,768]{3,2,1,0:T(8,128)(2,1)S(1)} %to_cells.2) | data formatting | bytes 4423680
  188.2 10.4 %collective-permute-done.25.refs_5_ = bf16[4,2,16,768]{3,2,1,0:T(8,128)(2,1)} collective-permute-done((bf16[4,2,16,768]{3,2,1,0:T(8,128)(2,1)}, bf16[4,2,16,768]{3,2,1,0:T(8,128)(2,1)}, u32[]{:S(2)}, u32[]{:S(2)}) %collective-permute-start.25) | collective-permute-done | bytes 196640 | tf_op jit(solution)/shard_map/ppermute | solution.py:364
  198.6 5.8 %collective-permute-done.26.refs_6_ = bf16[4,2,16,768]{3,2,1,0:T(8,128)(2,1)} collective-permute-done((bf16[4,2,16,768]{3,2,1,0:T(8,128)(2,1)}, bf16[4,2,16,768]{3,2,1,0:T(8,128)(2,1)}, u32[]{:S(2)}, u32[]{:S(2)}) %collective-permute-start.26) | collective-permute-done | bytes 196640 | tf_op jit(solution)/shard_map/ppermute | solution.py:364
  204.4 8.0 %collective-permute-done.27.refs_7_ = bf16[4,2,16,768]{3,2,1,0:T(8,128)(2,1)} collective-permute-done((bf16[4,2,16,768]{3,2,1,0:T(8,128)(2,1)}, bf16[4,2,16,768]{3,2,1,0:T(8,128)(2,1)}, u32[]{:S(2)}, u32[]{:S(2)}) %collective-permute-start.27) | collective-permute-done | bytes 196640 | tf_op jit(solution)/shard_map/ppermute | solution.py:364
  212.5 2.8 %to_cells.3 = bf16[4,2,180,768]{3,2,1,0:T(8,128)(2,1)S(1)} custom-call(s32[1]{0:T(128)} %bitcast.me_ref, bf16[180,128]{1,0:T(8,128)(2,1)S(1)} %copy-done.17, bf16[4,2,180,768]{3,2,1,0:T(8,128)(2,1)S(1)} %copy-done.1, bf16[4,2,16,768]{3,2,1,0:T(8,128)(2,1)S(1)} %get-tuple-element.97.refs_0_, bf16[4,2,16,768]{3,2,1,0:T(8,128)(2,1)S(1)} %copy-done.6, ...), custom_call_target="tpu_custom_call" | custom-call | flops 283115520 | bytes 5996544 | tf_op jit(solution)/shard_map/to_cells/pallas_call | solution.py:156
  215.3 3.1 %copy.38 = bf16[4,2,180,768]{3,1,2,0:T(2,128)(2,1)} copy(bf16[4,2,180,768]{3,2,1,0:T(8,128)(2,1)S(1)} %to_cells.3) | data formatting | bytes 4423680
  (224 shorter events, 90.3 us)
Async XLA Ops:
  5.7 16.5 %collective-permute-start.2 = (bf16[4,2,16,768]{3,2,1,0:T(8,128)(2,1)S(1)}, bf16[4,2,16,768]{3,2,1,0:T(8,128)(2,1)S(1)}, u32[]{:S(2)}, u32[]{:S(2)}) collective-permute-start(bf16[4,2,16,768]{3,2,1,0:T(8,128)(2,1)S(1)} %get-tuple-element.71), channel_id=1, source_target_pairs={{0,6},{2,4},{4,2},{6,0},{8,14},{10,12},{12,10},{14,8},{1,7},{3,5},... | collective-permute-start | bytes 589832 | tf_op jit(solution)/shard_map/ppermute | solution.py:364
  8.1 15.4 %collective-permute-start.3 = (bf16[4,2,16,768]{3,2,1,0:T(8,128)(2,1)S(1)}, bf16[4,2,16,768]{3,2,1,0:T(8,128)(2,1)S(1)}, u32[]{:S(2)}, u32[]{:S(2)}) collective-permute-start(bf16[4,2,16,768]{3,2,1,0:T(8,128)(2,1)S(1)} %get-tuple-element.72), channel_id=1, source_target_pairs={{0,8},{2,10},{4,12},{6,14},{8,0},{10,2},{12,4},{14,6},{1,9},{3,11}... | collective-permute-start | bytes 589832 | tf_op jit(solution)/shard_map/ppermute | solution.py:364
  10.5 23.8 %collective-permute-start.4 = (bf16[4,2,16,768]{3,2,1,0:T(8,128)(2,1)}, bf16[4,2,16,768]{3,2,1,0:T(8,128)(2,1)}, u32[]{:S(2)}, u32[]{:S(2)}) collective-permute-start(bf16[4,2,16,768]{3,2,1,0:T(8,128)(2,1)} %get-tuple-element.73), channel_id=1, source_target_pairs={{0,10},{2,8},{4,14},{6,12},{8,2},{10,0},{12,6},{14,4},{1,11},{3,9}... | collective-permute-start | bytes 589832 | tf_op jit(solution)/shard_map/ppermute | solution.py:364
  19.2 20.1 %collective-permute-start.5 = (bf16[4,2,16,768]{3,2,1,0:T(8,128)(2,1)}, bf16[4,2,16,768]{3,2,1,0:T(8,128)(2,1)}, u32[]{:S(2)}, u32[]{:S(2)}) collective-permute-start(bf16[4,2,16,768]{3,2,1,0:T(8,128)(2,1)} %get-tuple-element.74), channel_id=1, source_target_pairs={{0,12},{2,14},{4,8},{6,10},{8,4},{10,6},{12,0},{14,2},{1,13},{3,15... | collective-permute-start | bytes 589832 | tf_op jit(solution)/shard_map/ppermute | solution.py:364
  21.1 26.3 %collective-permute-start.6 = (bf16[4,2,16,768]{3,2,1,0:T(8,128)(2,1)}, bf16[4,2,16,768]{3,2,1,0:T(8,128)(2,1)}, u32[]{:S(2)}, u32[]{:S(2)}) collective-permute-start(bf16[4,2,16,768]{3,2,1,0:T(8,128)(2,1)} %get-tuple-element.75), channel_id=1, source_target_pairs={{0,14},{2,12},{4,10},{6,8},{8,6},{10,4},{12,2},{14,0},{1,15},{3,13... | collective-permute-start | bytes 589832 | tf_op jit(solution)/shard_map/ppermute | solution.py:364
  22.9 24.5 %collective-permute-start.14 = (bf16[4,2,16,768]{3,2,1,0:T(8,128)(2,1)}, bf16[4,2,16,768]{3,2,1,0:T(8,128)(2,1)S(1)}, u32[]{:S(2)}, u32[]{:S(2)}) collective-permute-start(bf16[4,2,16,768]{3,2,1,0:T(8,128)(2,1)} %get-tuple-element.90), channel_id=1, source_target_pairs={{0,2},{2,0},{4,6},{6,4},{8,10},{10,8},{12,14},{14,12},{1,3},{3,1},... | collective-permute-start | bytes 589832 | tf_op jit(solution)/shard_map/ppermute | solution.py:364
  24.2 23.9 %collective-permute-start.15 = (bf16[4,2,16,768]{3,2,1,0:T(8,128)(2,1)}, bf16[4,2,16,768]{3,2,1,0:T(8,128)(2,1)}, u32[]{:S(2)}, u32[]{:S(2)}) collective-permute-start(bf16[4,2,16,768]{3,2,1,0:T(8,128)(2,1)} %get-tuple-element.91), channel_id=1, source_target_pairs={{0,4},{2,6},{4,0},{6,2},{8,12},{10,14},{12,8},{14,10},{1,5},{3,7},... | collective-permute-start | bytes 589832 | tf_op jit(solution)/shard_map/ppermute | solution.py:364
  34.2 33.4 %collective-permute-start.16 = (bf16[4,2,16,768]{3,2,1,0:T(8,128)(2,1)}, bf16[4,2,16,768]{3,2,1,0:T(8,128)(2,1)S(1)}, u32[]{:S(2)}, u32[]{:S(2)}) collective-permute-start(bf16[4,2,16,768]{3,2,1,0:T(8,128)(2,1)} %copy-done.50), channel_id=1, source_target_pairs={{0,6},{2,4},{4,2},{6,0},{8,14},{10,12},{12,10},{14,8},{1,7},{3,5},... | collective-permute-start | bytes 589832 | tf_op jit(solution)/shard_map/ppermute | solution.py:364
  39.2 28.4 %collective-permute-start.17 = (bf16[4,2,16,768]{3,2,1,0:T(8,128)(2,1)}, bf16[4,2,16,768]{3,2,1,0:T(8,128)(2,1)S(1)}, u32[]{:S(2)}, u32[]{:S(2)}) collective-permute-start(bf16[4,2,16,768]{3,2,1,0:T(8,128)(2,1)} %copy-done.45), channel_id=1, source_target_pairs={{0,8},{2,10},{4,12},{6,14},{8,0},{10,2},{12,4},{14,6},{1,9},{3,11}... | collective-permute-start | bytes 589832 | tf_op jit(solution)/shard_map/ppermute | solution.py:364
  47.4 20.2 %collective-permute-start.18 = (bf16[4,2,16,768]{3,2,1,0:T(8,128)(2,1)}, bf16[4,2,16,768]{3,2,1,0:T(8,128)(2,1)S(1)}, u32[]{:S(2)}, u32[]{:S(2)}) collective-permute-start(bf16[4,2,16,768]{3,2,1,0:T(8,128)(2,1)} %copy-done.42), channel_id=1, source_target_pairs={{0,10},{2,8},{4,14},{6,12},{8,2},{10,0},{12,6},{14,4},{1,11},{3,9}... | collective-permute-start | bytes 589832 | tf_op jit(solution)/shard_map/ppermute | solution.py:364
  48.1 24.7 %collective-permute-start.19 = (bf16[4,2,16,768]{3,2,1,0:T(8,128)(2,1)}, bf16[4,2,16,768]{3,2,1,0:T(8,128)(2,1)S(1)}, u32[]{:S(2)}, u32[]{:S(2)}) collective-permute-start(bf16[4,2,16,768]{3,2,1,0:T(8,128)(2,1)} %copy-done.39), channel_id=1, source_target_pairs={{0,12},{2,14},{4,8},{6,10},{8,4},{10,6},{12,0},{14,2},{1,13},{3,15... | collective-permute-start | bytes 589832 | tf_op jit(solution)/shard_map/ppermute | solution.py:364
  48.1 28.5 %collective-permute-start.20 = (bf16[4,2,16,768]{3,2,1,0:T(8,128)(2,1)}, bf16[4,2,16,768]{3,2,1,0:T(8,128)(2,1)S(1)}, u32[]{:S(2)}, u32[]{:S(2)}) collective-permute-start(bf16[4,2,16,768]{3,2,1,0:T(8,128)(2,1)} %copy-done.36), channel_id=1, source_target_pairs={{0,14},{2,12},{4,10},{6,8},{8,6},{10,4},{12,2},{14,0},{1,15},{3,13... | collective-permute-start | bytes 589832 | tf_op jit(solution)/shard_map/ppermute | solution.py:364
  115.1 29.3 %collective-permute-start.7 = (bf16[4,2,16,768]{3,2,1,0:T(8,128)(2,1)}, bf16[4,2,16,768]{3,2,1,0:T(8,128)(2,1)S(1)}, u32[]{:S(2)}, u32[]{:S(2)}) collective-permute-start(bf16[4,2,16,768]{3,2,1,0:T(8,128)(2,1)} %get-tuple-element.77), channel_id=1, source_target_pairs={{0,2},{2,0},{4,6},{6,4},{8,10},{10,8},{12,14},{14,12},{1,3},{3,1},... | collective-permute-start | bytes 589832 | tf_op jit(solution)/shard_map/ppermute | solution.py:364
  117.1 31.4 %collective-permute-start.8 = (bf16[4,2,16,768]{3,2,1,0:T(8,128)(2,1)}, bf16[4,2,16,768]{3,2,1,0:T(8,128)(2,1)S(1)}, u32[]{:S(2)}, u32[]{:S(2)}) collective-permute-start(bf16[4,2,16,768]{3,2,1,0:T(8,128)(2,1)} %get-tuple-element.78), channel_id=1, source_target_pairs={{0,4},{2,6},{4,0},{6,2},{8,12},{10,14},{12,8},{14,10},{1,5},{3,7},... | collective-permute-start | bytes 589832 | tf_op jit(solution)/shard_map/ppermute | solution.py:364
  118.6 30.3 %collective-permute-start.9 = (bf16[4,2,16,768]{3,2,1,0:T(8,128)(2,1)}, bf16[4,2,16,768]{3,2,1,0:T(8,128)(2,1)S(1)}, u32[]{:S(2)}, u32[]{:S(2)}) collective-permute-start(bf16[4,2,16,768]{3,2,1,0:T(8,128)(2,1)} %get-tuple-element.79), channel_id=1, source_target_pairs={{0,6},{2,4},{4,2},{6,0},{8,14},{10,12},{12,10},{14,8},{1,7},{3,5},... | collective-permute-start | bytes 589832 | tf_op jit(solution)/shard_map/ppermute | solution.py:364
  118.6 31.6 %collective-permute-start.10 = (bf16[4,2,16,768]{3,2,1,0:T(8,128)(2,1)}, bf16[4,2,16,768]{3,2,1,0:T(8,128)(2,1)S(1)}, u32[]{:S(2)}, u32[]{:S(2)}) collective-permute-start(bf16[4,2,16,768]{3,2,1,0:T(8,128)(2,1)} %copy-done.31), channel_id=1, source_target_pairs={{0,8},{2,10},{4,12},{6,14},{8,0},{10,2},{12,4},{14,6},{1,9},{3,11}... | collective-permute-start | bytes 589832 | tf_op jit(solution)/shard_map/ppermute | solution.py:364
  148.9 24.4 %collective-permute-start.13 = (bf16[4,2,16,768]{3,2,1,0:T(8,128)(2,1)}, bf16[4,2,16,768]{3,2,1,0:T(8,128)(2,1)S(1)}, u32[]{:S(2)}, u32[]{:S(2)}) collective-permute-start(bf16[4,2,16,768]{3,2,1,0:T(8,128)(2,1)} %copy-done.25), channel_id=1, source_target_pairs={{0,14},{2,12},{4,10},{6,8},{8,6},{10,4},{12,2},{14,0},{1,15},{3,13... | collective-permute-start | bytes 589832 | tf_op jit(solution)/shard_map/ppermute | solution.py:364
  150.2 23.8 %collective-permute-start.21 = (bf16[4,2,16,768]{3,2,1,0:T(8,128)(2,1)}, bf16[4,2,16,768]{3,2,1,0:T(8,128)(2,1)S(1)}, u32[]{:S(2)}, u32[]{:S(2)}) collective-permute-start(bf16[4,2,16,768]{3,2,1,0:T(8,128)(2,1)} %copy-done.30), channel_id=1, source_target_pairs={{0,2},{2,0},{4,6},{6,4},{8,10},{10,8},{12,14},{14,12},{1,3},{3,1},... | collective-permute-start | bytes 589832 | tf_op jit(solution)/shard_map/ppermute | solution.py:364
  151.9 26.0 %collective-permute-start.22 = (bf16[4,2,16,768]{3,2,1,0:T(8,128)(2,1)}, bf16[4,2,16,768]{3,2,1,0:T(8,128)(2,1)S(1)}, u32[]{:S(2)}, u32[]{:S(2)}) collective-permute-start(bf16[4,2,16,768]{3,2,1,0:T(8,128)(2,1)} %copy-done.28), channel_id=1, source_target_pairs={{0,4},{2,6},{4,0},{6,2},{8,12},{10,14},{12,8},{14,10},{1,5},{3,7},... | collective-permute-start | bytes 589832 | tf_op jit(solution)/shard_map/ppermute | solution.py:364
  156.9 22.2 %collective-permute-start.23 = (bf16[4,2,16,768]{3,2,1,0:T(8,128)(2,1)}, bf16[4,2,16,768]{3,2,1,0:T(8,128)(2,1)S(1)}, u32[]{:S(2)}, u32[]{:S(2)}) collective-permute-start(bf16[4,2,16,768]{3,2,1,0:T(8,128)(2,1)} %copy-done.27), channel_id=1, source_target_pairs={{0,6},{2,4},{4,2},{6,0},{8,14},{10,12},{12,10},{14,8},{1,7},{3,5},... | collective-permute-start | bytes 589832 | tf_op jit(solution)/shard_map/ppermute | solution.py:364
  162.7 55.6 %collective-permute-start.43 = (bf16[8,56,384]{2,1,0:T(8,128)(2,1)}, bf16[8,56,384]{2,1,0:T(8,128)(2,1)}, u32[]{:S(2)}, u32[]{:S(2)}) collective-permute-start(bf16[8,56,384]{2,1,0:T(8,128)(2,1)} %bitcast_dynamic-update-slice_fusion), channel_id=1, source_target_pairs={{0,1},{1,0},{2,3},{3,2},{4,5},{5,4},{6,7},{7,6},{8,9},{9,8},{10,11... | collective-permute-start | bytes 1032200 | tf_op jit(solution)/shard_map/ppermute | solution.py:364
  174.7 23.9 %collective-permute-start.25 = (bf16[4,2,16,768]{3,2,1,0:T(8,128)(2,1)}, bf16[4,2,16,768]{3,2,1,0:T(8,128)(2,1)}, u32[]{:S(2)}, u32[]{:S(2)}) collective-permute-start(bf16[4,2,16,768]{3,2,1,0:T(8,128)(2,1)} %copy-done.23), channel_id=1, source_target_pairs={{0,10},{2,8},{4,14},{6,12},{8,2},{10,0},{12,6},{14,4},{1,11},{3,9}... | collective-permute-start | bytes 589832 | tf_op jit(solution)/shard_map/ppermute | solution.py:364
  178.6 25.8 %collective-permute-start.26 = (bf16[4,2,16,768]{3,2,1,0:T(8,128)(2,1)}, bf16[4,2,16,768]{3,2,1,0:T(8,128)(2,1)}, u32[]{:S(2)}, u32[]{:S(2)}) collective-permute-start(bf16[4,2,16,768]{3,2,1,0:T(8,128)(2,1)} %copy-done.22), channel_id=1, source_target_pairs={{0,12},{2,14},{4,8},{6,10},{8,4},{10,6},{12,0},{14,2},{1,13},{3,15... | collective-permute-start | bytes 589832 | tf_op jit(solution)/shard_map/ppermute | solution.py:364
  179.9 32.6 %collective-permute-start.27 = (bf16[4,2,16,768]{3,2,1,0:T(8,128)(2,1)}, bf16[4,2,16,768]{3,2,1,0:T(8,128)(2,1)}, u32[]{:S(2)}, u32[]{:S(2)}) collective-permute-start(bf16[4,2,16,768]{3,2,1,0:T(8,128)(2,1)} %copy-done.21), channel_id=1, source_target_pairs={{0,14},{2,12},{4,10},{6,8},{8,6},{10,4},{12,2},{14,0},{1,15},{3,13... | collective-permute-start | bytes 589832 | tf_op jit(solution)/shard_map/ppermute | solution.py:364
  (81 other events, 582.2 us)

commit v4 on v3

--- a/solution.py
+++ b/solution.py
@@ -12,7 +12,8 @@
 
 KW = 64
 shrink_level = 0.05
-VMEM_BYTES = 48 * 1024 * 1024
+HELD = 5
+MIB = 1024 * 1024
 
 
 def product_of(former, latter):
@@ -83,7 +84,7 @@
         out_shape=(shape,) * len(weights),
         in_specs=[pl.BlockSpec((2, per, size, size), lambda g: (0, g, 0, 0))] * len(weights),
         out_specs=(group_spec(lanes, lanes),) * len(weights),
-        compiler_params=params("arbitrary"),
+        compiler_params=params(12),
         cost_estimate=pl.CostEstimate(
             flops=len(weights) * 2 * count * size * size * lanes,
             bytes_accessed=len(weights) * 2 * groups * lanes * lanes,
@@ -93,8 +94,10 @@
     )(*weights)
 
 
-def params(*semantics):
-    return pltpu.CompilerParams(vmem_limit_bytes=VMEM_BYTES, dimension_semantics=semantics)
+def params(mebibytes):
+    return pltpu.CompilerParams(
+        vmem_limit_bytes=mebibytes * MIB, dimension_semantics=("arbitrary",)
+    )
 
 
 def place_of(me_ref, offset, rows):
@@ -128,7 +131,7 @@
             scratch_shapes=[pltpu.VMEM((rows, size, channels), jnp.bfloat16)],
         ),
         out_shape=(jax.ShapeDtypeStruct((samples,) + share, jnp.bfloat16),) * owners,
-        compiler_params=params("arbitrary"),
+        compiler_params=params(12),
         cost_estimate=pl.CostEstimate(
             flops=2 * samples * rows * size * width * channels,
             bytes_accessed=2 * samples * rows * channels * (width + size),
@@ -164,7 +167,7 @@
             scratch_shapes=[pltpu.VMEM((rows, size, channels), jnp.bfloat16)],
         ),
         out_shape=jax.ShapeDtypeStruct(base.shape, jnp.bfloat16),
-        compiler_params=params("arbitrary"),
+        compiler_params=params(12),
         cost_estimate=pl.CostEstimate(
             flops=2 * samples * rows * size * width * channels,
             bytes_accessed=2 * samples * rows * channels * (2 * width + size),
@@ -205,28 +208,32 @@
             bands_ref[sample] = band_ref[sample, place].reshape(rows, share, width)
 
 
+def activate(mixed_ref, w1_ref, b1_ref):
+    pre = product_of(mixed_ref[0], w1_ref[0]) + b1_ref[0]
+    logistic = sigmoid_of(pre)
+    return logistic, pre * logistic
+
+
+def bend(act_ref, w2_ref, b2_ref):
+    out = product_of(act_ref[...], w2_ref[0]) + b2_ref[0]
+    return out, jnp.tanh(out * (1.0 / shrink_level))
+
+
 def forward_kernel(owners, me_ref, lat_ref, unlat_ref, w1_ref, b1_ref, w2_ref, b2_ref, *refs):
     bands_refs, image_refs = refs[:owners], refs[owners : 2 * owners]
-    mixed_ref, act_ref, gate_ref, bend_ref, shrunk_ref, band_ref = refs[2 * owners :]
+    mixed_ref, act_ref, band_ref = refs[2 * owners :]
     mix_lat(me_ref, lat_ref, bands_refs, band_ref, mixed_ref.at[0])
-    pre = product_of(mixed_ref[0], w1_ref[0]) + b1_ref[0]
-    logistic = sigmoid_of(pre)
-    act = pre * logistic
-    act_ref[0] = act.astype(jnp.bfloat16)
-    gate_ref[0] = logistic + act * (1.0 - logistic)
-    out = product_of(act_ref[0], w2_ref[0]) + b2_ref[0]
-    bent = jnp.tanh(out * (1.0 / shrink_level))
-    bend_ref[0] = bent * bent
-    shrunk_ref[...] = (out - shrink_level * bent).astype(jnp.bfloat16)
-    unmix_lat(me_ref, unlat_ref, shrunk_ref, band_ref, image_refs)
+    act_ref[...] = activate(mixed_ref, w1_ref, b1_ref)[1].astype(jnp.bfloat16)
+    out, bent = bend(act_ref, w2_ref, b2_ref)
+    act_ref[...] = (out - shrink_level * bent).astype(jnp.bfloat16)
+    unmix_lat(me_ref, unlat_ref, act_ref, band_ref, image_refs)
 
 
 def backward_kernel(
-    block_size, owners, me_ref, lat_ref, unlat_ref, w1_ref, w2_ref,
-    mixed_ref, act_ref, gate_ref, bend_ref, *refs
+    block_size, owners, me_ref, lat_ref, unlat_ref, w1_ref, b1_ref, w2_ref, b2_ref, mixed_ref, *refs
 ):
     bands_refs, image_refs = refs[:owners], refs[owners : 2 * owners]
-    sums_ref, cot_ref, kept_ref, band_ref = refs[2 * owners :]
+    sums_ref, act_ref, gate_ref, cot_ref, kept_ref, band_ref = refs[2 * owners :]
     transposed = (((1,), (1,)), ((), ()))
     summed = (((0,), (0,)), ((), ()))
 
@@ -251,11 +258,15 @@
             row = bias[:, part * width : (part + 1) * width]
             sums_ref[slot, part, 0, size:] = jnp.where(first, row, 0.0)
 
+    logistic, act = activate(mixed_ref, w1_ref, b1_ref)
+    act_ref[...] = act.astype(jnp.bfloat16)
+    gate_ref[...] = logistic + act * (1.0 - logistic)
     mix_lat(me_ref, lat_ref, bands_refs, band_ref, cot_ref)
-    kept_ref[...] = (cot_ref[...].astype(jnp.float32) * bend_ref[0]).astype(jnp.bfloat16)
+    _, bent = bend(act_ref, w2_ref, b2_ref)
+    kept_ref[...] = (cot_ref[...].astype(jnp.float32) * (bent * bent)).astype(jnp.bfloat16)
     back = times(kept_ref[...], w2_ref[0], transposed)
-    cot_ref[...] = (back * gate_ref[0]).astype(jnp.bfloat16)
-    weight_sums(act_ref[0], kept_ref[...], 1)
+    cot_ref[...] = (back * gate_ref[...]).astype(jnp.bfloat16)
+    weight_sums(act_ref[...], kept_ref[...], 1)
     kept_ref[...] = times(cot_ref[...], w1_ref[0], transposed).astype(jnp.bfloat16)
     weight_sums(mixed_ref[0], cot_ref[...], 0)
     unmix_lat(me_ref, unlat_ref, kept_ref, band_ref, image_refs)
@@ -295,19 +306,14 @@
                 group_spec(lanes, lanes), group_spec(1, lanes),
                 *specs,
             ],
-            out_specs=specs + (state_spec,) * 4,
+            out_specs=specs + (state_spec,),
             scratch_shapes=[
                 pltpu.VMEM((positions, lanes), jnp.bfloat16),
                 pltpu.VMEM((samples, size, lanes // 2), jnp.bfloat16),
             ],
         ),
-        out_shape=shapes_of(bands) + (
-            jax.ShapeDtypeStruct(state, jnp.bfloat16),
-            jax.ShapeDtypeStruct(state, jnp.bfloat16),
-            jax.ShapeDtypeStruct(state, jnp.float32),
-            jax.ShapeDtypeStruct(state, jnp.float32),
-        ),
-        compiler_params=params("arbitrary"),
+        out_shape=shapes_of(bands) + (jax.ShapeDtypeStruct(state, jnp.bfloat16),),
+        compiler_params=params(28),
         cost_estimate=pl.CostEstimate(
             flops=4 * groups * positions * lanes * lanes,
             bytes_accessed=16 * groups * positions * lanes + 4 * groups * lanes * lanes,
@@ -315,16 +321,15 @@
         ),
         name="mix_forward",
     )(me, lat, unlat, w1, b1, w2, b2, *bands)
-    return results[: len(bands)], results[len(bands) :]
-
-
-def backward_mid(me, lat, unlat, bands, w1, w2, state, count):
+    return results[: len(bands)], results[len(bands)]
+
+
+def backward_mid(me, lat, unlat, bands, w1, b1, w2, b2, state, count):
     groups, lanes, _ = w1.shape
     size = lat.shape[0]
     samples = bands[0].shape[0]
     positions = samples * size // 2
     table = pl.BlockSpec((size, size), lambda g, _: (0, 0))
-    state_spec = group_spec(positions, lanes)
     specs = bands_specs(bands, groups)
     size_of_block = lanes // 2 // (count // groups)
     rows = size_of_block + 16
@@ -334,62 +339,111 @@
             num_scalar_prefetch=1,
             grid=(groups,),
             in_specs=[
-                table, table, group_spec(lanes, lanes), group_spec(lanes, lanes),
-                *([state_spec] * 4), *specs,
+                table, table,
+                group_spec(lanes, lanes), group_spec(1, lanes),
+                group_spec(lanes, lanes), group_spec(1, lanes),
+                group_spec(positions, lanes), *specs,
             ],
             out_specs=specs + (
                 pl.BlockSpec((2, 2, 1, rows, lanes // 2), lambda g, _: (0, 0, g, 0, 0)),
             ),
             scratch_shapes=[
                 pltpu.VMEM((positions, lanes), jnp.bfloat16),
+                pltpu.VMEM((positions, lanes), jnp.float32),
+                pltpu.VMEM((positions, lanes), jnp.bfloat16),
                 pltpu.VMEM((positions, lanes), jnp.bfloat16),
                 pltpu.VMEM((samples, size, lanes // 2), jnp.bfloat16),
             ],
         ),
         out_shape=shapes_of(bands)
         + (jax.ShapeDtypeStruct((2, 2, groups, rows, lanes // 2), jnp.float32),),
-        compiler_params=params("arbitrary"),
+        compiler_params=params(32),
         cost_estimate=pl.CostEstimate(
             flops=8 * groups * positions * lanes * lanes,
             bytes_accessed=16 * groups * positions * lanes + 4 * groups * lanes * lanes,
             transcendentals=0,
         ),
         name="mix_backward",
-    )(me, lat, unlat, w1, w2, *state, *bands)
+    )(me, lat, unlat, w1, b1, w2, b2, state, *bands)
     return results[: len(bands)], results[len(bands)]
 
 
-def swap_with(values, axis, distance):
-    size = lax.axis_size(axis)
-    return lax.ppermute(values, axis, [(i, i ^ distance) for i in range(size)])
-
-
-def far_first(size):
-    return sorted(range(1, size), key=lambda offset: (-(offset >> 2), offset))
-
-
-def summed_over_group(sums):
-    lanes = sums.shape[-1]
-    size = lax.axis_size("space")
-    me, side = lax.axis_index("space"), lax.axis_index("dp")
-    halves = sums.reshape(2, -1, lanes)
-    given = lax.dynamic_index_in_dim(halves, 1 - side, 0, keepdims=False)
-    held = lax.dynamic_index_in_dim(halves, side, 0, keepdims=False) + swap_with(given, "dp", 1)
-    shares = held.reshape(size, -1, lanes)
-    total = lax.dynamic_index_in_dim(shares, me, 0, keepdims=False)
-    for offset in far_first(size):
-        given = lax.dynamic_index_in_dim(shares, me ^ offset, 0, keepdims=False)
-        taken = swap_with(given.astype(jnp.bfloat16), "space", offset)
-        total = total + taken.astype(jnp.float32)
-    total = total.astype(jnp.bfloat16)
-    parts = jnp.zeros((size,) + total.shape, total.dtype)
-    parts = lax.dynamic_update_index_in_dim(parts, total, me, 0)
-    for offset in far_first(size):
-        taken = swap_with(total, "space", offset)
-        parts = lax.dynamic_update_index_in_dim(parts, taken, me ^ offset, 0)
-    other = swap_with(parts, "dp", 1)
-    both = jnp.where(side == 0, jnp.stack([parts, other]), jnp.stack([other, parts]))
-    return both.reshape(sums.shape)
+def swap_with(values, axis, distance, after=()):
+    if len(after) > 0:
+        values, _ = lax.optimization_barrier((values, tuple(after)))
+    pairs = [(i, i ^ distance) for i in range(lax.axis_size(axis))]
+    return lax.ppermute(values, axis, pairs)
+
+
+def mixed_order(size):
+    far = list(range(size // 2, size))
+    near = [offset for offset in (2, 3, 1) if offset < size // 2]
+    near += list(range(4, size // 2))
+    order = []
+    while far or near:
+        order += far[:1] + near[:1]
+        far, near = far[1:], near[1:]
+    return order
+
+
+def pick(pair, side):
+    return lax.dynamic_index_in_dim(pair, side, 0, keepdims=False)
+
+
+def by_place(blocks, bits):
+    shape = blocks.shape
+    for level, bit in enumerate(bits):
+        split = blocks.reshape((2**level, 2, -1) + shape[-2:])
+        blocks = jnp.where(bit == 0, split, jnp.concatenate([split[:, 1:], split[:, :1]], axis=1))
+    return blocks
+
+
+class GroupSum:
+    def __init__(self, sums):
+        self.lanes = sums.shape[-1]
+        self.shape = sums.shape
+        self.side = lax.axis_index("dp")
+        self.me = lax.axis_index("space")
+        self.count = lax.axis_size("space") // 2
+        self.held = sums.reshape(-1, self.lanes)
+
+    def halve(self, axis, distance, bit, after):
+        pair = self.held.reshape(2, -1, self.lanes)
+        taken = swap_with(pick(pair, 1 - bit), axis, distance, after)
+        self.held = pick(pair, bit) + taken
+
+    def over_dp(self, after):
+        self.halve("dp", 1, self.side, after)
+
+    def over_next(self, after):
+        self.halve("space", 1, self.me % 2, after)
+
+    def scatter(self, after):
+        shares = self.held.reshape(self.count, -1, self.lanes)
+        place = self.me // 2
+        total = pick(shares, place)
+        for offset in range(1, self.count):
+            given = pick(shares, place ^ offset).astype(jnp.bfloat16)
+            total += swap_with(given, "space", 2 * offset, after).astype(jnp.float32)
+        self.total = total.astype(jnp.bfloat16)
+
+    def gather(self, after):
+        taken = [self.total]
+        for offset in range(1, self.count):
+            taken.append(swap_with(self.total, "space", 2 * offset, after))
+        self.quarter = jnp.stack(taken)
+
+    def gather_next(self, after):
+        self.half = jnp.stack([self.quarter, swap_with(self.quarter, "space", 1, after)])
+
+    def join(self, after):
+        both = jnp.stack([self.half, swap_with(self.half, "dp", 1, after)])
+        bits = [self.side, self.me % 2]
+        level = self.count
+        while level > 1:
+            bits.append(self.me // level % 2)
+            level //= 2
+        return by_place(both, bits).reshape(self.shape)
 
 
 def body(fields, cotangent, w_first, b_first, w_second, b_second):
@@ -402,23 +456,20 @@
     direct = 2 * modes % 16 == 0
     lead = owners if direct else 1
 
-    def swapped(blocks):
-        taken = {0: blocks[0]}
-        for offset in far_first(owners):
-            taken[offset] = swap_with(blocks[offset], "space", offset)
-        return [taken[offset] for offset in range(owners)]
+    order = mixed_order(owners)
 
     def send_out(blocks):
         if direct:
-            return swapped(blocks)
+            taken = {0: blocks[0]}
+            for offset in order:
+                taken[offset] = swap_with(blocks[offset], "space", offset)
+            return [taken[offset] for offset in range(owners)]
         spectrum = blocks[0].reshape(samples, rows, owners, 2 * modes, channels)
         spectrum = jnp.transpose(spectrum, (2, 0, 1, 3, 4))
         arrived = lax.all_to_all(spectrum, "space", split_axis=0, concat_axis=0, tiled=True)
         return [jnp.transpose(arrived, (1, 0, 2, 3, 4)).reshape(samples, 1, -1, channels)]
 
     def send_back(blocks):
-        if direct:
-            return swapped(blocks)
         bands = blocks[0].reshape(samples, owners, rows, 2 * modes, channels)
         bands = jnp.transpose(bands, (1, 0, 2, 3, 4))
         arrived = lax.all_to_all(bands, "space", split_axis=0, concat_axis=0, tiled=True)
@@ -439,15 +490,31 @@
     b1, b2 = block_bias(b_first, groups), block_bias(b_second, groups)
 
     image, state = forward_mid(me, lat, lat.T, gathered, w1, b1, w2, b2)
-    image_band = send_back(image)
-    grad_image, sums = backward_mid(me, lat, lat.T, cot_gathered, w1, w2, state, count)
-    grad_band = send_back(grad_image)
+    image_band = send_out(image) if direct else send_back(image)
+    grad_image, sums = backward_mid(
+        me, lat, lat.T, cot_gathered, w1, b1, w2, b2, state, count
+    )
+    if direct:
+        early = tuple(image_band[offset] for offset in order[:HELD])
+        grad_image, sums, _ = lax.optimization_barrier((grad_image, sums, early))
+        late = [image_band[offset] for offset in order[HELD:]]
+        grad_band = send_out(grad_image)
+        sent = [grad_band[offset] for offset in order]
+    else:
+        grad_band = send_back(grad_image)
+        late, sent = [], []
+    group_sum = GroupSum(sums)
+    group_sum.over_dp([])
+    group_sum.over_next(late)
+    group_sum.scatter(sent[:2])
+    group_sum.gather(sent[2:4])
+    group_sum.gather_next(sent[4:6])
     output = to_cells(me, scaled.T, image_band, fields)
     grad_fields = to_cells(me, plain.T, grad_band, cotangent)
 
     positions = samples * lax.axis_size("dp") * lat_total * KW
     factor = 1.0 / math.sqrt(positions)
-    sums = summed_over_group(sums).astype(jnp.float32) * factor
+    sums = group_sum.join([]).astype(jnp.float32) * factor
     grads = []
     for which in range(2):
         blocks = sums[which, :, :, :edge].reshape(2, groups, edge, count // groups, edge)

time: 225 us -> 206 us (0.916)
  the two profiles are of different devices: /device:TPU:13 before, /device:TPU:0 now
where the time goes in v4:
time: 206 us; the launch traced here: 204 us
  starting transfers between devices  80.6 us (39%)
  waiting for transfers between devices  47.3 us (23%)
  local copies, waits for them, and re-layouts  40.5 us (20%)
  Pallas kernels  26.2 us (13%)
  other arithmetic  8.6 us (4%)
    ppermute x38, starting transfers between devices, swap_with(): return lax.ppermute(values, axis, pairs)  80.6 us
    ppermute x38, waiting for transfers between devices, swap_with(): return lax.ppermute(values, axis, pairs)  47.3 us
    unnamed x137, local copies, waits for them, and re-layouts  33.1 us
    pallas_call x1, Pallas kernels, backward_mid(): pl.pallas_call(functools.partial(backward_kernel, size_of_block, len(band...  11.1 us
    pallas_call x1, Pallas kernels, forward_mid(): pl.pallas_call(functools.partial(forward_kernel, len(bands)), grid_spec=p...  5.92 us
    pallas_call x2, Pallas kernels, to_modes(): pl.pallas_call(to_modes_kernel, grid_spec=pltpu.PrefetchScalarGridSpec(nu...  4.37 us
  transfers between devices with their start and end apart: 38, of which 13 were waited for; matrix products, arithmetic and copies ran while one was open for 6% of the time, Pallas kernels for 12%

profile of v4, /device:TPU:0, one launch (start us, length us, event | category | flops | bytes accessed | tf_op | source)
XLA Modules:
  0.0 204.4 jit_solution(17595766628078559927)
XLA Ops:
  5.5 3.0 %collective-permute-start = (bf16[4,2,16,768]{3,2,1,0:T(8,128)(2,1)S(1)}, bf16[4,2,16,768]{3,2,1,0:T(8,128)(2,1)S(1)}, u32[]{:S(2)}, u32[]{:S(2)}) collective-permute-start(bf16[4,2,16,768]{3,2,1,0:T(8,128)(2,1)S(1)} %get-tuple-element.81), channel_id=1, source_target_pairs={{0,2},{2,0},{4,6},{6,4},{8,10},{10,8},{12,14},{14,12},{1,3},{3,1},... | collective-permute-start | bytes 589832 | tf_op jit(solution)/shard_map/ppermute | solution.py:375
  10.0 3.0 %collective-permute-start.3 = (bf16[4,2,16,768]{3,2,1,0:T(8,128)(2,1)S(1)}, bf16[4,2,16,768]{3,2,1,0:T(8,128)(2,1)S(1)}, u32[]{:S(2)}, u32[]{:S(2)}) collective-permute-start(bf16[4,2,16,768]{3,2,1,0:T(8,128)(2,1)S(1)} %get-tuple-element.84), channel_id=1, source_target_pairs={{0,8},{2,10},{4,12},{6,14},{8,0},{10,2},{12,4},{14,6},{1,9},{3,11}... | collective-permute-start | bytes 589832 | tf_op jit(solution)/shard_map/ppermute | solution.py:375
  22.3 3.6 %collective-permute-start.5 = (bf16[4,2,16,768]{3,2,1,0:T(8,128)(2,1)}, bf16[4,2,16,768]{3,2,1,0:T(8,128)(2,1)}, u32[]{:S(2)}, u32[]{:S(2)}) collective-permute-start(bf16[4,2,16,768]{3,2,1,0:T(8,128)(2,1)} %get-tuple-element.86), channel_id=1, source_target_pairs={{0,12},{2,14},{4,8},{6,10},{8,4},{10,6},{12,0},{14,2},{1,13},{3,15... | collective-permute-start | bytes 589832 | tf_op jit(solution)/shard_map/ppermute | solution.py:375
  31.3 9.2 %collective-permute-done.4.refs_5_ = bf16[4,2,16,768]{3,2,1,0:T(8,128)(2,1)} collective-permute-done((bf16[4,2,16,768]{3,2,1,0:T(8,128)(2,1)}, bf16[4,2,16,768]{3,2,1,0:T(8,128)(2,1)}, u32[]{:S(2)}, u32[]{:S(2)}) %collective-permute-start.4) | collective-permute-done | bytes 196640 | tf_op jit(solution)/shard_map/ppermute | solution.py:375
  42.2 5.2 %collective-permute-start.17 = (bf16[4,2,16,768]{3,2,1,0:T(8,128)(2,1)}, bf16[4,2,16,768]{3,2,1,0:T(8,128)(2,1)S(1)}, u32[]{:S(2)}, u32[]{:S(2)}) collective-permute-start(bf16[4,2,16,768]{3,2,1,0:T(8,128)(2,1)} %copy-done.49), channel_id=1, source_target_pairs={{0,8},{2,10},{4,12},{6,14},{8,0},{10,2},{12,4},{14,6},{1,9},{3,11}... | collective-permute-start | bytes 589832 | tf_op jit(solution)/shard_map/ppermute | solution.py:375
  47.4 15.6 %collective-permute-start.18 = (bf16[4,2,16,768]{3,2,1,0:T(8,128)(2,1)}, bf16[4,2,16,768]{3,2,1,0:T(8,128)(2,1)S(1)}, u32[]{:S(2)}, u32[]{:S(2)}) collective-permute-start(bf16[4,2,16,768]{3,2,1,0:T(8,128)(2,1)} %copy-done.42), channel_id=1, source_target_pairs={{0,10},{2,8},{4,14},{6,12},{8,2},{10,0},{12,6},{14,4},{1,11},{3,9}... | collective-permute-start | bytes 589832 | tf_op jit(solution)/shard_map/ppermute | solution.py:375
  63.5 4.3 %collective-permute-start.20 = (bf16[4,2,16,768]{3,2,1,0:T(8,128)(2,1)}, bf16[4,2,16,768]{3,2,1,0:T(8,128)(2,1)S(1)}, u32[]{:S(2)}, u32[]{:S(2)}) collective-permute-start(bf16[4,2,16,768]{3,2,1,0:T(8,128)(2,1)} %copy-done.38), channel_id=1, source_target_pairs={{0,14},{2,12},{4,10},{6,8},{8,6},{10,4},{12,2},{14,0},{1,15},{3,13... | collective-permute-start | bytes 589832 | tf_op jit(solution)/shard_map/ppermute | solution.py:375
  74.2 5.9 %mix_forward.1 = (bf16[4,2,16,768]{3,2,1,0:T(8,128)(2,1)S(1)}, bf16[4,2,16,768]{3,2,1,0:T(8,128)(2,1)S(1)}, bf16[4,2,16,768]{3,2,1,0:T(8,128)(2,1)S(1)}, bf16[4,...) custom-call(s32[1]{0:T(128)} %bitcast.me_ref, ...), custom_call_target="tpu_custom_call" | custom-call | flops 2415919104 | bytes 17301504 | tf_op jit(solution)/shard_map/mix_forward/pallas_call | solution.py:298
  83.5 4.7 %collective-permute-start.11 = (bf16[4,2,16,768]{3,2,1,0:T(8,128)(2,1)S(1)}, bf16[4,2,16,768]{3,2,1,0:T(8,128)(2,1)S(1)}, u32[]{:S(2)}, u32[]{:S(2)}) collective-permute-start(bf16[4,2,16,768]{3,2,1,0:T(8,128)(2,1)S(1)} %get-tuple-element.93), channel_id=1, source_target_pairs={{0,10},{2,8},{4,14},{6,12},{8,2},{10,0},{12,6},{14,4},{1,11},{3,9}... | collective-permute-start | bytes 589832 | tf_op jit(solution)/shard_map/ppermute | solution.py:375
  88.8 11.1 %mix_backward.1 = (bf16[4,2,16,768]{3,2,1,0:T(8,128)(2,1)S(1)}, bf16[4,2,16,768]{3,2,1,0:T(8,128)(2,1)S(1)}, bf16[4,2,16,768]{3,2,1,0:T(8,128)(2,1)S(1)}, bf16[4...) custom-call(s32[1]{0:T(128)} %bitcast.me_ref, ...), custom_call_target="tpu_custom_call" | custom-call | flops 4831838208 | bytes 17301504 | tf_op jit(solution)/shard_map/mix_backward/pallas_call | solution.py:336
  100.7 3.9 %collective-permute-done.11.refs_5_ = bf16[4,2,16,768]{3,2,1,0:T(8,128)(2,1)S(1)} collective-permute-done((bf16[4,2,16,768]{3,2,1,0:T(8,128)(2,1)S(1)}, bf16[4,2,16,768]{3,2,1,0:T(8,128)(2,1)S(1)}, u32[]{:S(2)}, u32[]{:S(2)}) %collective-permute-start.11) | collective-permute-done | bytes 196640 | tf_op jit(solution)/shard_map/ppermute | solution.py:375
  106.9 3.7 %collective-permute-start.13 = (bf16[4,2,16,768]{3,2,1,0:T(8,128)(2,1)}, bf16[4,2,16,768]{3,2,1,0:T(8,128)(2,1)S(1)}, u32[]{:S(2)}, u32[]{:S(2)}) collective-permute-start(bf16[4,2,16,768]{3,2,1,0:T(8,128)(2,1)} %copy-done.36), channel_id=1, source_target_pairs={{0,14},{2,12},{4,10},{6,8},{8,6},{10,4},{12,2},{14,0},{1,15},{3,13... | collective-permute-start | bytes 589832 | tf_op jit(solution)/shard_map/ppermute | solution.py:375
  112.8 4.5 %collective-permute-done.7.refs_1_ = bf16[4,2,16,768]{3,2,1,0:T(8,128)(2,1)S(1)} collective-permute-done((bf16[4,2,16,768]{3,2,1,0:T(8,128)(2,1)}, bf16[4,2,16,768]{3,2,1,0:T(8,128)(2,1)S(1)}, u32[]{:S(2)}, u32[]{:S(2)}) %collective-permute-start.7) | collective-permute-done | bytes 196640 | tf_op jit(solution)/shard_map/ppermute | solution.py:375
  120.0 6.9 %collective-permute-start.22 = (bf16[4,2,16,768]{3,2,1,0:T(8,128)(2,1)}, bf16[4,2,16,768]{3,2,1,0:T(8,128)(2,1)S(1)}, u32[]{:S(2)}, u32[]{:S(2)}) collective-permute-start(bf16[4,2,16,768]{3,2,1,0:T(8,128)(2,1)} %copy-done.33), channel_id=1, source_target_pairs={{0,4},{2,6},{4,0},{6,2},{8,12},{10,14},{12,8},{14,10},{1,5},{3,7},... | collective-permute-start | bytes 589832 | tf_op jit(solution)/shard_map/ppermute | solution.py:375
  130.0 4.7 %collective-permute-done.22.refs_2_ = bf16[4,2,16,768]{3,2,1,0:T(8,128)(2,1)S(1)} collective-permute-done((bf16[4,2,16,768]{3,2,1,0:T(8,128)(2,1)}, bf16[4,2,16,768]{3,2,1,0:T(8,128)(2,1)S(1)}, u32[]{:S(2)}, u32[]{:S(2)}) %collective-permute-start.22) | collective-permute-done | bytes 196640 | tf_op jit(solution)/shard_map/ppermute | solution.py:375
  135.3 2.7 %collective-permute-done.24.refs_4_ = bf16[4,2,16,768]{3,2,1,0:T(8,128)(2,1)S(1)} collective-permute-done((bf16[4,2,16,768]{3,2,1,0:T(8,128)(2,1)}, bf16[4,2,16,768]{3,2,1,0:T(8,128)(2,1)S(1)}, u32[]{:S(2)}, u32[]{:S(2)}) %collective-permute-start.24) | collective-permute-done | bytes 196640 | tf_op jit(solution)/shard_map/ppermute | solution.py:375
  146.2 3.7 %collective-permute-start.26 = (bf16[4,2,16,768]{3,2,1,0:T(8,128)(2,1)}, bf16[4,2,16,768]{3,2,1,0:T(8,128)(2,1)S(1)}, u32[]{:S(2)}, u32[]{:S(2)}) collective-permute-start(bf16[4,2,16,768]{3,2,1,0:T(8,128)(2,1)} %copy-done.28), channel_id=1, source_target_pairs={{0,12},{2,14},{4,8},{6,10},{8,4},{10,6},{12,0},{14,2},{1,13},{3,15... | collective-permute-start | bytes 589832 | tf_op jit(solution)/shard_map/ppermute | solution.py:375
  153.1 10.4 %collective-permute-done.25.refs_5_ = bf16[4,2,16,768]{3,2,1,0:T(8,128)(2,1)S(1)} collective-permute-done((bf16[4,2,16,768]{3,2,1,0:T(8,128)(2,1)}, bf16[4,2,16,768]{3,2,1,0:T(8,128)(2,1)S(1)}, u32[]{:S(2)}, u32[]{:S(2)}) %collective-permute-start.25) | collective-permute-done | bytes 196640 | tf_op jit(solution)/shard_map/ppermute | solution.py:375
  164.7 3.2 %collective-permute-start.33 = (bf16[56,384]{1,0:T(8,128)(2,1)S(1)}, bf16[56,384]{1,0:T(8,128)(2,1)S(1)}, u32[]{:S(2)}, u32[]{:S(2)}) collective-permute-start(bf16[56,384]{1,0:T(8,128)(2,1)S(1)} %fusion.5), channel_id=1, source_target_pairs={{0,4},{2,6},{4,0},{6,2},{8,12},{10,14},{12,8},{14,10},{1,5},{3,7},... | collective-permute-start | bytes 129032 | tf_op jit(solution)/shard_map/ppermute | solution.py:375
  172.7 4.5 %collective-permute-done.36 = bf16[4,56,384]{2,1,0:T(8,128)(2,1)S(1)} collective-permute-done((bf16[4,56,384]{2,1,0:T(8,128)(2,1)S(1)}, bf16[4,56,384]{2,1,0:T(8,128)(2,1)S(1)}, u32[]{:S(2)}, u32[]{:S(2)}) %collective-permute-start.36) | collective-permute-done | bytes 172064 | tf_op jit(solution)/shard_map/ppermute | solution.py:375
  178.7 2.3 %collective-permute-start.27 = (bf16[4,2,16,768]{3,2,1,0:T(8,128)(2,1)}, bf16[4,2,16,768]{3,2,1,0:T(8,128)(2,1)}, u32[]{:S(2)}, u32[]{:S(2)}) collective-permute-start(bf16[4,2,16,768]{3,2,1,0:T(8,128)(2,1)} %copy-done.27), channel_id=1, source_target_pairs={{0,14},{2,12},{4,10},{6,8},{8,6},{10,4},{12,2},{14,0},{1,15},{3,13... | collective-permute-start | bytes 589832 | tf_op jit(solution)/shard_map/ppermute | solution.py:375
  185.2 3.1 %copy.37 = bf16[4,2,180,768]{3,1,2,0:T(2,128)(2,1)} copy(bf16[4,2,180,768]{3,2,1,0:T(8,128)(2,1)S(1)} %to_cells.2) | data formatting | bytes 4423680
  189.2 2.6 %to_cells.3 = bf16[4,2,180,768]{3,2,1,0:T(8,128)(2,1)S(1)} custom-call(s32[1]{0:T(128)} %bitcast.me_ref, bf16[180,128]{1,0:T(8,128)(2,1)S(1)} %copy-done.23, bf16[4,2,180,768]{3,2,1,0:T(8,128)(2,1)S(1)} %copy-done.1, bf16[4,2,16,768]{3,2,1,0:T(8,128)(2,1)S(1)} %get-tuple-element.115.refs_0_, bf16[4,2,16,768]{3,2,1,0:T(8,128)(2,1)S(1)} %copy-done.14, ...), custom_call_target="tpu_custom_call" | custom-call | flops 283115520 | bytes 5996544 | tf_op jit(solution)/shard_map/to_cells/pallas_call | solution.py:159
  191.9 3.1 %copy.38 = bf16[4,2,180,768]{3,1,2,0:T(2,128)(2,1)} copy(bf16[4,2,180,768]{3,2,1,0:T(8,128)(2,1)S(1)} %to_cells.3) | data formatting | bytes 4423680
  (228 shorter events, 78.4 us)
Async XLA Ops:
  5.5 16.1 %collective-permute-start = (bf16[4,2,16,768]{3,2,1,0:T(8,128)(2,1)S(1)}, bf16[4,2,16,768]{3,2,1,0:T(8,128)(2,1)S(1)}, u32[]{:S(2)}, u32[]{:S(2)}) collective-permute-start(bf16[4,2,16,768]{3,2,1,0:T(8,128)(2,1)S(1)} %get-tuple-element.81), channel_id=1, source_target_pairs={{0,2},{2,0},{4,6},{6,4},{8,10},{10,8},{12,14},{14,12},{1,3},{3,1},... | collective-permute-start | bytes 589832 | tf_op jit(solution)/shard_map/ppermute | solution.py:375
  8.5 17.4 %collective-permute-start.1 = (bf16[4,2,16,768]{3,2,1,0:T(8,128)(2,1)S(1)}, bf16[4,2,16,768]{3,2,1,0:T(8,128)(2,1)S(1)}, u32[]{:S(2)}, u32[]{:S(2)}) collective-permute-start(bf16[4,2,16,768]{3,2,1,0:T(8,128)(2,1)S(1)} %get-tuple-element.82), channel_id=1, source_target_pairs={{0,4},{2,6},{4,0},{6,2},{8,12},{10,14},{12,8},{14,10},{1,5},{3,7},... | collective-permute-start | bytes 589832 | tf_op jit(solution)/shard_map/ppermute | solution.py:375
  10.0 16.5 %collective-permute-start.2 = (bf16[4,2,16,768]{3,2,1,0:T(8,128)(2,1)S(1)}, bf16[4,2,16,768]{3,2,1,0:T(8,128)(2,1)S(1)}, u32[]{:S(2)}, u32[]{:S(2)}) collective-permute-start(bf16[4,2,16,768]{3,2,1,0:T(8,128)(2,1)S(1)} %get-tuple-element.83), channel_id=1, source_target_pairs={{0,6},{2,4},{4,2},{6,0},{8,14},{10,12},{12,10},{14,8},{1,7},{3,5},... | collective-permute-start | bytes 589832 | tf_op jit(solution)/shard_map/ppermute | solution.py:375
  10.0 19.4 %collective-permute-start.3 = (bf16[4,2,16,768]{3,2,1,0:T(8,128)(2,1)S(1)}, bf16[4,2,16,768]{3,2,1,0:T(8,128)(2,1)S(1)}, u32[]{:S(2)}, u32[]{:S(2)}) collective-permute-start(bf16[4,2,16,768]{3,2,1,0:T(8,128)(2,1)S(1)} %get-tuple-element.84), channel_id=1, source_target_pairs={{0,8},{2,10},{4,12},{6,14},{8,0},{10,2},{12,4},{14,6},{1,9},{3,11}... | collective-permute-start | bytes 589832 | tf_op jit(solution)/shard_map/ppermute | solution.py:375
  13.0 27.5 %collective-permute-start.4 = (bf16[4,2,16,768]{3,2,1,0:T(8,128)(2,1)}, bf16[4,2,16,768]{3,2,1,0:T(8,128)(2,1)}, u32[]{:S(2)}, u32[]{:S(2)}) collective-permute-start(bf16[4,2,16,768]{3,2,1,0:T(8,128)(2,1)} %get-tuple-element.85), channel_id=1, source_target_pairs={{0,10},{2,8},{4,14},{6,12},{8,2},{10,0},{12,6},{14,4},{1,11},{3,9}... | collective-permute-start | bytes 589832 | tf_op jit(solution)/shard_map/ppermute | solution.py:375
  22.3 19.9 %collective-permute-start.5 = (bf16[4,2,16,768]{3,2,1,0:T(8,128)(2,1)}, bf16[4,2,16,768]{3,2,1,0:T(8,128)(2,1)}, u32[]{:S(2)}, u32[]{:S(2)}) collective-permute-start(bf16[4,2,16,768]{3,2,1,0:T(8,128)(2,1)} %get-tuple-element.86), channel_id=1, source_target_pairs={{0,12},{2,14},{4,8},{6,10},{8,4},{10,6},{12,0},{14,2},{1,13},{3,15... | collective-permute-start | bytes 589832 | tf_op jit(solution)/shard_map/ppermute | solution.py:375
  26.6 20.8 %collective-permute-start.6 = (bf16[4,2,16,768]{3,2,1,0:T(8,128)(2,1)}, bf16[4,2,16,768]{3,2,1,0:T(8,128)(2,1)}, u32[]{:S(2)}, u32[]{:S(2)}) collective-permute-start(bf16[4,2,16,768]{3,2,1,0:T(8,128)(2,1)} %get-tuple-element.87), channel_id=1, source_target_pairs={{0,14},{2,12},{4,10},{6,8},{8,6},{10,4},{12,2},{14,0},{1,15},{3,13... | collective-permute-start | bytes 589832 | tf_op jit(solution)/shard_map/ppermute | solution.py:375
  27.3 35.7 %collective-permute-start.14 = (bf16[4,2,16,768]{3,2,1,0:T(8,128)(2,1)}, bf16[4,2,16,768]{3,2,1,0:T(8,128)(2,1)}, u32[]{:S(2)}, u32[]{:S(2)}) collective-permute-start(bf16[4,2,16,768]{3,2,1,0:T(8,128)(2,1)} %get-tuple-element.99), channel_id=1, source_target_pairs={{0,2},{2,0},{4,6},{6,4},{8,10},{10,8},{12,14},{14,12},{1,3},{3,1},... | collective-permute-start | bytes 589832 | tf_op jit(solution)/shard_map/ppermute | solution.py:375
  30.1 33.4 %collective-permute-start.15 = (bf16[4,2,16,768]{3,2,1,0:T(8,128)(2,1)}, bf16[4,2,16,768]{3,2,1,0:T(8,128)(2,1)}, u32[]{:S(2)}, u32[]{:S(2)}) collective-permute-start(bf16[4,2,16,768]{3,2,1,0:T(8,128)(2,1)} %get-tuple-element.100), channel_id=1, source_target_pairs={{0,4},{2,6},{4,0},{6,2},{8,12},{10,14},{12,8},{14,10},{1,5},{3,7},... | collective-permute-start | bytes 589832 | tf_op jit(solution)/shard_map/ppermute | solution.py:375
  40.5 41.0 %collective-permute-start.16 = (bf16[4,2,16,768]{3,2,1,0:T(8,128)(2,1)}, bf16[4,2,16,768]{3,2,1,0:T(8,128)(2,1)S(1)}, u32[]{:S(2)}, u32[]{:S(2)}) collective-permute-start(bf16[4,2,16,768]{3,2,1,0:T(8,128)(2,1)} %copy-done.52), channel_id=1, source_target_pairs={{0,6},{2,4},{4,2},{6,0},{8,14},{10,12},{12,10},{14,8},{1,7},{3,5},... | collective-permute-start | bytes 589832 | tf_op jit(solution)/shard_map/ppermute | solution.py:375
  42.2 39.4 %collective-permute-start.17 = (bf16[4,2,16,768]{3,2,1,0:T(8,128)(2,1)}, bf16[4,2,16,768]{3,2,1,0:T(8,128)(2,1)S(1)}, u32[]{:S(2)}, u32[]{:S(2)}) collective-permute-start(bf16[4,2,16,768]{3,2,1,0:T(8,128)(2,1)} %copy-done.49), channel_id=1, source_target_pairs={{0,8},{2,10},{4,12},{6,14},{8,0},{10,2},{12,4},{14,6},{1,9},{3,11}... | collective-permute-start | bytes 589832 | tf_op jit(solution)/shard_map/ppermute | solution.py:375
  47.4 36.1 %collective-permute-start.18 = (bf16[4,2,16,768]{3,2,1,0:T(8,128)(2,1)}, bf16[4,2,16,768]{3,2,1,0:T(8,128)(2,1)S(1)}, u32[]{:S(2)}, u32[]{:S(2)}) collective-permute-start(bf16[4,2,16,768]{3,2,1,0:T(8,128)(2,1)} %copy-done.42), channel_id=1, source_target_pairs={{0,10},{2,8},{4,14},{6,12},{8,2},{10,0},{12,6},{14,4},{1,11},{3,9}... | collective-permute-start | bytes 589832 | tf_op jit(solution)/shard_map/ppermute | solution.py:375
  63.0 20.5 %collective-permute-start.19 = (bf16[4,2,16,768]{3,2,1,0:T(8,128)(2,1)}, bf16[4,2,16,768]{3,2,1,0:T(8,128)(2,1)S(1)}, u32[]{:S(2)}, u32[]{:S(2)}) collective-permute-start(bf16[4,2,16,768]{3,2,1,0:T(8,128)(2,1)} %copy-done.39), channel_id=1, source_target_pairs={{0,12},{2,14},{4,8},{6,10},{8,4},{10,6},{12,0},{14,2},{1,13},{3,15... | collective-permute-start | bytes 589832 | tf_op jit(solution)/shard_map/ppermute | solution.py:375
  63.5 24.7 %collective-permute-start.20 = (bf16[4,2,16,768]{3,2,1,0:T(8,128)(2,1)}, bf16[4,2,16,768]{3,2,1,0:T(8,128)(2,1)S(1)}, u32[]{:S(2)}, u32[]{:S(2)}) collective-permute-start(bf16[4,2,16,768]{3,2,1,0:T(8,128)(2,1)} %copy-done.38), channel_id=1, source_target_pairs={{0,14},{2,12},{4,10},{6,8},{8,6},{10,4},{12,2},{14,0},{1,15},{3,13... | collective-permute-start | bytes 589832 | tf_op jit(solution)/shard_map/ppermute | solution.py:375
  81.5 19.1 %collective-permute-start.8 = (bf16[4,2,16,768]{3,2,1,0:T(8,128)(2,1)S(1)}, bf16[4,2,16,768]{3,2,1,0:T(8,128)(2,1)S(1)}, u32[]{:S(2)}, u32[]{:S(2)}) collective-permute-start(bf16[4,2,16,768]{3,2,1,0:T(8,128)(2,1)S(1)} %get-tuple-element.90), channel_id=1, source_target_pairs={{0,4},{2,6},{4,0},{6,2},{8,12},{10,14},{12,8},{14,10},{1,5},{3,7},... | collective-permute-start | bytes 589832 | tf_op jit(solution)/shard_map/ppermute | solution.py:375
  81.5 19.1 %collective-permute-start.9 = (bf16[4,2,16,768]{3,2,1,0:T(8,128)(2,1)S(1)}, bf16[4,2,16,768]{3,2,1,0:T(8,128)(2,1)S(1)}, u32[]{:S(2)}, u32[]{:S(2)}) collective-permute-start(bf16[4,2,16,768]{3,2,1,0:T(8,128)(2,1)S(1)} %get-tuple-element.91), channel_id=1, source_target_pairs={{0,6},{2,4},{4,2},{6,0},{8,14},{10,12},{12,10},{14,8},{1,7},{3,5},... | collective-permute-start | bytes 589832 | tf_op jit(solution)/shard_map/ppermute | solution.py:375
  83.5 17.2 %collective-permute-start.10 = (bf16[4,2,16,768]{3,2,1,0:T(8,128)(2,1)S(1)}, bf16[4,2,16,768]{3,2,1,0:T(8,128)(2,1)S(1)}, u32[]{:S(2)}, u32[]{:S(2)}) collective-permute-start(bf16[4,2,16,768]{3,2,1,0:T(8,128)(2,1)S(1)} %get-tuple-element.92), channel_id=1, source_target_pairs={{0,8},{2,10},{4,12},{6,14},{8,0},{10,2},{12,4},{14,6},{1,9},{3,11}... | collective-permute-start | bytes 589832 | tf_op jit(solution)/shard_map/ppermute | solution.py:375
  83.5 21.1 %collective-permute-start.11 = (bf16[4,2,16,768]{3,2,1,0:T(8,128)(2,1)S(1)}, bf16[4,2,16,768]{3,2,1,0:T(8,128)(2,1)S(1)}, u32[]{:S(2)}, u32[]{:S(2)}) collective-permute-start(bf16[4,2,16,768]{3,2,1,0:T(8,128)(2,1)S(1)} %get-tuple-element.93), channel_id=1, source_target_pairs={{0,10},{2,8},{4,14},{6,12},{8,2},{10,0},{12,6},{14,4},{1,11},{3,9}... | collective-permute-start | bytes 589832 | tf_op jit(solution)/shard_map/ppermute | solution.py:375
  88.2 16.3 %collective-permute-start.12 = (bf16[4,2,16,768]{3,2,1,0:T(8,128)(2,1)S(1)}, bf16[4,2,16,768]{3,2,1,0:T(8,128)(2,1)S(1)}, u32[]{:S(2)}, u32[]{:S(2)}) collective-permute-start(bf16[4,2,16,768]{3,2,1,0:T(8,128)(2,1)S(1)} %get-tuple-element.94), channel_id=1, source_target_pairs={{0,12},{2,14},{4,8},{6,10},{8,4},{10,6},{12,0},{14,2},{1,13},{3,15... | collective-permute-start | bytes 589832 | tf_op jit(solution)/shard_map/ppermute | solution.py:375
  120.0 14.7 %collective-permute-start.22 = (bf16[4,2,16,768]{3,2,1,0:T(8,128)(2,1)}, bf16[4,2,16,768]{3,2,1,0:T(8,128)(2,1)S(1)}, u32[]{:S(2)}, u32[]{:S(2)}) collective-permute-start(bf16[4,2,16,768]{3,2,1,0:T(8,128)(2,1)} %copy-done.33), channel_id=1, source_target_pairs={{0,4},{2,6},{4,0},{6,2},{8,12},{10,14},{12,8},{14,10},{1,5},{3,7},... | collective-permute-start | bytes 589832 | tf_op jit(solution)/shard_map/ppermute | solution.py:375
  143.1 27.2 %collective-permute-start.21 = (bf16[4,2,16,768]{3,2,1,0:T(8,128)(2,1)}, bf16[4,2,16,768]{3,2,1,0:T(8,128)(2,1)S(1)}, u32[]{:S(2)}, u32[]{:S(2)}) collective-permute-start(bf16[4,2,16,768]{3,2,1,0:T(8,128)(2,1)} %copy-done.29), channel_id=1, source_target_pairs={{0,2},{2,0},{4,6},{6,4},{8,10},{10,8},{12,14},{14,12},{1,3},{3,1},... | collective-permute-start | bytes 589832 | tf_op jit(solution)/shard_map/ppermute | solution.py:375
  145.3 18.1 %collective-permute-start.25 = (bf16[4,2,16,768]{3,2,1,0:T(8,128)(2,1)}, bf16[4,2,16,768]{3,2,1,0:T(8,128)(2,1)S(1)}, u32[]{:S(2)}, u32[]{:S(2)}) collective-permute-start(bf16[4,2,16,768]{3,2,1,0:T(8,128)(2,1)} %copy-done.30), channel_id=1, source_target_pairs={{0,10},{2,8},{4,14},{6,12},{8,2},{10,0},{12,6},{14,4},{1,11},{3,9}... | collective-permute-start | bytes 589832 | tf_op jit(solution)/shard_map/ppermute | solution.py:375
  146.2 24.9 %collective-permute-start.26 = (bf16[4,2,16,768]{3,2,1,0:T(8,128)(2,1)}, bf16[4,2,16,768]{3,2,1,0:T(8,128)(2,1)S(1)}, u32[]{:S(2)}, u32[]{:S(2)}) collective-permute-start(bf16[4,2,16,768]{3,2,1,0:T(8,128)(2,1)} %copy-done.28), channel_id=1, source_target_pairs={{0,12},{2,14},{4,8},{6,10},{8,4},{10,6},{12,0},{14,2},{1,13},{3,15... | collective-permute-start | bytes 589832 | tf_op jit(solution)/shard_map/ppermute | solution.py:375
  178.7 16.2 %collective-permute-start.37 = (bf16[2,4,56,384]{3,2,1,0:T(8,128)(2,1)}, bf16[2,4,56,384]{3,2,1,0:T(8,128)(2,1)}, u32[]{:S(2)}, u32[]{:S(2)}) collective-permute-start(bf16[2,4,56,384]{3,2,1,0:T(8,128)(2,1)} %get-tuple-element.155), channel_id=1, source_target_pairs={{0,1},{1,0},{2,3},{3,2},{4,5},{5,4},{6,7},{7,6},{8,9},{9,8},{10,11... | collective-permute-start | bytes 1032200 | tf_op jit(solution)/shard_map/ppermute | solution.py:375
  (81 other events, 492.2 us)

commit v5 on v4

--- a/solution.py
+++ b/solution.py
@@ -13,6 +13,9 @@
 KW = 64
 shrink_level = 0.05
 HELD = 5
+FIRST = 4
+STEPS_BEFORE = (0, 2, 3, 5, 6)
+DEPTH = 5
 MIB = 1024 * 1024
 
 
@@ -130,7 +133,7 @@
             out_specs=(pl.BlockSpec((1,) + share, lambda b, _: (b, 0, 0, 0)),) * owners,
             scratch_shapes=[pltpu.VMEM((rows, size, channels), jnp.bfloat16)],
         ),
-        out_shape=(jax.ShapeDtypeStruct((samples,) + share, jnp.bfloat16),) * owners,
+        out_shape=(in_hbm((samples,) + share, jnp.bfloat16),) * owners,
         compiler_params=params(12),
         cost_estimate=pl.CostEstimate(
             flops=2 * samples * rows * size * width * channels,
@@ -174,7 +177,7 @@
             transcendentals=0,
         ),
         name="to_cells",
-    )(me, table, base, *modes)
+    )(me, table, base, *held_in_hbm(modes))
 
 
 def sigmoid_of(values):
@@ -282,8 +285,16 @@
     return (pl.BlockSpec(block, lambda g, *_: (0, 0, 0, g)),) * len(bands)
 
 
+def in_hbm(shape, dtype):
+    return pltpu.HBM(shape, dtype)
+
+
 def shapes_of(bands):
-    return tuple(jax.ShapeDtypeStruct(band.shape, band.dtype) for band in bands)
+    return tuple(in_hbm(band.shape, band.dtype) for band in bands)
+
+
+def held_in_hbm(bands):
+    return [pltpu.with_memory_space_constraint(band, pltpu.HBM) for band in bands]
 
 
 def forward_mid(me, lat, unlat, bands, w1, b1, w2, b2):
@@ -320,7 +331,7 @@
             transcendentals=2 * groups * positions * lanes,
         ),
         name="mix_forward",
-    )(me, lat, unlat, w1, b1, w2, b2, *bands)
+    )(me, lat, unlat, w1, b1, w2, b2, *held_in_hbm(bands))
     return results[: len(bands)], results[len(bands)]
 
 
@@ -364,15 +375,25 @@
             transcendentals=0,
         ),
         name="mix_backward",
-    )(me, lat, unlat, w1, b1, w2, b2, state, *bands)
+    )(me, lat, unlat, w1, b1, w2, b2, state, *held_in_hbm(bands))
     return results[: len(bands)], results[len(bands)]
 
 
-def swap_with(values, axis, distance, after=()):
-    if len(after) > 0:
-        values, _ = lax.optimization_barrier((values, tuple(after)))
+def swap_with(values, axis, distance):
     pairs = [(i, i ^ distance) for i in range(lax.axis_size(axis))]
     return lax.ppermute(values, axis, pairs)
+
+
+class Chain:
+    def __init__(self, depth, arrived):
+        self.depth = depth
+        self.arrived = list(arrived)
+
+    def swap(self, values, axis, distance):
+        if len(self.arrived) >= self.depth:
+            values, _ = lax.optimization_barrier((values, self.arrived[-self.depth]))
+        self.arrived.append(swap_with(values, axis, distance))
+        return self.arrived[-1]
 
 
 def mixed_order(size):
@@ -399,7 +420,8 @@
 
 
 class GroupSum:
-    def __init__(self, sums):
+    def __init__(self, chain, sums):
+        self.chain = chain
         self.lanes = sums.shape[-1]
         self.shape = sums.shape
         self.side = lax.axis_index("dp")
@@ -407,43 +429,86 @@
         self.count = lax.axis_size("space") // 2
         self.held = sums.reshape(-1, self.lanes)
 
-    def halve(self, axis, distance, bit, after):
+    def halve(self, axis, distance, bit):
         pair = self.held.reshape(2, -1, self.lanes)
-        taken = swap_with(pick(pair, 1 - bit), axis, distance, after)
+        taken = self.chain.swap(pick(pair, 1 - bit), axis, distance)
         self.held = pick(pair, bit) + taken
 
-    def over_dp(self, after):
-        self.halve("dp", 1, self.side, after)
-
-    def over_next(self, after):
-        self.halve("space", 1, self.me % 2, after)
-
-    def scatter(self, after):
+    def over_dp(self):
+        self.halve("dp", 1, self.side)
+
+    def over_next(self):
+        self.halve("space", 1, self.me % 2)
+
+    def scatter(self):
         shares = self.held.reshape(self.count, -1, self.lanes)
         place = self.me // 2
         total = pick(shares, place)
         for offset in range(1, self.count):
             given = pick(shares, place ^ offset).astype(jnp.bfloat16)
-            total += swap_with(given, "space", 2 * offset, after).astype(jnp.float32)
+            total += self.chain.swap(given, "space", 2 * offset).astype(jnp.float32)
         self.total = total.astype(jnp.bfloat16)
 
-    def gather(self, after):
+    def gather(self):
         taken = [self.total]
         for offset in range(1, self.count):
-            taken.append(swap_with(self.total, "space", 2 * offset, after))
+            taken.append(self.chain.swap(self.total, "space", 2 * offset))
         self.quarter = jnp.stack(taken)
 
-    def gather_next(self, after):
-        self.half = jnp.stack([self.quarter, swap_with(self.quarter, "space", 1, after)])
-
-    def join(self, after):
-        both = jnp.stack([self.half, swap_with(self.half, "dp", 1, after)])
+    def gather_next(self):
+        self.half = jnp.stack([self.quarter, self.chain.swap(self.quarter, "space", 1)])
+
+    def gather_dp(self):
+        self.other = self.chain.swap(self.half, "dp", 1)
+
+    def joined(self):
         bits = [self.side, self.me % 2]
         level = self.count
         while level > 1:
             bits.append(self.me // level % 2)
             level //= 2
-        return by_place(both, bits).reshape(self.shape)
+        return by_place(jnp.stack([self.half, self.other]), bits).reshape(self.shape)
+
+
+def finish_kernel(factor, me_ref, half_ref, other_ref, *out_refs):
+    side, near, place = me_ref[0], me_ref[1], me_ref[2]
+    for which in range(2):
+        blocks_ref, bias_ref = out_refs[2 * which : 2 * which + 2]
+        edge = blocks_ref.shape[-1]
+        per_group = half_ref.shape[3] // edge
+        groups = blocks_ref.shape[1] // per_group
+        pieces = half_ref.shape[1] // groups
+        height = half_ref.shape[2]
+        for part in range(2):
+            for piece in range(groups * pieces):
+                spot = (part ^ near, piece ^ place)
+                own = half_ref[spot].astype(jnp.float32)
+                value = jnp.where(side == which, own, other_ref[spot].astype(jnp.float32)) * factor
+                group, first = piece // pieces, piece % pieces * height
+                count = max(0, min(edge - first, height))
+                for block in range(per_group):
+                    lanes = slice(block * edge, (block + 1) * edge)
+                    index = group * per_group + block
+                    if count > 0:
+                        rows = pl.ds(first, count)
+                        blocks_ref[part, index, rows] = value[:count, lanes]
+                    if first <= edge < first + height:
+                        row = edge - first
+                        bias_ref[part, pl.ds(index, 1)] = value[row : row + 1, lanes]
+
+
+def finish_sums(me, half, other, factor, weight_shape, bias_shape):
+    outs = [weight_shape, bias_shape] * 2
+    return pl.pallas_call(
+        functools.partial(finish_kernel, factor),
+        out_shape=[jax.ShapeDtypeStruct(shape, jnp.float32) for shape in outs],
+        in_specs=[pl.BlockSpec(memory_space=pltpu.SMEM)]
+        + [pl.BlockSpec(memory_space=pltpu.VMEM)] * 2,
+        out_specs=[pl.BlockSpec(memory_space=pltpu.VMEM)] * 4,
+        compiler_params=pltpu.CompilerParams(vmem_limit_bytes=12 * MIB),
+        cost_estimate=pl.CostEstimate(flops=0, bytes_accessed=4 * MIB, transcendentals=0),
+        name="finish_sums",
+    )(me, half, other)
 
 
 def body(fields, cotangent, w_first, b_first, w_second, b_second):
@@ -485,36 +550,56 @@
         (spectrum, cotangent, w_first, w_second)
     )
     gathered = send_out(spectrum)
-    cot_gathered = send_out(to_modes(me, scaled, cotangent, lead))
+    cot_spec = to_modes(me, scaled, cotangent, lead)
     w1, w2 = spread_weights(groups, w_first, w_second)
     b1, b2 = block_bias(b_first, groups), block_bias(b_second, groups)
 
     image, state = forward_mid(me, lat, lat.T, gathered, w1, b1, w2, b2)
+    if direct:
+        late = tuple(cot_spec[offset] for offset in order[FIRST:])
+        late, image = lax.optimization_barrier((late, image))
+        cot_spec = list(cot_spec)
+        for offset, block in zip(order[FIRST:], late):
+            cot_spec[offset] = block
+    cot_gathered = send_out(cot_spec)
     image_band = send_out(image) if direct else send_back(image)
     grad_image, sums = backward_mid(
         me, lat, lat.T, cot_gathered, w1, b1, w2, b2, state, count
     )
+    positions = samples * lax.axis_size("dp") * lat_total * KW
+    factor = 1.0 / math.sqrt(positions)
     if direct:
         early = tuple(image_band[offset] for offset in order[:HELD])
         grad_image, sums, _ = lax.optimization_barrier((grad_image, sums, early))
-        late = [image_band[offset] for offset in order[HELD:]]
-        grad_band = send_out(grad_image)
-        sent = [grad_band[offset] for offset in order]
+        chain = Chain(DEPTH, [image_band[offset] for offset in order])
+    else:
+        chain = Chain(DEPTH, [])
+    group_sum = GroupSum(chain, sums)
+    steps = [
+        group_sum.over_dp, group_sum.over_next, group_sum.scatter,
+        group_sum.gather, group_sum.gather_next, group_sum.gather_dp,
+    ]
+    if direct:
+        grad_band = [grad_image[0]] + [None] * (owners - 1)
+        for place, offset in enumerate(order):
+            for _ in range(STEPS_BEFORE.count(place)):
+                steps.pop(0)()
+            grad_band[offset] = chain.swap(grad_image[offset], "space", offset)
     else:
         grad_band = send_back(grad_image)
-        late, sent = [], []
-    group_sum = GroupSum(sums)
-    group_sum.over_dp([])
-    group_sum.over_next(late)
-    group_sum.scatter(sent[:2])
-    group_sum.gather(sent[2:4])
-    group_sum.gather_next(sent[4:6])
+    for step in steps:
+        step()
     output = to_cells(me, scaled.T, image_band, fields)
     grad_fields = to_cells(me, plain.T, grad_band, cotangent)
 
-    positions = samples * lax.axis_size("dp") * lat_total * KW
-    factor = 1.0 / math.sqrt(positions)
-    sums = group_sum.join([]).astype(jnp.float32) * factor
+    if direct and owners // 2 % groups == 0:
+        place = lax.axis_index("space")
+        here = jnp.stack([lax.axis_index("dp"), place % 2, place // 2]).astype(jnp.int32)
+        grads = finish_sums(
+            here, group_sum.half, group_sum.other, factor, w_first.shape, b_first.shape
+        )
+        return (output, grad_fields) + tuple(grads)
+    sums = group_sum.joined().astype(jnp.float32) * factor
     grads = []
     for which in range(2):
         blocks = sums[which, :, :, :edge].reshape(2, groups, edge, count // groups, edge)

time: 206 us -> 197 us (0.956)
  local copies, waits for them, and re-layouts: 40.5 us -> 19 us
  starting transfers between devices: 80.6 us -> 98.4 us
  Pallas kernels: 26.2 us -> 33.1 us
  other arithmetic: 8.6 us -> 2.58 us
  waiting for transfers between devices: 47.3 us -> 41.7 us
    ppermute x38, starting transfers between devices: 80.6 us -> 98.4 us  [swap_with(): return lax.ppermute(values, axis, pairs)]
    unnamed x137 -> x71, local copies, waits for them, and re-layouts: 33.1 us -> 17 us
    ppermute x38, waiting for transfers between devices: 47.3 us -> 41.7 us  [swap_with(): return lax.ppermute(values, axis, pairs)]
    another operation x4 -> x0, local copies, waits for them, and re-layouts: 2.28 us -> none  [the longest x2 1.35 us: body(): grads.append(sums[which, :, :, edge].reshape(b_first.shape))]
    pallas_call x2, Pallas kernels: 3.92 us -> 6.16 us  [to_cells(): pl.pallas_call(to_cells_kernel, grid_spec=pltpu.PrefetchScalarGridSpec(nu...]
    pallas_call x0 -> x1, Pallas kernels: none -> 2.19 us  [finish_sums(): pl.pallas_call(functools.partial(finish_kernel, factor), out_shape=[jax.S...]
  transfers between devices with their start and end apart: 38 -> 38, of which waited for: 13 -> 12; matrix products, arithmetic and copies ran while one was open for 6% -> 5% of each run, Pallas kernels for 12% -> 15%
where the time goes in v5:
time: 197 us; the launch traced here: 196 us
  starting transfers between devices  98.4 us (50%)
  waiting for transfers between devices  41.7 us (21%)
  Pallas kernels  33.1 us (17%)
  local copies, waits for them, and re-layouts  19 us (10%)
  other arithmetic  2.58 us (1%)
    ppermute x38, starting transfers between devices, swap_with(): return lax.ppermute(values, axis, pairs)  98.4 us
    ppermute x38, waiting for transfers between devices, swap_with(): return lax.ppermute(values, axis, pairs)  41.7 us
    unnamed x71, local copies, waits for them, and re-layouts  17 us
    pallas_call x1, Pallas kernels, backward_mid(): pl.pallas_call(functools.partial(backward_kernel, size_of_block, len(band...  11.7 us
    pallas_call x1, Pallas kernels, forward_mid(): pl.pallas_call(functools.partial(forward_kernel, len(bands)), grid_spec=p...  6.75 us
    pallas_call x2, Pallas kernels, to_cells(): pl.pallas_call(to_cells_kernel, grid_spec=pltpu.PrefetchScalarGridSpec(nu...  6.16 us
    pallas_call x2, Pallas kernels, to_modes(): pl.pallas_call(to_modes_kernel, grid_spec=pltpu.PrefetchScalarGridSpec(nu...  5.38 us
  transfers between devices with their start and end apart: 38, of which 12 were waited for; matrix products, arithmetic and copies ran while one was open for 5% of the time, Pallas kernels for 15%

profile of v5, /device:TPU:0, one launch (start us, length us, event | category | flops | bytes accessed | tf_op | source)
XLA Modules:
  0.0 195.9 jit_solution(12285630408180440630)
XLA Ops:
  5.0 3.0 %collective-permute-start = (bf16[4,2,16,768]{3,2,1,0:T(8,128)(2,1)}, bf16[4,2,16,768]{3,2,1,0:T(8,128)(2,1)}, u32[]{:S(2)}, u32[]{:S(2)}) collective-permute-start(bf16[4,2,16,768]{3,2,1,0:T(8,128)(2,1)} %get-tuple-element.111), channel_id=1, source_target_pairs={{0,2},{2,0},{4,6},{6,4},{8,10},{10,8},{12,14},{14,12},{1,3},{3,1},... | collective-permute-start | bytes 589832 | tf_op jit(solution)/shard_map/ppermute | solution.py:384
  9.6 3.0 %collective-permute-start.3 = (bf16[4,2,16,768]{3,2,1,0:T(8,128)(2,1)}, bf16[4,2,16,768]{3,2,1,0:T(8,128)(2,1)}, u32[]{:S(2)}, u32[]{:S(2)}) collective-permute-start(bf16[4,2,16,768]{3,2,1,0:T(8,128)(2,1)} %get-tuple-element.114), channel_id=1, source_target_pairs={{0,8},{2,10},{4,12},{6,14},{8,0},{10,2},{12,4},{14,6},{1,9},{3,11}... | collective-permute-start | bytes 589832 | tf_op jit(solution)/shard_map/ppermute | solution.py:384
  13.9 3.6 %collective-permute-start.5 = (bf16[4,2,16,768]{3,2,1,0:T(8,128)(2,1)}, bf16[4,2,16,768]{3,2,1,0:T(8,128)(2,1)}, u32[]{:S(2)}, u32[]{:S(2)}) collective-permute-start(bf16[4,2,16,768]{3,2,1,0:T(8,128)(2,1)} %get-tuple-element.116), channel_id=1, source_target_pairs={{0,12},{2,14},{4,8},{6,10},{8,4},{10,6},{12,0},{14,2},{1,13},{3,15... | collective-permute-start | bytes 589832 | tf_op jit(solution)/shard_map/ppermute | solution.py:384
  17.5 6.3 %collective-permute-done.1.refs_2_ = bf16[4,2,16,768]{3,2,1,0:T(8,128)(2,1)} collective-permute-done((bf16[4,2,16,768]{3,2,1,0:T(8,128)(2,1)}, bf16[4,2,16,768]{3,2,1,0:T(8,128)(2,1)}, u32[]{:S(2)}, u32[]{:S(2)}) %collective-permute-start.1) | collective-permute-done | bytes 196640 | tf_op jit(solution)/shard_map/ppermute | solution.py:384
  29.2 3.0 %to_modes.3 = (bf16[4,2,16,768]{3,2,1,0:T(8,128)(2,1)}, bf16[4,2,16,768]{3,2,1,0:T(8,128)(2,1)}, bf16[4,2,16,768]{3,2,1,0:T(8,128)(2,1)}, bf16[4,2,16,768]{3,2,1...) custom-call(s32[1]{0:T(128)} %bitcast.me_ref, ...), custom_call_target="tpu_custom_call" | custom-call | flops 283115520 | bytes 3784704 | tf_op jit(solution)/shard_map/to_modes/pallas_call | solution.py:124
  32.3 4.8 %collective-permute-start.16 = (bf16[4,2,16,768]{3,2,1,0:T(8,128)(2,1)}, bf16[4,2,16,768]{3,2,1,0:T(8,128)(2,1)}, u32[]{:S(2)}, u32[]{:S(2)}) collective-permute-start(bf16[4,2,16,768]{3,2,1,0:T(8,128)(2,1)} %get-tuple-element.138), channel_id=1, source_target_pairs={{0,6},{2,4},{4,2},{6,0},{8,14},{10,12},{12,10},{14,8},{1,7},{3,5},... | collective-permute-start | bytes 589832 | tf_op jit(solution)/shard_map/ppermute | solution.py:384
  37.1 4.0 %collective-permute-done.4.refs_5_ = bf16[4,2,16,768]{3,2,1,0:T(8,128)(2,1)} collective-permute-done((bf16[4,2,16,768]{3,2,1,0:T(8,128)(2,1)}, bf16[4,2,16,768]{3,2,1,0:T(8,128)(2,1)}, u32[]{:S(2)}, u32[]{:S(2)}) %collective-permute-start.4) | collective-permute-done | bytes 196640 | tf_op jit(solution)/shard_map/ppermute | solution.py:384
  41.1 13.2 %collective-permute-start.18 = (bf16[4,2,16,768]{3,2,1,0:T(8,128)(2,1)}, bf16[4,2,16,768]{3,2,1,0:T(8,128)(2,1)S(1)}, u32[]{:S(2)}, u32[]{:S(2)}) collective-permute-start(bf16[4,2,16,768]{3,2,1,0:T(8,128)(2,1)} %get-tuple-element.140), channel_id=1, source_target_pairs={{0,10},{2,8},{4,14},{6,12},{8,2},{10,0},{12,6},{14,4},{1,11},{3,9}... | collective-permute-start | bytes 589832 | tf_op jit(solution)/shard_map/ppermute | solution.py:384
  54.4 6.7 %mix_forward.1 = (bf16[4,2,16,768]{3,2,1,0:T(8,128)(2,1)}, bf16[4,2,16,768]{3,2,1,0:T(8,128)(2,1)}, bf16[4,2,16,768]{3,2,1,0:T(8,128)(2,1)}, bf16[4,2,16,768]{3,...) custom-call(s32[1]{0:T(128)} %bitcast.me_ref, ...), custom_call_target="tpu_custom_call" | custom-call | flops 2415919104 | bytes 17301504 | tf_op jit(solution)/shard_map/mix_forward/pallas_call | solution.py:309
  62.9 4.7 %collective-permute-start.20 = (bf16[4,2,16,768]{3,2,1,0:T(8,128)(2,1)S(1)}, bf16[4,2,16,768]{3,2,1,0:T(8,128)(2,1)}, u32[]{:S(2)}, u32[]{:S(2)}) collective-permute-start(bf16[4,2,16,768]{3,2,1,0:T(8,128)(2,1)S(1)} %copy-done.31), channel_id=1, source_target_pairs={{0,14},{2,12},{4,10},{6,8},{8,6},{10,4},{12,2},{14,0},{1,15},{3,13... | collective-permute-start | bytes 589832 | tf_op jit(solution)/shard_map/ppermute | solution.py:384
  67.6 7.4 %collective-permute-start.8 = (bf16[4,2,16,768]{3,2,1,0:T(8,128)(2,1)}, bf16[4,2,16,768]{3,2,1,0:T(8,128)(2,1)S(1)}, u32[]{:S(2)}, u32[]{:S(2)}) collective-permute-start(bf16[4,2,16,768]{3,2,1,0:T(8,128)(2,1)} %get-tuple-element.128), channel_id=1, source_target_pairs={{0,4},{2,6},{4,0},{6,2},{8,12},{10,14},{12,8},{14,10},{1,5},{3,7},... | collective-permute-start | bytes 589832 | tf_op jit(solution)/shard_map/ppermute | solution.py:384
  77.8 3.2 %collective-permute-start.10 = (bf16[4,2,16,768]{3,2,1,0:T(8,128)(2,1)}, bf16[4,2,16,768]{3,2,1,0:T(8,128)(2,1)S(1)}, u32[]{:S(2)}, u32[]{:S(2)}) collective-permute-start(bf16[4,2,16,768]{3,2,1,0:T(8,128)(2,1)} %get-tuple-element.130), channel_id=1, source_target_pairs={{0,8},{2,10},{4,12},{6,14},{8,0},{10,2},{12,4},{14,6},{1,9},{3,11}... | collective-permute-start | bytes 589832 | tf_op jit(solution)/shard_map/ppermute | solution.py:384
  81.0 2.9 %collective-permute-start.11 = (bf16[4,2,16,768]{3,2,1,0:T(8,128)(2,1)}, bf16[4,2,16,768]{3,2,1,0:T(8,128)(2,1)S(1)}, u32[]{:S(2)}, u32[]{:S(2)}) collective-permute-start(bf16[4,2,16,768]{3,2,1,0:T(8,128)(2,1)} %get-tuple-element.131), channel_id=1, source_target_pairs={{0,10},{2,8},{4,14},{6,12},{8,2},{10,0},{12,6},{14,4},{1,11},{3,9}... | collective-permute-start | bytes 589832 | tf_op jit(solution)/shard_map/ppermute | solution.py:384
  91.2 11.7 %mix_backward.1 = (bf16[4,2,16,768]{3,2,1,0:T(8,128)(2,1)}, bf16[4,2,16,768]{3,2,1,0:T(8,128)(2,1)}, bf16[4,2,16,768]{3,2,1,0:T(8,128)(2,1)}, bf16[4,2,16,768]{3...) custom-call(s32[1]{0:T(128)} %bitcast.me_ref, ...), custom_call_target="tpu_custom_call" | custom-call | flops 4831838208 | bytes 17301504 | tf_op jit(solution)/shard_map/mix_backward/pallas_call | solution.py:347
  109.3 3.8 %collective-permute-done.7.refs_1_ = bf16[4,2,16,768]{3,2,1,0:T(8,128)(2,1)S(1)} collective-permute-done((bf16[4,2,16,768]{3,2,1,0:T(8,128)(2,1)}, bf16[4,2,16,768]{3,2,1,0:T(8,128)(2,1)S(1)}, u32[]{:S(2)}, u32[]{:S(2)}) %collective-permute-start.7) | collective-permute-done | bytes 196640 | tf_op jit(solution)/shard_map/ppermute | solution.py:384
  114.4 3.9 %collective-permute-start.13 = (bf16[4,2,16,768]{3,2,1,0:T(8,128)(2,1)}, bf16[4,2,16,768]{3,2,1,0:T(8,128)(2,1)}, u32[]{:S(2)}, u32[]{:S(2)}) collective-permute-start(bf16[4,2,16,768]{3,2,1,0:T(8,128)(2,1)} %get-tuple-element.133), channel_id=1, source_target_pairs={{0,14},{2,12},{4,10},{6,8},{8,6},{10,4},{12,2},{14,0},{1,15},{3,13... | collective-permute-start | bytes 589832 | tf_op jit(solution)/shard_map/ppermute | solution.py:384
  118.3 8.7 %collective-permute-start.25 = (bf16[4,2,16,768]{3,2,1,0:T(8,128)(2,1)}, bf16[4,2,16,768]{3,2,1,0:T(8,128)(2,1)}, u32[]{:S(2)}, u32[]{:S(2)}) collective-permute-start(bf16[4,2,16,768]{3,2,1,0:T(8,128)(2,1)} %get-tuple-element.161), channel_id=1, source_target_pairs={{0,4},{2,6},{4,0},{6,2},{8,12},{10,14},{12,8},{14,10},{1,5},{3,7},... | collective-permute-start | bytes 589832 | tf_op jit(solution)/shard_map/ppermute | solution.py:384
  128.2 14.1 %collective-permute-start.27 = (bf16[4,2,16,768]{3,2,1,0:T(8,128)(2,1)}, bf16[4,2,16,768]{3,2,1,0:T(8,128)(2,1)}, u32[]{:S(2)}, u32[]{:S(2)}) collective-permute-start(bf16[4,2,16,768]{3,2,1,0:T(8,128)(2,1)} %get-tuple-element.165), channel_id=1, source_target_pairs={{0,10},{2,8},{4,14},{6,12},{8,2},{10,0},{12,6},{14,4},{1,11},{3,9}... | collective-permute-start | bytes 589832 | tf_op jit(solution)/shard_map/ppermute | solution.py:384
  147.8 7.5 %collective-permute-done.27.refs_5_ = bf16[4,2,16,768]{3,2,1,0:T(8,128)(2,1)} collective-permute-done((bf16[4,2,16,768]{3,2,1,0:T(8,128)(2,1)}, bf16[4,2,16,768]{3,2,1,0:T(8,128)(2,1)}, u32[]{:S(2)}, u32[]{:S(2)}) %collective-permute-start.27) | collective-permute-done | bytes 196640 | tf_op jit(solution)/shard_map/ppermute | solution.py:384
  167.0 6.8 %collective-permute-done.36 = bf16[4,56,384]{2,1,0:T(8,128)(2,1)S(1)} collective-permute-done((bf16[4,56,384]{2,1,0:T(8,128)(2,1)S(1)}, bf16[4,56,384]{2,1,0:T(8,128)(2,1)S(1)}, u32[]{:S(2)}, u32[]{:S(2)}) %collective-permute-start.36) | collective-permute-done | bytes 172064 | tf_op jit(solution)/shard_map/ppermute | solution.py:384
  176.6 3.2 %to_cells.2 = bf16[4,2,180,768]{3,2,1,0:T(8,128)(2,1)S(1)} custom-call(s32[1]{0:T(128)} %bitcast.me_ref, bf16[180,128]{1,0:T(8,128)(2,1)S(1)} %copy-done.6, bf16[4,2,180,768]{3,2,1,0:T(8,128)(2,1)S(1)} %copy.23.cells_ref.base_ref, bf16[4,2,16,768]{3,2,1,0:T(8,128)(2,1)} %get-tuple-element.126.refs_0_, bf16[4,2,16,768]{3,2,1,0:T(8,128)(2,1)} %copy-done.23, ...), custom_call_target="tpu_custom_call" | custom-call | flops 283115520 | bytes 5996544 | tf_op jit(solution)/shard_map/to_cells/pallas_call | solution.py:162
  179.8 3.1 %copy.25 = bf16[4,2,180,768]{3,1,2,0:T(2,128)(2,1)} copy(bf16[4,2,180,768]{3,2,1,0:T(8,128)(2,1)S(1)} %to_cells.2) | data formatting | bytes 4423680
  187.6 3.0 %to_cells.3 = bf16[4,2,180,768]{3,2,1,0:T(8,128)(2,1)S(1)} custom-call(s32[1]{0:T(128)} %bitcast.me_ref, bf16[180,128]{1,0:T(8,128)(2,1)S(1)} %copy-done.5, bf16[4,2,180,768]{3,2,1,0:T(8,128)(2,1)S(1)} %copy-done.1, bf16[4,2,16,768]{3,2,1,0:T(8,128)(2,1)} %get-tuple-element.152.refs_0_, bf16[4,2,16,768]{3,2,1,0:T(8,128)(2,1)} %copy-done.27, ...), custom_call_target="tpu_custom_call" | custom-call | flops 283115520 | bytes 5996544 | tf_op jit(solution)/shard_map/to_cells/pallas_call | solution.py:162
  190.6 3.1 %copy.26 = bf16[4,2,180,768]{3,1,2,0:T(2,128)(2,1)} copy(bf16[4,2,180,768]{3,2,1,0:T(8,128)(2,1)S(1)} %to_cells.3) | data formatting | bytes 4423680
  (147 shorter events, 60.0 us)
Async XLA Ops:
  8.1 15.8 %collective-permute-start.1 = (bf16[4,2,16,768]{3,2,1,0:T(8,128)(2,1)}, bf16[4,2,16,768]{3,2,1,0:T(8,128)(2,1)}, u32[]{:S(2)}, u32[]{:S(2)}) collective-permute-start(bf16[4,2,16,768]{3,2,1,0:T(8,128)(2,1)} %get-tuple-element.112), channel_id=1, source_target_pairs={{0,4},{2,6},{4,0},{6,2},{8,12},{10,14},{12,8},{14,10},{1,5},{3,7},... | collective-permute-start | bytes 589832 | tf_op jit(solution)/shard_map/ppermute | solution.py:384
  9.6 22.6 %collective-permute-start.2 = (bf16[4,2,16,768]{3,2,1,0:T(8,128)(2,1)}, bf16[4,2,16,768]{3,2,1,0:T(8,128)(2,1)}, u32[]{:S(2)}, u32[]{:S(2)}) collective-permute-start(bf16[4,2,16,768]{3,2,1,0:T(8,128)(2,1)} %get-tuple-element.113), channel_id=1, source_target_pairs={{0,6},{2,4},{4,2},{6,0},{8,14},{10,12},{12,10},{14,8},{1,7},{3,5},... | collective-permute-start | bytes 589832 | tf_op jit(solution)/shard_map/ppermute | solution.py:384
  9.6 22.7 %collective-permute-start.3 = (bf16[4,2,16,768]{3,2,1,0:T(8,128)(2,1)}, bf16[4,2,16,768]{3,2,1,0:T(8,128)(2,1)}, u32[]{:S(2)}, u32[]{:S(2)}) collective-permute-start(bf16[4,2,16,768]{3,2,1,0:T(8,128)(2,1)} %get-tuple-element.114), channel_id=1, source_target_pairs={{0,8},{2,10},{4,12},{6,14},{8,0},{10,2},{12,4},{14,6},{1,9},{3,11}... | collective-permute-start | bytes 589832 | tf_op jit(solution)/shard_map/ppermute | solution.py:384
  12.6 28.5 %collective-permute-start.4 = (bf16[4,2,16,768]{3,2,1,0:T(8,128)(2,1)}, bf16[4,2,16,768]{3,2,1,0:T(8,128)(2,1)}, u32[]{:S(2)}, u32[]{:S(2)}) collective-permute-start(bf16[4,2,16,768]{3,2,1,0:T(8,128)(2,1)} %get-tuple-element.115), channel_id=1, source_target_pairs={{0,10},{2,8},{4,14},{6,12},{8,2},{10,0},{12,6},{14,4},{1,11},{3,9}... | collective-permute-start | bytes 589832 | tf_op jit(solution)/shard_map/ppermute | solution.py:384
  13.9 27.2 %collective-permute-start.5 = (bf16[4,2,16,768]{3,2,1,0:T(8,128)(2,1)}, bf16[4,2,16,768]{3,2,1,0:T(8,128)(2,1)}, u32[]{:S(2)}, u32[]{:S(2)}) collective-permute-start(bf16[4,2,16,768]{3,2,1,0:T(8,128)(2,1)} %get-tuple-element.116), channel_id=1, source_target_pairs={{0,12},{2,14},{4,8},{6,10},{8,4},{10,6},{12,0},{14,2},{1,13},{3,15... | collective-permute-start | bytes 589832 | tf_op jit(solution)/shard_map/ppermute | solution.py:384
  23.8 30.5 %collective-permute-start.6 = (bf16[4,2,16,768]{3,2,1,0:T(8,128)(2,1)}, bf16[4,2,16,768]{3,2,1,0:T(8,128)(2,1)}, u32[]{:S(2)}, u32[]{:S(2)}) collective-permute-start(bf16[4,2,16,768]{3,2,1,0:T(8,128)(2,1)} %get-tuple-element.117), channel_id=1, source_target_pairs={{0,14},{2,12},{4,10},{6,8},{8,6},{10,4},{12,2},{14,0},{1,15},{3,13... | collective-permute-start | bytes 589832 | tf_op jit(solution)/shard_map/ppermute | solution.py:384
  32.2 30.6 %collective-permute-start.15 = (bf16[4,2,16,768]{3,2,1,0:T(8,128)(2,1)}, bf16[4,2,16,768]{3,2,1,0:T(8,128)(2,1)}, u32[]{:S(2)}, u32[]{:S(2)}) collective-permute-start(bf16[4,2,16,768]{3,2,1,0:T(8,128)(2,1)} %get-tuple-element.137), channel_id=1, source_target_pairs={{0,4},{2,6},{4,0},{6,2},{8,12},{10,14},{12,8},{14,10},{1,5},{3,7},... | collective-permute-start | bytes 589832 | tf_op jit(solution)/shard_map/ppermute | solution.py:384
  32.3 30.6 %collective-permute-start.16 = (bf16[4,2,16,768]{3,2,1,0:T(8,128)(2,1)}, bf16[4,2,16,768]{3,2,1,0:T(8,128)(2,1)}, u32[]{:S(2)}, u32[]{:S(2)}) collective-permute-start(bf16[4,2,16,768]{3,2,1,0:T(8,128)(2,1)} %get-tuple-element.138), channel_id=1, source_target_pairs={{0,6},{2,4},{4,2},{6,0},{8,14},{10,12},{12,10},{14,8},{1,7},{3,5},... | collective-permute-start | bytes 589832 | tf_op jit(solution)/shard_map/ppermute | solution.py:384
  41.1 26.5 %collective-permute-start.17 = (bf16[4,2,16,768]{3,2,1,0:T(8,128)(2,1)}, bf16[4,2,16,768]{3,2,1,0:T(8,128)(2,1)S(1)}, u32[]{:S(2)}, u32[]{:S(2)}) collective-permute-start(bf16[4,2,16,768]{3,2,1,0:T(8,128)(2,1)} %get-tuple-element.139), channel_id=1, source_target_pairs={{0,8},{2,10},{4,12},{6,14},{8,0},{10,2},{12,4},{14,6},{1,9},{3,11}... | collective-permute-start | bytes 589832 | tf_op jit(solution)/shard_map/ppermute | solution.py:384
  41.1 33.9 %collective-permute-start.18 = (bf16[4,2,16,768]{3,2,1,0:T(8,128)(2,1)}, bf16[4,2,16,768]{3,2,1,0:T(8,128)(2,1)S(1)}, u32[]{:S(2)}, u32[]{:S(2)}) collective-permute-start(bf16[4,2,16,768]{3,2,1,0:T(8,128)(2,1)} %get-tuple-element.140), channel_id=1, source_target_pairs={{0,10},{2,8},{4,14},{6,12},{8,2},{10,0},{12,6},{14,4},{1,11},{3,9}... | collective-permute-start | bytes 589832 | tf_op jit(solution)/shard_map/ppermute | solution.py:384
  62.3 15.5 %collective-permute-start.14 = (bf16[4,2,16,768]{3,2,1,0:T(8,128)(2,1)}, bf16[4,2,16,768]{3,2,1,0:T(8,128)(2,1)}, u32[]{:S(2)}, u32[]{:S(2)}) collective-permute-start(bf16[4,2,16,768]{3,2,1,0:T(8,128)(2,1)} %get-tuple-element.136), channel_id=1, source_target_pairs={{0,2},{2,0},{4,6},{6,4},{8,10},{10,8},{12,14},{14,12},{1,3},{3,1},... | collective-permute-start | bytes 589832 | tf_op jit(solution)/shard_map/ppermute | solution.py:384
  62.9 18.2 %collective-permute-start.19 = (bf16[4,2,16,768]{3,2,1,0:T(8,128)(2,1)S(1)}, bf16[4,2,16,768]{3,2,1,0:T(8,128)(2,1)}, u32[]{:S(2)}, u32[]{:S(2)}) collective-permute-start(bf16[4,2,16,768]{3,2,1,0:T(8,128)(2,1)S(1)} %copy-done.33), channel_id=1, source_target_pairs={{0,12},{2,14},{4,8},{6,10},{8,4},{10,6},{12,0},{14,2},{1,13},{3,15... | collective-permute-start | bytes 589832 | tf_op jit(solution)/shard_map/ppermute | solution.py:384
  62.9 21.0 %collective-permute-start.20 = (bf16[4,2,16,768]{3,2,1,0:T(8,128)(2,1)S(1)}, bf16[4,2,16,768]{3,2,1,0:T(8,128)(2,1)}, u32[]{:S(2)}, u32[]{:S(2)}) collective-permute-start(bf16[4,2,16,768]{3,2,1,0:T(8,128)(2,1)S(1)} %copy-done.31), channel_id=1, source_target_pairs={{0,14},{2,12},{4,10},{6,8},{8,6},{10,4},{12,2},{14,0},{1,15},{3,13... | collective-permute-start | bytes 589832 | tf_op jit(solution)/shard_map/ppermute | solution.py:384
  67.6 35.3 %collective-permute-start.8 = (bf16[4,2,16,768]{3,2,1,0:T(8,128)(2,1)}, bf16[4,2,16,768]{3,2,1,0:T(8,128)(2,1)S(1)}, u32[]{:S(2)}, u32[]{:S(2)}) collective-permute-start(bf16[4,2,16,768]{3,2,1,0:T(8,128)(2,1)} %get-tuple-element.128), channel_id=1, source_target_pairs={{0,4},{2,6},{4,0},{6,2},{8,12},{10,14},{12,8},{14,10},{1,5},{3,7},... | collective-permute-start | bytes 589832 | tf_op jit(solution)/shard_map/ppermute | solution.py:384
  75.0 28.0 %collective-permute-start.9 = (bf16[4,2,16,768]{3,2,1,0:T(8,128)(2,1)}, bf16[4,2,16,768]{3,2,1,0:T(8,128)(2,1)S(1)}, u32[]{:S(2)}, u32[]{:S(2)}) collective-permute-start(bf16[4,2,16,768]{3,2,1,0:T(8,128)(2,1)} %get-tuple-element.129), channel_id=1, source_target_pairs={{0,6},{2,4},{4,2},{6,0},{8,14},{10,12},{12,10},{14,8},{1,7},{3,5},... | collective-permute-start | bytes 589832 | tf_op jit(solution)/shard_map/ppermute | solution.py:384
  77.8 25.2 %collective-permute-start.10 = (bf16[4,2,16,768]{3,2,1,0:T(8,128)(2,1)}, bf16[4,2,16,768]{3,2,1,0:T(8,128)(2,1)S(1)}, u32[]{:S(2)}, u32[]{:S(2)}) collective-permute-start(bf16[4,2,16,768]{3,2,1,0:T(8,128)(2,1)} %get-tuple-element.130), channel_id=1, source_target_pairs={{0,8},{2,10},{4,12},{6,14},{8,0},{10,2},{12,4},{14,6},{1,9},{3,11}... | collective-permute-start | bytes 589832 | tf_op jit(solution)/shard_map/ppermute | solution.py:384
  81.0 23.7 %collective-permute-start.11 = (bf16[4,2,16,768]{3,2,1,0:T(8,128)(2,1)}, bf16[4,2,16,768]{3,2,1,0:T(8,128)(2,1)S(1)}, u32[]{:S(2)}, u32[]{:S(2)}) collective-permute-start(bf16[4,2,16,768]{3,2,1,0:T(8,128)(2,1)} %get-tuple-element.131), channel_id=1, source_target_pairs={{0,10},{2,8},{4,14},{6,12},{8,2},{10,0},{12,6},{14,4},{1,11},{3,9}... | collective-permute-start | bytes 589832 | tf_op jit(solution)/shard_map/ppermute | solution.py:384
  83.9 20.8 %collective-permute-start.12 = (bf16[4,2,16,768]{3,2,1,0:T(8,128)(2,1)}, bf16[4,2,16,768]{3,2,1,0:T(8,128)(2,1)S(1)}, u32[]{:S(2)}, u32[]{:S(2)}) collective-permute-start(bf16[4,2,16,768]{3,2,1,0:T(8,128)(2,1)} %get-tuple-element.132), channel_id=1, source_target_pairs={{0,12},{2,14},{4,8},{6,10},{8,4},{10,6},{12,0},{14,2},{1,13},{3,15... | collective-permute-start | bytes 589832 | tf_op jit(solution)/shard_map/ppermute | solution.py:384
  113.1 29.2 %collective-permute-start.22 = (f32[224,384]{1,0:T(8,128)S(1)}, f32[224,384]{1,0:T(8,128)}, u32[]{:S(2)}, u32[]{:S(2)}) collective-permute-start(f32[224,384]{1,0:T(8,128)S(1)} %dynamic-slice_bitcast_fusion.1), channel_id=1, source_target_pairs={{0,2},{2,0},{4,6},{6,4},{8,10},{10,8},{12,14},{14,12},{1,3},{3,1},... | collective-permute-start | bytes 1032200 | tf_op jit(solution)/shard_map/ppermute | solution.py:384
  114.4 13.8 %collective-permute-start.13 = (bf16[4,2,16,768]{3,2,1,0:T(8,128)(2,1)}, bf16[4,2,16,768]{3,2,1,0:T(8,128)(2,1)}, u32[]{:S(2)}, u32[]{:S(2)}) collective-permute-start(bf16[4,2,16,768]{3,2,1,0:T(8,128)(2,1)} %get-tuple-element.133), channel_id=1, source_target_pairs={{0,14},{2,12},{4,10},{6,8},{8,6},{10,4},{12,2},{14,0},{1,15},{3,13... | collective-permute-start | bytes 589832 | tf_op jit(solution)/shard_map/ppermute | solution.py:384
  118.3 25.0 %collective-permute-start.25 = (bf16[4,2,16,768]{3,2,1,0:T(8,128)(2,1)}, bf16[4,2,16,768]{3,2,1,0:T(8,128)(2,1)}, u32[]{:S(2)}, u32[]{:S(2)}) collective-permute-start(bf16[4,2,16,768]{3,2,1,0:T(8,128)(2,1)} %get-tuple-element.161), channel_id=1, source_target_pairs={{0,4},{2,6},{4,0},{6,2},{8,12},{10,14},{12,8},{14,10},{1,5},{3,7},... | collective-permute-start | bytes 589832 | tf_op jit(solution)/shard_map/ppermute | solution.py:384
  127.0 19.1 %collective-permute-start.26 = (bf16[4,2,16,768]{3,2,1,0:T(8,128)(2,1)}, bf16[4,2,16,768]{3,2,1,0:T(8,128)(2,1)}, u32[]{:S(2)}, u32[]{:S(2)}) collective-permute-start(bf16[4,2,16,768]{3,2,1,0:T(8,128)(2,1)} %get-tuple-element.163), channel_id=1, source_target_pairs={{0,8},{2,10},{4,12},{6,14},{8,0},{10,2},{12,4},{14,6},{1,9},{3,11}... | collective-permute-start | bytes 589832 | tf_op jit(solution)/shard_map/ppermute | solution.py:384
  128.2 27.1 %collective-permute-start.27 = (bf16[4,2,16,768]{3,2,1,0:T(8,128)(2,1)}, bf16[4,2,16,768]{3,2,1,0:T(8,128)(2,1)}, u32[]{:S(2)}, u32[]{:S(2)}) collective-permute-start(bf16[4,2,16,768]{3,2,1,0:T(8,128)(2,1)} %get-tuple-element.165), channel_id=1, source_target_pairs={{0,10},{2,8},{4,14},{6,12},{8,2},{10,0},{12,6},{14,4},{1,11},{3,9}... | collective-permute-start | bytes 589832 | tf_op jit(solution)/shard_map/ppermute | solution.py:384
  173.9 19.8 %collective-permute-start.37 = (bf16[2,4,56,384]{3,2,1,0:T(8,128)(2,1)S(1)}, bf16[2,4,56,384]{3,2,1,0:T(8,128)(2,1)S(1)}, u32[]{:S(2)}, u32[]{:S(2)}) collective-permute-start(bf16[2,4,56,384]{3,2,1,0:T(8,128)(2,1)S(1)} %pad_maximum_fusion.half_ref), channel_id=1, source_target_pairs={{0,1},{1,0},{2,3},{3,2},{4,5},{5,4},{6,7},{7,6},{8,9},{9,8},{10,11... | collective-permute-start | bytes 1032200 | tf_op jit(solution)/shard_map/ppermute | solution.py:384
  (48 other events, 567.0 us)

commit v6 on v4

--- a/solution.py
+++ b/solution.py
@@ -13,6 +13,7 @@
 KW = 64
 shrink_level = 0.05
 HELD = 5
+FIRST = 4
 MIB = 1024 * 1024
 
 
@@ -77,7 +78,7 @@
     _, count, size, _ = weights[0].shape
     per = count // groups
     lanes = 2 * per * size
-    shape = jax.ShapeDtypeStruct((groups, lanes, lanes), jnp.bfloat16)
+    shape = in_hbm((groups, lanes, lanes), jnp.bfloat16)
     return pl.pallas_call(
         spread_kernel,
         grid=(groups,),
@@ -104,20 +105,29 @@
     return pl.ds(pl.multiple_of((me_ref[0] ^ offset) * rows, rows), rows)
 
 
+def in_hbm(shape, dtype):
+    return pltpu.HBM(shape, dtype)
+
+
+def hbm(*arrays):
+    return [pltpu.with_memory_space_constraint(array, pltpu.HBM) for array in arrays]
+
+
 def to_modes_kernel(me_ref, table_ref, cells_ref, *refs):
     modes_refs, held_ref = refs[:-1], refs[-1]
-    share = modes_refs[0].shape[2]
-    for row in range(cells_ref.shape[1]):
+    rows = cells_ref.shape[1]
+    share = modes_refs[0].shape[0] // rows
+    for row in range(rows):
         spectrum = product_of(table_ref[...], cells_ref[0, row])
         held_ref[row] = spectrum.astype(jnp.bfloat16)
         for offset, modes_ref in enumerate(modes_refs):
-            modes_ref[0, row] = held_ref[row, place_of(me_ref, offset, share)]
+            modes_ref[pl.ds(row * share, share)] = held_ref[row, place_of(me_ref, offset, share)]
 
 
 def to_modes(me, table, cells, owners):
     samples, rows, width, channels = cells.shape
     size = table.shape[0]
-    share = (rows, size // owners, channels)
+    part = rows * size // owners
     return pl.pallas_call(
         to_modes_kernel,
         grid_spec=pltpu.PrefetchScalarGridSpec(
@@ -127,10 +137,10 @@
                 pl.BlockSpec((size, width), lambda b, _: (0, 0)),
                 pl.BlockSpec((1, rows, width, channels), lambda b, _: (b, 0, 0, 0)),
             ],
-            out_specs=(pl.BlockSpec((1,) + share, lambda b, _: (b, 0, 0, 0)),) * owners,
+            out_specs=(pl.BlockSpec((part, channels), lambda b, _: (b, 0)),) * owners,
             scratch_shapes=[pltpu.VMEM((rows, size, channels), jnp.bfloat16)],
         ),
-        out_shape=(jax.ShapeDtypeStruct((samples,) + share, jnp.bfloat16),) * owners,
+        out_shape=(in_hbm((samples * part, channels), jnp.bfloat16),) * owners,
         compiler_params=params(12),
         cost_estimate=pl.CostEstimate(
             flops=2 * samples * rows * size * width * channels,
@@ -138,15 +148,17 @@
             transcendentals=0,
         ),
         name="to_modes",
-    )(me, table, cells)
+    )(me, table, *hbm(cells))
 
 
 def to_cells_kernel(me_ref, table_ref, base_ref, *refs):
     modes_refs, out_ref, held_ref = refs[:-2], refs[-2], refs[-1]
-    share = modes_refs[0].shape[2]
-    for row in range(base_ref.shape[1]):
+    rows = base_ref.shape[1]
+    share = modes_refs[0].shape[0] // rows
+    for row in range(rows):
         for offset, modes_ref in enumerate(modes_refs):
-            held_ref[row, place_of(me_ref, offset, share)] = modes_ref[0, row]
+            spot = place_of(me_ref, offset, share)
+            held_ref[row, spot] = modes_ref[pl.ds(row * share, share)]
         image = product_of(table_ref[...], held_ref[row])
         out_ref[0, row] = (base_ref[0, row].astype(jnp.float32) + image).astype(jnp.bfloat16)
 
@@ -154,7 +166,7 @@
 def to_cells(me, table, modes, base):
     samples, rows, width, channels = base.shape
     size = table.shape[1]
-    share = modes[0].shape[1:]
+    part = rows * size // len(modes)
     block = pl.BlockSpec((1, rows, width, channels), lambda b, _: (b, 0, 0, 0))
     return pl.pallas_call(
         to_cells_kernel,
@@ -162,7 +174,7 @@
             num_scalar_prefetch=1,
             grid=(samples,),
             in_specs=[pl.BlockSpec((width, size), lambda b, _: (0, 0)), block]
-            + [pl.BlockSpec((1,) + share, lambda b, _: (b, 0, 0, 0))] * len(modes),
+            + [pl.BlockSpec((part, channels), lambda b, _: (b, 0))] * len(modes),
             out_specs=block,
             scratch_shapes=[pltpu.VMEM((rows, size, channels), jnp.bfloat16)],
         ),
@@ -174,7 +186,7 @@
             transcendentals=0,
         ),
         name="to_cells",
-    )(me, table, base, *modes)
+    )(me, table, *hbm(base, *modes))
 
 
 def sigmoid_of(values):
@@ -182,12 +194,12 @@
 
 
 def mix_lat(me_ref, table_ref, bands_refs, band_ref, mixed_ref):
-    samples, rows, share, width = bands_refs[0].shape
-    half = table_ref.shape[0] // 2
+    samples, size, width = band_ref.shape
+    part, half = size // len(bands_refs), size // 2
     for sample in range(samples):
         for offset, bands_ref in enumerate(bands_refs):
-            place = place_of(me_ref, offset, rows * share)
-            band_ref[sample, place] = bands_ref[sample].reshape(rows * share, width)
+            place = place_of(me_ref, offset, part)
+            band_ref[sample, place] = bands_ref[pl.ds(sample * part, part)]
         mixed = product_of(table_ref[...], band_ref[sample]).astype(jnp.bfloat16)
         spot = pl.ds(sample * half, half)
         mixed_ref[spot, 0:width] = mixed[:half]
@@ -195,8 +207,8 @@
 
 
 def unmix_lat(me_ref, table_ref, mixed_ref, band_ref, bands_refs):
-    samples, rows, share, width = bands_refs[0].shape
-    half = table_ref.shape[0] // 2
+    samples, size, width = band_ref.shape
+    part, half = size // len(bands_refs), size // 2
     for sample in range(samples):
         spot = pl.ds(sample * half, half)
         joined = jnp.concatenate(
@@ -204,8 +216,8 @@
         )
         band_ref[sample] = product_of(table_ref[...], joined).astype(jnp.bfloat16)
         for offset, bands_ref in enumerate(bands_refs):
-            place = place_of(me_ref, offset, rows * share)
-            bands_ref[sample] = band_ref[sample, place].reshape(rows, share, width)
+            place = place_of(me_ref, offset, part)
+            bands_ref[pl.ds(sample * part, part)] = band_ref[sample, place]
 
 
 def activate(mixed_ref, w1_ref, b1_ref):
@@ -234,6 +246,7 @@
 ):
     bands_refs, image_refs = refs[:owners], refs[owners : 2 * owners]
     sums_ref, act_ref, gate_ref, cot_ref, kept_ref, band_ref = refs[2 * owners :]
+    size_of_image = band_ref.shape[0] * band_ref.shape[1] // owners
     transposed = (((1,), (1,)), ((), ()))
     summed = (((0,), (0,)), ((), ()))
 
@@ -248,15 +261,15 @@
         bias = jnp.sum(grads.astype(jnp.float32), axis=0, keepdims=True)
         size = block_size
         owner = lax.broadcasted_iota(jnp.int32, (size, width), 1) // size
-        extra = sums_ref.shape[3] - size
+        extra = sums_ref.shape[2] - size
         first = lax.broadcasted_iota(jnp.int32, (extra, width), 0) == 0
         for part, values in enumerate((real, imag)):
             joined = values[:size]
             for block in range(1, width // size):
                 joined = jnp.where(owner == block, values[block * size : (block + 1) * size], joined)
-            sums_ref[slot, part, 0, 0:size] = joined
+            sums_ref[slot, part, 0:size] = joined.astype(sums_ref.dtype)
             row = bias[:, part * width : (part + 1) * width]
-            sums_ref[slot, part, 0, size:] = jnp.where(first, row, 0.0)
+            sums_ref[slot, part, size:] = jnp.where(first, row, 0.0).astype(sums_ref.dtype)
 
     logistic, act = activate(mixed_ref, w1_ref, b1_ref)
     act_ref[...] = act.astype(jnp.bfloat16)
@@ -270,31 +283,35 @@
     kept_ref[...] = times(cot_ref[...], w1_ref[0], transposed).astype(jnp.bfloat16)
     weight_sums(mixed_ref[0], cot_ref[...], 0)
     unmix_lat(me_ref, unlat_ref, kept_ref, band_ref, image_refs)
+    share = image_refs[0].shape[0] - size_of_image
+    if share > 0:
+        runs = sums_ref.shape[2] // share
+        for offset, image_ref in enumerate(image_refs):
+            owner = me_ref[0] ^ offset
+            pair, run = owner // runs, owner % runs
+            rows = pl.ds(pl.multiple_of(run * share, share), share)
+            image_ref[pl.ds(size_of_image, share)] = sums_ref[pair // 2, pair % 2, rows].astype(
+                jnp.bfloat16
+            )
 
 
 def group_spec(*shape):
     return pl.BlockSpec((1,) + shape, lambda g, *_: (g,) + (0,) * len(shape))
 
 
-def bands_specs(bands, groups):
-    shape = bands[0].shape
-    block = shape[:-1] + (shape[-1] // groups,)
-    return (pl.BlockSpec(block, lambda g, *_: (0, 0, 0, g)),) * len(bands)
-
-
-def shapes_of(bands):
-    return tuple(jax.ShapeDtypeStruct(band.shape, band.dtype) for band in bands)
+def bands_specs(rows, bands, groups):
+    block = (rows, bands[0].shape[1] // groups)
+    return (pl.BlockSpec(block, lambda g, *_: (0, g)),) * len(bands)
 
 
 def forward_mid(me, lat, unlat, bands, w1, b1, w2, b2):
     groups, lanes, _ = w1.shape
     size = lat.shape[0]
-    samples = bands[0].shape[0]
+    samples = bands[0].shape[0] * len(bands) // size
     positions = samples * size // 2
     table = pl.BlockSpec((size, size), lambda g, _: (0, 0))
     state = (groups, positions, lanes)
-    state_spec = group_spec(positions, lanes)
-    specs = bands_specs(bands, groups)
+    specs = bands_specs(bands[0].shape[0], bands, groups)
     results = pl.pallas_call(
         functools.partial(forward_kernel, len(bands)),
         grid_spec=pltpu.PrefetchScalarGridSpec(
@@ -306,13 +323,14 @@
                 group_spec(lanes, lanes), group_spec(1, lanes),
                 *specs,
             ],
-            out_specs=specs + (state_spec,),
+            out_specs=specs + (group_spec(positions, lanes),),
             scratch_shapes=[
                 pltpu.VMEM((positions, lanes), jnp.bfloat16),
                 pltpu.VMEM((samples, size, lanes // 2), jnp.bfloat16),
             ],
         ),
-        out_shape=shapes_of(bands) + (jax.ShapeDtypeStruct(state, jnp.bfloat16),),
+        out_shape=tuple(in_hbm(band.shape, band.dtype) for band in bands)
+        + (in_hbm(state, jnp.bfloat16),),
         compiler_params=params(28),
         cost_estimate=pl.CostEstimate(
             flops=4 * groups * positions * lanes * lanes,
@@ -320,19 +338,34 @@
             transcendentals=2 * groups * positions * lanes,
         ),
         name="mix_forward",
-    )(me, lat, unlat, w1, b1, w2, b2, *bands)
+    )(me, lat, unlat, *hbm(w1), b1, *hbm(w2), b2, *hbm(*bands))
     return results[: len(bands)], results[len(bands)]
 
 
-def backward_mid(me, lat, unlat, bands, w1, b1, w2, b2, state, count):
+def backward_mid(me, lat, unlat, bands, w1, b1, w2, b2, state, count, share):
     groups, lanes, _ = w1.shape
     size = lat.shape[0]
-    samples = bands[0].shape[0]
+    image_rows = bands[0].shape[0]
+    samples = image_rows * len(bands) // size
     positions = samples * size // 2
     table = pl.BlockSpec((size, size), lambda g, _: (0, 0))
-    specs = bands_specs(bands, groups)
     size_of_block = lanes // 2 // (count // groups)
     rows = size_of_block + 16
+    sums = (2, 2, rows, lanes // 2)
+    out_shape = (in_hbm((image_rows + share, bands[0].shape[1]), jnp.bfloat16),) * len(bands)
+    out_specs = bands_specs(image_rows + share, bands, groups)
+    scratch_shapes = [
+        pltpu.VMEM((positions, lanes), jnp.bfloat16),
+        pltpu.VMEM((positions, lanes), jnp.float32),
+        pltpu.VMEM((positions, lanes), jnp.bfloat16),
+        pltpu.VMEM((positions, lanes), jnp.bfloat16),
+        pltpu.VMEM((samples, size, lanes // 2), jnp.bfloat16),
+    ]
+    if share > 0:
+        scratch_shapes = [pltpu.VMEM(sums, jnp.float32)] + scratch_shapes
+    else:
+        out_shape += (jax.ShapeDtypeStruct(sums[:3] + (groups * sums[3],), jnp.float32),)
+        out_specs += (pl.BlockSpec(sums, lambda g, _: (0, 0, 0, g)),)
     results = pl.pallas_call(
         functools.partial(backward_kernel, size_of_block, len(bands)),
         grid_spec=pltpu.PrefetchScalarGridSpec(
@@ -342,21 +375,12 @@
                 table, table,
                 group_spec(lanes, lanes), group_spec(1, lanes),
                 group_spec(lanes, lanes), group_spec(1, lanes),
-                group_spec(positions, lanes), *specs,
+                group_spec(positions, lanes), *bands_specs(image_rows, bands, groups),
             ],
-            out_specs=specs + (
-                pl.BlockSpec((2, 2, 1, rows, lanes // 2), lambda g, _: (0, 0, g, 0, 0)),
-            ),
-            scratch_shapes=[
-                pltpu.VMEM((positions, lanes), jnp.bfloat16),
-                pltpu.VMEM((positions, lanes), jnp.float32),
-                pltpu.VMEM((positions, lanes), jnp.bfloat16),
-                pltpu.VMEM((positions, lanes), jnp.bfloat16),
-                pltpu.VMEM((samples, size, lanes // 2), jnp.bfloat16),
-            ],
-        ),
-        out_shape=shapes_of(bands)
-        + (jax.ShapeDtypeStruct((2, 2, groups, rows, lanes // 2), jnp.float32),),
+            out_specs=out_specs,
+            scratch_shapes=scratch_shapes,
+        ),
+        out_shape=out_shape,
         compiler_params=params(32),
         cost_estimate=pl.CostEstimate(
             flops=8 * groups * positions * lanes * lanes,
@@ -364,13 +388,11 @@
             transcendentals=0,
         ),
         name="mix_backward",
-    )(me, lat, unlat, w1, b1, w2, b2, state, *bands)
-    return results[: len(bands)], results[len(bands)]
-
-
-def swap_with(values, axis, distance, after=()):
-    if len(after) > 0:
-        values, _ = lax.optimization_barrier((values, tuple(after)))
+    )(me, lat, unlat, *hbm(w1), b1, *hbm(w2), b2, *hbm(state, *bands))
+    return results[: len(bands)], results[len(bands) :]
+
+
+def swap_with(values, axis, distance):
     pairs = [(i, i ^ distance) for i in range(lax.axis_size(axis))]
     return lax.ppermute(values, axis, pairs)
 
@@ -386,64 +408,43 @@
     return order
 
 
-def pick(pair, side):
-    return lax.dynamic_index_in_dim(pair, side, 0, keepdims=False)
-
-
-def by_place(blocks, bits):
-    shape = blocks.shape
-    for level, bit in enumerate(bits):
-        split = blocks.reshape((2**level, 2, -1) + shape[-2:])
-        blocks = jnp.where(bit == 0, split, jnp.concatenate([split[:, 1:], split[:, :1]], axis=1))
-    return blocks
-
-
-class GroupSum:
-    def __init__(self, sums):
-        self.lanes = sums.shape[-1]
-        self.shape = sums.shape
-        self.side = lax.axis_index("dp")
-        self.me = lax.axis_index("space")
-        self.count = lax.axis_size("space") // 2
-        self.held = sums.reshape(-1, self.lanes)
-
-    def halve(self, axis, distance, bit, after):
-        pair = self.held.reshape(2, -1, self.lanes)
-        taken = swap_with(pick(pair, 1 - bit), axis, distance, after)
-        self.held = pick(pair, bit) + taken
-
-    def over_dp(self, after):
-        self.halve("dp", 1, self.side, after)
-
-    def over_next(self, after):
-        self.halve("space", 1, self.me % 2, after)
-
-    def scatter(self, after):
-        shares = self.held.reshape(self.count, -1, self.lanes)
-        place = self.me // 2
-        total = pick(shares, place)
-        for offset in range(1, self.count):
-            given = pick(shares, place ^ offset).astype(jnp.bfloat16)
-            total += swap_with(given, "space", 2 * offset, after).astype(jnp.float32)
-        self.total = total.astype(jnp.bfloat16)
-
-    def gather(self, after):
-        taken = [self.total]
-        for offset in range(1, self.count):
-            taken.append(swap_with(self.total, "space", 2 * offset, after))
-        self.quarter = jnp.stack(taken)
-
-    def gather_next(self, after):
-        self.half = jnp.stack([self.quarter, swap_with(self.quarter, "space", 1, after)])
-
-    def join(self, after):
-        both = jnp.stack([self.half, swap_with(self.half, "dp", 1, after)])
-        bits = [self.side, self.me % 2]
-        level = self.count
-        while level > 1:
-            bits.append(self.me // level % 2)
-            level //= 2
-        return by_place(both, bits).reshape(self.shape)
+def finish_kernel(factor, me_ref, *refs):
+    shares_refs, out_refs = refs[:-5], refs[-5:-1]
+    held_ref = refs[-1]
+    run = shares_refs[0].shape[0]
+    for offset, shares_ref in enumerate(shares_refs):
+        held_ref[me_ref[0] ^ offset] = shares_ref[...].astype(jnp.float32) * factor
+    runs = len(shares_refs) // 4
+    for which in range(2):
+        blocks_ref, bias_ref = out_refs[2 * which : 2 * which + 2]
+        edge = blocks_ref.shape[-1]
+        for part in range(2):
+            for piece in range(runs):
+                value = held_ref[(2 * which + part) * runs + piece]
+                first = piece * run
+                count = max(0, min(edge - first, run))
+                for block in range(blocks_ref.shape[1]):
+                    lanes = slice(block * edge, (block + 1) * edge)
+                    if count > 0:
+                        blocks_ref[part, block, pl.ds(first, count)] = value[:count, lanes]
+                    if first <= edge < first + run:
+                        row = edge - first
+                        bias_ref[part, pl.ds(block, 1)] = value[row : row + 1, lanes]
+
+
+def finish_sums(me, shares, factor, weight_shape, bias_shape):
+    outs = [weight_shape, bias_shape] * 2
+    return pl.pallas_call(
+        functools.partial(finish_kernel, factor),
+        out_shape=[jax.ShapeDtypeStruct(shape, jnp.float32) for shape in outs],
+        in_specs=[pl.BlockSpec(memory_space=pltpu.SMEM)]
+        + [pl.BlockSpec(memory_space=pltpu.VMEM)] * len(shares),
+        out_specs=[pl.BlockSpec(memory_space=pltpu.VMEM)] * 4,
+        scratch_shapes=[pltpu.VMEM((len(shares),) + shares[0].shape, jnp.float32)],
+        compiler_params=pltpu.CompilerParams(vmem_limit_bytes=16 * MIB),
+        cost_estimate=pl.CostEstimate(flops=0, bytes_accessed=4 * MIB, transcendentals=0),
+        name="finish_sums",
+    )(me, *shares)
 
 
 def body(fields, cotangent, w_first, b_first, w_second, b_second):
@@ -467,13 +468,13 @@
         spectrum = blocks[0].reshape(samples, rows, owners, 2 * modes, channels)
         spectrum = jnp.transpose(spectrum, (2, 0, 1, 3, 4))
         arrived = lax.all_to_all(spectrum, "space", split_axis=0, concat_axis=0, tiled=True)
-        return [jnp.transpose(arrived, (1, 0, 2, 3, 4)).reshape(samples, 1, -1, channels)]
+        return [jnp.transpose(arrived, (1, 0, 2, 3, 4)).reshape(-1, channels)]
 
     def send_back(blocks):
         bands = blocks[0].reshape(samples, owners, rows, 2 * modes, channels)
         bands = jnp.transpose(bands, (1, 0, 2, 3, 4))
         arrived = lax.all_to_all(bands, "space", split_axis=0, concat_axis=0, tiled=True)
-        return [jnp.transpose(arrived, (1, 2, 0, 3, 4)).reshape(samples, rows, -1, channels)]
+        return [jnp.transpose(arrived, (1, 2, 0, 3, 4)).reshape(-1, channels)]
 
     me = lax.axis_index("space") if direct else 0
     me = jnp.full((1,), me, jnp.int32)
@@ -485,41 +486,45 @@
         (spectrum, cotangent, w_first, w_second)
     )
     gathered = send_out(spectrum)
-    cot_gathered = send_out(to_modes(me, scaled, cotangent, lead))
+    cot_spec = to_modes(me, scaled, cotangent, lead)
     w1, w2 = spread_weights(groups, w_first, w_second)
     b1, b2 = block_bias(b_first, groups), block_bias(b_second, groups)
 
     image, state = forward_mid(me, lat, lat.T, gathered, w1, b1, w2, b2)
+    if direct:
+        late = tuple(cot_spec[offset] for offset in order[FIRST:])
+        late, image = lax.optimization_barrier((late, image))
+        cot_spec = list(cot_spec)
+        for offset, block in zip(order[FIRST:], late):
+            cot_spec[offset] = block
+    cot_gathered = send_out(cot_spec)
     image_band = send_out(image) if direct else send_back(image)
-    grad_image, sums = backward_mid(
-        me, lat, lat.T, cot_gathered, w1, b1, w2, b2, state, count
+    share = 4 * (edge + 16) // owners if direct else 0
+    grad_image, rest = backward_mid(
+        me, lat, lat.T, cot_gathered, w1, b1, w2, b2, state, count, share
     )
+    positions = samples * lax.axis_size("dp") * lat_total * KW
+    factor = 1.0 / math.sqrt(positions)
     if direct:
         early = tuple(image_band[offset] for offset in order[:HELD])
-        grad_image, sums, _ = lax.optimization_barrier((grad_image, sums, early))
-        late = [image_band[offset] for offset in order[HELD:]]
+        grad_image, _ = lax.optimization_barrier((grad_image, early))
         grad_band = send_out(grad_image)
-        sent = [grad_band[offset] for offset in order]
     else:
         grad_band = send_back(grad_image)
-        late, sent = [], []
-    group_sum = GroupSum(sums)
-    group_sum.over_dp([])
-    group_sum.over_next(late)
-    group_sum.scatter(sent[:2])
-    group_sum.gather(sent[2:4])
-    group_sum.gather_next(sent[4:6])
     output = to_cells(me, scaled.T, image_band, fields)
     grad_fields = to_cells(me, plain.T, grad_band, cotangent)
 
-    positions = samples * lax.axis_size("dp") * lat_total * KW
-    factor = 1.0 / math.sqrt(positions)
-    sums = group_sum.join([]).astype(jnp.float32) * factor
+    if direct:
+        total = sum(band[-share:].astype(jnp.float32) for band in grad_band)
+        total = (total + swap_with(total, "dp", 1)).astype(jnp.bfloat16)
+        grads = finish_sums(me, send_out([total] * owners), factor, w_first.shape, b_first.shape)
+        return (output, grad_fields) + tuple(grads)
+    sums = lax.psum(rest[0], ("space", "dp")) * factor
     grads = []
     for which in range(2):
-        blocks = sums[which, :, :, :edge].reshape(2, groups, edge, count // groups, edge)
-        grads.append(jnp.transpose(blocks, (0, 1, 3, 2, 4)).reshape(w_first.shape))
-        grads.append(sums[which, :, :, edge].reshape(b_first.shape))
+        blocks = sums[which, :, :edge].reshape(2, edge, count, edge)
+        grads.append(jnp.transpose(blocks, (0, 2, 1, 3)))
+        grads.append(sums[which, :, edge].reshape(b_first.shape))
     return (output, grad_fields) + tuple(grads)
 
 

time: 206 us -> 200 us (0.971)
  local copies, waits for them, and re-layouts: 40.5 us -> 11.5 us
  starting transfers between devices: 80.6 us -> 96.7 us
  Pallas kernels: 26.2 us -> 40.2 us
  other arithmetic: 8.6 us -> 1.12 us
    unnamed x137 -> x81, local copies, waits for them, and re-layouts: 33.1 us -> 9.62 us
    ppermute x38 -> x36, starting transfers between devices: 80.6 us -> 96.7 us  [swap_with(): return lax.ppermute(values, axis, pairs)]
    pallas_call x2, Pallas kernels: 4.37 us -> 8.55 us  [to_modes(): pl.pallas_call(to_modes_kernel, grid_spec=pltpu.PrefetchScalarGridSpec(nu...]
    pallas_call x2, Pallas kernels: 3.92 us -> 6.97 us  [to_cells(): pl.pallas_call(to_cells_kernel, grid_spec=pltpu.PrefetchScalarGridSpec(nu...]
    another operation x4 -> x0, local copies, waits for them, and re-layouts: 2.28 us -> none  [the longest x2 1.35 us: body(): grads.append(sums[which, :, :, edge].reshape(b_first.shape))]
    ppermute x38 -> x36, waiting for transfers between devices: 47.3 us -> 49.1 us  [swap_with(): return lax.ppermute(values, axis, pairs)]
  transfers between devices with their start and end apart: 38 -> 36, of which waited for: 13 -> 8; matrix products, arithmetic and copies ran while one was open for 6% -> 4% of each run, Pallas kernels for 12% -> 17%
where the time goes in v6:
time: 200 us
  starting transfers between devices  96.7 us (48%)
  waiting for transfers between devices  49.1 us (25%)
  Pallas kernels  40.2 us (20%)
  local copies, waits for them, and re-layouts  11.5 us (6%)
    ppermute x36, starting transfers between devices, swap_with(): return lax.ppermute(values, axis, pairs)  96.7 us
    ppermute x36, waiting for transfers between devices, swap_with(): return lax.ppermute(values, axis, pairs)  49.1 us
    pallas_call x1, Pallas kernels, backward_mid(): pl.pallas_call(functools.partial(backward_kernel, size_of_block, len(band...  12.8 us
    unnamed x81, local copies, waits for them, and re-layouts  9.62 us
    pallas_call x2, Pallas kernels, to_modes(): pl.pallas_call(to_modes_kernel, grid_spec=pltpu.PrefetchScalarGridSpec(nu...  8.55 us
    pallas_call x1, Pallas kernels, forward_mid(): pl.pallas_call(functools.partial(forward_kernel, len(bands)), grid_spec=p...  7.64 us
    pallas_call x2, Pallas kernels, to_cells(): pl.pallas_call(to_cells_kernel, grid_spec=pltpu.PrefetchScalarGridSpec(nu...  6.97 us
  transfers between devices with their start and end apart: 36, of which 8 were waited for; matrix products, arithmetic and copies ran while one was open for 4% of the time, Pallas kernels for 17%

profile of v6, /device:TPU:0, one launch (start us, length us, event | category | flops | bytes accessed | tf_op | source)
XLA Modules:
  0.0 199.7 jit_solution(15942097118843182698)
XLA Ops:
  0.6 3.3 %copy.23.cells_ref.base_ref = bf16[4,2,180,768]{3,2,1,0:T(8,128)(2,1)} copy(bf16[4,2,180,768]{3,1,2,0:T(2,128)(2,1)} %param.13) | data formatting | bytes 4423680 | tf_op args[0]
  4.0 4.3 %to_modes.2 = (bf16[128,768]{1,0:T(8,128)(2,1)}, bf16[128,768]{1,0:T(8,128)(2,1)}, bf16[128,768]{1,0:T(8,128)(2,1)}, bf16[128,768]{1,0:T(8,128)(2,1)}, bf16[128,...) custom-call(s32[1]{0:T(128)} %bitcast.me_ref, ...), custom_call_target="tpu_custom_call" | custom-call | flops 283115520 | bytes 3784704 | tf_op jit(solution)/shard_map/to_modes/pallas_call | solution.py:131
  17.2 3.6 %collective-permute-start.5 = (bf16[128,768]{1,0:T(8,128)(2,1)}, bf16[128,768]{1,0:T(8,128)(2,1)}, u32[]{:S(2)}, u32[]{:S(2)}) collective-permute-start(bf16[128,768]{1,0:T(8,128)(2,1)} %get-tuple-element.97), channel_id=1, source_target_pairs={{0,12},{2,14},{4,8},{6,10},{8,4},{10,6},{12,0},{14,2},{1,13},{3,15... | collective-permute-start | bytes 589832 | tf_op jit(solution)/shard_map/ppermute | solution.py:397
  20.8 6.2 %collective-permute-done.1.refs_2_ = bf16[128,768]{1,0:T(8,128)(2,1)S(1)} collective-permute-done((bf16[128,768]{1,0:T(8,128)(2,1)}, bf16[128,768]{1,0:T(8,128)(2,1)S(1)}, u32[]{:S(2)}, u32[]{:S(2)}) %collective-permute-start.1) | collective-permute-done | bytes 196640 | tf_op jit(solution)/shard_map/ppermute | solution.py:397
  32.4 4.2 %to_modes.3 = (bf16[128,768]{1,0:T(8,128)(2,1)}, bf16[128,768]{1,0:T(8,128)(2,1)}, bf16[128,768]{1,0:T(8,128)(2,1)}, bf16[128,768]{1,0:T(8,128)(2,1)}, bf16[128,...) custom-call(s32[1]{0:T(128)} %bitcast.me_ref, ...), custom_call_target="tpu_custom_call" | custom-call | flops 283115520 | bytes 3784704 | tf_op jit(solution)/shard_map/to_modes/pallas_call | solution.py:131
  36.8 4.0 %collective-permute-start.16 = (bf16[128,768]{1,0:T(8,128)(2,1)}, bf16[128,768]{1,0:T(8,128)(2,1)S(1)}, u32[]{:S(2)}, u32[]{:S(2)}) collective-permute-start(bf16[128,768]{1,0:T(8,128)(2,1)} %get-tuple-element.119), channel_id=1, source_target_pairs={{0,6},{2,4},{4,2},{6,0},{8,14},{10,12},{12,10},{14,8},{1,7},{3,5},... | collective-permute-start | bytes 589832 | tf_op jit(solution)/shard_map/ppermute | solution.py:397
  40.7 3.7 %collective-permute-done.4.refs_5_ = bf16[128,768]{1,0:T(8,128)(2,1)} collective-permute-done((bf16[128,768]{1,0:T(8,128)(2,1)}, bf16[128,768]{1,0:T(8,128)(2,1)}, u32[]{:S(2)}, u32[]{:S(2)}) %collective-permute-start.4) | collective-permute-done | bytes 196640 | tf_op jit(solution)/shard_map/ppermute | solution.py:397
  44.4 13.2 %collective-permute-start.18 = (bf16[128,768]{1,0:T(8,128)(2,1)}, bf16[128,768]{1,0:T(8,128)(2,1)S(1)}, u32[]{:S(2)}, u32[]{:S(2)}) collective-permute-start(bf16[128,768]{1,0:T(8,128)(2,1)} %get-tuple-element.121), channel_id=1, source_target_pairs={{0,10},{2,8},{4,14},{6,12},{8,2},{10,0},{12,6},{14,4},{1,11},{3,9}... | collective-permute-start | bytes 589832 | tf_op jit(solution)/shard_map/ppermute | solution.py:397
  57.7 7.6 %mix_forward.1 = (bf16[128,768]{1,0:T(8,128)(2,1)}, bf16[128,768]{1,0:T(8,128)(2,1)}, bf16[128,768]{1,0:T(8,128)(2,1)}, bf16[128,768]{1,0:T(8,128)(2,1)}, bf16[1...) custom-call(s32[1]{0:T(128)} %bitcast.me_ref, ...), custom_call_target="tpu_custom_call" | custom-call | flops 2415919104 | bytes 17301504 | tf_op jit(solution)/shard_map/mix_forward/pallas_call | solution.py:315
  66.0 4.8 %collective-permute-start.20 = (bf16[128,768]{1,0:T(8,128)(2,1)S(1)}, bf16[128,768]{1,0:T(8,128)(2,1)S(1)}, u32[]{:S(2)}, u32[]{:S(2)}) collective-permute-start(bf16[128,768]{1,0:T(8,128)(2,1)S(1)} %copy-done.30), channel_id=1, source_target_pairs={{0,14},{2,12},{4,10},{6,8},{8,6},{10,4},{12,2},{14,0},{1,15},{3,13... | collective-permute-start | bytes 589832 | tf_op jit(solution)/shard_map/ppermute | solution.py:397
  70.8 7.3 %collective-permute-start.8 = (bf16[128,768]{1,0:T(8,128)(2,1)}, bf16[128,768]{1,0:T(8,128)(2,1)S(1)}, u32[]{:S(2)}, u32[]{:S(2)}) collective-permute-start(bf16[128,768]{1,0:T(8,128)(2,1)} %get-tuple-element.109), channel_id=1, source_target_pairs={{0,4},{2,6},{4,0},{6,2},{8,12},{10,14},{12,8},{14,10},{1,5},{3,7},... | collective-permute-start | bytes 589832 | tf_op jit(solution)/shard_map/ppermute | solution.py:397
  81.1 3.2 %collective-permute-start.10 = (bf16[128,768]{1,0:T(8,128)(2,1)}, bf16[128,768]{1,0:T(8,128)(2,1)S(1)}, u32[]{:S(2)}, u32[]{:S(2)}) collective-permute-start(bf16[128,768]{1,0:T(8,128)(2,1)} %get-tuple-element.111), channel_id=1, source_target_pairs={{0,8},{2,10},{4,12},{6,14},{8,0},{10,2},{12,4},{14,6},{1,9},{3,11}... | collective-permute-start | bytes 589832 | tf_op jit(solution)/shard_map/ppermute | solution.py:397
  89.6 12.8 %mix_backward.1 = (bf16[184,768]{1,0:T(8,128)(2,1)}, bf16[184,768]{1,0:T(8,128)(2,1)}, bf16[184,768]{1,0:T(8,128)(2,1)}, bf16[184,768]{1,0:T(8,128)(2,1)}, bf16[...) custom-call(s32[1]{0:T(128)} %bitcast.me_ref, ...), custom_call_target="tpu_custom_call" | custom-call | flops 4831838208 | bytes 17301504 | tf_op jit(solution)/shard_map/mix_backward/pallas_call | solution.py:369
  104.7 3.5 %collective-permute-done.11.refs_5_ = bf16[128,768]{1,0:T(8,128)(2,1)S(1)} collective-permute-done((bf16[128,768]{1,0:T(8,128)(2,1)}, bf16[128,768]{1,0:T(8,128)(2,1)S(1)}, u32[]{:S(2)}, u32[]{:S(2)}) %collective-permute-start.11) | collective-permute-done | bytes 196640 | tf_op jit(solution)/shard_map/ppermute | solution.py:397
  109.6 6.6 %collective-permute-start.22 = (bf16[184,768]{1,0:T(8,128)(2,1)}, bf16[184,768]{1,0:T(8,128)(2,1)S(1)}, u32[]{:S(2)}, u32[]{:S(2)}) collective-permute-start(bf16[184,768]{1,0:T(8,128)(2,1)} %get-tuple-element.134), channel_id=1, source_target_pairs={{0,4},{2,6},{4,0},{6,2},{8,12},{10,14},{12,8},{14,10},{1,5},{3,7},... | collective-permute-start | bytes 847880 | tf_op jit(solution)/shard_map/ppermute | solution.py:397
  122.3 4.7 %collective-permute-done.22.refs_2_ = bf16[184,768]{1,0:T(8,128)(2,1)S(1)} collective-permute-done((bf16[184,768]{1,0:T(8,128)(2,1)}, bf16[184,768]{1,0:T(8,128)(2,1)S(1)}, u32[]{:S(2)}, u32[]{:S(2)}) %collective-permute-start.22) | collective-permute-done | bytes 282656 | tf_op jit(solution)/shard_map/ppermute | solution.py:397
  128.0 3.5 %collective-permute-done.23.refs_3_ = bf16[184,768]{1,0:T(8,128)(2,1)S(1)} collective-permute-done((bf16[184,768]{1,0:T(8,128)(2,1)}, bf16[184,768]{1,0:T(8,128)(2,1)S(1)}, u32[]{:S(2)}, u32[]{:S(2)}) %collective-permute-start.23) | collective-permute-done | bytes 282656 | tf_op jit(solution)/shard_map/ppermute | solution.py:397
  131.5 19.6 %collective-permute-done.24.refs_4_ = bf16[184,768]{1,0:T(8,128)(2,1)S(1)} collective-permute-done((bf16[184,768]{1,0:T(8,128)(2,1)}, bf16[184,768]{1,0:T(8,128)(2,1)S(1)}, u32[]{:S(2)}, u32[]{:S(2)}) %collective-permute-start.24) | collective-permute-done | bytes 282656 | tf_op jit(solution)/shard_map/ppermute | solution.py:397
  151.1 5.6 %collective-permute-done.25.refs_5_ = bf16[184,768]{1,0:T(8,128)(2,1)S(1)} collective-permute-done((bf16[184,768]{1,0:T(8,128)(2,1)}, bf16[184,768]{1,0:T(8,128)(2,1)S(1)}, u32[]{:S(2)}, u32[]{:S(2)}) %collective-permute-start.25) | collective-permute-done | bytes 282656 | tf_op jit(solution)/shard_map/ppermute | solution.py:397
  160.0 4.2 %collective-permute-start.35 = (bf16[56,768]{1,0:T(8,128)(2,1)S(1)}, bf16[56,768]{1,0:T(8,128)(2,1)S(1)}, u32[]{:S(2)}, u32[]{:S(2)}) collective-permute-start(bf16[56,768]{1,0:T(8,128)(2,1)S(1)} %add_convert_fusion.refs_0_), channel_id=1, source_target_pairs={{0,14},{2,12},{4,10},{6,8},{8,6},{10,4},{12,2},{14,0},{1,15},{3,13... | collective-permute-start | bytes 258056 | tf_op jit(solution)/shard_map/ppermute | solution.py:397
  165.3 5.8 %collective-permute-start.33 = (bf16[56,768]{1,0:T(8,128)(2,1)S(1)}, bf16[56,768]{1,0:T(8,128)(2,1)S(1)}, u32[]{:S(2)}, u32[]{:S(2)}) collective-permute-start(bf16[56,768]{1,0:T(8,128)(2,1)S(1)} %add_convert_fusion.refs_0_), channel_id=1, source_target_pairs={{0,10},{2,8},{4,14},{6,12},{8,2},{10,0},{12,6},{14,4},{1,11},{3,9}... | collective-permute-start | bytes 258056 | tf_op jit(solution)/shard_map/ppermute | solution.py:397
  171.1 10.1 %collective-permute-start.32 = (bf16[56,768]{1,0:T(8,128)(2,1)S(1)}, bf16[56,768]{1,0:T(8,128)(2,1)S(1)}, u32[]{:S(2)}, u32[]{:S(2)}) collective-permute-start(bf16[56,768]{1,0:T(8,128)(2,1)S(1)} %add_convert_fusion.refs_0_), channel_id=1, source_target_pairs={{0,8},{2,10},{4,12},{6,14},{8,0},{10,2},{12,4},{14,6},{1,9},{3,11}... | collective-permute-start | bytes 258056 | tf_op jit(solution)/shard_map/ppermute | solution.py:397
  184.8 3.6 %to_cells.2 = bf16[4,2,180,768]{3,2,1,0:T(8,128)(2,1)S(1)} custom-call(s32[1]{0:T(128)} %bitcast.me_ref, bf16[180,128]{1,0:T(8,128)(2,1)S(1)} %copy-done.3, bf16[4,2,180,768]{3,2,1,0:T(8,128)(2,1)} %copy.23.cells_ref.base_ref, bf16[128,768]{1,0:T(8,128)(2,1)} %get-tuple-element.107.refs_0_, bf16[128,768]{1,0:T(8,128)(2,1)} %copy-done.21, ...), custom_call_target="tpu_custom_call" | custom-call | flops 283115520 | bytes 5996544 | tf_op jit(solution)/shard_map/to_cells/pallas_call | solution.py:171
  191.6 3.3 %to_cells.3 = bf16[4,2,180,768]{3,2,1,0:T(8,128)(2,1)S(1)} custom-call(s32[1]{0:T(128)} %bitcast.me_ref, bf16[180,128]{1,0:T(8,128)(2,1)S(1)} %copy-done.2, bf16[4,2,180,768]{3,2,1,0:T(8,128)(2,1)} %copy.20.cells_ref.base_ref, bf16[184,768]{1,0:T(8,128)(2,1)} %get-tuple-element.132.refs_0_, bf16[184,768]{1,0:T(8,128)(2,1)} %copy-done.9, ...), custom_call_target="tpu_custom_call" | custom-call | flops 283115520 | bytes 5996544 | tf_op jit(solution)/shard_map/to_cells/pallas_call | solution.py:171
  (146 shorter events, 49.6 us)
Async XLA Ops:
  12.9 23.8 %collective-permute-start.2 = (bf16[128,768]{1,0:T(8,128)(2,1)}, bf16[128,768]{1,0:T(8,128)(2,1)}, u32[]{:S(2)}, u32[]{:S(2)}) collective-permute-start(bf16[128,768]{1,0:T(8,128)(2,1)} %get-tuple-element.94), channel_id=1, source_target_pairs={{0,6},{2,4},{4,2},{6,0},{8,14},{10,12},{12,10},{14,8},{1,7},{3,5},... | collective-permute-start | bytes 589832 | tf_op jit(solution)/shard_map/ppermute | solution.py:397
  12.9 23.9 %collective-permute-start.3 = (bf16[128,768]{1,0:T(8,128)(2,1)}, bf16[128,768]{1,0:T(8,128)(2,1)}, u32[]{:S(2)}, u32[]{:S(2)}) collective-permute-start(bf16[128,768]{1,0:T(8,128)(2,1)} %get-tuple-element.95), channel_id=1, source_target_pairs={{0,8},{2,10},{4,12},{6,14},{8,0},{10,2},{12,4},{14,6},{1,9},{3,11}... | collective-permute-start | bytes 589832 | tf_op jit(solution)/shard_map/ppermute | solution.py:397
  15.9 28.5 %collective-permute-start.4 = (bf16[128,768]{1,0:T(8,128)(2,1)}, bf16[128,768]{1,0:T(8,128)(2,1)}, u32[]{:S(2)}, u32[]{:S(2)}) collective-permute-start(bf16[128,768]{1,0:T(8,128)(2,1)} %get-tuple-element.96), channel_id=1, source_target_pairs={{0,10},{2,8},{4,14},{6,12},{8,2},{10,0},{12,6},{14,4},{1,11},{3,9}... | collective-permute-start | bytes 589832 | tf_op jit(solution)/shard_map/ppermute | solution.py:397
  17.2 27.2 %collective-permute-start.5 = (bf16[128,768]{1,0:T(8,128)(2,1)}, bf16[128,768]{1,0:T(8,128)(2,1)}, u32[]{:S(2)}, u32[]{:S(2)}) collective-permute-start(bf16[128,768]{1,0:T(8,128)(2,1)} %get-tuple-element.97), channel_id=1, source_target_pairs={{0,12},{2,14},{4,8},{6,10},{8,4},{10,6},{12,0},{14,2},{1,13},{3,15... | collective-permute-start | bytes 589832 | tf_op jit(solution)/shard_map/ppermute | solution.py:397
  27.0 30.6 %collective-permute-start.6 = (bf16[128,768]{1,0:T(8,128)(2,1)}, bf16[128,768]{1,0:T(8,128)(2,1)}, u32[]{:S(2)}, u32[]{:S(2)}) collective-permute-start(bf16[128,768]{1,0:T(8,128)(2,1)} %get-tuple-element.98), channel_id=1, source_target_pairs={{0,14},{2,12},{4,10},{6,8},{8,6},{10,4},{12,2},{14,0},{1,15},{3,13... | collective-permute-start | bytes 589832 | tf_op jit(solution)/shard_map/ppermute | solution.py:397
  36.7 29.2 %collective-permute-start.15 = (bf16[128,768]{1,0:T(8,128)(2,1)}, bf16[128,768]{1,0:T(8,128)(2,1)S(1)}, u32[]{:S(2)}, u32[]{:S(2)}) collective-permute-start(bf16[128,768]{1,0:T(8,128)(2,1)} %get-tuple-element.118), channel_id=1, source_target_pairs={{0,4},{2,6},{4,0},{6,2},{8,12},{10,14},{12,8},{14,10},{1,5},{3,7},... | collective-permute-start | bytes 589832 | tf_op jit(solution)/shard_map/ppermute | solution.py:397
  36.8 29.2 %collective-permute-start.16 = (bf16[128,768]{1,0:T(8,128)(2,1)}, bf16[128,768]{1,0:T(8,128)(2,1)S(1)}, u32[]{:S(2)}, u32[]{:S(2)}) collective-permute-start(bf16[128,768]{1,0:T(8,128)(2,1)} %get-tuple-element.119), channel_id=1, source_target_pairs={{0,6},{2,4},{4,2},{6,0},{8,14},{10,12},{12,10},{14,8},{1,7},{3,5},... | collective-permute-start | bytes 589832 | tf_op jit(solution)/shard_map/ppermute | solution.py:397
  44.4 26.4 %collective-permute-start.17 = (bf16[128,768]{1,0:T(8,128)(2,1)}, bf16[128,768]{1,0:T(8,128)(2,1)S(1)}, u32[]{:S(2)}, u32[]{:S(2)}) collective-permute-start(bf16[128,768]{1,0:T(8,128)(2,1)} %get-tuple-element.120), channel_id=1, source_target_pairs={{0,8},{2,10},{4,12},{6,14},{8,0},{10,2},{12,4},{14,6},{1,9},{3,11}... | collective-permute-start | bytes 589832 | tf_op jit(solution)/shard_map/ppermute | solution.py:397
  44.4 33.7 %collective-permute-start.18 = (bf16[128,768]{1,0:T(8,128)(2,1)}, bf16[128,768]{1,0:T(8,128)(2,1)S(1)}, u32[]{:S(2)}, u32[]{:S(2)}) collective-permute-start(bf16[128,768]{1,0:T(8,128)(2,1)} %get-tuple-element.121), channel_id=1, source_target_pairs={{0,10},{2,8},{4,14},{6,12},{8,2},{10,0},{12,6},{14,4},{1,11},{3,9}... | collective-permute-start | bytes 589832 | tf_op jit(solution)/shard_map/ppermute | solution.py:397
  66.0 21.2 %collective-permute-start.20 = (bf16[128,768]{1,0:T(8,128)(2,1)S(1)}, bf16[128,768]{1,0:T(8,128)(2,1)S(1)}, u32[]{:S(2)}, u32[]{:S(2)}) collective-permute-start(bf16[128,768]{1,0:T(8,128)(2,1)S(1)} %copy-done.30), channel_id=1, source_target_pairs={{0,14},{2,12},{4,10},{6,8},{8,6},{10,4},{12,2},{14,0},{1,15},{3,13... | collective-permute-start | bytes 589832 | tf_op jit(solution)/shard_map/ppermute | solution.py:397
  70.8 31.6 %collective-permute-start.8 = (bf16[128,768]{1,0:T(8,128)(2,1)}, bf16[128,768]{1,0:T(8,128)(2,1)S(1)}, u32[]{:S(2)}, u32[]{:S(2)}) collective-permute-start(bf16[128,768]{1,0:T(8,128)(2,1)} %get-tuple-element.109), channel_id=1, source_target_pairs={{0,4},{2,6},{4,0},{6,2},{8,12},{10,14},{12,8},{14,10},{1,5},{3,7},... | collective-permute-start | bytes 589832 | tf_op jit(solution)/shard_map/ppermute | solution.py:397
  78.1 24.3 %collective-permute-start.9 = (bf16[128,768]{1,0:T(8,128)(2,1)}, bf16[128,768]{1,0:T(8,128)(2,1)S(1)}, u32[]{:S(2)}, u32[]{:S(2)}) collective-permute-start(bf16[128,768]{1,0:T(8,128)(2,1)} %get-tuple-element.110), channel_id=1, source_target_pairs={{0,6},{2,4},{4,2},{6,0},{8,14},{10,12},{12,10},{14,8},{1,7},{3,5},... | collective-permute-start | bytes 589832 | tf_op jit(solution)/shard_map/ppermute | solution.py:397
  81.1 23.6 %collective-permute-start.10 = (bf16[128,768]{1,0:T(8,128)(2,1)}, bf16[128,768]{1,0:T(8,128)(2,1)S(1)}, u32[]{:S(2)}, u32[]{:S(2)}) collective-permute-start(bf16[128,768]{1,0:T(8,128)(2,1)} %get-tuple-element.111), channel_id=1, source_target_pairs={{0,8},{2,10},{4,12},{6,14},{8,0},{10,2},{12,4},{14,6},{1,9},{3,11}... | collective-permute-start | bytes 589832 | tf_op jit(solution)/shard_map/ppermute | solution.py:397
  84.3 23.9 %collective-permute-start.11 = (bf16[128,768]{1,0:T(8,128)(2,1)}, bf16[128,768]{1,0:T(8,128)(2,1)S(1)}, u32[]{:S(2)}, u32[]{:S(2)}) collective-permute-start(bf16[128,768]{1,0:T(8,128)(2,1)} %get-tuple-element.112), channel_id=1, source_target_pairs={{0,10},{2,8},{4,14},{6,12},{8,2},{10,0},{12,6},{14,4},{1,11},{3,9}... | collective-permute-start | bytes 589832 | tf_op jit(solution)/shard_map/ppermute | solution.py:397
  87.3 20.9 %collective-permute-start.12 = (bf16[128,768]{1,0:T(8,128)(2,1)}, bf16[128,768]{1,0:T(8,128)(2,1)S(1)}, u32[]{:S(2)}, u32[]{:S(2)}) collective-permute-start(bf16[128,768]{1,0:T(8,128)(2,1)} %get-tuple-element.113), channel_id=1, source_target_pairs={{0,12},{2,14},{4,8},{6,10},{8,4},{10,6},{12,0},{14,2},{1,13},{3,15... | collective-permute-start | bytes 589832 | tf_op jit(solution)/shard_map/ppermute | solution.py:397
  117.5 33.5 %collective-permute-start.24 = (bf16[184,768]{1,0:T(8,128)(2,1)}, bf16[184,768]{1,0:T(8,128)(2,1)S(1)}, u32[]{:S(2)}, u32[]{:S(2)}) collective-permute-start(bf16[184,768]{1,0:T(8,128)(2,1)} %get-tuple-element.136), channel_id=1, source_target_pairs={{0,8},{2,10},{4,12},{6,14},{8,0},{10,2},{12,4},{14,6},{1,9},{3,11}... | collective-permute-start | bytes 847880 | tf_op jit(solution)/shard_map/ppermute | solution.py:397
  119.5 37.1 %collective-permute-start.25 = (bf16[184,768]{1,0:T(8,128)(2,1)}, bf16[184,768]{1,0:T(8,128)(2,1)S(1)}, u32[]{:S(2)}, u32[]{:S(2)}) collective-permute-start(bf16[184,768]{1,0:T(8,128)(2,1)} %get-tuple-element.137), channel_id=1, source_target_pairs={{0,10},{2,8},{4,14},{6,12},{8,2},{10,0},{12,6},{14,4},{1,11},{3,9}... | collective-permute-start | bytes 847880 | tf_op jit(solution)/shard_map/ppermute | solution.py:397
  120.5 36.2 %collective-permute-start.26 = (bf16[184,768]{1,0:T(8,128)(2,1)}, bf16[184,768]{1,0:T(8,128)(2,1)S(1)}, u32[]{:S(2)}, u32[]{:S(2)}) collective-permute-start(bf16[184,768]{1,0:T(8,128)(2,1)} %get-tuple-element.138), channel_id=1, source_target_pairs={{0,12},{2,14},{4,8},{6,10},{8,4},{10,6},{12,0},{14,2},{1,13},{3,15... | collective-permute-start | bytes 847880 | tf_op jit(solution)/shard_map/ppermute | solution.py:397
  127.1 29.6 %collective-permute-start.27 = (bf16[184,768]{1,0:T(8,128)(2,1)}, bf16[184,768]{1,0:T(8,128)(2,1)S(1)}, u32[]{:S(2)}, u32[]{:S(2)}) collective-permute-start(bf16[184,768]{1,0:T(8,128)(2,1)} %get-tuple-element.139), channel_id=1, source_target_pairs={{0,14},{2,12},{4,10},{6,8},{8,6},{10,4},{12,2},{14,0},{1,15},{3,13... | collective-permute-start | bytes 847880 | tf_op jit(solution)/shard_map/ppermute | solution.py:397
  159.4 21.9 %collective-permute-start.13 = (bf16[128,768]{1,0:T(8,128)(2,1)S(1)}, bf16[128,768]{1,0:T(8,128)(2,1)S(1)}, u32[]{:S(2)}, u32[]{:S(2)}) collective-permute-start(bf16[128,768]{1,0:T(8,128)(2,1)S(1)} %copy-done.25), channel_id=1, source_target_pairs={{0,14},{2,12},{4,10},{6,8},{8,6},{10,4},{12,2},{14,0},{1,15},{3,13... | collective-permute-start | bytes 589832 | tf_op jit(solution)/shard_map/ppermute | solution.py:397
  160.0 21.3 %collective-permute-start.35 = (bf16[56,768]{1,0:T(8,128)(2,1)S(1)}, bf16[56,768]{1,0:T(8,128)(2,1)S(1)}, u32[]{:S(2)}, u32[]{:S(2)}) collective-permute-start(bf16[56,768]{1,0:T(8,128)(2,1)S(1)} %add_convert_fusion.refs_0_), channel_id=1, source_target_pairs={{0,14},{2,12},{4,10},{6,8},{8,6},{10,4},{12,2},{14,0},{1,15},{3,13... | collective-permute-start | bytes 258056 | tf_op jit(solution)/shard_map/ppermute | solution.py:397
  164.2 18.9 %collective-permute-start.34 = (bf16[56,768]{1,0:T(8,128)(2,1)S(1)}, bf16[56,768]{1,0:T(8,128)(2,1)S(1)}, u32[]{:S(2)}, u32[]{:S(2)}) collective-permute-start(bf16[56,768]{1,0:T(8,128)(2,1)S(1)} %add_convert_fusion.refs_0_), channel_id=1, source_target_pairs={{0,12},{2,14},{4,8},{6,10},{8,4},{10,6},{12,0},{14,2},{1,13},{3,15... | collective-permute-start | bytes 258056 | tf_op jit(solution)/shard_map/ppermute | solution.py:397
  165.3 32.8 %collective-permute-start.33 = (bf16[56,768]{1,0:T(8,128)(2,1)S(1)}, bf16[56,768]{1,0:T(8,128)(2,1)S(1)}, u32[]{:S(2)}, u32[]{:S(2)}) collective-permute-start(bf16[56,768]{1,0:T(8,128)(2,1)S(1)} %add_convert_fusion.refs_0_), channel_id=1, source_target_pairs={{0,10},{2,8},{4,14},{6,12},{8,2},{10,0},{12,6},{14,4},{1,11},{3,9}... | collective-permute-start | bytes 258056 | tf_op jit(solution)/shard_map/ppermute | solution.py:397
  171.1 26.9 %collective-permute-start.32 = (bf16[56,768]{1,0:T(8,128)(2,1)S(1)}, bf16[56,768]{1,0:T(8,128)(2,1)S(1)}, u32[]{:S(2)}, u32[]{:S(2)}) collective-permute-start(bf16[56,768]{1,0:T(8,128)(2,1)S(1)} %add_convert_fusion.refs_0_), channel_id=1, source_target_pairs={{0,8},{2,10},{4,12},{6,14},{8,0},{10,2},{12,4},{14,6},{1,9},{3,11}... | collective-permute-start | bytes 258056 | tf_op jit(solution)/shard_map/ppermute | solution.py:397
  (51 other events, 1410.9 us)

commit v7 on v6

--- a/solution.py
+++ b/solution.py
@@ -148,33 +148,42 @@
             transcendentals=0,
         ),
         name="to_modes",
-    )(me, table, *hbm(cells))
+    )(me, table, cells)
 
 
 def to_cells_kernel(me_ref, table_ref, base_ref, *refs):
     modes_refs, out_ref, held_ref = refs[:-2], refs[-2], refs[-1]
     rows = base_ref.shape[1]
-    share = modes_refs[0].shape[0] // rows
+    share = modes_refs[0].shape[-2] // rows
     for row in range(rows):
-        for offset, modes_ref in enumerate(modes_refs):
-            spot = place_of(me_ref, offset, share)
-            held_ref[row, spot] = modes_ref[pl.ds(row * share, share)]
-        image = product_of(table_ref[...], held_ref[row])
+        run = pl.ds(row * share, share)
+        if len(modes_refs) == 1:
+            spectrum = modes_refs[0][:, run].reshape(held_ref.shape[1:])
+        else:
+            for offset, modes_ref in enumerate(modes_refs):
+                held_ref[row, place_of(me_ref, offset, share)] = modes_ref[run]
+            spectrum = held_ref[row]
+        image = product_of(table_ref[...], spectrum)
         out_ref[0, row] = (base_ref[0, row].astype(jnp.float32) + image).astype(jnp.bfloat16)
 
 
 def to_cells(me, table, modes, base):
     samples, rows, width, channels = base.shape
     size = table.shape[1]
-    part = rows * size // len(modes)
     block = pl.BlockSpec((1, rows, width, channels), lambda b, _: (b, 0, 0, 0))
+    if len(modes) == 1:
+        lead = modes[0].shape[0]
+        part = rows * size // lead
+        specs = [pl.BlockSpec((lead, part, channels), lambda b, _: (0, b, 0))]
+    else:
+        part = rows * size // len(modes)
+        specs = [pl.BlockSpec((part, channels), lambda b, _: (b, 0))] * len(modes)
     return pl.pallas_call(
         to_cells_kernel,
         grid_spec=pltpu.PrefetchScalarGridSpec(
             num_scalar_prefetch=1,
             grid=(samples,),
-            in_specs=[pl.BlockSpec((width, size), lambda b, _: (0, 0)), block]
-            + [pl.BlockSpec((part, channels), lambda b, _: (b, 0))] * len(modes),
+            in_specs=[pl.BlockSpec((width, size), lambda b, _: (0, 0)), block] + specs,
             out_specs=block,
             scratch_shapes=[pltpu.VMEM((rows, size, channels), jnp.bfloat16)],
         ),
@@ -186,7 +195,7 @@
             transcendentals=0,
         ),
         name="to_cells",
-    )(me, table, *hbm(base, *modes))
+    )(me, table, base, *hbm(*modes))
 
 
 def sigmoid_of(values):
@@ -214,10 +223,16 @@
         joined = jnp.concatenate(
             [mixed_ref[spot, 0:width], mixed_ref[spot, width : 2 * width]], axis=0
         )
-        band_ref[sample] = product_of(table_ref[...], joined).astype(jnp.bfloat16)
-        for offset, bands_ref in enumerate(bands_refs):
-            place = place_of(me_ref, offset, part)
-            bands_ref[pl.ds(sample * part, part)] = band_ref[sample, place]
+        bands = product_of(table_ref[...], joined).astype(jnp.bfloat16)
+        if len(bands_refs) == 1:
+            lead = bands_refs[0].shape[0]
+            run = pl.ds(sample * size // lead, size // lead)
+            bands_refs[0][:, run] = bands.reshape(lead, size // lead, width)
+        else:
+            band_ref[sample] = bands
+            for offset, bands_ref in enumerate(bands_refs):
+                place = place_of(me_ref, offset, part)
+                bands_ref[pl.ds(sample * part, part)] = band_ref[sample, place]
 
 
 def activate(mixed_ref, w1_ref, b1_ref):
@@ -231,9 +246,9 @@
     return out, jnp.tanh(out * (1.0 / shrink_level))
 
 
-def forward_kernel(owners, me_ref, lat_ref, unlat_ref, w1_ref, b1_ref, w2_ref, b2_ref, *refs):
-    bands_refs, image_refs = refs[:owners], refs[owners : 2 * owners]
-    mixed_ref, act_ref, band_ref = refs[2 * owners :]
+def forward_kernel(blocks, me_ref, lat_ref, unlat_ref, w1_ref, b1_ref, w2_ref, b2_ref, *refs):
+    bands_refs, image_refs = refs[:blocks], refs[blocks : 2 * blocks]
+    mixed_ref, act_ref, band_ref = refs[2 * blocks :]
     mix_lat(me_ref, lat_ref, bands_refs, band_ref, mixed_ref.at[0])
     act_ref[...] = activate(mixed_ref, w1_ref, b1_ref)[1].astype(jnp.bfloat16)
     out, bent = bend(act_ref, w2_ref, b2_ref)
@@ -242,11 +257,10 @@
 
 
 def backward_kernel(
-    block_size, owners, me_ref, lat_ref, unlat_ref, w1_ref, b1_ref, w2_ref, b2_ref, mixed_ref, *refs
+    block_size, blocks, me_ref, lat_ref, unlat_ref, w1_ref, b1_ref, w2_ref, b2_ref, mixed_ref, *refs
 ):
-    bands_refs, image_refs = refs[:owners], refs[owners : 2 * owners]
-    sums_ref, act_ref, gate_ref, cot_ref, kept_ref, band_ref = refs[2 * owners :]
-    size_of_image = band_ref.shape[0] * band_ref.shape[1] // owners
+    bands_refs, image_ref = refs[:blocks], refs[blocks]
+    sums_ref, act_ref, gate_ref, cot_ref, kept_ref, band_ref = refs[blocks + 1 :]
     transposed = (((1,), (1,)), ((), ()))
     summed = (((0,), (0,)), ((), ()))
 
@@ -282,17 +296,7 @@
     weight_sums(act_ref[...], kept_ref[...], 1)
     kept_ref[...] = times(cot_ref[...], w1_ref[0], transposed).astype(jnp.bfloat16)
     weight_sums(mixed_ref[0], cot_ref[...], 0)
-    unmix_lat(me_ref, unlat_ref, kept_ref, band_ref, image_refs)
-    share = image_refs[0].shape[0] - size_of_image
-    if share > 0:
-        runs = sums_ref.shape[2] // share
-        for offset, image_ref in enumerate(image_refs):
-            owner = me_ref[0] ^ offset
-            pair, run = owner // runs, owner % runs
-            rows = pl.ds(pl.multiple_of(run * share, share), share)
-            image_ref[pl.ds(size_of_image, share)] = sums_ref[pair // 2, pair % 2, rows].astype(
-                jnp.bfloat16
-            )
+    unmix_lat(me_ref, unlat_ref, kept_ref, band_ref, [image_ref])
 
 
 def group_spec(*shape):
@@ -302,6 +306,11 @@
 def bands_specs(rows, bands, groups):
     block = (rows, bands[0].shape[1] // groups)
     return (pl.BlockSpec(block, lambda g, *_: (0, g)),) * len(bands)
+
+
+def stacked(lead, rows, groups, width):
+    shape = in_hbm((lead, rows // lead, groups * width), jnp.bfloat16)
+    return (shape,), (pl.BlockSpec((lead, rows // lead, width), lambda g, *_: (0, 0, g)),)
 
 
 def forward_mid(me, lat, unlat, bands, w1, b1, w2, b2):
@@ -312,6 +321,11 @@
     table = pl.BlockSpec((size, size), lambda g, _: (0, 0))
     state = (groups, positions, lanes)
     specs = bands_specs(bands[0].shape[0], bands, groups)
+    if len(bands) == 1:
+        images, image_specs = stacked(1, samples * size, groups, lanes // 2)
+    else:
+        images = tuple(in_hbm(band.shape, band.dtype) for band in bands)
+        image_specs = specs
     results = pl.pallas_call(
         functools.partial(forward_kernel, len(bands)),
         grid_spec=pltpu.PrefetchScalarGridSpec(
@@ -323,14 +337,13 @@
                 group_spec(lanes, lanes), group_spec(1, lanes),
                 *specs,
             ],
-            out_specs=specs + (group_spec(positions, lanes),),
+            out_specs=image_specs + (group_spec(positions, lanes),),
             scratch_shapes=[
                 pltpu.VMEM((positions, lanes), jnp.bfloat16),
                 pltpu.VMEM((samples, size, lanes // 2), jnp.bfloat16),
             ],
         ),
-        out_shape=tuple(in_hbm(band.shape, band.dtype) for band in bands)
-        + (in_hbm(state, jnp.bfloat16),),
+        out_shape=images + (in_hbm(state, jnp.bfloat16),),
         compiler_params=params(28),
         cost_estimate=pl.CostEstimate(
             flops=4 * groups * positions * lanes * lanes,
@@ -342,31 +355,16 @@
     return results[: len(bands)], results[len(bands)]
 
 
-def backward_mid(me, lat, unlat, bands, w1, b1, w2, b2, state, count, share):
+def backward_mid(me, lat, unlat, bands, w1, b1, w2, b2, state, count):
     groups, lanes, _ = w1.shape
     size = lat.shape[0]
-    image_rows = bands[0].shape[0]
-    samples = image_rows * len(bands) // size
+    samples = bands[0].shape[0] * len(bands) // size
     positions = samples * size // 2
     table = pl.BlockSpec((size, size), lambda g, _: (0, 0))
     size_of_block = lanes // 2 // (count // groups)
-    rows = size_of_block + 16
-    sums = (2, 2, rows, lanes // 2)
-    out_shape = (in_hbm((image_rows + share, bands[0].shape[1]), jnp.bfloat16),) * len(bands)
-    out_specs = bands_specs(image_rows + share, bands, groups)
-    scratch_shapes = [
-        pltpu.VMEM((positions, lanes), jnp.bfloat16),
-        pltpu.VMEM((positions, lanes), jnp.float32),
-        pltpu.VMEM((positions, lanes), jnp.bfloat16),
-        pltpu.VMEM((positions, lanes), jnp.bfloat16),
-        pltpu.VMEM((samples, size, lanes // 2), jnp.bfloat16),
-    ]
-    if share > 0:
-        scratch_shapes = [pltpu.VMEM(sums, jnp.float32)] + scratch_shapes
-    else:
-        out_shape += (jax.ShapeDtypeStruct(sums[:3] + (groups * sums[3],), jnp.float32),)
-        out_specs += (pl.BlockSpec(sums, lambda g, _: (0, 0, 0, g)),)
-    results = pl.pallas_call(
+    sums = (2, 2, size_of_block + 32, lanes // 2)
+    image, image_specs = stacked(len(bands), samples * size, groups, lanes // 2)
+    return pl.pallas_call(
         functools.partial(backward_kernel, size_of_block, len(bands)),
         grid_spec=pltpu.PrefetchScalarGridSpec(
             num_scalar_prefetch=1,
@@ -375,12 +373,19 @@
                 table, table,
                 group_spec(lanes, lanes), group_spec(1, lanes),
                 group_spec(lanes, lanes), group_spec(1, lanes),
-                group_spec(positions, lanes), *bands_specs(image_rows, bands, groups),
+                group_spec(positions, lanes),
+                *bands_specs(bands[0].shape[0], bands, groups),
             ],
-            out_specs=out_specs,
-            scratch_shapes=scratch_shapes,
-        ),
-        out_shape=out_shape,
+            out_specs=image_specs + (pl.BlockSpec(sums, lambda g, _: (0, 0, 0, g)),),
+            scratch_shapes=[
+                pltpu.VMEM((positions, lanes), jnp.bfloat16),
+                pltpu.VMEM((positions, lanes), jnp.float32),
+                pltpu.VMEM((positions, lanes), jnp.bfloat16),
+                pltpu.VMEM((positions, lanes), jnp.bfloat16),
+                pltpu.VMEM((samples, size, lanes // 2), jnp.bfloat16),
+            ],
+        ),
+        out_shape=image + (in_hbm(sums[:3] + (groups * sums[3],), jnp.float32),),
         compiler_params=params(32),
         cost_estimate=pl.CostEstimate(
             flops=8 * groups * positions * lanes * lanes,
@@ -389,7 +394,6 @@
         ),
         name="mix_backward",
     )(me, lat, unlat, *hbm(w1), b1, *hbm(w2), b2, *hbm(state, *bands))
-    return results[: len(bands)], results[len(bands) :]
 
 
 def swap_with(values, axis, distance):
@@ -408,19 +412,56 @@
     return order
 
 
-def finish_kernel(factor, me_ref, *refs):
-    shares_refs, out_refs = refs[:-5], refs[-5:-1]
-    held_ref = refs[-1]
-    run = shares_refs[0].shape[0]
-    for offset, shares_ref in enumerate(shares_refs):
-        held_ref[me_ref[0] ^ offset] = shares_ref[...].astype(jnp.float32) * factor
-    runs = len(shares_refs) // 4
+def pick(pair, side):
+    return lax.dynamic_index_in_dim(pair, side, 0, keepdims=False)
+
+
+class GroupSum:
+    def __init__(self, sums):
+        self.lanes = sums.shape[-1]
+        self.side = lax.axis_index("dp")
+        self.me = lax.axis_index("space")
+        self.count = lax.axis_size("space") // 2
+        self.held = sums.reshape(-1, self.lanes)
+
+    def halve(self, axis, distance, bit):
+        pair = self.held.reshape(2, -1, self.lanes)
+        given = pick(pair, 1 - bit)
+        self.held = pick(pair, bit) + swap_with(given, axis, distance)
+
+    def scatter(self, arrived):
+        self.halve("dp", 1, self.side)
+        if len(arrived) > 0:
+            self.held, _ = lax.optimization_barrier((self.held, tuple(arrived)))
+        self.halve("space", 1, self.me % 2)
+        shares = self.held.reshape(self.count, -1, self.lanes)
+        place = self.me // 2
+        total = pick(shares, place)
+        for offset in range(1, self.count):
+            given = pick(shares, place ^ offset).astype(jnp.bfloat16)
+            total += swap_with(given, "space", 2 * offset).astype(jnp.float32)
+        self.total = total.astype(jnp.bfloat16)
+
+    def gather(self):
+        taken = [self.total]
+        for offset in range(1, self.count):
+            taken.append(swap_with(self.total, "space", 2 * offset))
+        quarter = jnp.stack(taken)
+        half = jnp.stack([quarter, swap_with(quarter, "space", 1)])
+        return half, swap_with(half, "dp", 1)
+
+
+def finish_kernel(factor, me_ref, half_ref, other_ref, *out_refs):
+    side, near, place = me_ref[0], me_ref[1], me_ref[2]
+    run = half_ref.shape[2]
     for which in range(2):
         blocks_ref, bias_ref = out_refs[2 * which : 2 * which + 2]
         edge = blocks_ref.shape[-1]
         for part in range(2):
-            for piece in range(runs):
-                value = held_ref[(2 * which + part) * runs + piece]
+            for piece in range(half_ref.shape[1]):
+                spot = (part ^ near, piece ^ place)
+                own = half_ref[spot].astype(jnp.float32)
+                value = jnp.where(side == which, own, other_ref[spot].astype(jnp.float32)) * factor
                 first = piece * run
                 count = max(0, min(edge - first, run))
                 for block in range(blocks_ref.shape[1]):
@@ -432,19 +473,18 @@
                         bias_ref[part, pl.ds(block, 1)] = value[row : row + 1, lanes]
 
 
-def finish_sums(me, shares, factor, weight_shape, bias_shape):
+def finish_sums(here, half, other, factor, weight_shape, bias_shape):
     outs = [weight_shape, bias_shape] * 2
     return pl.pallas_call(
         functools.partial(finish_kernel, factor),
         out_shape=[jax.ShapeDtypeStruct(shape, jnp.float32) for shape in outs],
         in_specs=[pl.BlockSpec(memory_space=pltpu.SMEM)]
-        + [pl.BlockSpec(memory_space=pltpu.VMEM)] * len(shares),
+        + [pl.BlockSpec(memory_space=pltpu.VMEM)] * 2,
         out_specs=[pl.BlockSpec(memory_space=pltpu.VMEM)] * 4,
-        scratch_shapes=[pltpu.VMEM((len(shares),) + shares[0].shape, jnp.float32)],
         compiler_params=pltpu.CompilerParams(vmem_limit_bytes=16 * MIB),
         cost_estimate=pl.CostEstimate(flops=0, bytes_accessed=4 * MIB, transcendentals=0),
         name="finish_sums",
-    )(me, *shares)
+    )(here, half, other)
 
 
 def body(fields, cotangent, w_first, b_first, w_second, b_second):
@@ -470,11 +510,13 @@
         arrived = lax.all_to_all(spectrum, "space", split_axis=0, concat_axis=0, tiled=True)
         return [jnp.transpose(arrived, (1, 0, 2, 3, 4)).reshape(-1, channels)]
 
-    def send_back(blocks):
-        bands = blocks[0].reshape(samples, owners, rows, 2 * modes, channels)
+    def send_back(bands):
+        if direct:
+            return [lax.all_to_all(bands, "space", split_axis=0, concat_axis=0, tiled=True)]
+        bands = bands.reshape(samples, owners, rows, 2 * modes, channels)
         bands = jnp.transpose(bands, (1, 0, 2, 3, 4))
         arrived = lax.all_to_all(bands, "space", split_axis=0, concat_axis=0, tiled=True)
-        return [jnp.transpose(arrived, (1, 2, 0, 3, 4)).reshape(-1, channels)]
+        return [jnp.transpose(arrived, (1, 2, 0, 3, 4)).reshape(1, -1, channels)]
 
     me = lax.axis_index("space") if direct else 0
     me = jnp.full((1,), me, jnp.int32)
@@ -498,28 +540,30 @@
         for offset, block in zip(order[FIRST:], late):
             cot_spec[offset] = block
     cot_gathered = send_out(cot_spec)
-    image_band = send_out(image) if direct else send_back(image)
-    share = 4 * (edge + 16) // owners if direct else 0
-    grad_image, rest = backward_mid(
-        me, lat, lat.T, cot_gathered, w1, b1, w2, b2, state, count, share
+    image_band = send_out(image) if direct else send_back(image[0])
+    grad_image, sums = backward_mid(
+        me, lat, lat.T, cot_gathered, w1, b1, w2, b2, state, count
     )
+    late = []
+    if direct:
+        early = tuple(image_band[offset] for offset in order[:HELD])
+        late = [image_band[offset] for offset in order[HELD:]]
+        grad_image, sums, _ = lax.optimization_barrier((grad_image, sums, early))
+    grad_band = send_back(grad_image)
+    output = to_cells(me, scaled.T, image_band, fields)
+    grad_fields = to_cells(me, plain.T, grad_band, cotangent)
+
     positions = samples * lax.axis_size("dp") * lat_total * KW
     factor = 1.0 / math.sqrt(positions)
     if direct:
-        early = tuple(image_band[offset] for offset in order[:HELD])
-        grad_image, _ = lax.optimization_barrier((grad_image, early))
-        grad_band = send_out(grad_image)
-    else:
-        grad_band = send_back(grad_image)
-    output = to_cells(me, scaled.T, image_band, fields)
-    grad_fields = to_cells(me, plain.T, grad_band, cotangent)
-
-    if direct:
-        total = sum(band[-share:].astype(jnp.float32) for band in grad_band)
-        total = (total + swap_with(total, "dp", 1)).astype(jnp.bfloat16)
-        grads = finish_sums(me, send_out([total] * owners), factor, w_first.shape, b_first.shape)
+        group_sum = GroupSum(sums)
+        group_sum.scatter(late)
+        half, other = group_sum.gather()
+        place = lax.axis_index("space")
+        here = jnp.stack([lax.axis_index("dp"), place % 2, place // 2]).astype(jnp.int32)
+        grads = finish_sums(here, half, other, factor, w_first.shape, b_first.shape)
         return (output, grad_fields) + tuple(grads)
-    sums = lax.psum(rest[0], ("space", "dp")) * factor
+    sums = lax.psum(sums, ("space", "dp")) * factor
     grads = []
     for which in range(2):
         blocks = sums[which, :, :edge].reshape(2, edge, count, edge)

time: 200 us -> 210 us (1.050)
  waiting for transfers between devices: 49.1 us -> 65 us
  starting transfers between devices: 96.7 us -> 91 us
  Pallas kernels: 40.2 us -> 35.7 us
  local copies, waits for them, and re-layouts: 11.5 us -> 13.7 us
    ppermute x36 -> x31, waiting for transfers between devices: 49.1 us -> 65 us  [swap_with(): return lax.ppermute(values, axis, pairs)]
    ppermute x36 -> x31, starting transfers between devices: 96.7 us -> 80.7 us  [swap_with(): return lax.ppermute(values, axis, pairs)]
    all_to_all x0 -> x1, starting transfers between devices: none -> 10.3 us  [send_back(): lax.all_to_all(bands, 'space', split_axis=0, concat_axis=0, tiled=True)]
    pallas_call x2, Pallas kernels: 8.55 us -> 4.73 us  [to_modes(): pl.pallas_call(to_modes_kernel, grid_spec=pltpu.PrefetchScalarGridSpec(nu...]
    unnamed x81 -> x57, local copies, waits for them, and re-layouts: 9.62 us -> 10.5 us
  transfers between devices with their start and end apart: 36 -> 32, of which waited for: 8 -> 12; matrix products, arithmetic and copies ran while one was open for 4% -> 4% of each run, Pallas kernels for 17% -> 15%
where the time goes in v7:
time: 210 us; the launch traced here: 209 us
  starting transfers between devices  91 us (43%)
  waiting for transfers between devices  65 us (31%)
  Pallas kernels  35.7 us (17%)
  local copies, waits for them, and re-layouts  13.7 us (7%)
  other arithmetic  2.67 us (1%)
    ppermute x31, starting transfers between devices, swap_with(): return lax.ppermute(values, axis, pairs)  80.7 us
    ppermute x31, waiting for transfers between devices, swap_with(): return lax.ppermute(values, axis, pairs)  65 us
    pallas_call x1, Pallas kernels, backward_mid(): pl.pallas_call(functools.partial(backward_kernel, size_of_block, len(band...  12.6 us
    unnamed x57, local copies, waits for them, and re-layouts  10.5 us
    all_to_all x1, starting transfers between devices, send_back(): lax.all_to_all(bands, 'space', split_axis=0, concat_axis=0, tiled=True)  10.3 us
    pallas_call x1, Pallas kernels, forward_mid(): pl.pallas_call(functools.partial(forward_kernel, len(bands)), grid_spec=p...  7.61 us
    pallas_call x2, Pallas kernels, to_cells(): pl.pallas_call(to_cells_kernel, grid_spec=pltpu.PrefetchScalarGridSpec(nu...  5.98 us
    pallas_call x2, Pallas kernels, to_modes(): pl.pallas_call(to_modes_kernel, grid_spec=pltpu.PrefetchScalarGridSpec(nu...  4.73 us
  transfers between devices with their start and end apart: 32, of which 12 were waited for; matrix products, arithmetic and copies ran while one was open for 4% of the time, Pallas kernels for 15%

profile of v7, /device:TPU:0, one launch (start us, length us, event | category | flops | bytes accessed | tf_op | source)
XLA Modules:
  0.0 209.3 jit_solution(14451618963466173750)
XLA Ops:
  5.0 3.0 %collective-permute-start = (bf16[128,768]{1,0:T(8,128)(2,1)}, bf16[128,768]{1,0:T(8,128)(2,1)}, u32[]{:S(2)}, u32[]{:S(2)}) collective-permute-start(bf16[128,768]{1,0:T(8,128)(2,1)} %get-tuple-element.81), channel_id=1, source_target_pairs={{0,2},{2,0},{4,6},{6,4},{8,10},{10,8},{12,14},{14,12},{1,3},{3,1},... | collective-permute-start | bytes 589832 | tf_op jit(solution)/shard_map/ppermute | solution.py:401
  13.9 3.6 %collective-permute-start.5 = (bf16[128,768]{1,0:T(8,128)(2,1)}, bf16[128,768]{1,0:T(8,128)(2,1)}, u32[]{:S(2)}, u32[]{:S(2)}) collective-permute-start(bf16[128,768]{1,0:T(8,128)(2,1)} %get-tuple-element.86), channel_id=1, source_target_pairs={{0,12},{2,14},{4,8},{6,10},{8,4},{10,6},{12,0},{14,2},{1,13},{3,15... | collective-permute-start | bytes 589832 | tf_op jit(solution)/shard_map/ppermute | solution.py:401
  17.5 6.3 %collective-permute-done.1.refs_2_ = bf16[128,768]{1,0:T(8,128)(2,1)} collective-permute-done((bf16[128,768]{1,0:T(8,128)(2,1)}, bf16[128,768]{1,0:T(8,128)(2,1)}, u32[]{:S(2)}, u32[]{:S(2)}) %collective-permute-start.1) | collective-permute-done | bytes 196640 | tf_op jit(solution)/shard_map/ppermute | solution.py:401
  33.3 4.0 %collective-permute-start.16 = (bf16[128,768]{1,0:T(8,128)(2,1)}, bf16[128,768]{1,0:T(8,128)(2,1)S(1)}, u32[]{:S(2)}, u32[]{:S(2)}) collective-permute-start(bf16[128,768]{1,0:T(8,128)(2,1)} %get-tuple-element.108), channel_id=1, source_target_pairs={{0,6},{2,4},{4,2},{6,0},{8,14},{10,12},{12,10},{14,8},{1,7},{3,5},... | collective-permute-start | bytes 589832 | tf_op jit(solution)/shard_map/ppermute | solution.py:401
  37.2 3.9 %collective-permute-done.4.refs_5_ = bf16[128,768]{1,0:T(8,128)(2,1)} collective-permute-done((bf16[128,768]{1,0:T(8,128)(2,1)}, bf16[128,768]{1,0:T(8,128)(2,1)}, u32[]{:S(2)}, u32[]{:S(2)}) %collective-permute-start.4) | collective-permute-done | bytes 196640 | tf_op jit(solution)/shard_map/ppermute | solution.py:401
  41.1 13.2 %collective-permute-start.18 = (bf16[128,768]{1,0:T(8,128)(2,1)}, bf16[128,768]{1,0:T(8,128)(2,1)}, u32[]{:S(2)}, u32[]{:S(2)}) collective-permute-start(bf16[128,768]{1,0:T(8,128)(2,1)} %get-tuple-element.110), channel_id=1, source_target_pairs={{0,10},{2,8},{4,14},{6,12},{8,2},{10,0},{12,6},{14,4},{1,11},{3,9}... | collective-permute-start | bytes 589832 | tf_op jit(solution)/shard_map/ppermute | solution.py:401
  54.4 7.6 %mix_forward.1 = (bf16[128,768]{1,0:T(8,128)(2,1)}, bf16[128,768]{1,0:T(8,128)(2,1)}, bf16[128,768]{1,0:T(8,128)(2,1)}, bf16[128,768]{1,0:T(8,128)(2,1)}, bf16[1...) custom-call(s32[1]{0:T(128)} %bitcast.me_ref, ...), custom_call_target="tpu_custom_call" | custom-call | flops 2415919104 | bytes 17301504 | tf_op jit(solution)/shard_map/mix_forward/pallas_call | solution.py:329
  62.7 4.8 %collective-permute-start.20 = (bf16[128,768]{1,0:T(8,128)(2,1)S(1)}, bf16[128,768]{1,0:T(8,128)(2,1)}, u32[]{:S(2)}, u32[]{:S(2)}) collective-permute-start(bf16[128,768]{1,0:T(8,128)(2,1)S(1)} %copy-done.24), channel_id=1, source_target_pairs={{0,14},{2,12},{4,10},{6,8},{8,6},{10,4},{12,2},{14,0},{1,15},{3,13... | collective-permute-start | bytes 589832 | tf_op jit(solution)/shard_map/ppermute | solution.py:401
  67.5 7.3 %collective-permute-start.8 = (bf16[128,768]{1,0:T(8,128)(2,1)}, bf16[128,768]{1,0:T(8,128)(2,1)S(1)}, u32[]{:S(2)}, u32[]{:S(2)}) collective-permute-start(bf16[128,768]{1,0:T(8,128)(2,1)} %get-tuple-element.98), channel_id=1, source_target_pairs={{0,4},{2,6},{4,0},{6,2},{8,12},{10,14},{12,8},{14,10},{1,5},{3,7},... | collective-permute-start | bytes 589832 | tf_op jit(solution)/shard_map/ppermute | solution.py:401
  77.8 3.3 %collective-permute-start.10 = (bf16[128,768]{1,0:T(8,128)(2,1)}, bf16[128,768]{1,0:T(8,128)(2,1)S(1)}, u32[]{:S(2)}, u32[]{:S(2)}) collective-permute-start(bf16[128,768]{1,0:T(8,128)(2,1)} %get-tuple-element.100), channel_id=1, source_target_pairs={{0,8},{2,10},{4,12},{6,14},{8,0},{10,2},{12,4},{14,6},{1,9},{3,11}... | collective-permute-start | bytes 589832 | tf_op jit(solution)/shard_map/ppermute | solution.py:401
  86.5 12.6 %mix_backward.1 = (bf16[8,128,768]{2,1,0:T(8,128)(2,1)}, f32[2,2,128,768]{3,2,1,0:T(8,128)}) custom-call(s32[1]{0:T(128)} %bitcast.me_ref, bf16[256,256]{1,0:T(8,128)(2,1)S(1)} %copy-done.8, bf16[256,256]{1,0:T(8,128)(2,1)S(1)} %copy-done.9, bf16[2,768,768]{2,1,0:T(8,128)(2,1)} %get-tuple-element.78.w1_ref, f32[2,1,768]{2,1,0:T(1,128)S(1)} %reshape.34.b1_ref, ...), custom_call_target="tpu_custom_call" | custom-call | flops 4831838208 | bytes 17301504 | tf_op jit(solution)/shard_map/mix_backward/pallas_call | solution.py:367
  101.4 3.0 %collective-permute-done.11.refs_5_ = bf16[128,768]{1,0:T(8,128)(2,1)S(1)} collective-permute-done((bf16[128,768]{1,0:T(8,128)(2,1)}, bf16[128,768]{1,0:T(8,128)(2,1)S(1)}, u32[]{:S(2)}, u32[]{:S(2)}) %collective-permute-start.11) | collective-permute-done | bytes 196640 | tf_op jit(solution)/shard_map/ppermute | solution.py:401
  105.9 10.3 %all-to-all-start = ((bf16[8,128,768]{2,1,0:T(8,128)(2,1)}), bf16[8,128,768]{2,1,0:T(8,128)(2,1)}, u32[]{:S(2)}, u32[]{:S(2)}) async-start(bf16[8,128,768]{2,1,0:T(8,128)(2,1)} %get-tuple-element.115), calls=%async_computation | async-start | bytes 3145728 | tf_op jit(solution)/shard_map/all_to_all | solution.py:515
  118.3 3.3 %collective-permute-start.13 = (bf16[128,768]{1,0:T(8,128)(2,1)S(1)}, bf16[128,768]{1,0:T(8,128)(2,1)S(1)}, u32[]{:S(2)}, u32[]{:S(2)}) collective-permute-start(bf16[128,768]{1,0:T(8,128)(2,1)S(1)} %copy-done.20), channel_id=1, source_target_pairs={{0,14},{2,12},{4,10},{6,8},{8,6},{10,4},{12,2},{14,0},{1,15},{3,13... | collective-permute-start | bytes 589832 | tf_op jit(solution)/shard_map/ppermute | solution.py:401
  123.0 12.0 %collective-permute-done.7.refs_1_ = bf16[128,768]{1,0:T(8,128)(2,1)S(1)} collective-permute-done((bf16[128,768]{1,0:T(8,128)(2,1)S(1)}, bf16[128,768]{1,0:T(8,128)(2,1)S(1)}, u32[]{:S(2)}, u32[]{:S(2)}) %collective-permute-start.7) | collective-permute-done | bytes 196640 | tf_op jit(solution)/shard_map/ppermute | solution.py:401
  135.0 16.6 %collective-permute-done.13.refs_7_ = bf16[128,768]{1,0:T(8,128)(2,1)S(1)} collective-permute-done((bf16[128,768]{1,0:T(8,128)(2,1)S(1)}, bf16[128,768]{1,0:T(8,128)(2,1)S(1)}, u32[]{:S(2)}, u32[]{:S(2)}) %collective-permute-start.13) | collective-permute-done | bytes 196640 | tf_op jit(solution)/shard_map/ppermute | solution.py:401
  153.0 9.8 %collective-permute-done.22 = f32[128,768]{1,0:T(8,128)} collective-permute-done((f32[128,768]{1,0:T(8,128)S(1)}, f32[128,768]{1,0:T(8,128)}, u32[]{:S(2)}, u32[]{:S(2)}) %collective-permute-start.22) | collective-permute-done | bytes 393248 | tf_op jit(solution)/shard_map/ppermute | solution.py:401
  165.2 12.4 %collective-permute-start.24 = (bf16[32,768]{1,0:T(8,128)(2,1)S(1)}, bf16[32,768]{1,0:T(8,128)(2,1)S(1)}, u32[]{:S(2)}, u32[]{:S(2)}) collective-permute-start(bf16[32,768]{1,0:T(8,128)(2,1)S(1)} %get-tuple-element.130), channel_id=1, source_target_pairs={{0,8},{2,10},{4,12},{6,14},{8,0},{10,2},{12,4},{14,6},{1,9},{3,11}... | collective-permute-start | bytes 147464 | tf_op jit(solution)/shard_map/ppermute | solution.py:401
  177.6 3.1 %collective-permute-done.24 = bf16[32,768]{1,0:T(8,128)(2,1)S(1)} collective-permute-done((bf16[32,768]{1,0:T(8,128)(2,1)S(1)}, bf16[32,768]{1,0:T(8,128)(2,1)S(1)}, u32[]{:S(2)}, u32[]{:S(2)}) %collective-permute-start.24) | collective-permute-done | bytes 49184 | tf_op jit(solution)/shard_map/ppermute | solution.py:401
  190.5 4.2 %collective-permute-done.29 = bf16[4,32,768]{2,1,0:T(8,128)(2,1)S(1)} collective-permute-done((bf16[4,32,768]{2,1,0:T(8,128)(2,1)S(1)}, bf16[4,32,768]{2,1,0:T(8,128)(2,1)S(1)}, u32[]{:S(2)}, u32[]{:S(2)}) %collective-permute-start.29) | collective-permute-done | bytes 196640 | tf_op jit(solution)/shard_map/ppermute | solution.py:401
  194.9 3.0 %to_cells.2 = bf16[4,2,180,768]{3,2,1,0:T(8,128)(2,1)S(1)} custom-call(s32[1]{0:T(128)} %bitcast.me_ref, bf16[180,128]{1,0:T(8,128)(2,1)S(1)} %copy-done.5, bf16[4,2,180,768]{3,2,1,0:T(8,128)(2,1)S(1)} %copy.23.cells_ref.base_ref, bf16[128,768]{1,0:T(8,128)(2,1)} %get-tuple-element.96.refs_0_, bf16[128,768]{1,0:T(8,128)(2,1)} %copy-done.16, ...), custom_call_target="tpu_custom_call" | custom-call | flops 283115520 | bytes 5996544 | tf_op jit(solution)/shard_map/to_cells/pallas_call | solution.py:181
  197.9 3.1 %copy.25 = bf16[4,2,180,768]{3,1,2,0:T(2,128)(2,1)} copy(bf16[4,2,180,768]{3,2,1,0:T(8,128)(2,1)S(1)} %to_cells.2) | data formatting | bytes 4423680
  203.2 3.0 %to_cells.3 = bf16[4,2,180,768]{3,2,1,0:T(8,128)(2,1)S(1)} custom-call(s32[1]{0:T(128)} %bitcast.me_ref, bf16[180,128]{1,0:T(8,128)(2,1)S(1)} %copy-done.4, bf16[4,2,180,768]{3,2,1,0:T(8,128)(2,1)S(1)} %copy-done.1, bf16[8,128,768]{2,1,0:T(8,128)(2,1)} %all-to-all-done.refs_0_), custom_call_target="tpu_custom_call" | custom-call | flops 283115520 | bytes 5996544 | tf_op jit(solution)/shard_map/to_cells/pallas_call | solution.py:181
  206.2 3.1 %copy.26 = bf16[4,2,180,768]{3,1,2,0:T(2,128)(2,1)} copy(bf16[4,2,180,768]{3,2,1,0:T(8,128)(2,1)S(1)} %to_cells.3) | data formatting | bytes 4423680
  (121 shorter events, 51.7 us)
Async XLA Ops:
  8.1 15.8 %collective-permute-start.1 = (bf16[128,768]{1,0:T(8,128)(2,1)}, bf16[128,768]{1,0:T(8,128)(2,1)}, u32[]{:S(2)}, u32[]{:S(2)}) collective-permute-start(bf16[128,768]{1,0:T(8,128)(2,1)} %get-tuple-element.82), channel_id=1, source_target_pairs={{0,4},{2,6},{4,0},{6,2},{8,12},{10,14},{12,8},{14,10},{1,5},{3,7},... | collective-permute-start | bytes 589832 | tf_op jit(solution)/shard_map/ppermute | solution.py:401
  9.6 23.6 %collective-permute-start.2 = (bf16[128,768]{1,0:T(8,128)(2,1)}, bf16[128,768]{1,0:T(8,128)(2,1)}, u32[]{:S(2)}, u32[]{:S(2)}) collective-permute-start(bf16[128,768]{1,0:T(8,128)(2,1)} %get-tuple-element.83), channel_id=1, source_target_pairs={{0,6},{2,4},{4,2},{6,0},{8,14},{10,12},{12,10},{14,8},{1,7},{3,5},... | collective-permute-start | bytes 589832 | tf_op jit(solution)/shard_map/ppermute | solution.py:401
  9.6 23.6 %collective-permute-start.3 = (bf16[128,768]{1,0:T(8,128)(2,1)}, bf16[128,768]{1,0:T(8,128)(2,1)}, u32[]{:S(2)}, u32[]{:S(2)}) collective-permute-start(bf16[128,768]{1,0:T(8,128)(2,1)} %get-tuple-element.84), channel_id=1, source_target_pairs={{0,8},{2,10},{4,12},{6,14},{8,0},{10,2},{12,4},{14,6},{1,9},{3,11}... | collective-permute-start | bytes 589832 | tf_op jit(solution)/shard_map/ppermute | solution.py:401
  12.6 28.5 %collective-permute-start.4 = (bf16[128,768]{1,0:T(8,128)(2,1)}, bf16[128,768]{1,0:T(8,128)(2,1)}, u32[]{:S(2)}, u32[]{:S(2)}) collective-permute-start(bf16[128,768]{1,0:T(8,128)(2,1)} %get-tuple-element.85), channel_id=1, source_target_pairs={{0,10},{2,8},{4,14},{6,12},{8,2},{10,0},{12,6},{14,4},{1,11},{3,9}... | collective-permute-start | bytes 589832 | tf_op jit(solution)/shard_map/ppermute | solution.py:401
  13.9 27.2 %collective-permute-start.5 = (bf16[128,768]{1,0:T(8,128)(2,1)}, bf16[128,768]{1,0:T(8,128)(2,1)}, u32[]{:S(2)}, u32[]{:S(2)}) collective-permute-start(bf16[128,768]{1,0:T(8,128)(2,1)} %get-tuple-element.86), channel_id=1, source_target_pairs={{0,12},{2,14},{4,8},{6,10},{8,4},{10,6},{12,0},{14,2},{1,13},{3,15... | collective-permute-start | bytes 589832 | tf_op jit(solution)/shard_map/ppermute | solution.py:401
  23.8 30.5 %collective-permute-start.6 = (bf16[128,768]{1,0:T(8,128)(2,1)}, bf16[128,768]{1,0:T(8,128)(2,1)}, u32[]{:S(2)}, u32[]{:S(2)}) collective-permute-start(bf16[128,768]{1,0:T(8,128)(2,1)} %get-tuple-element.87), channel_id=1, source_target_pairs={{0,14},{2,12},{4,10},{6,8},{8,6},{10,4},{12,2},{14,0},{1,15},{3,13... | collective-permute-start | bytes 589832 | tf_op jit(solution)/shard_map/ppermute | solution.py:401
  33.2 29.4 %collective-permute-start.15 = (bf16[128,768]{1,0:T(8,128)(2,1)}, bf16[128,768]{1,0:T(8,128)(2,1)S(1)}, u32[]{:S(2)}, u32[]{:S(2)}) collective-permute-start(bf16[128,768]{1,0:T(8,128)(2,1)} %get-tuple-element.107), channel_id=1, source_target_pairs={{0,4},{2,6},{4,0},{6,2},{8,12},{10,14},{12,8},{14,10},{1,5},{3,7},... | collective-permute-start | bytes 589832 | tf_op jit(solution)/shard_map/ppermute | solution.py:401
  33.3 29.4 %collective-permute-start.16 = (bf16[128,768]{1,0:T(8,128)(2,1)}, bf16[128,768]{1,0:T(8,128)(2,1)S(1)}, u32[]{:S(2)}, u32[]{:S(2)}) collective-permute-start(bf16[128,768]{1,0:T(8,128)(2,1)} %get-tuple-element.108), channel_id=1, source_target_pairs={{0,6},{2,4},{4,2},{6,0},{8,14},{10,12},{12,10},{14,8},{1,7},{3,5},... | collective-permute-start | bytes 589832 | tf_op jit(solution)/shard_map/ppermute | solution.py:401
  41.1 26.4 %collective-permute-start.17 = (bf16[128,768]{1,0:T(8,128)(2,1)}, bf16[128,768]{1,0:T(8,128)(2,1)S(1)}, u32[]{:S(2)}, u32[]{:S(2)}) collective-permute-start(bf16[128,768]{1,0:T(8,128)(2,1)} %get-tuple-element.109), channel_id=1, source_target_pairs={{0,8},{2,10},{4,12},{6,14},{8,0},{10,2},{12,4},{14,6},{1,9},{3,11}... | collective-permute-start | bytes 589832 | tf_op jit(solution)/shard_map/ppermute | solution.py:401
  41.1 33.7 %collective-permute-start.18 = (bf16[128,768]{1,0:T(8,128)(2,1)}, bf16[128,768]{1,0:T(8,128)(2,1)}, u32[]{:S(2)}, u32[]{:S(2)}) collective-permute-start(bf16[128,768]{1,0:T(8,128)(2,1)} %get-tuple-element.110), channel_id=1, source_target_pairs={{0,10},{2,8},{4,14},{6,12},{8,2},{10,0},{12,6},{14,4},{1,11},{3,9}... | collective-permute-start | bytes 589832 | tf_op jit(solution)/shard_map/ppermute | solution.py:401
  62.0 15.8 %collective-permute-start.14 = (bf16[128,768]{1,0:T(8,128)(2,1)}, bf16[128,768]{1,0:T(8,128)(2,1)}, u32[]{:S(2)}, u32[]{:S(2)}) collective-permute-start(bf16[128,768]{1,0:T(8,128)(2,1)} %get-tuple-element.106), channel_id=1, source_target_pairs={{0,2},{2,0},{4,6},{6,4},{8,10},{10,8},{12,14},{14,12},{1,3},{3,1},... | collective-permute-start | bytes 589832 | tf_op jit(solution)/shard_map/ppermute | solution.py:401
  62.6 18.5 %collective-permute-start.19 = (bf16[128,768]{1,0:T(8,128)(2,1)S(1)}, bf16[128,768]{1,0:T(8,128)(2,1)}, u32[]{:S(2)}, u32[]{:S(2)}) collective-permute-start(bf16[128,768]{1,0:T(8,128)(2,1)S(1)} %copy-done.26), channel_id=1, source_target_pairs={{0,12},{2,14},{4,8},{6,10},{8,4},{10,6},{12,0},{14,2},{1,13},{3,15... | collective-permute-start | bytes 589832 | tf_op jit(solution)/shard_map/ppermute | solution.py:401
  62.7 21.2 %collective-permute-start.20 = (bf16[128,768]{1,0:T(8,128)(2,1)S(1)}, bf16[128,768]{1,0:T(8,128)(2,1)}, u32[]{:S(2)}, u32[]{:S(2)}) collective-permute-start(bf16[128,768]{1,0:T(8,128)(2,1)S(1)} %copy-done.24), channel_id=1, source_target_pairs={{0,14},{2,12},{4,10},{6,8},{8,6},{10,4},{12,2},{14,0},{1,15},{3,13... | collective-permute-start | bytes 589832 | tf_op jit(solution)/shard_map/ppermute | solution.py:401
  67.5 31.6 %collective-permute-start.8 = (bf16[128,768]{1,0:T(8,128)(2,1)}, bf16[128,768]{1,0:T(8,128)(2,1)S(1)}, u32[]{:S(2)}, u32[]{:S(2)}) collective-permute-start(bf16[128,768]{1,0:T(8,128)(2,1)} %get-tuple-element.98), channel_id=1, source_target_pairs={{0,4},{2,6},{4,0},{6,2},{8,12},{10,14},{12,8},{14,10},{1,5},{3,7},... | collective-permute-start | bytes 589832 | tf_op jit(solution)/shard_map/ppermute | solution.py:401
  74.8 24.3 %collective-permute-start.9 = (bf16[128,768]{1,0:T(8,128)(2,1)}, bf16[128,768]{1,0:T(8,128)(2,1)S(1)}, u32[]{:S(2)}, u32[]{:S(2)}) collective-permute-start(bf16[128,768]{1,0:T(8,128)(2,1)} %get-tuple-element.99), channel_id=1, source_target_pairs={{0,6},{2,4},{4,2},{6,0},{8,14},{10,12},{12,10},{14,8},{1,7},{3,5},... | collective-permute-start | bytes 589832 | tf_op jit(solution)/shard_map/ppermute | solution.py:401
  77.8 23.6 %collective-permute-start.10 = (bf16[128,768]{1,0:T(8,128)(2,1)}, bf16[128,768]{1,0:T(8,128)(2,1)S(1)}, u32[]{:S(2)}, u32[]{:S(2)}) collective-permute-start(bf16[128,768]{1,0:T(8,128)(2,1)} %get-tuple-element.100), channel_id=1, source_target_pairs={{0,8},{2,10},{4,12},{6,14},{8,0},{10,2},{12,4},{14,6},{1,9},{3,11}... | collective-permute-start | bytes 589832 | tf_op jit(solution)/shard_map/ppermute | solution.py:401
  81.1 23.3 %collective-permute-start.11 = (bf16[128,768]{1,0:T(8,128)(2,1)}, bf16[128,768]{1,0:T(8,128)(2,1)S(1)}, u32[]{:S(2)}, u32[]{:S(2)}) collective-permute-start(bf16[128,768]{1,0:T(8,128)(2,1)} %get-tuple-element.101), channel_id=1, source_target_pairs={{0,10},{2,8},{4,14},{6,12},{8,2},{10,0},{12,6},{14,4},{1,11},{3,9}... | collective-permute-start | bytes 589832 | tf_op jit(solution)/shard_map/ppermute | solution.py:401
  83.9 20.5 %collective-permute-start.12 = (bf16[128,768]{1,0:T(8,128)(2,1)}, bf16[128,768]{1,0:T(8,128)(2,1)S(1)}, u32[]{:S(2)}, u32[]{:S(2)}) collective-permute-start(bf16[128,768]{1,0:T(8,128)(2,1)} %get-tuple-element.102), channel_id=1, source_target_pairs={{0,12},{2,14},{4,8},{6,10},{8,4},{10,6},{12,0},{14,2},{1,13},{3,15... | collective-permute-start | bytes 589832 | tf_op jit(solution)/shard_map/ppermute | solution.py:401
  105.9 15.7 %collective-permute-start.21 = (f32[256,768]{1,0:T(8,128)S(1)}, f32[256,768]{1,0:T(8,128)}, u32[]{:S(2)}, u32[]{:S(2)}) collective-permute-start(f32[256,768]{1,0:T(8,128)S(1)} %dynamic-slice_bitcast_fusion), channel_id=1, source_target_pairs={{0,1},{1,0},{2,3},{3,2},{4,5},{5,4},{6,7},{7,6},{8,9},{9,8},{10,11... | collective-permute-start | bytes 2359304 | tf_op jit(solution)/shard_map/ppermute | solution.py:401
  105.9 97.2 %all-to-all-start = ((bf16[8,128,768]{2,1,0:T(8,128)(2,1)}), bf16[8,128,768]{2,1,0:T(8,128)(2,1)}, u32[]{:S(2)}, u32[]{:S(2)}) async-start(bf16[8,128,768]{2,1,0:T(8,128)(2,1)} %get-tuple-element.115), calls=%async_computation | async-start | bytes 3145728 | tf_op jit(solution)/shard_map/all_to_all | solution.py:515
  116.2 18.8 %collective-permute-start.7 = (bf16[128,768]{1,0:T(8,128)(2,1)S(1)}, bf16[128,768]{1,0:T(8,128)(2,1)S(1)}, u32[]{:S(2)}, u32[]{:S(2)}) collective-permute-start(bf16[128,768]{1,0:T(8,128)(2,1)S(1)} %copy-done.21), channel_id=1, source_target_pairs={{0,2},{2,0},{4,6},{6,4},{8,10},{10,8},{12,14},{14,12},{1,3},{3,1},... | collective-permute-start | bytes 589832 | tf_op jit(solution)/shard_map/ppermute | solution.py:401
  118.3 33.4 %collective-permute-start.13 = (bf16[128,768]{1,0:T(8,128)(2,1)S(1)}, bf16[128,768]{1,0:T(8,128)(2,1)S(1)}, u32[]{:S(2)}, u32[]{:S(2)}) collective-permute-start(bf16[128,768]{1,0:T(8,128)(2,1)S(1)} %copy-done.20), channel_id=1, source_target_pairs={{0,14},{2,12},{4,10},{6,8},{8,6},{10,4},{12,2},{14,0},{1,15},{3,13... | collective-permute-start | bytes 589832 | tf_op jit(solution)/shard_map/ppermute | solution.py:401
  163.8 13.7 %collective-permute-start.25 = (bf16[32,768]{1,0:T(8,128)(2,1)S(1)}, bf16[32,768]{1,0:T(8,128)(2,1)S(1)}, u32[]{:S(2)}, u32[]{:S(2)}) collective-permute-start(bf16[32,768]{1,0:T(8,128)(2,1)S(1)} %get-tuple-element.129), channel_id=1, source_target_pairs={{0,12},{2,14},{4,8},{6,10},{8,4},{10,6},{12,0},{14,2},{1,13},{3,15... | collective-permute-start | bytes 147464 | tf_op jit(solution)/shard_map/ppermute | solution.py:401
  165.2 15.5 %collective-permute-start.24 = (bf16[32,768]{1,0:T(8,128)(2,1)S(1)}, bf16[32,768]{1,0:T(8,128)(2,1)S(1)}, u32[]{:S(2)}, u32[]{:S(2)}) collective-permute-start(bf16[32,768]{1,0:T(8,128)(2,1)S(1)} %get-tuple-element.130), channel_id=1, source_target_pairs={{0,8},{2,10},{4,12},{6,14},{8,0},{10,2},{12,4},{14,6},{1,9},{3,11}... | collective-permute-start | bytes 147464 | tf_op jit(solution)/shard_map/ppermute | solution.py:401
  (35 other events, 471.0 us)

commit v8 on v7

--- a/solution.py
+++ b/solution.py
@@ -12,8 +12,10 @@
 
 KW = 64
 shrink_level = 0.05
-HELD = 5
-FIRST = 4
+DEPTH = 3
+DEPTH_LATE = 4
+BESIDE = (3, 3)
+STEPS_AHEAD = (0, 0, 1, 3, 5, 6)
 MIB = 1024 * 1024
 
 
@@ -259,8 +261,8 @@
 def backward_kernel(
     block_size, blocks, me_ref, lat_ref, unlat_ref, w1_ref, b1_ref, w2_ref, b2_ref, mixed_ref, *refs
 ):
-    bands_refs, image_ref = refs[:blocks], refs[blocks]
-    sums_ref, act_ref, gate_ref, cot_ref, kept_ref, band_ref = refs[blocks + 1 :]
+    bands_refs, image_refs = refs[:blocks], refs[blocks : 2 * blocks]
+    sums_ref, act_ref, gate_ref, cot_ref, kept_ref, band_ref = refs[2 * blocks :]
     transposed = (((1,), (1,)), ((), ()))
     summed = (((0,), (0,)), ((), ()))
 
@@ -296,7 +298,7 @@
     weight_sums(act_ref[...], kept_ref[...], 1)
     kept_ref[...] = times(cot_ref[...], w1_ref[0], transposed).astype(jnp.bfloat16)
     weight_sums(mixed_ref[0], cot_ref[...], 0)
-    unmix_lat(me_ref, unlat_ref, kept_ref, band_ref, [image_ref])
+    unmix_lat(me_ref, unlat_ref, kept_ref, band_ref, image_refs)
 
 
 def group_spec(*shape):
@@ -308,9 +310,14 @@
     return (pl.BlockSpec(block, lambda g, *_: (0, g)),) * len(bands)
 
 
-def stacked(lead, rows, groups, width):
-    shape = in_hbm((lead, rows // lead, groups * width), jnp.bfloat16)
-    return (shape,), (pl.BlockSpec((lead, rows // lead, width), lambda g, *_: (0, 0, g)),)
+def images_like(bands, samples, size, groups):
+    if len(bands) > 1:
+        shapes = tuple(in_hbm(band.shape, band.dtype) for band in bands)
+        return shapes, bands_specs(bands[0].shape[0], bands, groups)
+    channels = bands[0].shape[1]
+    shape = (1, samples * size, channels)
+    spec = pl.BlockSpec(shape[:2] + (channels // groups,), lambda g, *_: (0, 0, g))
+    return (in_hbm(shape, jnp.bfloat16),), (spec,)
 
 
 def forward_mid(me, lat, unlat, bands, w1, b1, w2, b2):
@@ -321,11 +328,7 @@
     table = pl.BlockSpec((size, size), lambda g, _: (0, 0))
     state = (groups, positions, lanes)
     specs = bands_specs(bands[0].shape[0], bands, groups)
-    if len(bands) == 1:
-        images, image_specs = stacked(1, samples * size, groups, lanes // 2)
-    else:
-        images = tuple(in_hbm(band.shape, band.dtype) for band in bands)
-        image_specs = specs
+    images, image_specs = images_like(bands, samples, size, groups)
     results = pl.pallas_call(
         functools.partial(forward_kernel, len(bands)),
         grid_spec=pltpu.PrefetchScalarGridSpec(
@@ -363,8 +366,8 @@
     table = pl.BlockSpec((size, size), lambda g, _: (0, 0))
     size_of_block = lanes // 2 // (count // groups)
     sums = (2, 2, size_of_block + 32, lanes // 2)
-    image, image_specs = stacked(len(bands), samples * size, groups, lanes // 2)
-    return pl.pallas_call(
+    images, image_specs = images_like(bands, samples, size, groups)
+    results = pl.pallas_call(
         functools.partial(backward_kernel, size_of_block, len(bands)),
         grid_spec=pltpu.PrefetchScalarGridSpec(
             num_scalar_prefetch=1,
@@ -385,7 +388,7 @@
                 pltpu.VMEM((samples, size, lanes // 2), jnp.bfloat16),
             ],
         ),
-        out_shape=image + (in_hbm(sums[:3] + (groups * sums[3],), jnp.float32),),
+        out_shape=images + (in_hbm(sums[:3] + (groups * sums[3],), jnp.float32),),
         compiler_params=params(32),
         cost_estimate=pl.CostEstimate(
             flops=8 * groups * positions * lanes * lanes,
@@ -394,11 +397,27 @@
         ),
         name="mix_backward",
     )(me, lat, unlat, *hbm(w1), b1, *hbm(w2), b2, *hbm(state, *bands))
+    return results[: len(bands)], results[len(bands)]
 
 
 def swap_with(values, axis, distance):
     pairs = [(i, i ^ distance) for i in range(lax.axis_size(axis))]
     return lax.ppermute(values, axis, pairs)
+
+
+def waiting(values, arrived):
+    return lax.optimization_barrier((values, tuple(arrived)))[0]
+
+
+class Chain:
+    def __init__(self):
+        self.arrived = []
+
+    def swap(self, values, axis, distance, depth):
+        if len(self.arrived) >= depth:
+            values = waiting(values, self.arrived[-depth:][:1])
+        self.arrived.append(swap_with(values, axis, distance))
+        return self.arrived[-1]
 
 
 def mixed_order(size):
@@ -417,38 +436,48 @@
 
 
 class GroupSum:
-    def __init__(self, sums):
+    def __init__(self, chain, sums):
+        self.chain = chain
         self.lanes = sums.shape[-1]
         self.side = lax.axis_index("dp")
         self.me = lax.axis_index("space")
         self.count = lax.axis_size("space") // 2
         self.held = sums.reshape(-1, self.lanes)
 
+    def swap(self, values, axis, distance):
+        return self.chain.swap(values, axis, distance, DEPTH_LATE)
+
     def halve(self, axis, distance, bit):
         pair = self.held.reshape(2, -1, self.lanes)
         given = pick(pair, 1 - bit)
-        self.held = pick(pair, bit) + swap_with(given, axis, distance)
-
-    def scatter(self, arrived):
+        self.held = pick(pair, bit) + self.swap(given, axis, distance)
+
+    def over_dp(self):
         self.halve("dp", 1, self.side)
-        if len(arrived) > 0:
-            self.held, _ = lax.optimization_barrier((self.held, tuple(arrived)))
+
+    def over_next(self):
         self.halve("space", 1, self.me % 2)
+
+    def scatter(self):
         shares = self.held.reshape(self.count, -1, self.lanes)
         place = self.me // 2
         total = pick(shares, place)
         for offset in range(1, self.count):
             given = pick(shares, place ^ offset).astype(jnp.bfloat16)
-            total += swap_with(given, "space", 2 * offset).astype(jnp.float32)
+            total += self.swap(given, "space", 2 * offset).astype(jnp.float32)
         self.total = total.astype(jnp.bfloat16)
 
     def gather(self):
         taken = [self.total]
         for offset in range(1, self.count):
-            taken.append(swap_with(self.total, "space", 2 * offset))
-        quarter = jnp.stack(taken)
-        half = jnp.stack([quarter, swap_with(quarter, "space", 1)])
-        return half, swap_with(half, "dp", 1)
+            taken.append(self.swap(self.total, "space", 2 * offset))
+        self.quarter = jnp.stack(taken)
+
+    def gather_next(self):
+        self.half = jnp.stack([self.quarter, self.swap(self.quarter, "space", 1)])
+
+    def gather_dp(self):
+        self.other = self.swap(self.half, "dp", 1)
 
 
 def finish_kernel(factor, me_ref, half_ref, other_ref, *out_refs):
@@ -499,20 +528,19 @@
 
     order = mixed_order(owners)
 
-    def send_out(blocks):
-        if direct:
-            taken = {0: blocks[0]}
-            for offset in order:
-                taken[offset] = swap_with(blocks[offset], "space", offset)
-            return [taken[offset] for offset in range(owners)]
-        spectrum = blocks[0].reshape(samples, rows, owners, 2 * modes, channels)
+    chain = Chain()
+
+    def send(blocks, offsets, taken, depth):
+        for offset in offsets:
+            taken[offset] = chain.swap(blocks[offset], "space", offset, depth)
+
+    def send_all(spectrum):
+        spectrum = spectrum.reshape(samples, rows, owners, 2 * modes, channels)
         spectrum = jnp.transpose(spectrum, (2, 0, 1, 3, 4))
         arrived = lax.all_to_all(spectrum, "space", split_axis=0, concat_axis=0, tiled=True)
         return [jnp.transpose(arrived, (1, 0, 2, 3, 4)).reshape(-1, channels)]
 
-    def send_back(bands):
-        if direct:
-            return [lax.all_to_all(bands, "space", split_axis=0, concat_axis=0, tiled=True)]
+    def send_all_back(bands):
         bands = bands.reshape(samples, owners, rows, 2 * modes, channels)
         bands = jnp.transpose(bands, (1, 0, 2, 3, 4))
         arrived = lax.all_to_all(bands, "space", split_axis=0, concat_axis=0, tiled=True)
@@ -527,48 +555,66 @@
     spectrum, cotangent, w_first, w_second = lax.optimization_barrier(
         (spectrum, cotangent, w_first, w_second)
     )
-    gathered = send_out(spectrum)
     cot_spec = to_modes(me, scaled, cotangent, lead)
     w1, w2 = spread_weights(groups, w_first, w_second)
     b1, b2 = block_bias(b_first, groups), block_bias(b_second, groups)
-
+    positions = samples * lax.axis_size("dp") * lat_total * KW
+    factor = 1.0 / math.sqrt(positions)
+
+    if not direct:
+        gathered = send_all(spectrum[0])
+        image, state = forward_mid(me, lat, lat.T, gathered, w1, b1, w2, b2)
+        image_band = send_all_back(image[0])
+        gathered = send_all(cot_spec[0])
+        grad_image, sums = backward_mid(me, lat, lat.T, gathered, w1, b1, w2, b2, state, count)
+        grad_band = send_all_back(grad_image[0])
+        output = to_cells(me, scaled.T, image_band, fields)
+        grad_fields = to_cells(me, plain.T, grad_band, cotangent)
+        sums = lax.psum(sums, ("space", "dp")) * factor
+        grads = []
+        for which in range(2):
+            blocks = sums[which, :, :edge].reshape(2, edge, count, edge)
+            grads.append(jnp.transpose(blocks, (0, 2, 1, 3)))
+            grads.append(sums[which, :, edge].reshape(b_first.shape))
+        return (output, grad_fields) + tuple(grads)
+
+    gathered, cot_gathered = {0: spectrum[0]}, {0: cot_spec[0]}
+    image_band, grad_band = {}, {}
+    send(spectrum, order, gathered, DEPTH)
+    send(cot_spec, order, cot_gathered, DEPTH)
+    gathered = [gathered[offset] for offset in range(owners)]
     image, state = forward_mid(me, lat, lat.T, gathered, w1, b1, w2, b2)
-    if direct:
-        late = tuple(cot_spec[offset] for offset in order[FIRST:])
-        late, image = lax.optimization_barrier((late, image))
-        cot_spec = list(cot_spec)
-        for offset, block in zip(order[FIRST:], late):
-            cot_spec[offset] = block
-    cot_gathered = send_out(cot_spec)
-    image_band = send_out(image) if direct else send_back(image[0])
+    image, state = waiting((image, state), [cot_gathered[offset] for offset in order[:BESIDE[0]]])
+    image_band[0] = image[0]
+    send(image, order, image_band, DEPTH)
+    cot_gathered = [cot_gathered[offset] for offset in range(owners)]
     grad_image, sums = backward_mid(
         me, lat, lat.T, cot_gathered, w1, b1, w2, b2, state, count
     )
-    late = []
-    if direct:
-        early = tuple(image_band[offset] for offset in order[:HELD])
-        late = [image_band[offset] for offset in order[HELD:]]
-        grad_image, sums, _ = lax.optimization_barrier((grad_image, sums, early))
-    grad_band = send_back(grad_image)
+    grad_image, sums = waiting(
+        (grad_image, sums), [image_band[offset] for offset in order[:BESIDE[1]]]
+    )
+    grad_band[0] = grad_image[0]
+    group_sum = GroupSum(chain, sums)
+    steps = [
+        group_sum.over_dp, group_sum.over_next, group_sum.scatter,
+        group_sum.gather, group_sum.gather_next, group_sum.gather_dp,
+    ]
+    for place, offset in enumerate(order):
+        for _ in range(STEPS_AHEAD.count(place)):
+            steps.pop(0)()
+        send(grad_image, [offset], grad_band, DEPTH_LATE)
+    for step in steps:
+        step()
+    image_band = [image_band[offset] for offset in range(owners)]
+    grad_band = [grad_band[offset] for offset in range(owners)]
     output = to_cells(me, scaled.T, image_band, fields)
     grad_fields = to_cells(me, plain.T, grad_band, cotangent)
-
-    positions = samples * lax.axis_size("dp") * lat_total * KW
-    factor = 1.0 / math.sqrt(positions)
-    if direct:
-        group_sum = GroupSum(sums)
-        group_sum.scatter(late)
-        half, other = group_sum.gather()
-        place = lax.axis_index("space")
-        here = jnp.stack([lax.axis_index("dp"), place % 2, place // 2]).astype(jnp.int32)
-        grads = finish_sums(here, half, other, factor, w_first.shape, b_first.shape)
-        return (output, grad_fields) + tuple(grads)
-    sums = lax.psum(sums, ("space", "dp")) * factor
-    grads = []
-    for which in range(2):
-        blocks = sums[which, :, :edge].reshape(2, edge, count, edge)
-        grads.append(jnp.transpose(blocks, (0, 2, 1, 3)))
-        grads.append(sums[which, :, edge].reshape(b_first.shape))
+    place = lax.axis_index("space")
+    here = jnp.stack([lax.axis_index("dp"), place % 2, place // 2]).astype(jnp.int32)
+    grads = finish_sums(
+        here, group_sum.half, group_sum.other, factor, w_first.shape, b_first.shape
+    )
     return (output, grad_fields) + tuple(grads)
 
 

time: 210 us -> 208 us (level)
  starting transfers between devices: 91 us -> 75.3 us
  waiting for transfers between devices: 65 us -> 76.5 us
    ppermute x31 -> x38, waiting for transfers between devices: 65 us -> 76.5 us  [swap_with(): return lax.ppermute(values, axis, pairs)]
    all_to_all x1 -> x0, starting transfers between devices: 10.3 us -> none  [send_back(): lax.all_to_all(bands, 'space', split_axis=0, concat_axis=0, tiled=True)]
    ppermute x31 -> x38, starting transfers between devices: 80.7 us -> 75.3 us  [swap_with(): return lax.ppermute(values, axis, pairs)]
    unnamed x57 -> x77, local copies, waits for them, and re-layouts: 10.5 us -> 13.7 us
  transfers between devices with their start and end apart: 32 -> 38, of which waited for: 12 -> 17; matrix products, arithmetic and copies ran while one was open for 4% -> 5% of each run, Pallas kernels for 15% -> 15%
where the time goes in v8:
time: 208 us; the launch traced here: 207 us
  waiting for transfers between devices  76.5 us (37%)
  starting transfers between devices  75.3 us (36%)
  Pallas kernels  36 us (17%)
  local copies, waits for them, and re-layouts  15.5 us (7%)
  other arithmetic  2.67 us (1%)
    ppermute x38, waiting for transfers between devices, swap_with(): return lax.ppermute(values, axis, pairs)  76.5 us
    ppermute x38, starting transfers between devices, swap_with(): return lax.ppermute(values, axis, pairs)  75.3 us
    unnamed x77, local copies, waits for them, and re-layouts  13.7 us
    pallas_call x1, Pallas kernels, backward_mid(): pl.pallas_call(functools.partial(backward_kernel, size_of_block, len(band...  12.7 us
    pallas_call x1, Pallas kernels, forward_mid(): pl.pallas_call(functools.partial(forward_kernel, len(bands)), grid_spec=p...  7.63 us
    pallas_call x2, Pallas kernels, to_cells(): pl.pallas_call(to_cells_kernel, grid_spec=pltpu.PrefetchScalarGridSpec(nu...  6.16 us
    pallas_call x2, Pallas kernels, to_modes(): pl.pallas_call(to_modes_kernel, grid_spec=pltpu.PrefetchScalarGridSpec(nu...  4.72 us
  transfers between devices with their start and end apart: 38, of which 17 were waited for; matrix products, arithmetic and copies ran while one was open for 5% of the time, Pallas kernels for 15%

profile of v8, /device:TPU:0, one launch (start us, length us, event | category | flops | bytes accessed | tf_op | source)
XLA Modules:
  0.0 206.9 jit_solution(9189773280703298114)
XLA Ops:
  5.0 4.1 %collective-permute-start.3 = (bf16[128,768]{1,0:T(8,128)(2,1)}, bf16[128,768]{1,0:T(8,128)(2,1)S(1)}, u32[]{:S(2)}, u32[]{:S(2)}) collective-permute-start(bf16[128,768]{1,0:T(8,128)(2,1)} %get-tuple-element.128), channel_id=1, source_target_pairs={{0,8},{2,10},{4,12},{6,14},{8,0},{10,2},{12,4},{14,6},{1,9},{3,11}... | collective-permute-start | bytes 589832 | tf_op jit(solution)/shard_map/ppermute | solution.py:405
  11.9 8.2 %collective-permute-done.3.refs_4_ = bf16[128,768]{1,0:T(8,128)(2,1)S(1)} collective-permute-done((bf16[128,768]{1,0:T(8,128)(2,1)}, bf16[128,768]{1,0:T(8,128)(2,1)S(1)}, u32[]{:S(2)}, u32[]{:S(2)}) %collective-permute-start.3) | collective-permute-done | bytes 196640 | tf_op jit(solution)/shard_map/ppermute | solution.py:405
  23.3 5.8 %collective-permute-done.refs_5_ = bf16[128,768]{1,0:T(8,128)(2,1)S(1)} collective-permute-done((bf16[128,768]{1,0:T(8,128)(2,1)}, bf16[128,768]{1,0:T(8,128)(2,1)S(1)}, u32[]{:S(2)}, u32[]{:S(2)}) %collective-permute-start) | collective-permute-done | bytes 196640 | tf_op jit(solution)/shard_map/ppermute | solution.py:405
  34.0 5.9 %collective-permute-start.6 = (bf16[128,768]{1,0:T(8,128)(2,1)}, bf16[128,768]{1,0:T(8,128)(2,1)}, u32[]{:S(2)}, u32[]{:S(2)}) collective-permute-start(bf16[128,768]{1,0:T(8,128)(2,1)} %get-tuple-element.133), channel_id=1, source_target_pairs={{0,14},{2,12},{4,10},{6,8},{8,6},{10,4},{12,2},{14,0},{1,15},{3,13... | collective-permute-start | bytes 589832 | tf_op jit(solution)/shard_map/ppermute | solution.py:405
  46.0 8.7 %collective-permute-start.9 = (bf16[128,768]{1,0:T(8,128)(2,1)}, bf16[128,768]{1,0:T(8,128)(2,1)S(1)}, u32[]{:S(2)}, u32[]{:S(2)}) collective-permute-start(bf16[128,768]{1,0:T(8,128)(2,1)} %get-tuple-element.149), channel_id=1, source_target_pairs={{0,10},{2,8},{4,14},{6,12},{8,2},{10,0},{12,6},{14,4},{1,11},{3,9}... | collective-permute-start | bytes 589832 | tf_op jit(solution)/shard_map/ppermute | solution.py:405
  54.6 3.9 %collective-permute-done.7.refs_4_ = bf16[128,768]{1,0:T(8,128)(2,1)S(1)} collective-permute-done((bf16[128,768]{1,0:T(8,128)(2,1)}, bf16[128,768]{1,0:T(8,128)(2,1)S(1)}, u32[]{:S(2)}, u32[]{:S(2)}) %collective-permute-start.7) | collective-permute-done | bytes 196640 | tf_op jit(solution)/shard_map/ppermute | solution.py:405
  58.8 3.0 %collective-permute-start.16 = (bf16[128,768]{1,0:T(8,128)(2,1)}, bf16[128,768]{1,0:T(8,128)(2,1)S(1)}, u32[]{:S(2)}, u32[]{:S(2)}) collective-permute-start(bf16[128,768]{1,0:T(8,128)(2,1)} %get-tuple-element.166), channel_id=1, source_target_pairs={{0,12},{2,14},{4,8},{6,10},{8,4},{10,6},{12,0},{14,2},{1,13},{3,15... | collective-permute-start | bytes 589832 | tf_op jit(solution)/shard_map/ppermute | solution.py:405
  61.8 7.6 %mix_forward.1 = (bf16[128,768]{1,0:T(8,128)(2,1)}, bf16[128,768]{1,0:T(8,128)(2,1)}, bf16[128,768]{1,0:T(8,128)(2,1)}, bf16[128,768]{1,0:T(8,128)(2,1)}, bf16[1...) custom-call(s32[1]{0:T(128)} %bitcast.me_ref, ...), custom_call_target="tpu_custom_call" | custom-call | flops 2415919104 | bytes 17301504 | tf_op jit(solution)/shard_map/mix_forward/pallas_call | solution.py:332
  73.7 2.9 %collective-permute-start.14 = (bf16[128,768]{1,0:T(8,128)(2,1)S(1)}, bf16[128,768]{1,0:T(8,128)(2,1)}, u32[]{:S(2)}, u32[]{:S(2)}) collective-permute-start(bf16[128,768]{1,0:T(8,128)(2,1)S(1)} %copy-done.25), channel_id=1, source_target_pairs={{0,2},{2,0},{4,6},{6,4},{8,10},{10,8},{12,14},{14,12},{1,3},{3,1},... | collective-permute-start | bytes 589832 | tf_op jit(solution)/shard_map/ppermute | solution.py:405
  77.3 4.0 %collective-permute-done.11.refs_7_ = bf16[128,768]{1,0:T(8,128)(2,1)S(1)} collective-permute-done((bf16[128,768]{1,0:T(8,128)(2,1)S(1)}, bf16[128,768]{1,0:T(8,128)(2,1)S(1)}, u32[]{:S(2)}, u32[]{:S(2)}) %collective-permute-start.11) | collective-permute-done | bytes 196640 | tf_op jit(solution)/shard_map/ppermute | solution.py:405
  81.3 10.4 %collective-permute-start.12 = (bf16[128,768]{1,0:T(8,128)(2,1)}, bf16[128,768]{1,0:T(8,128)(2,1)S(1)}, u32[]{:S(2)}, u32[]{:S(2)}) collective-permute-start(bf16[128,768]{1,0:T(8,128)(2,1)} %get-tuple-element.157), channel_id=1, source_target_pairs={{0,10},{2,8},{4,14},{6,12},{8,2},{10,0},{12,6},{14,4},{1,11},{3,9}... | collective-permute-start | bytes 589832 | tf_op jit(solution)/shard_map/ppermute | solution.py:405
  93.0 12.7 %mix_backward.1 = (bf16[128,768]{1,0:T(8,128)(2,1)}, bf16[128,768]{1,0:T(8,128)(2,1)}, bf16[128,768]{1,0:T(8,128)(2,1)}, bf16[128,768]{1,0:T(8,128)(2,1)}, bf16[...) custom-call(s32[1]{0:T(128)} %bitcast.me_ref, ...), custom_call_target="tpu_custom_call" | custom-call | flops 4831838208 | bytes 17301504 | tf_op jit(solution)/shard_map/mix_backward/pallas_call | solution.py:370
  107.8 3.1 %collective-permute-start.19 = (bf16[128,768]{1,0:T(8,128)(2,1)}, bf16[128,768]{1,0:T(8,128)(2,1)S(1)}, u32[]{:S(2)}, u32[]{:S(2)}) collective-permute-start(bf16[128,768]{1,0:T(8,128)(2,1)} %get-tuple-element.170), channel_id=1, source_target_pairs={{0,12},{2,14},{4,8},{6,10},{8,4},{10,6},{12,0},{14,2},{1,13},{3,15... | collective-permute-start | bytes 589832 | tf_op jit(solution)/shard_map/ppermute | solution.py:405
  112.3 4.9 %collective-permute-done.19.refs_6_ = bf16[128,768]{1,0:T(8,128)(2,1)S(1)} collective-permute-done((bf16[128,768]{1,0:T(8,128)(2,1)}, bf16[128,768]{1,0:T(8,128)(2,1)S(1)}, u32[]{:S(2)}, u32[]{:S(2)}) %collective-permute-start.19) | collective-permute-done | bytes 196640 | tf_op jit(solution)/shard_map/ppermute | solution.py:405
  122.4 14.5 %collective-permute-done.13.refs_1_ = bf16[128,768]{1,0:T(8,128)(2,1)} collective-permute-done((bf16[128,768]{1,0:T(8,128)(2,1)}, bf16[128,768]{1,0:T(8,128)(2,1)}, u32[]{:S(2)}, u32[]{:S(2)}) %collective-permute-start.13) | collective-permute-done | bytes 196640 | tf_op jit(solution)/shard_map/ppermute | solution.py:405
  136.9 4.8 %collective-permute-start.26 = (bf16[128,768]{1,0:T(8,128)(2,1)}, bf16[128,768]{1,0:T(8,128)(2,1)}, u32[]{:S(2)}, u32[]{:S(2)}) collective-permute-start(bf16[128,768]{1,0:T(8,128)(2,1)} %get-tuple-element.194), channel_id=1, source_target_pairs={{0,8},{2,10},{4,12},{6,14},{8,0},{10,2},{12,4},{14,6},{1,9},{3,11}... | collective-permute-start | bytes 589832 | tf_op jit(solution)/shard_map/ppermute | solution.py:405
  147.2 6.2 %collective-permute-done.26.refs_4_ = bf16[128,768]{1,0:T(8,128)(2,1)} collective-permute-done((bf16[128,768]{1,0:T(8,128)(2,1)}, bf16[128,768]{1,0:T(8,128)(2,1)}, u32[]{:S(2)}, u32[]{:S(2)}) %collective-permute-start.26) | collective-permute-done | bytes 196640 | tf_op jit(solution)/shard_map/ppermute | solution.py:405
  154.2 4.9 %collective-permute-done.27.refs_2_ = bf16[128,768]{1,0:T(8,128)(2,1)S(1)} collective-permute-done((bf16[128,768]{1,0:T(8,128)(2,1)}, bf16[128,768]{1,0:T(8,128)(2,1)S(1)}, u32[]{:S(2)}, u32[]{:S(2)}) %collective-permute-start.27) | collective-permute-done | bytes 196640 | tf_op jit(solution)/shard_map/ppermute | solution.py:405
  168.9 5.5 %collective-permute-done.30.refs_5_ = bf16[128,768]{1,0:T(8,128)(2,1)S(1)} collective-permute-done((bf16[128,768]{1,0:T(8,128)(2,1)}, bf16[128,768]{1,0:T(8,128)(2,1)S(1)}, u32[]{:S(2)}, u32[]{:S(2)}) %collective-permute-start.30) | collective-permute-done | bytes 196640 | tf_op jit(solution)/shard_map/ppermute | solution.py:405
  176.5 9.1 %collective-permute-done.31.refs_3_ = bf16[128,768]{1,0:T(8,128)(2,1)S(1)} collective-permute-done((bf16[128,768]{1,0:T(8,128)(2,1)}, bf16[128,768]{1,0:T(8,128)(2,1)S(1)}, u32[]{:S(2)}, u32[]{:S(2)}) %collective-permute-start.31) | collective-permute-done | bytes 196640 | tf_op jit(solution)/shard_map/ppermute | solution.py:405
  189.4 3.2 %to_cells.2 = bf16[4,2,180,768]{3,2,1,0:T(8,128)(2,1)S(1)} custom-call(s32[1]{0:T(128)} %bitcast.me_ref, bf16[180,128]{1,0:T(8,128)(2,1)S(1)} %copy-done.5, bf16[4,2,180,768]{3,2,1,0:T(8,128)(2,1)S(1)} %copy.23.cells_ref.base_ref, bf16[128,768]{1,0:T(8,128)(2,1)} %get-tuple-element.150.refs_0_, bf16[128,768]{1,0:T(8,128)(2,1)} %collective-permute-done.13.refs_1_, ...), custom_call_target="tpu_custom_call" | custom-call | flops 283115520 | bytes 5996544 | tf_op jit(solution)/shard_map/to_cells/pallas_call | solution.py:183
  192.6 3.1 %copy.25 = bf16[4,2,180,768]{3,1,2,0:T(2,128)(2,1)} copy(bf16[4,2,180,768]{3,2,1,0:T(8,128)(2,1)S(1)} %to_cells.2) | data formatting | bytes 4423680
  198.7 3.0 %to_cells.3 = bf16[4,2,180,768]{3,2,1,0:T(8,128)(2,1)S(1)} custom-call(s32[1]{0:T(128)} %bitcast.me_ref, bf16[180,128]{1,0:T(8,128)(2,1)S(1)} %copy-done.4, bf16[4,2,180,768]{3,2,1,0:T(8,128)(2,1)S(1)} %copy-done.1, bf16[128,768]{1,0:T(8,128)(2,1)} %get-tuple-element.184.refs_0_, bf16[128,768]{1,0:T(8,128)(2,1)} %copy-done.20, bf16[128,768]{1,0:T(8,128)(2,1)} %copy-done.16, ...), custom_call_target="tpu_custom_call" | custom-call | flops 283115520 | bytes 5996544 | tf_op jit(solution)/shard_map/to_cells/pallas_call | solution.py:183
  201.7 3.1 %copy.26 = bf16[4,2,180,768]{3,1,2,0:T(2,128)(2,1)} copy(bf16[4,2,180,768]{3,2,1,0:T(8,128)(2,1)S(1)} %to_cells.3) | data formatting | bytes 4423680
  (153 shorter events, 63.6 us)
Async XLA Ops:
  5.0 15.2 %collective-permute-start.3 = (bf16[128,768]{1,0:T(8,128)(2,1)}, bf16[128,768]{1,0:T(8,128)(2,1)S(1)}, u32[]{:S(2)}, u32[]{:S(2)}) collective-permute-start(bf16[128,768]{1,0:T(8,128)(2,1)} %get-tuple-element.128), channel_id=1, source_target_pairs={{0,8},{2,10},{4,12},{6,14},{8,0},{10,2},{12,4},{14,6},{1,9},{3,11}... | collective-permute-start | bytes 589832 | tf_op jit(solution)/shard_map/ppermute | solution.py:405
  9.1 12.1 %collective-permute-start.2 = (bf16[128,768]{1,0:T(8,128)(2,1)}, bf16[128,768]{1,0:T(8,128)(2,1)S(1)}, u32[]{:S(2)}, u32[]{:S(2)}) collective-permute-start(bf16[128,768]{1,0:T(8,128)(2,1)} %get-tuple-element.126), channel_id=1, source_target_pairs={{0,4},{2,6},{4,0},{6,2},{8,12},{10,14},{12,8},{14,10},{1,5},{3,7},... | collective-permute-start | bytes 589832 | tf_op jit(solution)/shard_map/ppermute | solution.py:405
  10.7 18.4 %collective-permute-start = (bf16[128,768]{1,0:T(8,128)(2,1)}, bf16[128,768]{1,0:T(8,128)(2,1)S(1)}, u32[]{:S(2)}, u32[]{:S(2)}) collective-permute-start(bf16[128,768]{1,0:T(8,128)(2,1)} %get-tuple-element.124), channel_id=1, source_target_pairs={{0,10},{2,8},{4,14},{6,12},{8,2},{10,0},{12,6},{14,4},{1,11},{3,9}... | collective-permute-start | bytes 589832 | tf_op jit(solution)/shard_map/ppermute | solution.py:405
  20.1 13.8 %collective-permute-start.4 = (bf16[128,768]{1,0:T(8,128)(2,1)}, bf16[128,768]{1,0:T(8,128)(2,1)S(1)}, u32[]{:S(2)}, u32[]{:S(2)}) collective-permute-start(bf16[128,768]{1,0:T(8,128)(2,1)} %get-tuple-element.129), channel_id=1, source_target_pairs={{0,6},{2,4},{4,2},{6,0},{8,14},{10,12},{12,10},{14,8},{1,7},{3,5},... | collective-permute-start | bytes 589832 | tf_op jit(solution)/shard_map/ppermute | solution.py:405
  21.1 18.7 %collective-permute-start.5 = (bf16[128,768]{1,0:T(8,128)(2,1)}, bf16[128,768]{1,0:T(8,128)(2,1)S(1)}, u32[]{:S(2)}, u32[]{:S(2)}) collective-permute-start(bf16[128,768]{1,0:T(8,128)(2,1)} %get-tuple-element.131), channel_id=1, source_target_pairs={{0,12},{2,14},{4,8},{6,10},{8,4},{10,6},{12,0},{14,2},{1,13},{3,15... | collective-permute-start | bytes 589832 | tf_op jit(solution)/shard_map/ppermute | solution.py:405
  34.0 12.0 %collective-permute-start.6 = (bf16[128,768]{1,0:T(8,128)(2,1)}, bf16[128,768]{1,0:T(8,128)(2,1)}, u32[]{:S(2)}, u32[]{:S(2)}) collective-permute-start(bf16[128,768]{1,0:T(8,128)(2,1)} %get-tuple-element.133), channel_id=1, source_target_pairs={{0,14},{2,12},{4,10},{6,8},{8,6},{10,4},{12,2},{14,0},{1,15},{3,13... | collective-permute-start | bytes 589832 | tf_op jit(solution)/shard_map/ppermute | solution.py:405
  39.8 18.7 %collective-permute-start.7 = (bf16[128,768]{1,0:T(8,128)(2,1)}, bf16[128,768]{1,0:T(8,128)(2,1)S(1)}, u32[]{:S(2)}, u32[]{:S(2)}) collective-permute-start(bf16[128,768]{1,0:T(8,128)(2,1)} %get-tuple-element.145), channel_id=1, source_target_pairs={{0,8},{2,10},{4,12},{6,14},{8,0},{10,2},{12,4},{14,6},{1,9},{3,11}... | collective-permute-start | bytes 589832 | tf_op jit(solution)/shard_map/ppermute | solution.py:405
  40.6 18.2 %collective-permute-start.8 = (bf16[128,768]{1,0:T(8,128)(2,1)}, bf16[128,768]{1,0:T(8,128)(2,1)}, u32[]{:S(2)}, u32[]{:S(2)}) collective-permute-start(bf16[128,768]{1,0:T(8,128)(2,1)} %get-tuple-element.147), channel_id=1, source_target_pairs={{0,4},{2,6},{4,0},{6,2},{8,12},{10,14},{12,8},{14,10},{1,5},{3,7},... | collective-permute-start | bytes 589832 | tf_op jit(solution)/shard_map/ppermute | solution.py:405
  46.0 27.7 %collective-permute-start.9 = (bf16[128,768]{1,0:T(8,128)(2,1)}, bf16[128,768]{1,0:T(8,128)(2,1)S(1)}, u32[]{:S(2)}, u32[]{:S(2)}) collective-permute-start(bf16[128,768]{1,0:T(8,128)(2,1)} %get-tuple-element.149), channel_id=1, source_target_pairs={{0,10},{2,8},{4,14},{6,12},{8,2},{10,0},{12,6},{14,4},{1,11},{3,9}... | collective-permute-start | bytes 589832 | tf_op jit(solution)/shard_map/ppermute | solution.py:405
  58.6 12.2 %collective-permute-start.10 = (bf16[128,768]{1,0:T(8,128)(2,1)}, bf16[128,768]{1,0:T(8,128)(2,1)S(1)}, u32[]{:S(2)}, u32[]{:S(2)}) collective-permute-start(bf16[128,768]{1,0:T(8,128)(2,1)} %get-tuple-element.155), channel_id=1, source_target_pairs={{0,6},{2,4},{4,2},{6,0},{8,14},{10,12},{12,10},{14,8},{1,7},{3,5},... | collective-permute-start | bytes 589832 | tf_op jit(solution)/shard_map/ppermute | solution.py:405
  58.8 17.8 %collective-permute-start.16 = (bf16[128,768]{1,0:T(8,128)(2,1)}, bf16[128,768]{1,0:T(8,128)(2,1)S(1)}, u32[]{:S(2)}, u32[]{:S(2)}) collective-permute-start(bf16[128,768]{1,0:T(8,128)(2,1)} %get-tuple-element.166), channel_id=1, source_target_pairs={{0,12},{2,14},{4,8},{6,10},{8,4},{10,6},{12,0},{14,2},{1,13},{3,15... | collective-permute-start | bytes 589832 | tf_op jit(solution)/shard_map/ppermute | solution.py:405
  73.7 18.0 %collective-permute-start.14 = (bf16[128,768]{1,0:T(8,128)(2,1)S(1)}, bf16[128,768]{1,0:T(8,128)(2,1)}, u32[]{:S(2)}, u32[]{:S(2)}) collective-permute-start(bf16[128,768]{1,0:T(8,128)(2,1)S(1)} %copy-done.25), channel_id=1, source_target_pairs={{0,2},{2,0},{4,6},{6,4},{8,10},{10,8},{12,14},{14,12},{1,3},{3,1},... | collective-permute-start | bytes 589832 | tf_op jit(solution)/shard_map/ppermute | solution.py:405
  77.3 14.4 %collective-permute-start.17 = (bf16[128,768]{1,0:T(8,128)(2,1)}, bf16[128,768]{1,0:T(8,128)(2,1)S(1)}, u32[]{:S(2)}, u32[]{:S(2)}) collective-permute-start(bf16[128,768]{1,0:T(8,128)(2,1)} %get-tuple-element.167), channel_id=1, source_target_pairs={{0,8},{2,10},{4,12},{6,14},{8,0},{10,2},{12,4},{14,6},{1,9},{3,11}... | collective-permute-start | bytes 589832 | tf_op jit(solution)/shard_map/ppermute | solution.py:405
  81.3 24.4 %collective-permute-start.12 = (bf16[128,768]{1,0:T(8,128)(2,1)}, bf16[128,768]{1,0:T(8,128)(2,1)S(1)}, u32[]{:S(2)}, u32[]{:S(2)}) collective-permute-start(bf16[128,768]{1,0:T(8,128)(2,1)} %get-tuple-element.157), channel_id=1, source_target_pairs={{0,10},{2,8},{4,14},{6,12},{8,2},{10,0},{12,6},{14,4},{1,11},{3,9}... | collective-permute-start | bytes 589832 | tf_op jit(solution)/shard_map/ppermute | solution.py:405
  91.7 14.0 %collective-permute-start.15 = (bf16[128,768]{1,0:T(8,128)(2,1)}, bf16[128,768]{1,0:T(8,128)(2,1)S(1)}, u32[]{:S(2)}, u32[]{:S(2)}) collective-permute-start(bf16[128,768]{1,0:T(8,128)(2,1)} %get-tuple-element.162), channel_id=1, source_target_pairs={{0,4},{2,6},{4,0},{6,2},{8,12},{10,14},{12,8},{14,10},{1,5},{3,7},... | collective-permute-start | bytes 589832 | tf_op jit(solution)/shard_map/ppermute | solution.py:405
  91.7 15.4 %collective-permute-start.18 = (bf16[128,768]{1,0:T(8,128)(2,1)}, bf16[128,768]{1,0:T(8,128)(2,1)S(1)}, u32[]{:S(2)}, u32[]{:S(2)}) collective-permute-start(bf16[128,768]{1,0:T(8,128)(2,1)} %get-tuple-element.168), channel_id=1, source_target_pairs={{0,6},{2,4},{4,2},{6,0},{8,14},{10,12},{12,10},{14,8},{1,7},{3,5},... | collective-permute-start | bytes 589832 | tf_op jit(solution)/shard_map/ppermute | solution.py:405
  117.2 24.4 %collective-permute-start.22 = (f32[128,768]{1,0:T(8,128)S(1)}, f32[128,768]{1,0:T(8,128)}, u32[]{:S(2)}, u32[]{:S(2)}) collective-permute-start(f32[128,768]{1,0:T(8,128)S(1)} %dynamic-slice_bitcast_fusion.1), channel_id=1, source_target_pairs={{0,2},{2,0},{4,6},{6,4},{8,10},{10,8},{12,14},{14,12},{1,3},{3,1},... | collective-permute-start | bytes 1179656 | tf_op jit(solution)/shard_map/ppermute | solution.py:405
  119.4 17.5 %collective-permute-start.13 = (bf16[128,768]{1,0:T(8,128)(2,1)}, bf16[128,768]{1,0:T(8,128)(2,1)}, u32[]{:S(2)}, u32[]{:S(2)}) collective-permute-start(bf16[128,768]{1,0:T(8,128)(2,1)} %get-tuple-element.158), channel_id=1, source_target_pairs={{0,2},{2,0},{4,6},{6,4},{8,10},{10,8},{12,14},{14,12},{1,3},{3,1},... | collective-permute-start | bytes 589832 | tf_op jit(solution)/shard_map/ppermute | solution.py:405
  120.1 24.7 %collective-permute-start.20 = (bf16[128,768]{1,0:T(8,128)(2,1)}, bf16[128,768]{1,0:T(8,128)(2,1)}, u32[]{:S(2)}, u32[]{:S(2)}) collective-permute-start(bf16[128,768]{1,0:T(8,128)(2,1)} %get-tuple-element.172), channel_id=1, source_target_pairs={{0,14},{2,12},{4,10},{6,8},{8,6},{10,4},{12,2},{14,0},{1,15},{3,13... | collective-permute-start | bytes 589832 | tf_op jit(solution)/shard_map/ppermute | solution.py:405
  136.9 16.4 %collective-permute-start.26 = (bf16[128,768]{1,0:T(8,128)(2,1)}, bf16[128,768]{1,0:T(8,128)(2,1)}, u32[]{:S(2)}, u32[]{:S(2)}) collective-permute-start(bf16[128,768]{1,0:T(8,128)(2,1)} %get-tuple-element.194), channel_id=1, source_target_pairs={{0,8},{2,10},{4,12},{6,14},{8,0},{10,2},{12,4},{14,6},{1,9},{3,11}... | collective-permute-start | bytes 589832 | tf_op jit(solution)/shard_map/ppermute | solution.py:405
  174.4 11.2 %collective-permute-start.31 = (bf16[128,768]{1,0:T(8,128)(2,1)}, bf16[128,768]{1,0:T(8,128)(2,1)S(1)}, u32[]{:S(2)}, u32[]{:S(2)}) collective-permute-start(bf16[128,768]{1,0:T(8,128)(2,1)} %get-tuple-element.201), channel_id=1, source_target_pairs={{0,6},{2,4},{4,2},{6,0},{8,14},{10,12},{12,10},{14,8},{1,7},{3,5},... | collective-permute-start | bytes 589832 | tf_op jit(solution)/shard_map/ppermute | solution.py:405
  174.4 12.4 %collective-permute-start.33 = (bf16[128,768]{1,0:T(8,128)(2,1)}, bf16[128,768]{1,0:T(8,128)(2,1)S(1)}, u32[]{:S(2)}, u32[]{:S(2)}) collective-permute-start(bf16[128,768]{1,0:T(8,128)(2,1)} %get-tuple-element.204), channel_id=1, source_target_pairs={{0,12},{2,14},{4,8},{6,10},{8,4},{10,6},{12,0},{14,2},{1,13},{3,15... | collective-permute-start | bytes 589832 | tf_op jit(solution)/shard_map/ppermute | solution.py:405
  185.6 19.2 %collective-permute-start.37 = (bf16[2,4,32,768]{3,2,1,0:T(8,128)(2,1)S(1)}, bf16[2,4,32,768]{3,2,1,0:T(8,128)(2,1)S(1)}, u32[]{:S(2)}, u32[]{:S(2)}) collective-permute-start(bf16[2,4,32,768]{3,2,1,0:T(8,128)(2,1)S(1)} %pad_maximum_fusion.half_ref), channel_id=1, source_target_pairs={{0,1},{1,0},{2,3},{3,2},{4,5},{5,4},{6,7},{7,6},{8,9},{9,8},{10,11... | collective-permute-start | bytes 1179656 | tf_op jit(solution)/shard_map/ppermute | solution.py:405
  185.6 11.7 %collective-permute-start.29 = (bf16[128,768]{1,0:T(8,128)(2,1)}, bf16[128,768]{1,0:T(8,128)(2,1)S(1)}, u32[]{:S(2)}, u32[]{:S(2)}) collective-permute-start(bf16[128,768]{1,0:T(8,128)(2,1)} %get-tuple-element.197), channel_id=1, source_target_pairs={{0,2},{2,0},{4,6},{6,4},{8,10},{10,8},{12,14},{14,12},{1,3},{3,1},... | collective-permute-start | bytes 589832 | tf_op jit(solution)/shard_map/ppermute | solution.py:405
  (51 other events, 546.5 us)

commit v9 on v8

--- a/solution.py
+++ b/solution.py
@@ -12,10 +12,8 @@
 
 KW = 64
 shrink_level = 0.05
-DEPTH = 3
-DEPTH_LATE = 4
-BESIDE = (3, 3)
-STEPS_AHEAD = (0, 0, 1, 3, 5, 6)
+FIRST = 4
+HELD = 5
 MIB = 1024 * 1024
 
 
@@ -409,17 +407,6 @@
     return lax.optimization_barrier((values, tuple(arrived)))[0]
 
 
-class Chain:
-    def __init__(self):
-        self.arrived = []
-
-    def swap(self, values, axis, distance, depth):
-        if len(self.arrived) >= depth:
-            values = waiting(values, self.arrived[-depth:][:1])
-        self.arrived.append(swap_with(values, axis, distance))
-        return self.arrived[-1]
-
-
 def mixed_order(size):
     far = list(range(size // 2, size))
     near = [offset for offset in (2, 3, 1) if offset < size // 2]
@@ -436,48 +423,42 @@
 
 
 class GroupSum:
-    def __init__(self, chain, sums):
-        self.chain = chain
+    def __init__(self, sums):
         self.lanes = sums.shape[-1]
         self.side = lax.axis_index("dp")
         self.me = lax.axis_index("space")
         self.count = lax.axis_size("space") // 2
         self.held = sums.reshape(-1, self.lanes)
 
-    def swap(self, values, axis, distance):
-        return self.chain.swap(values, axis, distance, DEPTH_LATE)
-
     def halve(self, axis, distance, bit):
         pair = self.held.reshape(2, -1, self.lanes)
-        given = pick(pair, 1 - bit)
-        self.held = pick(pair, bit) + self.swap(given, axis, distance)
+        taken = swap_with(pick(pair, 1 - bit), axis, distance)
+        self.held = pick(pair, bit) + taken
+        return taken
 
     def over_dp(self):
-        self.halve("dp", 1, self.side)
+        return self.halve("dp", 1, self.side)
 
     def over_next(self):
-        self.halve("space", 1, self.me % 2)
-
-    def scatter(self):
-        shares = self.held.reshape(self.count, -1, self.lanes)
+        return self.halve("space", 1, self.me % 2)
+
+    def scatter(self, arrived):
+        shares = waiting(self.held, arrived).reshape(self.count, -1, self.lanes)
         place = self.me // 2
         total = pick(shares, place)
         for offset in range(1, self.count):
             given = pick(shares, place ^ offset).astype(jnp.bfloat16)
-            total += self.swap(given, "space", 2 * offset).astype(jnp.float32)
+            total += swap_with(given, "space", 2 * offset).astype(jnp.float32)
         self.total = total.astype(jnp.bfloat16)
 
-    def gather(self):
-        taken = [self.total]
+    def gather(self, arrived):
+        total = waiting(self.total, arrived)
+        taken = [total]
         for offset in range(1, self.count):
-            taken.append(self.swap(self.total, "space", 2 * offset))
-        self.quarter = jnp.stack(taken)
-
-    def gather_next(self):
-        self.half = jnp.stack([self.quarter, self.swap(self.quarter, "space", 1)])
-
-    def gather_dp(self):
-        self.other = self.swap(self.half, "dp", 1)
+            taken.append(swap_with(total, "space", 2 * offset))
+        quarter = jnp.stack(taken)
+        half = jnp.stack([quarter, swap_with(quarter, "space", 1)])
+        return half, swap_with(half, "dp", 1)
 
 
 def finish_kernel(factor, me_ref, half_ref, other_ref, *out_refs):
@@ -528,11 +509,9 @@
 
     order = mixed_order(owners)
 
-    chain = Chain()
-
-    def send(blocks, offsets, taken, depth):
+    def send(blocks, offsets, taken):
         for offset in offsets:
-            taken[offset] = chain.swap(blocks[offset], "space", offset, depth)
+            taken[offset] = swap_with(blocks[offset], "space", offset)
 
     def send_all(spectrum):
         spectrum = spectrum.reshape(samples, rows, owners, 2 * modes, channels)
@@ -579,41 +558,46 @@
         return (output, grad_fields) + tuple(grads)
 
     gathered, cot_gathered = {0: spectrum[0]}, {0: cot_spec[0]}
-    image_band, grad_band = {}, {}
-    send(spectrum, order, gathered, DEPTH)
-    send(cot_spec, order, cot_gathered, DEPTH)
+    send(spectrum, order, gathered)
     gathered = [gathered[offset] for offset in range(owners)]
     image, state = forward_mid(me, lat, lat.T, gathered, w1, b1, w2, b2)
-    image, state = waiting((image, state), [cot_gathered[offset] for offset in order[:BESIDE[0]]])
-    image_band[0] = image[0]
-    send(image, order, image_band, DEPTH)
+    cot_spec, image = list(cot_spec), list(image)
+    send(cot_spec, order[:FIRST], cot_gathered)
+    cot_spec, image = waiting((cot_spec, image), [image[0]])
+    send(cot_spec, order[FIRST:], cot_gathered)
+
+    image_band = {0: image[0]}
+    send(image, order, image_band)
     cot_gathered = [cot_gathered[offset] for offset in range(owners)]
     grad_image, sums = backward_mid(
         me, lat, lat.T, cot_gathered, w1, b1, w2, b2, state, count
     )
-    grad_image, sums = waiting(
-        (grad_image, sums), [image_band[offset] for offset in order[:BESIDE[1]]]
-    )
-    grad_band[0] = grad_image[0]
-    group_sum = GroupSum(chain, sums)
-    steps = [
-        group_sum.over_dp, group_sum.over_next, group_sum.scatter,
-        group_sum.gather, group_sum.gather_next, group_sum.gather_dp,
-    ]
-    for place, offset in enumerate(order):
-        for _ in range(STEPS_AHEAD.count(place)):
-            steps.pop(0)()
-        send(grad_image, [offset], grad_band, DEPTH_LATE)
-    for step in steps:
-        step()
+    early = [image_band[offset] for offset in order[:HELD]]
+    late = [image_band[offset] for offset in order[HELD:]]
+    grad_image, sums = waiting((list(grad_image), sums), early)
+    group_sum = GroupSum(sums)
+    over_dp = group_sum.over_dp()
+    group_sum.held = waiting(group_sum.held, late[:1])
+    over_next = group_sum.over_next()
+    grad_band = {0: grad_image[0]}
+    send(grad_image, order[:2], grad_band)
+    grad_image = waiting(grad_image, late)
+    send(grad_image, order[2:4], grad_band)
+    grad_image = waiting(grad_image, [over_dp])
+    send(grad_image, order[4:5], grad_band)
+    grad_image = waiting(grad_image, [over_next])
+    send(grad_image, order[5:], grad_band)
+    arrived = [grad_band[offset] for offset in order]
     image_band = [image_band[offset] for offset in range(owners)]
     grad_band = [grad_band[offset] for offset in range(owners)]
     output = to_cells(me, scaled.T, image_band, fields)
+    group_sum.scatter(arrived)
+    half, other = group_sum.gather([output])
     grad_fields = to_cells(me, plain.T, grad_band, cotangent)
     place = lax.axis_index("space")
     here = jnp.stack([lax.axis_index("dp"), place % 2, place // 2]).astype(jnp.int32)
     grads = finish_sums(
-        here, group_sum.half, group_sum.other, factor, w_first.shape, b_first.shape
+        here, half, other, factor, w_first.shape, b_first.shape
     )
     return (output, grad_fields) + tuple(grads)
 

time: 208 us -> 201 us (0.966)
  waiting for transfers between devices: 76.5 us -> 46.2 us
  starting transfers between devices: 75.3 us -> 97.2 us
    ppermute x38, waiting for transfers between devices: 76.5 us -> 46.2 us  [swap_with(): return lax.ppermute(values, axis, pairs)]
    ppermute x38, starting transfers between devices: 75.3 us -> 97.2 us  [swap_with(): return lax.ppermute(values, axis, pairs)]
    unnamed x77 -> x61, local copies, waits for them, and re-layouts: 13.7 us -> 13.2 us
  transfers between devices with their start and end apart: 38 -> 38, of which waited for: 17 -> 14; matrix products, arithmetic and copies ran while one was open for 5% -> 6% of each run, Pallas kernels for 15% -> 16%
where the time goes in v9:
time: 201 us
  starting transfers between devices  97.2 us (48%)
  waiting for transfers between devices  46.2 us (23%)
  Pallas kernels  36 us (18%)
  local copies, waits for them, and re-layouts  17.5 us (9%)
  other arithmetic  2.67 us (1%)
    ppermute x38, starting transfers between devices, swap_with(): return lax.ppermute(values, axis, pairs)  97.2 us
    ppermute x38, waiting for transfers between devices, swap_with(): return lax.ppermute(values, axis, pairs)  46.2 us
    unnamed x61, local copies, waits for them, and re-layouts  13.2 us
    pallas_call x1, Pallas kernels, backward_mid(): pl.pallas_call(functools.partial(backward_kernel, size_of_block, len(band...  12.8 us
    pallas_call x1, Pallas kernels, forward_mid(): pl.pallas_call(functools.partial(forward_kernel, len(bands)), grid_spec=p...  7.55 us
    pallas_call x2, Pallas kernels, to_cells(): pl.pallas_call(to_cells_kernel, grid_spec=pltpu.PrefetchScalarGridSpec(nu...  6.14 us
    pallas_call x2, Pallas kernels, to_modes(): pl.pallas_call(to_modes_kernel, grid_spec=pltpu.PrefetchScalarGridSpec(nu...  4.78 us
  transfers between devices with their start and end apart: 38, of which 14 were waited for; matrix products, arithmetic and copies ran while one was open for 6% of the time, Pallas kernels for 16%

profile of v9, /device:TPU:0, one launch (start us, length us, event | category | flops | bytes accessed | tf_op | source)
XLA Modules:
  0.0 200.7 jit_solution(13057705293615126019)
XLA Ops:
  10.9 3.0 %collective-permute-start.3 = (bf16[128,768]{1,0:T(8,128)(2,1)}, bf16[128,768]{1,0:T(8,128)(2,1)S(1)}, u32[]{:S(2)}, u32[]{:S(2)}) collective-permute-start(bf16[128,768]{1,0:T(8,128)(2,1)} %get-tuple-element.115), channel_id=1, source_target_pairs={{0,8},{2,10},{4,12},{6,14},{8,0},{10,2},{12,4},{14,6},{1,9},{3,11}... | collective-permute-start | bytes 589832 | tf_op jit(solution)/shard_map/ppermute | solution.py:403
  15.2 3.6 %collective-permute-start.5 = (bf16[128,768]{1,0:T(8,128)(2,1)}, bf16[128,768]{1,0:T(8,128)(2,1)}, u32[]{:S(2)}, u32[]{:S(2)}) collective-permute-start(bf16[128,768]{1,0:T(8,128)(2,1)} %get-tuple-element.117), channel_id=1, source_target_pairs={{0,12},{2,14},{4,8},{6,10},{8,4},{10,6},{12,0},{14,2},{1,13},{3,15... | collective-permute-start | bytes 589832 | tf_op jit(solution)/shard_map/ppermute | solution.py:403
  18.8 6.2 %collective-permute-done.1.refs_2_ = bf16[128,768]{1,0:T(8,128)(2,1)S(1)} collective-permute-done((bf16[128,768]{1,0:T(8,128)(2,1)}, bf16[128,768]{1,0:T(8,128)(2,1)S(1)}, u32[]{:S(2)}, u32[]{:S(2)}) %collective-permute-start.1) | collective-permute-done | bytes 196640 | tf_op jit(solution)/shard_map/ppermute | solution.py:403
  34.5 4.5 %collective-permute-start.16 = (bf16[128,768]{1,0:T(8,128)(2,1)}, bf16[128,768]{1,0:T(8,128)(2,1)S(1)}, u32[]{:S(2)}, u32[]{:S(2)}) collective-permute-start(bf16[128,768]{1,0:T(8,128)(2,1)} %get-tuple-element.102), channel_id=1, source_target_pairs={{0,6},{2,4},{4,2},{6,0},{8,14},{10,12},{12,10},{14,8},{1,7},{3,5},... | collective-permute-start | bytes 589832 | tf_op jit(solution)/shard_map/ppermute | solution.py:403
  39.1 3.2 %collective-permute-done.4.refs_5_ = bf16[128,768]{1,0:T(8,128)(2,1)S(1)} collective-permute-done((bf16[128,768]{1,0:T(8,128)(2,1)}, bf16[128,768]{1,0:T(8,128)(2,1)S(1)}, u32[]{:S(2)}, u32[]{:S(2)}) %collective-permute-start.4) | collective-permute-done | bytes 196640 | tf_op jit(solution)/shard_map/ppermute | solution.py:403
  42.9 12.7 %collective-permute-start.18 = (bf16[128,768]{1,0:T(8,128)(2,1)}, bf16[128,768]{1,0:T(8,128)(2,1)}, u32[]{:S(2)}, u32[]{:S(2)}) collective-permute-start(bf16[128,768]{1,0:T(8,128)(2,1)} %get-tuple-element.104), channel_id=1, source_target_pairs={{0,10},{2,8},{4,14},{6,12},{8,2},{10,0},{12,6},{14,4},{1,11},{3,9}... | collective-permute-start | bytes 589832 | tf_op jit(solution)/shard_map/ppermute | solution.py:403
  55.7 7.5 %mix_forward.1 = (bf16[128,768]{1,0:T(8,128)(2,1)}, bf16[128,768]{1,0:T(8,128)(2,1)}, bf16[128,768]{1,0:T(8,128)(2,1)}, bf16[128,768]{1,0:T(8,128)(2,1)}, bf16[1...) custom-call(s32[1]{0:T(128)} %bitcast.me_ref, ...), custom_call_target="tpu_custom_call" | custom-call | flops 2415919104 | bytes 17301504 | tf_op jit(solution)/shard_map/mix_forward/pallas_call | solution.py:330
  63.9 4.8 %collective-permute-start.20 = (bf16[128,768]{1,0:T(8,128)(2,1)S(1)}, bf16[128,768]{1,0:T(8,128)(2,1)}, u32[]{:S(2)}, u32[]{:S(2)}) collective-permute-start(bf16[128,768]{1,0:T(8,128)(2,1)S(1)} %copy-done.23), channel_id=1, source_target_pairs={{0,14},{2,12},{4,10},{6,8},{8,6},{10,4},{12,2},{14,0},{1,15},{3,13... | collective-permute-start | bytes 589832 | tf_op jit(solution)/shard_map/ppermute | solution.py:403
  68.7 7.3 %collective-permute-start.8 = (bf16[128,768]{1,0:T(8,128)(2,1)}, bf16[128,768]{1,0:T(8,128)(2,1)S(1)}, u32[]{:S(2)}, u32[]{:S(2)}) collective-permute-start(bf16[128,768]{1,0:T(8,128)(2,1)} %get-tuple-element.129), channel_id=1, source_target_pairs={{0,4},{2,6},{4,0},{6,2},{8,12},{10,14},{12,8},{14,10},{1,5},{3,7},... | collective-permute-start | bytes 589832 | tf_op jit(solution)/shard_map/ppermute | solution.py:403
  79.1 3.3 %collective-permute-start.10 = (bf16[128,768]{1,0:T(8,128)(2,1)}, bf16[128,768]{1,0:T(8,128)(2,1)S(1)}, u32[]{:S(2)}, u32[]{:S(2)}) collective-permute-start(bf16[128,768]{1,0:T(8,128)(2,1)} %get-tuple-element.131), channel_id=1, source_target_pairs={{0,8},{2,10},{4,12},{6,14},{8,0},{10,2},{12,4},{14,6},{1,9},{3,11}... | collective-permute-start | bytes 589832 | tf_op jit(solution)/shard_map/ppermute | solution.py:403
  88.1 12.8 %mix_backward.1 = (bf16[128,768]{1,0:T(8,128)(2,1)}, bf16[128,768]{1,0:T(8,128)(2,1)}, bf16[128,768]{1,0:T(8,128)(2,1)}, bf16[128,768]{1,0:T(8,128)(2,1)}, bf16[...) custom-call(s32[1]{0:T(128)} %bitcast.me_ref, ...), custom_call_target="tpu_custom_call" | custom-call | flops 4831838208 | bytes 17301504 | tf_op jit(solution)/shard_map/mix_backward/pallas_call | solution.py:368
  102.7 3.3 %collective-permute-done.11.refs_5_ = bf16[128,768]{1,0:T(8,128)(2,1)S(1)} collective-permute-done((bf16[128,768]{1,0:T(8,128)(2,1)}, bf16[128,768]{1,0:T(8,128)(2,1)S(1)}, u32[]{:S(2)}, u32[]{:S(2)}) %collective-permute-start.11) | collective-permute-done | bytes 196640 | tf_op jit(solution)/shard_map/ppermute | solution.py:403
  109.1 3.7 %collective-permute-start.13 = (bf16[128,768]{1,0:T(8,128)(2,1)}, bf16[128,768]{1,0:T(8,128)(2,1)}, u32[]{:S(2)}, u32[]{:S(2)}) collective-permute-start(bf16[128,768]{1,0:T(8,128)(2,1)} %get-tuple-element.134), channel_id=1, source_target_pairs={{0,14},{2,12},{4,10},{6,8},{8,6},{10,4},{12,2},{14,0},{1,15},{3,13... | collective-permute-start | bytes 589832 | tf_op jit(solution)/shard_map/ppermute | solution.py:403
  114.3 3.7 %collective-permute-done.7.refs_1_ = bf16[128,768]{1,0:T(8,128)(2,1)S(1)} collective-permute-done((bf16[128,768]{1,0:T(8,128)(2,1)S(1)}, bf16[128,768]{1,0:T(8,128)(2,1)S(1)}, u32[]{:S(2)}, u32[]{:S(2)}) %collective-permute-start.7) | collective-permute-done | bytes 196640 | tf_op jit(solution)/shard_map/ppermute | solution.py:403
  122.0 8.4 %collective-permute-start.25 = (bf16[128,768]{1,0:T(8,128)(2,1)}, bf16[128,768]{1,0:T(8,128)(2,1)}, u32[]{:S(2)}, u32[]{:S(2)}) collective-permute-start(bf16[128,768]{1,0:T(8,128)(2,1)} %get-tuple-element.157), channel_id=1, source_target_pairs={{0,6},{2,4},{4,2},{6,0},{8,14},{10,12},{12,10},{14,8},{1,7},{3,5},... | collective-permute-start | bytes 589832 | tf_op jit(solution)/shard_map/ppermute | solution.py:403
  133.3 4.1 %collective-permute-done.22 = f32[128,768]{1,0:T(8,128)S(1)} collective-permute-done((f32[128,768]{1,0:T(8,128)}, f32[128,768]{1,0:T(8,128)S(1)}, u32[]{:S(2)}, u32[]{:S(2)}) %collective-permute-start.22) | collective-permute-done | bytes 393248 | tf_op jit(solution)/shard_map/ppermute | solution.py:403
  137.4 5.1 %collective-permute-start.28 = (bf16[128,768]{1,0:T(8,128)(2,1)}, bf16[128,768]{1,0:T(8,128)(2,1)}, u32[]{:S(2)}, u32[]{:S(2)}) collective-permute-start(bf16[128,768]{1,0:T(8,128)(2,1)} %get-tuple-element.163), channel_id=1, source_target_pairs={{0,12},{2,14},{4,8},{6,10},{8,4},{10,6},{12,0},{14,2},{1,13},{3,15... | collective-permute-start | bytes 589832 | tf_op jit(solution)/shard_map/ppermute | solution.py:403
  147.5 12.3 %collective-permute-done.26.refs_4_ = bf16[128,768]{1,0:T(8,128)(2,1)} collective-permute-done((bf16[128,768]{1,0:T(8,128)(2,1)}, bf16[128,768]{1,0:T(8,128)(2,1)}, u32[]{:S(2)}, u32[]{:S(2)}) %collective-permute-start.26) | collective-permute-done | bytes 196640 | tf_op jit(solution)/shard_map/ppermute | solution.py:403
  159.8 8.6 %collective-permute-start.30 = (bf16[32,768]{1,0:T(8,128)(2,1)S(1)}, bf16[32,768]{1,0:T(8,128)(2,1)S(1)}, u32[]{:S(2)}, u32[]{:S(2)}) collective-permute-start(bf16[32,768]{1,0:T(8,128)(2,1)S(1)} %get-tuple-element.180), channel_id=1, source_target_pairs={{0,4},{2,6},{4,0},{6,2},{8,12},{10,14},{12,8},{14,10},{1,5},{3,7},... | collective-permute-start | bytes 147464 | tf_op jit(solution)/shard_map/ppermute | solution.py:403
  171.6 3.2 %to_cells.2 = bf16[4,2,180,768]{3,2,1,0:T(8,128)(2,1)S(1)} custom-call(s32[1]{0:T(128)} %bitcast.me_ref, bf16[180,128]{1,0:T(8,128)(2,1)S(1)} %copy-done.5, bf16[4,2,180,768]{3,2,1,0:T(8,128)(2,1)S(1)} %copy-done.1, bf16[128,768]{1,0:T(8,128)(2,1)} %get-tuple-element.127.refs_0_, bf16[128,768]{1,0:T(8,128)(2,1)} %copy-done.16, bf16[128,768]{1,0:T(8,128)(2,1)} %copy-done.11, ...), custom_call_target="tpu_custom_call" | custom-call | flops 283115520 | bytes 5996544 | tf_op jit(solution)/shard_map/to_cells/pallas_call | solution.py:181
  183.9 5.2 %collective-permute-done.36 = bf16[4,32,768]{2,1,0:T(8,128)(2,1)S(1)} collective-permute-done((bf16[4,32,768]{2,1,0:T(8,128)(2,1)S(1)}, bf16[4,32,768]{2,1,0:T(8,128)(2,1)S(1)}, u32[]{:S(2)}, u32[]{:S(2)}) %collective-permute-start.36) | collective-permute-done | bytes 196640 | tf_op jit(solution)/shard_map/ppermute | solution.py:403
  189.4 3.1 %copy.25 = bf16[4,2,180,768]{3,1,2,0:T(2,128)(2,1)} copy(bf16[4,2,180,768]{3,2,1,0:T(8,128)(2,1)S(1)} %to_cells.2) | data formatting | bytes 4423680
  192.4 3.0 %to_cells.3 = bf16[4,2,180,768]{3,2,1,0:T(8,128)(2,1)S(1)} custom-call(s32[1]{0:T(128)} %bitcast.me_ref, bf16[180,128]{1,0:T(8,128)(2,1)S(1)} %copy-done.4, bf16[4,2,180,768]{3,2,1,0:T(8,128)(2,1)S(1)} %copy.20.cells_ref.base_ref, bf16[128,768]{1,0:T(8,128)(2,1)} %get-tuple-element.148.refs_0_, bf16[128,768]{1,0:T(8,128)(2,1)} %collective-permute-done.23.refs_1_, ...), custom_call_target="tpu_custom_call" | custom-call | flops 283115520 | bytes 5996544 | tf_op jit(solution)/shard_map/to_cells/pallas_call | solution.py:181
  195.4 3.1 %copy.26 = bf16[4,2,180,768]{3,1,2,0:T(2,128)(2,1)} copy(bf16[4,2,180,768]{3,2,1,0:T(8,128)(2,1)S(1)} %to_cells.3) | data formatting | bytes 4423680
  (137 shorter events, 63.9 us)
Async XLA Ops:
  9.3 15.7 %collective-permute-start.1 = (bf16[128,768]{1,0:T(8,128)(2,1)}, bf16[128,768]{1,0:T(8,128)(2,1)S(1)}, u32[]{:S(2)}, u32[]{:S(2)}) collective-permute-start(bf16[128,768]{1,0:T(8,128)(2,1)} %get-tuple-element.113), channel_id=1, source_target_pairs={{0,4},{2,6},{4,0},{6,2},{8,12},{10,14},{12,8},{14,10},{1,5},{3,7},... | collective-permute-start | bytes 589832 | tf_op jit(solution)/shard_map/ppermute | solution.py:403
  10.9 22.3 %collective-permute-start.2 = (bf16[128,768]{1,0:T(8,128)(2,1)}, bf16[128,768]{1,0:T(8,128)(2,1)S(1)}, u32[]{:S(2)}, u32[]{:S(2)}) collective-permute-start(bf16[128,768]{1,0:T(8,128)(2,1)} %get-tuple-element.114), channel_id=1, source_target_pairs={{0,6},{2,4},{4,2},{6,0},{8,14},{10,12},{12,10},{14,8},{1,7},{3,5},... | collective-permute-start | bytes 589832 | tf_op jit(solution)/shard_map/ppermute | solution.py:403
  10.9 23.0 %collective-permute-start.3 = (bf16[128,768]{1,0:T(8,128)(2,1)}, bf16[128,768]{1,0:T(8,128)(2,1)S(1)}, u32[]{:S(2)}, u32[]{:S(2)}) collective-permute-start(bf16[128,768]{1,0:T(8,128)(2,1)} %get-tuple-element.115), channel_id=1, source_target_pairs={{0,8},{2,10},{4,12},{6,14},{8,0},{10,2},{12,4},{14,6},{1,9},{3,11}... | collective-permute-start | bytes 589832 | tf_op jit(solution)/shard_map/ppermute | solution.py:403
  13.9 28.4 %collective-permute-start.4 = (bf16[128,768]{1,0:T(8,128)(2,1)}, bf16[128,768]{1,0:T(8,128)(2,1)S(1)}, u32[]{:S(2)}, u32[]{:S(2)}) collective-permute-start(bf16[128,768]{1,0:T(8,128)(2,1)} %get-tuple-element.116), channel_id=1, source_target_pairs={{0,10},{2,8},{4,14},{6,12},{8,2},{10,0},{12,6},{14,4},{1,11},{3,9}... | collective-permute-start | bytes 589832 | tf_op jit(solution)/shard_map/ppermute | solution.py:403
  15.2 27.7 %collective-permute-start.5 = (bf16[128,768]{1,0:T(8,128)(2,1)}, bf16[128,768]{1,0:T(8,128)(2,1)}, u32[]{:S(2)}, u32[]{:S(2)}) collective-permute-start(bf16[128,768]{1,0:T(8,128)(2,1)} %get-tuple-element.117), channel_id=1, source_target_pairs={{0,12},{2,14},{4,8},{6,10},{8,4},{10,6},{12,0},{14,2},{1,13},{3,15... | collective-permute-start | bytes 589832 | tf_op jit(solution)/shard_map/ppermute | solution.py:403
  25.0 30.6 %collective-permute-start.6 = (bf16[128,768]{1,0:T(8,128)(2,1)}, bf16[128,768]{1,0:T(8,128)(2,1)}, u32[]{:S(2)}, u32[]{:S(2)}) collective-permute-start(bf16[128,768]{1,0:T(8,128)(2,1)} %get-tuple-element.118), channel_id=1, source_target_pairs={{0,14},{2,12},{4,10},{6,8},{8,6},{10,4},{12,2},{14,0},{1,15},{3,13... | collective-permute-start | bytes 589832 | tf_op jit(solution)/shard_map/ppermute | solution.py:403
  33.8 30.0 %collective-permute-start.15 = (bf16[128,768]{1,0:T(8,128)(2,1)}, bf16[128,768]{1,0:T(8,128)(2,1)S(1)}, u32[]{:S(2)}, u32[]{:S(2)}) collective-permute-start(bf16[128,768]{1,0:T(8,128)(2,1)} %get-tuple-element.101), channel_id=1, source_target_pairs={{0,4},{2,6},{4,0},{6,2},{8,12},{10,14},{12,8},{14,10},{1,5},{3,7},... | collective-permute-start | bytes 589832 | tf_op jit(solution)/shard_map/ppermute | solution.py:403
  34.5 29.4 %collective-permute-start.16 = (bf16[128,768]{1,0:T(8,128)(2,1)}, bf16[128,768]{1,0:T(8,128)(2,1)S(1)}, u32[]{:S(2)}, u32[]{:S(2)}) collective-permute-start(bf16[128,768]{1,0:T(8,128)(2,1)} %get-tuple-element.102), channel_id=1, source_target_pairs={{0,6},{2,4},{4,2},{6,0},{8,14},{10,12},{12,10},{14,8},{1,7},{3,5},... | collective-permute-start | bytes 589832 | tf_op jit(solution)/shard_map/ppermute | solution.py:403
  42.3 26.4 %collective-permute-start.17 = (bf16[128,768]{1,0:T(8,128)(2,1)}, bf16[128,768]{1,0:T(8,128)(2,1)S(1)}, u32[]{:S(2)}, u32[]{:S(2)}) collective-permute-start(bf16[128,768]{1,0:T(8,128)(2,1)} %get-tuple-element.103), channel_id=1, source_target_pairs={{0,8},{2,10},{4,12},{6,14},{8,0},{10,2},{12,4},{14,6},{1,9},{3,11}... | collective-permute-start | bytes 589832 | tf_op jit(solution)/shard_map/ppermute | solution.py:403
  42.9 33.2 %collective-permute-start.18 = (bf16[128,768]{1,0:T(8,128)(2,1)}, bf16[128,768]{1,0:T(8,128)(2,1)}, u32[]{:S(2)}, u32[]{:S(2)}) collective-permute-start(bf16[128,768]{1,0:T(8,128)(2,1)} %get-tuple-element.104), channel_id=1, source_target_pairs={{0,10},{2,8},{4,14},{6,12},{8,2},{10,0},{12,6},{14,4},{1,11},{3,9}... | collective-permute-start | bytes 589832 | tf_op jit(solution)/shard_map/ppermute | solution.py:403
  63.2 15.8 %collective-permute-start.14 = (bf16[128,768]{1,0:T(8,128)(2,1)}, bf16[128,768]{1,0:T(8,128)(2,1)}, u32[]{:S(2)}, u32[]{:S(2)}) collective-permute-start(bf16[128,768]{1,0:T(8,128)(2,1)} %get-tuple-element.136), channel_id=1, source_target_pairs={{0,2},{2,0},{4,6},{6,4},{8,10},{10,8},{12,14},{14,12},{1,3},{3,1},... | collective-permute-start | bytes 589832 | tf_op jit(solution)/shard_map/ppermute | solution.py:403
  63.8 18.6 %collective-permute-start.19 = (bf16[128,768]{1,0:T(8,128)(2,1)}, bf16[128,768]{1,0:T(8,128)(2,1)}, u32[]{:S(2)}, u32[]{:S(2)}) collective-permute-start(bf16[128,768]{1,0:T(8,128)(2,1)} %get-tuple-element.137), channel_id=1, source_target_pairs={{0,12},{2,14},{4,8},{6,10},{8,4},{10,6},{12,0},{14,2},{1,13},{3,15... | collective-permute-start | bytes 589832 | tf_op jit(solution)/shard_map/ppermute | solution.py:403
  63.9 21.4 %collective-permute-start.20 = (bf16[128,768]{1,0:T(8,128)(2,1)S(1)}, bf16[128,768]{1,0:T(8,128)(2,1)}, u32[]{:S(2)}, u32[]{:S(2)}) collective-permute-start(bf16[128,768]{1,0:T(8,128)(2,1)S(1)} %copy-done.23), channel_id=1, source_target_pairs={{0,14},{2,12},{4,10},{6,8},{8,6},{10,4},{12,2},{14,0},{1,15},{3,13... | collective-permute-start | bytes 589832 | tf_op jit(solution)/shard_map/ppermute | solution.py:403
  68.7 32.2 %collective-permute-start.8 = (bf16[128,768]{1,0:T(8,128)(2,1)}, bf16[128,768]{1,0:T(8,128)(2,1)S(1)}, u32[]{:S(2)}, u32[]{:S(2)}) collective-permute-start(bf16[128,768]{1,0:T(8,128)(2,1)} %get-tuple-element.129), channel_id=1, source_target_pairs={{0,4},{2,6},{4,0},{6,2},{8,12},{10,14},{12,8},{14,10},{1,5},{3,7},... | collective-permute-start | bytes 589832 | tf_op jit(solution)/shard_map/ppermute | solution.py:403
  76.1 24.8 %collective-permute-start.9 = (bf16[128,768]{1,0:T(8,128)(2,1)}, bf16[128,768]{1,0:T(8,128)(2,1)S(1)}, u32[]{:S(2)}, u32[]{:S(2)}) collective-permute-start(bf16[128,768]{1,0:T(8,128)(2,1)} %get-tuple-element.130), channel_id=1, source_target_pairs={{0,6},{2,4},{4,2},{6,0},{8,14},{10,12},{12,10},{14,8},{1,7},{3,5},... | collective-permute-start | bytes 589832 | tf_op jit(solution)/shard_map/ppermute | solution.py:403
  79.1 23.6 %collective-permute-start.10 = (bf16[128,768]{1,0:T(8,128)(2,1)}, bf16[128,768]{1,0:T(8,128)(2,1)S(1)}, u32[]{:S(2)}, u32[]{:S(2)}) collective-permute-start(bf16[128,768]{1,0:T(8,128)(2,1)} %get-tuple-element.131), channel_id=1, source_target_pairs={{0,8},{2,10},{4,12},{6,14},{8,0},{10,2},{12,4},{14,6},{1,9},{3,11}... | collective-permute-start | bytes 589832 | tf_op jit(solution)/shard_map/ppermute | solution.py:403
  82.4 23.6 %collective-permute-start.11 = (bf16[128,768]{1,0:T(8,128)(2,1)}, bf16[128,768]{1,0:T(8,128)(2,1)S(1)}, u32[]{:S(2)}, u32[]{:S(2)}) collective-permute-start(bf16[128,768]{1,0:T(8,128)(2,1)} %get-tuple-element.132), channel_id=1, source_target_pairs={{0,10},{2,8},{4,14},{6,12},{8,2},{10,0},{12,6},{14,4},{1,11},{3,9}... | collective-permute-start | bytes 589832 | tf_op jit(solution)/shard_map/ppermute | solution.py:403
  85.2 20.7 %collective-permute-start.12 = (bf16[128,768]{1,0:T(8,128)(2,1)}, bf16[128,768]{1,0:T(8,128)(2,1)S(1)}, u32[]{:S(2)}, u32[]{:S(2)}) collective-permute-start(bf16[128,768]{1,0:T(8,128)(2,1)} %get-tuple-element.133), channel_id=1, source_target_pairs={{0,12},{2,14},{4,8},{6,10},{8,4},{10,6},{12,0},{14,2},{1,13},{3,15... | collective-permute-start | bytes 589832 | tf_op jit(solution)/shard_map/ppermute | solution.py:403
  119.5 17.9 %collective-permute-start.22 = (f32[128,768]{1,0:T(8,128)}, f32[128,768]{1,0:T(8,128)S(1)}, u32[]{:S(2)}, u32[]{:S(2)}) collective-permute-start(f32[128,768]{1,0:T(8,128)} %dynamic-slice_bitcast_fusion.1), channel_id=1, source_target_pairs={{0,2},{2,0},{4,6},{6,4},{8,10},{10,8},{12,14},{14,12},{1,3},{3,1},... | collective-permute-start | bytes 1179656 | tf_op jit(solution)/shard_map/ppermute | solution.py:403
  122.0 20.5 %collective-permute-start.25 = (bf16[128,768]{1,0:T(8,128)(2,1)}, bf16[128,768]{1,0:T(8,128)(2,1)}, u32[]{:S(2)}, u32[]{:S(2)}) collective-permute-start(bf16[128,768]{1,0:T(8,128)(2,1)} %get-tuple-element.157), channel_id=1, source_target_pairs={{0,6},{2,4},{4,2},{6,0},{8,14},{10,12},{12,10},{14,8},{1,7},{3,5},... | collective-permute-start | bytes 589832 | tf_op jit(solution)/shard_map/ppermute | solution.py:403
  130.4 17.1 %collective-permute-start.24 = (bf16[128,768]{1,0:T(8,128)(2,1)}, bf16[128,768]{1,0:T(8,128)(2,1)}, u32[]{:S(2)}, u32[]{:S(2)}) collective-permute-start(bf16[128,768]{1,0:T(8,128)(2,1)} %get-tuple-element.150), channel_id=1, source_target_pairs={{0,4},{2,6},{4,0},{6,2},{8,12},{10,14},{12,8},{14,10},{1,5},{3,7},... | collective-permute-start | bytes 589832 | tf_op jit(solution)/shard_map/ppermute | solution.py:403
  132.7 27.1 %collective-permute-start.26 = (bf16[128,768]{1,0:T(8,128)(2,1)}, bf16[128,768]{1,0:T(8,128)(2,1)}, u32[]{:S(2)}, u32[]{:S(2)}) collective-permute-start(bf16[128,768]{1,0:T(8,128)(2,1)} %get-tuple-element.152), channel_id=1, source_target_pairs={{0,8},{2,10},{4,12},{6,14},{8,0},{10,2},{12,4},{14,6},{1,9},{3,11}... | collective-permute-start | bytes 589832 | tf_op jit(solution)/shard_map/ppermute | solution.py:403
  137.4 22.4 %collective-permute-start.28 = (bf16[128,768]{1,0:T(8,128)(2,1)}, bf16[128,768]{1,0:T(8,128)(2,1)}, u32[]{:S(2)}, u32[]{:S(2)}) collective-permute-start(bf16[128,768]{1,0:T(8,128)(2,1)} %get-tuple-element.163), channel_id=1, source_target_pairs={{0,12},{2,14},{4,8},{6,10},{8,4},{10,6},{12,0},{14,2},{1,13},{3,15... | collective-permute-start | bytes 589832 | tf_op jit(solution)/shard_map/ppermute | solution.py:403
  142.5 17.3 %collective-permute-start.23 = (bf16[128,768]{1,0:T(8,128)(2,1)}, bf16[128,768]{1,0:T(8,128)(2,1)}, u32[]{:S(2)}, u32[]{:S(2)}) collective-permute-start(bf16[128,768]{1,0:T(8,128)(2,1)} %get-tuple-element.166), channel_id=1, source_target_pairs={{0,2},{2,0},{4,6},{6,4},{8,10},{10,8},{12,14},{14,12},{1,3},{3,1},... | collective-permute-start | bytes 589832 | tf_op jit(solution)/shard_map/ppermute | solution.py:403
  (43 other events, 454.8 us)

commit v10 on v9

--- a/solution.py
+++ b/solution.py
@@ -430,17 +430,15 @@
         self.count = lax.axis_size("space") // 2
         self.held = sums.reshape(-1, self.lanes)
 
-    def halve(self, axis, distance, bit):
-        pair = self.held.reshape(2, -1, self.lanes)
-        taken = swap_with(pick(pair, 1 - bit), axis, distance)
-        self.held = pick(pair, bit) + taken
-        return taken
+    def halve(self, axis, distance, bit, arrived):
+        pair = waiting(self.held, arrived).reshape(2, -1, self.lanes)
+        self.held = pick(pair, bit) + swap_with(pick(pair, 1 - bit), axis, distance)
 
     def over_dp(self):
-        return self.halve("dp", 1, self.side)
-
-    def over_next(self):
-        return self.halve("space", 1, self.me % 2)
+        self.halve("dp", 1, self.side, [])
+
+    def over_next(self, arrived):
+        self.halve("space", 1, self.me % 2, arrived)
 
     def scatter(self, arrived):
         shares = waiting(self.held, arrived).reshape(self.count, -1, self.lanes)
@@ -456,9 +454,14 @@
         taken = [total]
         for offset in range(1, self.count):
             taken.append(swap_with(total, "space", 2 * offset))
-        quarter = jnp.stack(taken)
-        half = jnp.stack([quarter, swap_with(quarter, "space", 1)])
-        return half, swap_with(half, "dp", 1)
+        self.quarter = jnp.stack(taken)
+
+    def gather_next(self, arrived):
+        quarter = waiting(self.quarter, arrived)
+        self.half = jnp.stack([quarter, swap_with(quarter, "space", 1)])
+
+    def gather_dp(self):
+        return self.half, swap_with(self.half, "dp", 1)
 
 
 def finish_kernel(factor, me_ref, half_ref, other_ref, *out_refs):
@@ -576,23 +579,18 @@
     late = [image_band[offset] for offset in order[HELD:]]
     grad_image, sums = waiting((list(grad_image), sums), early)
     group_sum = GroupSum(sums)
-    over_dp = group_sum.over_dp()
-    group_sum.held = waiting(group_sum.held, late[:1])
-    over_next = group_sum.over_next()
+    group_sum.over_dp()
+    group_sum.over_next(late)
     grad_band = {0: grad_image[0]}
-    send(grad_image, order[:2], grad_band)
-    grad_image = waiting(grad_image, late)
-    send(grad_image, order[2:4], grad_band)
-    grad_image = waiting(grad_image, [over_dp])
-    send(grad_image, order[4:5], grad_band)
-    grad_image = waiting(grad_image, [over_next])
-    send(grad_image, order[5:], grad_band)
+    send(grad_image, order, grad_band)
     arrived = [grad_band[offset] for offset in order]
     image_band = [image_band[offset] for offset in range(owners)]
     grad_band = [grad_band[offset] for offset in range(owners)]
     output = to_cells(me, scaled.T, image_band, fields)
-    group_sum.scatter(arrived)
-    half, other = group_sum.gather([output])
+    group_sum.scatter(arrived[:2])
+    group_sum.gather(arrived[2:4])
+    group_sum.gather_next(arrived[4:] + [output])
+    half, other = group_sum.gather_dp()
     grad_fields = to_cells(me, plain.T, grad_band, cotangent)
     place = lax.axis_index("space")
     here = jnp.stack([lax.axis_index("dp"), place % 2, place // 2]).astype(jnp.int32)

time: 201 us -> 194 us (0.965)
  starting transfers between devices: 97.2 us -> 87.8 us
  waiting for transfers between devices: 46.2 us -> 49.1 us
    ppermute x38, starting transfers between devices: 97.2 us -> 87.8 us  [swap_with(): return lax.ppermute(values, axis, pairs)]
    ppermute x38, waiting for transfers between devices: 46.2 us -> 49.1 us  [swap_with(): return lax.ppermute(values, axis, pairs)]
    unnamed x61 -> x77, local copies, waits for them, and re-layouts: 13.2 us -> 13 us
  transfers between devices with their start and end apart: 38 -> 38, of which waited for: 14 -> 13; matrix products, arithmetic and copies ran while one was open for 6% -> 6% of each run, Pallas kernels for 16% -> 16%
where the time goes in v10:
time: 194 us; the launch traced here: 193 us
  starting transfers between devices  87.8 us (45%)
  waiting for transfers between devices  49.1 us (25%)
  Pallas kernels  36.1 us (19%)
  local copies, waits for them, and re-layouts  16.6 us (9%)
  other arithmetic  2.66 us (1%)
    ppermute x38, starting transfers between devices, swap_with(): return lax.ppermute(values, axis, pairs)  87.8 us
    ppermute x38, waiting for transfers between devices, swap_with(): return lax.ppermute(values, axis, pairs)  49.1 us
    unnamed x77, local copies, waits for them, and re-layouts  13 us
    pallas_call x1, Pallas kernels, backward_mid(): pl.pallas_call(functools.partial(backward_kernel, size_of_block, len(band...  12.9 us
    pallas_call x1, Pallas kernels, forward_mid(): pl.pallas_call(functools.partial(forward_kernel, len(bands)), grid_spec=p...  7.57 us
    pallas_call x2, Pallas kernels, to_cells(): pl.pallas_call(to_cells_kernel, grid_spec=pltpu.PrefetchScalarGridSpec(nu...  6.16 us
    pallas_call x2, Pallas kernels, to_modes(): pl.pallas_call(to_modes_kernel, grid_spec=pltpu.PrefetchScalarGridSpec(nu...  4.76 us
  transfers between devices with their start and end apart: 38, of which 13 were waited for; matrix products, arithmetic and copies ran while one was open for 6% of the time, Pallas kernels for 16%

profile of v10, /device:TPU:0, one launch (start us, length us, event | category | flops | bytes accessed | tf_op | source)
XLA Modules:
  0.0 193.4 jit_solution(5247672211015844684)
XLA Ops:
  5.0 3.0 %collective-permute-start = (bf16[128,768]{1,0:T(8,128)(2,1)}, bf16[128,768]{1,0:T(8,128)(2,1)S(1)}, u32[]{:S(2)}, u32[]{:S(2)}) collective-permute-start(bf16[128,768]{1,0:T(8,128)(2,1)} %get-tuple-element.103), channel_id=1, source_target_pairs={{0,2},{2,0},{4,6},{6,4},{8,10},{10,8},{12,14},{14,12},{1,3},{3,1},... | collective-permute-start | bytes 589832 | tf_op jit(solution)/shard_map/ppermute | solution.py:403
  13.8 3.6 %collective-permute-start.5 = (bf16[128,768]{1,0:T(8,128)(2,1)}, bf16[128,768]{1,0:T(8,128)(2,1)S(1)}, u32[]{:S(2)}, u32[]{:S(2)}) collective-permute-start(bf16[128,768]{1,0:T(8,128)(2,1)} %get-tuple-element.108), channel_id=1, source_target_pairs={{0,12},{2,14},{4,8},{6,10},{8,4},{10,6},{12,0},{14,2},{1,13},{3,15... | collective-permute-start | bytes 589832 | tf_op jit(solution)/shard_map/ppermute | solution.py:403
  17.5 6.2 %collective-permute-done.1.refs_2_ = bf16[128,768]{1,0:T(8,128)(2,1)S(1)} collective-permute-done((bf16[128,768]{1,0:T(8,128)(2,1)}, bf16[128,768]{1,0:T(8,128)(2,1)S(1)}, u32[]{:S(2)}, u32[]{:S(2)}) %collective-permute-start.1) | collective-permute-done | bytes 196640 | tf_op jit(solution)/shard_map/ppermute | solution.py:403
  35.2 4.0 %collective-permute-start.16 = (bf16[128,768]{1,0:T(8,128)(2,1)}, bf16[128,768]{1,0:T(8,128)(2,1)S(1)}, u32[]{:S(2)}, u32[]{:S(2)}) collective-permute-start(bf16[128,768]{1,0:T(8,128)(2,1)} %get-tuple-element.93), channel_id=1, source_target_pairs={{0,6},{2,4},{4,2},{6,0},{8,14},{10,12},{12,10},{14,8},{1,7},{3,5},... | collective-permute-start | bytes 589832 | tf_op jit(solution)/shard_map/ppermute | solution.py:403
  42.2 12.0 %collective-permute-start.18 = (bf16[128,768]{1,0:T(8,128)(2,1)}, bf16[128,768]{1,0:T(8,128)(2,1)S(1)}, u32[]{:S(2)}, u32[]{:S(2)}) collective-permute-start(bf16[128,768]{1,0:T(8,128)(2,1)} %get-tuple-element.95), channel_id=1, source_target_pairs={{0,10},{2,8},{4,14},{6,12},{8,2},{10,0},{12,6},{14,4},{1,11},{3,9}... | collective-permute-start | bytes 589832 | tf_op jit(solution)/shard_map/ppermute | solution.py:403
  54.2 7.6 %mix_forward.1 = (bf16[128,768]{1,0:T(8,128)(2,1)}, bf16[128,768]{1,0:T(8,128)(2,1)}, bf16[128,768]{1,0:T(8,128)(2,1)}, bf16[128,768]{1,0:T(8,128)(2,1)}, bf16[1...) custom-call(s32[1]{0:T(128)} %bitcast.me_ref, ...), custom_call_target="tpu_custom_call" | custom-call | flops 2415919104 | bytes 17301504 | tf_op jit(solution)/shard_map/mix_forward/pallas_call | solution.py:330
  62.6 4.7 %collective-permute-start.20 = (bf16[128,768]{1,0:T(8,128)(2,1)S(1)}, bf16[128,768]{1,0:T(8,128)(2,1)}, u32[]{:S(2)}, u32[]{:S(2)}) collective-permute-start(bf16[128,768]{1,0:T(8,128)(2,1)S(1)} %copy-done.29), channel_id=1, source_target_pairs={{0,14},{2,12},{4,10},{6,8},{8,6},{10,4},{12,2},{14,0},{1,15},{3,13... | collective-permute-start | bytes 589832 | tf_op jit(solution)/shard_map/ppermute | solution.py:403
  67.2 7.4 %collective-permute-start.8 = (bf16[128,768]{1,0:T(8,128)(2,1)}, bf16[128,768]{1,0:T(8,128)(2,1)S(1)}, u32[]{:S(2)}, u32[]{:S(2)}) collective-permute-start(bf16[128,768]{1,0:T(8,128)(2,1)} %get-tuple-element.120), channel_id=1, source_target_pairs={{0,4},{2,6},{4,0},{6,2},{8,12},{10,14},{12,8},{14,10},{1,5},{3,7},... | collective-permute-start | bytes 589832 | tf_op jit(solution)/shard_map/ppermute | solution.py:403
  74.7 3.1 %collective-permute-start.9 = (bf16[128,768]{1,0:T(8,128)(2,1)}, bf16[128,768]{1,0:T(8,128)(2,1)S(1)}, u32[]{:S(2)}, u32[]{:S(2)}) collective-permute-start(bf16[128,768]{1,0:T(8,128)(2,1)} %get-tuple-element.121), channel_id=1, source_target_pairs={{0,6},{2,4},{4,2},{6,0},{8,14},{10,12},{12,10},{14,8},{1,7},{3,5},... | collective-permute-start | bytes 589832 | tf_op jit(solution)/shard_map/ppermute | solution.py:403
  77.7 3.2 %collective-permute-start.10 = (bf16[128,768]{1,0:T(8,128)(2,1)}, bf16[128,768]{1,0:T(8,128)(2,1)S(1)}, u32[]{:S(2)}, u32[]{:S(2)}) collective-permute-start(bf16[128,768]{1,0:T(8,128)(2,1)} %get-tuple-element.122), channel_id=1, source_target_pairs={{0,8},{2,10},{4,12},{6,14},{8,0},{10,2},{12,4},{14,6},{1,9},{3,11}... | collective-permute-start | bytes 589832 | tf_op jit(solution)/shard_map/ppermute | solution.py:403
  86.7 12.9 %mix_backward.1 = (bf16[128,768]{1,0:T(8,128)(2,1)}, bf16[128,768]{1,0:T(8,128)(2,1)}, bf16[128,768]{1,0:T(8,128)(2,1)}, bf16[128,768]{1,0:T(8,128)(2,1)}, bf16[...) custom-call(s32[1]{0:T(128)} %bitcast.me_ref, ...), custom_call_target="tpu_custom_call" | custom-call | flops 4831838208 | bytes 17301504 | tf_op jit(solution)/shard_map/mix_backward/pallas_call | solution.py:368
  101.4 3.3 %collective-permute-done.11.refs_5_ = bf16[128,768]{1,0:T(8,128)(2,1)S(1)} collective-permute-done((bf16[128,768]{1,0:T(8,128)(2,1)}, bf16[128,768]{1,0:T(8,128)(2,1)S(1)}, u32[]{:S(2)}, u32[]{:S(2)}) %collective-permute-start.11) | collective-permute-done | bytes 196640 | tf_op jit(solution)/shard_map/ppermute | solution.py:403
  107.8 3.7 %collective-permute-start.13 = (bf16[128,768]{1,0:T(8,128)(2,1)S(1)}, bf16[128,768]{1,0:T(8,128)(2,1)S(1)}, u32[]{:S(2)}, u32[]{:S(2)}) collective-permute-start(bf16[128,768]{1,0:T(8,128)(2,1)S(1)} %copy-done.24), channel_id=1, source_target_pairs={{0,14},{2,12},{4,10},{6,8},{8,6},{10,4},{12,2},{14,0},{1,15},{3,13... | collective-permute-start | bytes 589832 | tf_op jit(solution)/shard_map/ppermute | solution.py:403
  113.0 4.7 %collective-permute-done.7.refs_1_ = bf16[128,768]{1,0:T(8,128)(2,1)S(1)} collective-permute-done((bf16[128,768]{1,0:T(8,128)(2,1)S(1)}, bf16[128,768]{1,0:T(8,128)(2,1)S(1)}, u32[]{:S(2)}, u32[]{:S(2)}) %collective-permute-start.7) | collective-permute-done | bytes 196640 | tf_op jit(solution)/shard_map/ppermute | solution.py:403
  120.0 7.3 %collective-permute-start.22 = (bf16[128,768]{1,0:T(8,128)(2,1)}, bf16[128,768]{1,0:T(8,128)(2,1)}, u32[]{:S(2)}, u32[]{:S(2)}) collective-permute-start(bf16[128,768]{1,0:T(8,128)(2,1)} %get-tuple-element.141), channel_id=1, source_target_pairs={{0,4},{2,6},{4,0},{6,2},{8,12},{10,14},{12,8},{14,10},{1,5},{3,7},... | collective-permute-start | bytes 589832 | tf_op jit(solution)/shard_map/ppermute | solution.py:403
  130.0 5.7 %collective-permute-done.22.refs_2_ = bf16[128,768]{1,0:T(8,128)(2,1)} collective-permute-done((bf16[128,768]{1,0:T(8,128)(2,1)}, bf16[128,768]{1,0:T(8,128)(2,1)}, u32[]{:S(2)}, u32[]{:S(2)}) %collective-permute-start.22) | collective-permute-done | bytes 196640 | tf_op jit(solution)/shard_map/ppermute | solution.py:403
  135.7 3.2 %collective-permute-done.24.refs_4_ = bf16[128,768]{1,0:T(8,128)(2,1)} collective-permute-done((bf16[128,768]{1,0:T(8,128)(2,1)}, bf16[128,768]{1,0:T(8,128)(2,1)}, u32[]{:S(2)}, u32[]{:S(2)}) %collective-permute-start.24) | collective-permute-done | bytes 196640 | tf_op jit(solution)/shard_map/ppermute | solution.py:403
  147.0 4.2 %collective-permute-done.23.refs_3_ = bf16[128,768]{1,0:T(8,128)(2,1)S(1)} collective-permute-done((bf16[128,768]{1,0:T(8,128)(2,1)}, bf16[128,768]{1,0:T(8,128)(2,1)S(1)}, u32[]{:S(2)}, u32[]{:S(2)}) %collective-permute-start.23) | collective-permute-done | bytes 196640 | tf_op jit(solution)/shard_map/ppermute | solution.py:403
  151.2 4.7 %collective-permute-done.25.refs_5_ = bf16[128,768]{1,0:T(8,128)(2,1)S(1)} collective-permute-done((bf16[128,768]{1,0:T(8,128)(2,1)}, bf16[128,768]{1,0:T(8,128)(2,1)S(1)}, u32[]{:S(2)}, u32[]{:S(2)}) %collective-permute-start.25) | collective-permute-done | bytes 196640 | tf_op jit(solution)/shard_map/ppermute | solution.py:403
  165.5 3.2 %to_cells.2 = bf16[4,2,180,768]{3,2,1,0:T(8,128)(2,1)S(1)} custom-call(s32[1]{0:T(128)} %bitcast.me_ref, bf16[180,128]{1,0:T(8,128)(2,1)S(1)} %copy-done.5, bf16[4,2,180,768]{3,2,1,0:T(8,128)(2,1)S(1)} %copy.23.cells_ref.base_ref, bf16[128,768]{1,0:T(8,128)(2,1)} %get-tuple-element.118.refs_0_, bf16[128,768]{1,0:T(8,128)(2,1)} %copy-done.15, ...), custom_call_target="tpu_custom_call" | custom-call | flops 283115520 | bytes 5996544 | tf_op jit(solution)/shard_map/to_cells/pallas_call | solution.py:181
  168.7 7.3 %collective-permute-done.34 = bf16[32,768]{1,0:T(8,128)(2,1)S(1)} collective-permute-done((bf16[32,768]{1,0:T(8,128)(2,1)S(1)}, bf16[32,768]{1,0:T(8,128)(2,1)S(1)}, u32[]{:S(2)}, u32[]{:S(2)}) %collective-permute-start.34) | collective-permute-done | bytes 49184 | tf_op jit(solution)/shard_map/ppermute | solution.py:403
  177.7 4.2 %collective-permute-done.36 = bf16[4,32,768]{2,1,0:T(8,128)(2,1)S(1)} collective-permute-done((bf16[4,32,768]{2,1,0:T(8,128)(2,1)S(1)}, bf16[4,32,768]{2,1,0:T(8,128)(2,1)S(1)}, u32[]{:S(2)}, u32[]{:S(2)}) %collective-permute-start.36) | collective-permute-done | bytes 196640 | tf_op jit(solution)/shard_map/ppermute | solution.py:403
  182.1 3.1 %copy.25 = bf16[4,2,180,768]{3,1,2,0:T(2,128)(2,1)} copy(bf16[4,2,180,768]{3,2,1,0:T(8,128)(2,1)S(1)} %to_cells.2) | data formatting | bytes 4423680
  188.2 3.1 %copy.26 = bf16[4,2,180,768]{3,1,2,0:T(2,128)(2,1)} copy(bf16[4,2,180,768]{3,2,1,0:T(8,128)(2,1)S(1)} %to_cells.3) | data formatting | bytes 4423680
  (153 shorter events, 67.3 us)
Async XLA Ops:
  8.0 15.7 %collective-permute-start.1 = (bf16[128,768]{1,0:T(8,128)(2,1)}, bf16[128,768]{1,0:T(8,128)(2,1)S(1)}, u32[]{:S(2)}, u32[]{:S(2)}) collective-permute-start(bf16[128,768]{1,0:T(8,128)(2,1)} %get-tuple-element.104), channel_id=1, source_target_pairs={{0,4},{2,6},{4,0},{6,2},{8,12},{10,14},{12,8},{14,10},{1,5},{3,7},... | collective-permute-start | bytes 589832 | tf_op jit(solution)/shard_map/ppermute | solution.py:403
  9.6 24.3 %collective-permute-start.2 = (bf16[128,768]{1,0:T(8,128)(2,1)}, bf16[128,768]{1,0:T(8,128)(2,1)S(1)}, u32[]{:S(2)}, u32[]{:S(2)}) collective-permute-start(bf16[128,768]{1,0:T(8,128)(2,1)} %get-tuple-element.105), channel_id=1, source_target_pairs={{0,6},{2,4},{4,2},{6,0},{8,14},{10,12},{12,10},{14,8},{1,7},{3,5},... | collective-permute-start | bytes 589832 | tf_op jit(solution)/shard_map/ppermute | solution.py:403
  9.6 25.0 %collective-permute-start.3 = (bf16[128,768]{1,0:T(8,128)(2,1)}, bf16[128,768]{1,0:T(8,128)(2,1)S(1)}, u32[]{:S(2)}, u32[]{:S(2)}) collective-permute-start(bf16[128,768]{1,0:T(8,128)(2,1)} %get-tuple-element.106), channel_id=1, source_target_pairs={{0,8},{2,10},{4,12},{6,14},{8,0},{10,2},{12,4},{14,6},{1,9},{3,11}... | collective-permute-start | bytes 589832 | tf_op jit(solution)/shard_map/ppermute | solution.py:403
  12.6 28.4 %collective-permute-start.4 = (bf16[128,768]{1,0:T(8,128)(2,1)}, bf16[128,768]{1,0:T(8,128)(2,1)S(1)}, u32[]{:S(2)}, u32[]{:S(2)}) collective-permute-start(bf16[128,768]{1,0:T(8,128)(2,1)} %get-tuple-element.107), channel_id=1, source_target_pairs={{0,10},{2,8},{4,14},{6,12},{8,2},{10,0},{12,6},{14,4},{1,11},{3,9}... | collective-permute-start | bytes 589832 | tf_op jit(solution)/shard_map/ppermute | solution.py:403
  13.8 28.4 %collective-permute-start.5 = (bf16[128,768]{1,0:T(8,128)(2,1)}, bf16[128,768]{1,0:T(8,128)(2,1)S(1)}, u32[]{:S(2)}, u32[]{:S(2)}) collective-permute-start(bf16[128,768]{1,0:T(8,128)(2,1)} %get-tuple-element.108), channel_id=1, source_target_pairs={{0,12},{2,14},{4,8},{6,10},{8,4},{10,6},{12,0},{14,2},{1,13},{3,15... | collective-permute-start | bytes 589832 | tf_op jit(solution)/shard_map/ppermute | solution.py:403
  24.4 29.9 %collective-permute-start.6 = (bf16[128,768]{1,0:T(8,128)(2,1)}, bf16[128,768]{1,0:T(8,128)(2,1)}, u32[]{:S(2)}, u32[]{:S(2)}) collective-permute-start(bf16[128,768]{1,0:T(8,128)(2,1)} %get-tuple-element.109), channel_id=1, source_target_pairs={{0,14},{2,12},{4,10},{6,8},{8,6},{10,4},{12,2},{14,0},{1,15},{3,13... | collective-permute-start | bytes 589832 | tf_op jit(solution)/shard_map/ppermute | solution.py:403
  34.6 27.8 %collective-permute-start.15 = (bf16[128,768]{1,0:T(8,128)(2,1)}, bf16[128,768]{1,0:T(8,128)(2,1)S(1)}, u32[]{:S(2)}, u32[]{:S(2)}) collective-permute-start(bf16[128,768]{1,0:T(8,128)(2,1)} %get-tuple-element.92), channel_id=1, source_target_pairs={{0,4},{2,6},{4,0},{6,2},{8,12},{10,14},{12,8},{14,10},{1,5},{3,7},... | collective-permute-start | bytes 589832 | tf_op jit(solution)/shard_map/ppermute | solution.py:403
  35.2 27.3 %collective-permute-start.16 = (bf16[128,768]{1,0:T(8,128)(2,1)}, bf16[128,768]{1,0:T(8,128)(2,1)S(1)}, u32[]{:S(2)}, u32[]{:S(2)}) collective-permute-start(bf16[128,768]{1,0:T(8,128)(2,1)} %get-tuple-element.93), channel_id=1, source_target_pairs={{0,6},{2,4},{4,2},{6,0},{8,14},{10,12},{12,10},{14,8},{1,7},{3,5},... | collective-permute-start | bytes 589832 | tf_op jit(solution)/shard_map/ppermute | solution.py:403
  41.6 25.6 %collective-permute-start.17 = (bf16[128,768]{1,0:T(8,128)(2,1)}, bf16[128,768]{1,0:T(8,128)(2,1)S(1)}, u32[]{:S(2)}, u32[]{:S(2)}) collective-permute-start(bf16[128,768]{1,0:T(8,128)(2,1)} %get-tuple-element.94), channel_id=1, source_target_pairs={{0,8},{2,10},{4,12},{6,14},{8,0},{10,2},{12,4},{14,6},{1,9},{3,11}... | collective-permute-start | bytes 589832 | tf_op jit(solution)/shard_map/ppermute | solution.py:403
  42.2 32.4 %collective-permute-start.18 = (bf16[128,768]{1,0:T(8,128)(2,1)}, bf16[128,768]{1,0:T(8,128)(2,1)S(1)}, u32[]{:S(2)}, u32[]{:S(2)}) collective-permute-start(bf16[128,768]{1,0:T(8,128)(2,1)} %get-tuple-element.95), channel_id=1, source_target_pairs={{0,10},{2,8},{4,14},{6,12},{8,2},{10,0},{12,6},{14,4},{1,11},{3,9}... | collective-permute-start | bytes 589832 | tf_op jit(solution)/shard_map/ppermute | solution.py:403
  61.8 15.9 %collective-permute-start.14 = (bf16[128,768]{1,0:T(8,128)(2,1)}, bf16[128,768]{1,0:T(8,128)(2,1)}, u32[]{:S(2)}, u32[]{:S(2)}) collective-permute-start(bf16[128,768]{1,0:T(8,128)(2,1)} %get-tuple-element.127), channel_id=1, source_target_pairs={{0,2},{2,0},{4,6},{6,4},{8,10},{10,8},{12,14},{14,12},{1,3},{3,1},... | collective-permute-start | bytes 589832 | tf_op jit(solution)/shard_map/ppermute | solution.py:403
  62.4 18.6 %collective-permute-start.19 = (bf16[128,768]{1,0:T(8,128)(2,1)}, bf16[128,768]{1,0:T(8,128)(2,1)}, u32[]{:S(2)}, u32[]{:S(2)}) collective-permute-start(bf16[128,768]{1,0:T(8,128)(2,1)} %get-tuple-element.128), channel_id=1, source_target_pairs={{0,12},{2,14},{4,8},{6,10},{8,4},{10,6},{12,0},{14,2},{1,13},{3,15... | collective-permute-start | bytes 589832 | tf_op jit(solution)/shard_map/ppermute | solution.py:403
  62.6 21.3 %collective-permute-start.20 = (bf16[128,768]{1,0:T(8,128)(2,1)S(1)}, bf16[128,768]{1,0:T(8,128)(2,1)}, u32[]{:S(2)}, u32[]{:S(2)}) collective-permute-start(bf16[128,768]{1,0:T(8,128)(2,1)S(1)} %copy-done.29), channel_id=1, source_target_pairs={{0,14},{2,12},{4,10},{6,8},{8,6},{10,4},{12,2},{14,0},{1,15},{3,13... | collective-permute-start | bytes 589832 | tf_op jit(solution)/shard_map/ppermute | solution.py:403
  67.2 32.3 %collective-permute-start.8 = (bf16[128,768]{1,0:T(8,128)(2,1)}, bf16[128,768]{1,0:T(8,128)(2,1)S(1)}, u32[]{:S(2)}, u32[]{:S(2)}) collective-permute-start(bf16[128,768]{1,0:T(8,128)(2,1)} %get-tuple-element.120), channel_id=1, source_target_pairs={{0,4},{2,6},{4,0},{6,2},{8,12},{10,14},{12,8},{14,10},{1,5},{3,7},... | collective-permute-start | bytes 589832 | tf_op jit(solution)/shard_map/ppermute | solution.py:403
  74.7 24.9 %collective-permute-start.9 = (bf16[128,768]{1,0:T(8,128)(2,1)}, bf16[128,768]{1,0:T(8,128)(2,1)S(1)}, u32[]{:S(2)}, u32[]{:S(2)}) collective-permute-start(bf16[128,768]{1,0:T(8,128)(2,1)} %get-tuple-element.121), channel_id=1, source_target_pairs={{0,6},{2,4},{4,2},{6,0},{8,14},{10,12},{12,10},{14,8},{1,7},{3,5},... | collective-permute-start | bytes 589832 | tf_op jit(solution)/shard_map/ppermute | solution.py:403
  77.7 23.6 %collective-permute-start.10 = (bf16[128,768]{1,0:T(8,128)(2,1)}, bf16[128,768]{1,0:T(8,128)(2,1)S(1)}, u32[]{:S(2)}, u32[]{:S(2)}) collective-permute-start(bf16[128,768]{1,0:T(8,128)(2,1)} %get-tuple-element.122), channel_id=1, source_target_pairs={{0,8},{2,10},{4,12},{6,14},{8,0},{10,2},{12,4},{14,6},{1,9},{3,11}... | collective-permute-start | bytes 589832 | tf_op jit(solution)/shard_map/ppermute | solution.py:403
  81.0 23.7 %collective-permute-start.11 = (bf16[128,768]{1,0:T(8,128)(2,1)}, bf16[128,768]{1,0:T(8,128)(2,1)S(1)}, u32[]{:S(2)}, u32[]{:S(2)}) collective-permute-start(bf16[128,768]{1,0:T(8,128)(2,1)} %get-tuple-element.123), channel_id=1, source_target_pairs={{0,10},{2,8},{4,14},{6,12},{8,2},{10,0},{12,6},{14,4},{1,11},{3,9}... | collective-permute-start | bytes 589832 | tf_op jit(solution)/shard_map/ppermute | solution.py:403
  83.9 20.8 %collective-permute-start.12 = (bf16[128,768]{1,0:T(8,128)(2,1)}, bf16[128,768]{1,0:T(8,128)(2,1)S(1)}, u32[]{:S(2)}, u32[]{:S(2)}) collective-permute-start(bf16[128,768]{1,0:T(8,128)(2,1)} %get-tuple-element.124), channel_id=1, source_target_pairs={{0,12},{2,14},{4,8},{6,10},{8,4},{10,6},{12,0},{14,2},{1,13},{3,15... | collective-permute-start | bytes 589832 | tf_op jit(solution)/shard_map/ppermute | solution.py:403
  120.0 15.7 %collective-permute-start.22 = (bf16[128,768]{1,0:T(8,128)(2,1)}, bf16[128,768]{1,0:T(8,128)(2,1)}, u32[]{:S(2)}, u32[]{:S(2)}) collective-permute-start(bf16[128,768]{1,0:T(8,128)(2,1)} %get-tuple-element.141), channel_id=1, source_target_pairs={{0,4},{2,6},{4,0},{6,2},{8,12},{10,14},{12,8},{14,10},{1,5},{3,7},... | collective-permute-start | bytes 589832 | tf_op jit(solution)/shard_map/ppermute | solution.py:403
  157.8 18.2 %collective-permute-start.21 = (bf16[128,768]{1,0:T(8,128)(2,1)}, bf16[128,768]{1,0:T(8,128)(2,1)S(1)}, u32[]{:S(2)}, u32[]{:S(2)}) collective-permute-start(bf16[128,768]{1,0:T(8,128)(2,1)} %get-tuple-element.140), channel_id=1, source_target_pairs={{0,2},{2,0},{4,6},{6,4},{8,10},{10,8},{12,14},{14,12},{1,3},{3,1},... | collective-permute-start | bytes 589832 | tf_op jit(solution)/shard_map/ppermute | solution.py:403
  158.5 17.6 %collective-permute-start.26 = (bf16[128,768]{1,0:T(8,128)(2,1)}, bf16[128,768]{1,0:T(8,128)(2,1)S(1)}, u32[]{:S(2)}, u32[]{:S(2)}) collective-permute-start(bf16[128,768]{1,0:T(8,128)(2,1)} %get-tuple-element.145), channel_id=1, source_target_pairs={{0,12},{2,14},{4,8},{6,10},{8,4},{10,6},{12,0},{14,2},{1,13},{3,15... | collective-permute-start | bytes 589832 | tf_op jit(solution)/shard_map/ppermute | solution.py:403
  160.7 15.4 %collective-permute-start.27 = (bf16[128,768]{1,0:T(8,128)(2,1)}, bf16[128,768]{1,0:T(8,128)(2,1)S(1)}, u32[]{:S(2)}, u32[]{:S(2)}) collective-permute-start(bf16[128,768]{1,0:T(8,128)(2,1)} %get-tuple-element.146), channel_id=1, source_target_pairs={{0,14},{2,12},{4,10},{6,8},{8,6},{10,4},{12,2},{14,0},{1,15},{3,13... | collective-permute-start | bytes 589832 | tf_op jit(solution)/shard_map/ppermute | solution.py:403
  163.1 12.9 %collective-permute-start.34 = (bf16[32,768]{1,0:T(8,128)(2,1)S(1)}, bf16[32,768]{1,0:T(8,128)(2,1)S(1)}, u32[]{:S(2)}, u32[]{:S(2)}) collective-permute-start(bf16[32,768]{1,0:T(8,128)(2,1)S(1)} %fusion.2), channel_id=1, source_target_pairs={{0,8},{2,10},{4,12},{6,14},{8,0},{10,2},{12,4},{14,6},{1,9},{3,11}... | collective-permute-start | bytes 147464 | tf_op jit(solution)/shard_map/ppermute | solution.py:403
  163.1 12.9 %collective-permute-start.33 = (bf16[32,768]{1,0:T(8,128)(2,1)S(1)}, bf16[32,768]{1,0:T(8,128)(2,1)S(1)}, u32[]{:S(2)}, u32[]{:S(2)}) collective-permute-start(bf16[32,768]{1,0:T(8,128)(2,1)S(1)} %fusion.2), channel_id=1, source_target_pairs={{0,4},{2,6},{4,0},{6,2},{8,12},{10,14},{12,8},{14,10},{1,5},{3,7},... | collective-permute-start | bytes 147464 | tf_op jit(solution)/shard_map/ppermute | solution.py:403
  (51 other events, 527.7 us)

commit v11 on v10

--- a/solution.py
+++ b/solution.py
@@ -5,6 +5,7 @@
 import jax.numpy as jnp
 from jax import lax
 from jax.experimental import pallas as pl
+from jax.experimental.layout import Layout, with_layout_constraint
 from jax.experimental.pallas import tpu as pltpu
 from jax.sharding import PartitionSpec as P
 import ml_dtypes
@@ -196,6 +197,15 @@
         ),
         name="to_cells",
     )(me, table, base, *hbm(*modes))
+
+
+def rows_inside(cells):
+    inside = jnp.transpose(cells, (0, 2, 1, 3))
+    return with_layout_constraint(inside, Layout(major_to_minor=(0, 1, 2, 3)))
+
+
+def rows_outside(cells):
+    return jnp.transpose(cells, (0, 2, 1, 3))
 
 
 def sigmoid_of(values):
@@ -460,8 +470,9 @@
         quarter = waiting(self.quarter, arrived)
         self.half = jnp.stack([quarter, swap_with(quarter, "space", 1)])
 
-    def gather_dp(self):
-        return self.half, swap_with(self.half, "dp", 1)
+    def gather_dp(self, arrived):
+        half = waiting(self.half, arrived)
+        return half, swap_with(half, "dp", 1)
 
 
 def finish_kernel(factor, me_ref, half_ref, other_ref, *out_refs):
@@ -580,24 +591,26 @@
     grad_image, sums = waiting((list(grad_image), sums), early)
     group_sum = GroupSum(sums)
     group_sum.over_dp()
-    group_sum.over_next(late)
+    group_sum.over_next(late[:1])
     grad_band = {0: grad_image[0]}
     send(grad_image, order, grad_band)
     arrived = [grad_band[offset] for offset in order]
     image_band = [image_band[offset] for offset in range(owners)]
     grad_band = [grad_band[offset] for offset in range(owners)]
-    output = to_cells(me, scaled.T, image_band, fields)
-    group_sum.scatter(arrived[:2])
-    group_sum.gather(arrived[2:4])
-    group_sum.gather_next(arrived[4:] + [output])
-    half, other = group_sum.gather_dp()
-    grad_fields = to_cells(me, plain.T, grad_band, cotangent)
+    again = waiting(fields, early[:1])
+    output = rows_inside(to_cells(me, scaled.T, image_band, again))
+    group_sum.scatter(late[1:] + arrived[:1])
+    group_sum.gather(arrived[1:3])
+    group_sum.quarter, output = lax.optimization_barrier((group_sum.quarter, output))
+    group_sum.gather_next(arrived[3:6])
+    half, other = group_sum.gather_dp(arrived[6:])
+    grad_fields = rows_inside(to_cells(me, plain.T, grad_band, cotangent))
     place = lax.axis_index("space")
     here = jnp.stack([lax.axis_index("dp"), place % 2, place // 2]).astype(jnp.int32)
     grads = finish_sums(
         here, half, other, factor, w_first.shape, b_first.shape
     )
-    return (output, grad_fields) + tuple(grads)
+    return (rows_outside(output), rows_outside(grad_fields)) + tuple(grads)
 
 
 def solution(mesh):

time: 194 us -> 191 us (0.985)
  waiting for transfers between devices: 49.1 us -> 45.7 us
    unnamed x77 -> x67, local copies, waits for them, and re-layouts: 13 us -> 4.6 us
    pallas_call x0 -> x2, local copies, waits for them, and re-layouts: none -> 6.13 us  [to_cells(): pl.pallas_call(to_cells_kernel, grid_spec=pltpu.PrefetchScalarGridSpec(nu...]
    ppermute x38, waiting for transfers between devices: 49.1 us -> 45.7 us  [swap_with(): return lax.ppermute(values, axis, pairs)]
  transfers between devices with their start and end apart: 38 -> 38, of which waited for: 13 -> 14; matrix products, arithmetic and copies ran while one was open for 6% -> 7% of each run, Pallas kernels for 16% -> 17%
where the time goes in v11:
time: 191 us; the launch traced here: 190 us
  starting transfers between devices  88.1 us (46%)
  waiting for transfers between devices  45.7 us (24%)
  Pallas kernels  36.1 us (19%)
  local copies, waits for them, and re-layouts  16.2 us (8%)
  other arithmetic  2.66 us (1%)
    ppermute x38, starting transfers between devices, swap_with(): return lax.ppermute(values, axis, pairs)  88.1 us
    ppermute x38, waiting for transfers between devices, swap_with(): return lax.ppermute(values, axis, pairs)  45.7 us
    pallas_call x1, Pallas kernels, backward_mid(): pl.pallas_call(functools.partial(backward_kernel, size_of_block, len(band...  12.8 us
    pallas_call x1, Pallas kernels, forward_mid(): pl.pallas_call(functools.partial(forward_kernel, len(bands)), grid_spec=p...  7.55 us
    pallas_call x2, Pallas kernels, to_cells(): pl.pallas_call(to_cells_kernel, grid_spec=pltpu.PrefetchScalarGridSpec(nu...  6.17 us
    pallas_call x2, local copies, waits for them, and re-layouts, to_cells(): pl.pallas_call(to_cells_kernel, grid_spec=pltpu.PrefetchScalarGridSpec(nu...  6.13 us
    pallas_call x2, Pallas kernels, to_modes(): pl.pallas_call(to_modes_kernel, grid_spec=pltpu.PrefetchScalarGridSpec(nu...  4.81 us
    unnamed x67, local copies, waits for them, and re-layouts  4.6 us
  transfers between devices with their start and end apart: 38, of which 14 were waited for; matrix products, arithmetic and copies ran while one was open for 7% of the time, Pallas kernels for 17%

profile of v11, /device:TPU:0, one launch (start us, length us, event | category | flops | bytes accessed | tf_op | source)
XLA Modules:
  0.0 190.0 jit_solution(12286370758599614312)
XLA Ops:
  5.0 3.0 %collective-permute-start = (bf16[128,768]{1,0:T(8,128)(2,1)}, bf16[128,768]{1,0:T(8,128)(2,1)S(1)}, u32[]{:S(2)}, u32[]{:S(2)}) collective-permute-start(bf16[128,768]{1,0:T(8,128)(2,1)} %get-tuple-element.98), channel_id=1, source_target_pairs={{0,2},{2,0},{4,6},{6,4},{8,10},{10,8},{12,14},{14,12},{1,3},{3,1},... | collective-permute-start | bytes 589832 | tf_op jit(solution)/shard_map/ppermute | solution.py:413
  13.9 3.6 %collective-permute-start.5 = (bf16[128,768]{1,0:T(8,128)(2,1)}, bf16[128,768]{1,0:T(8,128)(2,1)}, u32[]{:S(2)}, u32[]{:S(2)}) collective-permute-start(bf16[128,768]{1,0:T(8,128)(2,1)} %get-tuple-element.103), channel_id=1, source_target_pairs={{0,12},{2,14},{4,8},{6,10},{8,4},{10,6},{12,0},{14,2},{1,13},{3,15... | collective-permute-start | bytes 589832 | tf_op jit(solution)/shard_map/ppermute | solution.py:413
  17.5 6.2 %collective-permute-done.1.refs_2_ = bf16[128,768]{1,0:T(8,128)(2,1)S(1)} collective-permute-done((bf16[128,768]{1,0:T(8,128)(2,1)}, bf16[128,768]{1,0:T(8,128)(2,1)S(1)}, u32[]{:S(2)}, u32[]{:S(2)}) %collective-permute-start.1) | collective-permute-done | bytes 196640 | tf_op jit(solution)/shard_map/ppermute | solution.py:413
  33.2 4.5 %collective-permute-start.9 = (bf16[128,768]{1,0:T(8,128)(2,1)}, bf16[128,768]{1,0:T(8,128)(2,1)S(1)}, u32[]{:S(2)}, u32[]{:S(2)}) collective-permute-start(bf16[128,768]{1,0:T(8,128)(2,1)} %get-tuple-element.110), channel_id=1, source_target_pairs={{0,6},{2,4},{4,2},{6,0},{8,14},{10,12},{12,10},{14,8},{1,7},{3,5},... | collective-permute-start | bytes 589832 | tf_op jit(solution)/shard_map/ppermute | solution.py:413
  37.7 3.2 %collective-permute-done.4.refs_5_ = bf16[128,768]{1,0:T(8,128)(2,1)S(1)} collective-permute-done((bf16[128,768]{1,0:T(8,128)(2,1)}, bf16[128,768]{1,0:T(8,128)(2,1)S(1)}, u32[]{:S(2)}, u32[]{:S(2)}) %collective-permute-start.4) | collective-permute-done | bytes 196640 | tf_op jit(solution)/shard_map/ppermute | solution.py:413
  41.6 12.8 %collective-permute-start.11 = (bf16[128,768]{1,0:T(8,128)(2,1)}, bf16[128,768]{1,0:T(8,128)(2,1)}, u32[]{:S(2)}, u32[]{:S(2)}) collective-permute-start(bf16[128,768]{1,0:T(8,128)(2,1)} %get-tuple-element.112), channel_id=1, source_target_pairs={{0,10},{2,8},{4,14},{6,12},{8,2},{10,0},{12,6},{14,4},{1,11},{3,9}... | collective-permute-start | bytes 589832 | tf_op jit(solution)/shard_map/ppermute | solution.py:413
  54.4 7.6 %mix_forward.1 = (bf16[128,768]{1,0:T(8,128)(2,1)}, bf16[128,768]{1,0:T(8,128)(2,1)}, bf16[128,768]{1,0:T(8,128)(2,1)}, bf16[128,768]{1,0:T(8,128)(2,1)}, bf16[1...) custom-call(s32[1]{0:T(128)} %bitcast.me_ref, ...), custom_call_target="tpu_custom_call" | custom-call | flops 2415919104 | bytes 17301504 | tf_op jit(solution)/shard_map/mix_forward/pallas_call | solution.py:340
  62.6 4.8 %collective-permute-start.13 = (bf16[128,768]{1,0:T(8,128)(2,1)S(1)}, bf16[128,768]{1,0:T(8,128)(2,1)}, u32[]{:S(2)}, u32[]{:S(2)}) collective-permute-start(bf16[128,768]{1,0:T(8,128)(2,1)S(1)} %copy-done.27), channel_id=1, source_target_pairs={{0,14},{2,12},{4,10},{6,8},{8,6},{10,4},{12,2},{14,0},{1,15},{3,13... | collective-permute-start | bytes 589832 | tf_op jit(solution)/shard_map/ppermute | solution.py:413
  67.3 8.7 %collective-permute-start.14 = (bf16[128,768]{1,0:T(8,128)(2,1)}, bf16[128,768]{1,0:T(8,128)(2,1)S(1)}, u32[]{:S(2)}, u32[]{:S(2)}) collective-permute-start(bf16[128,768]{1,0:T(8,128)(2,1)} %get-tuple-element.135), channel_id=1, source_target_pairs={{0,8},{2,10},{4,12},{6,14},{8,0},{10,2},{12,4},{14,6},{1,9},{3,11}... | collective-permute-start | bytes 589832 | tf_op jit(solution)/shard_map/ppermute | solution.py:413
  76.9 4.1 %collective-permute-start.16 = (bf16[128,768]{1,0:T(8,128)(2,1)}, bf16[128,768]{1,0:T(8,128)(2,1)S(1)}, u32[]{:S(2)}, u32[]{:S(2)}) collective-permute-start(bf16[128,768]{1,0:T(8,128)(2,1)} %get-tuple-element.137), channel_id=1, source_target_pairs={{0,10},{2,8},{4,14},{6,12},{8,2},{10,0},{12,6},{14,4},{1,11},{3,9}... | collective-permute-start | bytes 589832 | tf_op jit(solution)/shard_map/ppermute | solution.py:413
  81.0 5.1 %collective-permute-start.17 = (bf16[128,768]{1,0:T(8,128)(2,1)}, bf16[128,768]{1,0:T(8,128)(2,1)S(1)}, u32[]{:S(2)}, u32[]{:S(2)}) collective-permute-start(bf16[128,768]{1,0:T(8,128)(2,1)} %get-tuple-element.138), channel_id=1, source_target_pairs={{0,6},{2,4},{4,2},{6,0},{8,14},{10,12},{12,10},{14,8},{1,7},{3,5},... | collective-permute-start | bytes 589832 | tf_op jit(solution)/shard_map/ppermute | solution.py:413
  86.1 3.4 %collective-permute-start.18 = (bf16[128,768]{1,0:T(8,128)(2,1)}, bf16[128,768]{1,0:T(8,128)(2,1)S(1)}, u32[]{:S(2)}, u32[]{:S(2)}) collective-permute-start(bf16[128,768]{1,0:T(8,128)(2,1)} %get-tuple-element.139), channel_id=1, source_target_pairs={{0,12},{2,14},{4,8},{6,10},{8,4},{10,6},{12,0},{14,2},{1,13},{3,15... | collective-permute-start | bytes 589832 | tf_op jit(solution)/shard_map/ppermute | solution.py:413
  89.5 12.8 %mix_backward.1 = (bf16[128,768]{1,0:T(8,128)(2,1)}, bf16[128,768]{1,0:T(8,128)(2,1)}, bf16[128,768]{1,0:T(8,128)(2,1)}, bf16[128,768]{1,0:T(8,128)(2,1)}, bf16[...) custom-call(s32[1]{0:T(128)} %bitcast.me_ref, ...), custom_call_target="tpu_custom_call" | custom-call | flops 4831838208 | bytes 17301504 | tf_op jit(solution)/shard_map/mix_backward/pallas_call | solution.py:378
  109.6 3.5 %collective-permute-done.20.refs_1_ = bf16[128,768]{1,0:T(8,128)(2,1)S(1)} collective-permute-done((bf16[128,768]{1,0:T(8,128)(2,1)S(1)}, bf16[128,768]{1,0:T(8,128)(2,1)S(1)}, u32[]{:S(2)}, u32[]{:S(2)}) %collective-permute-start.20) | collective-permute-done | bytes 196640 | tf_op jit(solution)/shard_map/ppermute | solution.py:413
  115.4 3.5 %collective-permute-start.22 = (bf16[128,768]{1,0:T(8,128)(2,1)}, bf16[128,768]{1,0:T(8,128)(2,1)}, u32[]{:S(2)}, u32[]{:S(2)}) collective-permute-start(bf16[128,768]{1,0:T(8,128)(2,1)} %get-tuple-element.143), channel_id=1, source_target_pairs={{0,14},{2,12},{4,10},{6,8},{8,6},{10,4},{12,2},{14,0},{1,15},{3,13... | collective-permute-start | bytes 589832 | tf_op jit(solution)/shard_map/ppermute | solution.py:413
  118.9 6.1 %collective-permute-start.23 = (bf16[128,768]{1,0:T(8,128)(2,1)}, bf16[128,768]{1,0:T(8,128)(2,1)}, u32[]{:S(2)}, u32[]{:S(2)}) collective-permute-start(bf16[128,768]{1,0:T(8,128)(2,1)} %get-tuple-element.144), channel_id=1, source_target_pairs={{0,8},{2,10},{4,12},{6,14},{8,0},{10,2},{12,4},{14,6},{1,9},{3,11}... | collective-permute-start | bytes 589832 | tf_op jit(solution)/shard_map/ppermute | solution.py:413
  125.0 3.9 %collective-permute-done.21 = f32[128,768]{1,0:T(8,128)} collective-permute-done((f32[128,768]{1,0:T(8,128)S(1)}, f32[128,768]{1,0:T(8,128)}, u32[]{:S(2)}, u32[]{:S(2)}) %collective-permute-start.21) | collective-permute-done | bytes 393248 | tf_op jit(solution)/shard_map/ppermute | solution.py:413
  129.9 8.0 %collective-permute-done.23.refs_4_ = bf16[128,768]{1,0:T(8,128)(2,1)} collective-permute-done((bf16[128,768]{1,0:T(8,128)(2,1)}, bf16[128,768]{1,0:T(8,128)(2,1)}, u32[]{:S(2)}, u32[]{:S(2)}) %collective-permute-start.23) | collective-permute-done | bytes 196640 | tf_op jit(solution)/shard_map/ppermute | solution.py:413
  148.6 4.8 %collective-permute-done.27.refs_2_ = bf16[128,768]{1,0:T(8,128)(2,1)S(1)} collective-permute-done((bf16[128,768]{1,0:T(8,128)(2,1)}, bf16[128,768]{1,0:T(8,128)(2,1)S(1)}, u32[]{:S(2)}, u32[]{:S(2)}) %collective-permute-start.27) | collective-permute-done | bytes 196640 | tf_op jit(solution)/shard_map/ppermute | solution.py:413
  163.2 3.2 %to_cells.2 = bf16[4,2,180,768]{3,2,1,0:T(8,128)(2,1)S(1)} custom-call(s32[1]{0:T(128)} %bitcast.me_ref, bf16[180,128]{1,0:T(8,128)(2,1)S(1)} %copy-done.3, bf16[4,2,180,768]{3,2,1,0:T(8,128)(2,1)S(1)} %copy.23.base_ref, bf16[128,768]{1,0:T(8,128)(2,1)} %get-tuple-element.150.refs_0_, bf16[128,768]{1,0:T(8,128)(2,1)} %copy-done.13, ...), custom_call_target="tpu_custom_call" | custom-call | flops 283115520 | bytes 5996544 | tf_op jit(solution)/shard_map/to_cells/pallas_call | solution.py:182
  166.4 3.1 %copy.30 = bf16[4,2,180,768]{3,1,2,0:T(2,128)(2,1)} copy(bf16[4,2,180,768]{3,2,1,0:T(8,128)(2,1)S(1)} %to_cells.2) | data formatting | bytes 4423680 | tf_op jit(solution)/shard_map/to_cells/pallas_call | solution.py:182
  171.3 3.1 %collective-permute-start.35 = (bf16[128,768]{1,0:T(8,128)(2,1)S(1)}, bf16[128,768]{1,0:T(8,128)(2,1)S(1)}, u32[]{:S(2)}, u32[]{:S(2)}) collective-permute-start(bf16[128,768]{1,0:T(8,128)(2,1)S(1)} %copy-done.22), channel_id=1, source_target_pairs={{0,14},{2,12},{4,10},{6,8},{8,6},{10,4},{12,2},{14,0},{1,15},{3,13... | collective-permute-start | bytes 589832 | tf_op jit(solution)/shard_map/ppermute | solution.py:413
  174.4 6.6 %collective-permute-done.36 = bf16[4,32,768]{2,1,0:T(8,128)(2,1)S(1)} collective-permute-done((bf16[4,32,768]{2,1,0:T(8,128)(2,1)S(1)}, bf16[4,32,768]{2,1,0:T(8,128)(2,1)S(1)}, u32[]{:S(2)}, u32[]{:S(2)}) %collective-permute-start.36) | collective-permute-done | bytes 196640 | tf_op jit(solution)/shard_map/ppermute | solution.py:413
  184.7 3.1 %copy.26 = bf16[4,2,180,768]{3,1,2,0:T(2,128)(2,1)} copy(bf16[4,2,180,768]{3,2,1,0:T(8,128)(2,1)S(1)} %to_cells.3) | data formatting | bytes 4423680 | tf_op jit(solution)/shard_map/to_cells/pallas_call | solution.py:182
  (146 shorter events, 60.3 us)
Async XLA Ops:
  8.0 15.7 %collective-permute-start.1 = (bf16[128,768]{1,0:T(8,128)(2,1)}, bf16[128,768]{1,0:T(8,128)(2,1)S(1)}, u32[]{:S(2)}, u32[]{:S(2)}) collective-permute-start(bf16[128,768]{1,0:T(8,128)(2,1)} %get-tuple-element.99), channel_id=1, source_target_pairs={{0,4},{2,6},{4,0},{6,2},{8,12},{10,14},{12,8},{14,10},{1,5},{3,7},... | collective-permute-start | bytes 589832 | tf_op jit(solution)/shard_map/ppermute | solution.py:413
  9.6 22.3 %collective-permute-start.2 = (bf16[128,768]{1,0:T(8,128)(2,1)}, bf16[128,768]{1,0:T(8,128)(2,1)S(1)}, u32[]{:S(2)}, u32[]{:S(2)}) collective-permute-start(bf16[128,768]{1,0:T(8,128)(2,1)} %get-tuple-element.100), channel_id=1, source_target_pairs={{0,6},{2,4},{4,2},{6,0},{8,14},{10,12},{12,10},{14,8},{1,7},{3,5},... | collective-permute-start | bytes 589832 | tf_op jit(solution)/shard_map/ppermute | solution.py:413
  9.6 23.0 %collective-permute-start.3 = (bf16[128,768]{1,0:T(8,128)(2,1)}, bf16[128,768]{1,0:T(8,128)(2,1)S(1)}, u32[]{:S(2)}, u32[]{:S(2)}) collective-permute-start(bf16[128,768]{1,0:T(8,128)(2,1)} %get-tuple-element.101), channel_id=1, source_target_pairs={{0,8},{2,10},{4,12},{6,14},{8,0},{10,2},{12,4},{14,6},{1,9},{3,11}... | collective-permute-start | bytes 589832 | tf_op jit(solution)/shard_map/ppermute | solution.py:413
  12.6 28.4 %collective-permute-start.4 = (bf16[128,768]{1,0:T(8,128)(2,1)}, bf16[128,768]{1,0:T(8,128)(2,1)S(1)}, u32[]{:S(2)}, u32[]{:S(2)}) collective-permute-start(bf16[128,768]{1,0:T(8,128)(2,1)} %get-tuple-element.102), channel_id=1, source_target_pairs={{0,10},{2,8},{4,14},{6,12},{8,2},{10,0},{12,6},{14,4},{1,11},{3,9}... | collective-permute-start | bytes 589832 | tf_op jit(solution)/shard_map/ppermute | solution.py:413
  13.9 27.7 %collective-permute-start.5 = (bf16[128,768]{1,0:T(8,128)(2,1)}, bf16[128,768]{1,0:T(8,128)(2,1)}, u32[]{:S(2)}, u32[]{:S(2)}) collective-permute-start(bf16[128,768]{1,0:T(8,128)(2,1)} %get-tuple-element.103), channel_id=1, source_target_pairs={{0,12},{2,14},{4,8},{6,10},{8,4},{10,6},{12,0},{14,2},{1,13},{3,15... | collective-permute-start | bytes 589832 | tf_op jit(solution)/shard_map/ppermute | solution.py:413
  23.7 30.6 %collective-permute-start.6 = (bf16[128,768]{1,0:T(8,128)(2,1)}, bf16[128,768]{1,0:T(8,128)(2,1)}, u32[]{:S(2)}, u32[]{:S(2)}) collective-permute-start(bf16[128,768]{1,0:T(8,128)(2,1)} %get-tuple-element.104), channel_id=1, source_target_pairs={{0,14},{2,12},{4,10},{6,8},{8,6},{10,4},{12,2},{14,0},{1,15},{3,13... | collective-permute-start | bytes 589832 | tf_op jit(solution)/shard_map/ppermute | solution.py:413
  32.5 30.0 %collective-permute-start.8 = (bf16[128,768]{1,0:T(8,128)(2,1)}, bf16[128,768]{1,0:T(8,128)(2,1)S(1)}, u32[]{:S(2)}, u32[]{:S(2)}) collective-permute-start(bf16[128,768]{1,0:T(8,128)(2,1)} %get-tuple-element.109), channel_id=1, source_target_pairs={{0,4},{2,6},{4,0},{6,2},{8,12},{10,14},{12,8},{14,10},{1,5},{3,7},... | collective-permute-start | bytes 589832 | tf_op jit(solution)/shard_map/ppermute | solution.py:413
  33.2 29.4 %collective-permute-start.9 = (bf16[128,768]{1,0:T(8,128)(2,1)}, bf16[128,768]{1,0:T(8,128)(2,1)S(1)}, u32[]{:S(2)}, u32[]{:S(2)}) collective-permute-start(bf16[128,768]{1,0:T(8,128)(2,1)} %get-tuple-element.110), channel_id=1, source_target_pairs={{0,6},{2,4},{4,2},{6,0},{8,14},{10,12},{12,10},{14,8},{1,7},{3,5},... | collective-permute-start | bytes 589832 | tf_op jit(solution)/shard_map/ppermute | solution.py:413
  41.0 26.4 %collective-permute-start.10 = (bf16[128,768]{1,0:T(8,128)(2,1)}, bf16[128,768]{1,0:T(8,128)(2,1)S(1)}, u32[]{:S(2)}, u32[]{:S(2)}) collective-permute-start(bf16[128,768]{1,0:T(8,128)(2,1)} %get-tuple-element.111), channel_id=1, source_target_pairs={{0,8},{2,10},{4,12},{6,14},{8,0},{10,2},{12,4},{14,6},{1,9},{3,11}... | collective-permute-start | bytes 589832 | tf_op jit(solution)/shard_map/ppermute | solution.py:413
  41.6 35.3 %collective-permute-start.11 = (bf16[128,768]{1,0:T(8,128)(2,1)}, bf16[128,768]{1,0:T(8,128)(2,1)}, u32[]{:S(2)}, u32[]{:S(2)}) collective-permute-start(bf16[128,768]{1,0:T(8,128)(2,1)} %get-tuple-element.112), channel_id=1, source_target_pairs={{0,10},{2,8},{4,14},{6,12},{8,2},{10,0},{12,6},{14,4},{1,11},{3,9}... | collective-permute-start | bytes 589832 | tf_op jit(solution)/shard_map/ppermute | solution.py:413
  61.9 15.0 %collective-permute-start.7 = (bf16[128,768]{1,0:T(8,128)(2,1)}, bf16[128,768]{1,0:T(8,128)(2,1)}, u32[]{:S(2)}, u32[]{:S(2)}) collective-permute-start(bf16[128,768]{1,0:T(8,128)(2,1)} %get-tuple-element.123), channel_id=1, source_target_pairs={{0,2},{2,0},{4,6},{6,4},{8,10},{10,8},{12,14},{14,12},{1,3},{3,1},... | collective-permute-start | bytes 589832 | tf_op jit(solution)/shard_map/ppermute | solution.py:413
  62.5 18.5 %collective-permute-start.12 = (bf16[128,768]{1,0:T(8,128)(2,1)}, bf16[128,768]{1,0:T(8,128)(2,1)}, u32[]{:S(2)}, u32[]{:S(2)}) collective-permute-start(bf16[128,768]{1,0:T(8,128)(2,1)} %get-tuple-element.124), channel_id=1, source_target_pairs={{0,12},{2,14},{4,8},{6,10},{8,4},{10,6},{12,0},{14,2},{1,13},{3,15... | collective-permute-start | bytes 589832 | tf_op jit(solution)/shard_map/ppermute | solution.py:413
  62.6 23.6 %collective-permute-start.13 = (bf16[128,768]{1,0:T(8,128)(2,1)S(1)}, bf16[128,768]{1,0:T(8,128)(2,1)}, u32[]{:S(2)}, u32[]{:S(2)}) collective-permute-start(bf16[128,768]{1,0:T(8,128)(2,1)S(1)} %copy-done.27), channel_id=1, source_target_pairs={{0,14},{2,12},{4,10},{6,8},{8,6},{10,4},{12,2},{14,0},{1,15},{3,13... | collective-permute-start | bytes 589832 | tf_op jit(solution)/shard_map/ppermute | solution.py:413
  67.3 35.0 %collective-permute-start.14 = (bf16[128,768]{1,0:T(8,128)(2,1)}, bf16[128,768]{1,0:T(8,128)(2,1)S(1)}, u32[]{:S(2)}, u32[]{:S(2)}) collective-permute-start(bf16[128,768]{1,0:T(8,128)(2,1)} %get-tuple-element.135), channel_id=1, source_target_pairs={{0,8},{2,10},{4,12},{6,14},{8,0},{10,2},{12,4},{14,6},{1,9},{3,11}... | collective-permute-start | bytes 589832 | tf_op jit(solution)/shard_map/ppermute | solution.py:413
  76.9 25.4 %collective-permute-start.15 = (bf16[128,768]{1,0:T(8,128)(2,1)}, bf16[128,768]{1,0:T(8,128)(2,1)S(1)}, u32[]{:S(2)}, u32[]{:S(2)}) collective-permute-start(bf16[128,768]{1,0:T(8,128)(2,1)} %get-tuple-element.136), channel_id=1, source_target_pairs={{0,4},{2,6},{4,0},{6,2},{8,12},{10,14},{12,8},{14,10},{1,5},{3,7},... | collective-permute-start | bytes 589832 | tf_op jit(solution)/shard_map/ppermute | solution.py:413
  76.9 27.3 %collective-permute-start.16 = (bf16[128,768]{1,0:T(8,128)(2,1)}, bf16[128,768]{1,0:T(8,128)(2,1)S(1)}, u32[]{:S(2)}, u32[]{:S(2)}) collective-permute-start(bf16[128,768]{1,0:T(8,128)(2,1)} %get-tuple-element.137), channel_id=1, source_target_pairs={{0,10},{2,8},{4,14},{6,12},{8,2},{10,0},{12,6},{14,4},{1,11},{3,9}... | collective-permute-start | bytes 589832 | tf_op jit(solution)/shard_map/ppermute | solution.py:413
  81.0 23.2 %collective-permute-start.17 = (bf16[128,768]{1,0:T(8,128)(2,1)}, bf16[128,768]{1,0:T(8,128)(2,1)S(1)}, u32[]{:S(2)}, u32[]{:S(2)}) collective-permute-start(bf16[128,768]{1,0:T(8,128)(2,1)} %get-tuple-element.138), channel_id=1, source_target_pairs={{0,6},{2,4},{4,2},{6,0},{8,14},{10,12},{12,10},{14,8},{1,7},{3,5},... | collective-permute-start | bytes 589832 | tf_op jit(solution)/shard_map/ppermute | solution.py:413
  86.1 18.1 %collective-permute-start.18 = (bf16[128,768]{1,0:T(8,128)(2,1)}, bf16[128,768]{1,0:T(8,128)(2,1)S(1)}, u32[]{:S(2)}, u32[]{:S(2)}) collective-permute-start(bf16[128,768]{1,0:T(8,128)(2,1)} %get-tuple-element.139), channel_id=1, source_target_pairs={{0,12},{2,14},{4,8},{6,10},{8,4},{10,6},{12,0},{14,2},{1,13},{3,15... | collective-permute-start | bytes 589832 | tf_op jit(solution)/shard_map/ppermute | solution.py:413
  113.8 15.0 %collective-permute-start.21 = (f32[128,768]{1,0:T(8,128)S(1)}, f32[128,768]{1,0:T(8,128)}, u32[]{:S(2)}, u32[]{:S(2)}) collective-permute-start(f32[128,768]{1,0:T(8,128)S(1)} %dynamic-slice_bitcast_fusion.1), channel_id=1, source_target_pairs={{0,2},{2,0},{4,6},{6,4},{8,10},{10,8},{12,14},{14,12},{1,3},{3,1},... | collective-permute-start | bytes 1179656 | tf_op jit(solution)/shard_map/ppermute | solution.py:413
  115.4 14.5 %collective-permute-start.22 = (bf16[128,768]{1,0:T(8,128)(2,1)}, bf16[128,768]{1,0:T(8,128)(2,1)}, u32[]{:S(2)}, u32[]{:S(2)}) collective-permute-start(bf16[128,768]{1,0:T(8,128)(2,1)} %get-tuple-element.143), channel_id=1, source_target_pairs={{0,14},{2,12},{4,10},{6,8},{8,6},{10,4},{12,2},{14,0},{1,15},{3,13... | collective-permute-start | bytes 589832 | tf_op jit(solution)/shard_map/ppermute | solution.py:413
  118.9 19.0 %collective-permute-start.23 = (bf16[128,768]{1,0:T(8,128)(2,1)}, bf16[128,768]{1,0:T(8,128)(2,1)}, u32[]{:S(2)}, u32[]{:S(2)}) collective-permute-start(bf16[128,768]{1,0:T(8,128)(2,1)} %get-tuple-element.144), channel_id=1, source_target_pairs={{0,8},{2,10},{4,12},{6,14},{8,0},{10,2},{12,4},{14,6},{1,9},{3,11}... | collective-permute-start | bytes 589832 | tf_op jit(solution)/shard_map/ppermute | solution.py:413
  156.2 14.7 %collective-permute-start.32 = (bf16[128,768]{1,0:T(8,128)(2,1)}, bf16[128,768]{1,0:T(8,128)(2,1)S(1)}, u32[]{:S(2)}, u32[]{:S(2)}) collective-permute-start(bf16[128,768]{1,0:T(8,128)(2,1)} %get-tuple-element.153), channel_id=1, source_target_pairs={{0,2},{2,0},{4,6},{6,4},{8,10},{10,8},{12,14},{14,12},{1,3},{3,1},... | collective-permute-start | bytes 589832 | tf_op jit(solution)/shard_map/ppermute | solution.py:413
  156.2 14.7 %collective-permute-start.33 = (bf16[128,768]{1,0:T(8,128)(2,1)}, bf16[128,768]{1,0:T(8,128)(2,1)S(1)}, u32[]{:S(2)}, u32[]{:S(2)}) collective-permute-start(bf16[128,768]{1,0:T(8,128)(2,1)} %get-tuple-element.154), channel_id=1, source_target_pairs={{0,6},{2,4},{4,2},{6,0},{8,14},{10,12},{12,10},{14,8},{1,7},{3,5},... | collective-permute-start | bytes 589832 | tf_op jit(solution)/shard_map/ppermute | solution.py:413
  156.9 14.1 %collective-permute-start.34 = (bf16[128,768]{1,0:T(8,128)(2,1)}, bf16[128,768]{1,0:T(8,128)(2,1)S(1)}, u32[]{:S(2)}, u32[]{:S(2)}) collective-permute-start(bf16[128,768]{1,0:T(8,128)(2,1)} %get-tuple-element.155), channel_id=1, source_target_pairs={{0,12},{2,14},{4,8},{6,10},{8,4},{10,6},{12,0},{14,2},{1,13},{3,15... | collective-permute-start | bytes 589832 | tf_op jit(solution)/shard_map/ppermute | solution.py:413
  (47 other events, 448.9 us)

commit v12 on v11

--- a/solution.py
+++ b/solution.py
@@ -14,7 +14,7 @@
 KW = 64
 shrink_level = 0.05
 FIRST = 4
-HELD = 5
+HELD = 3
 MIB = 1024 * 1024
 
 
@@ -440,15 +440,16 @@
         self.count = lax.axis_size("space") // 2
         self.held = sums.reshape(-1, self.lanes)
 
-    def halve(self, axis, distance, bit, arrived):
+    def halve(self, axis, distance, bit, kind, arrived):
         pair = waiting(self.held, arrived).reshape(2, -1, self.lanes)
-        self.held = pick(pair, bit) + swap_with(pick(pair, 1 - bit), axis, distance)
+        taken = swap_with(pick(pair, 1 - bit).astype(kind), axis, distance)
+        self.held = pick(pair, bit) + taken.astype(jnp.float32)
 
     def over_dp(self):
-        self.halve("dp", 1, self.side, [])
+        self.halve("dp", 1, self.side, jnp.float32, [])
 
     def over_next(self, arrived):
-        self.halve("space", 1, self.me % 2, arrived)
+        self.halve("space", 1, self.me % 2, jnp.bfloat16, arrived)
 
     def scatter(self, arrived):
         shares = waiting(self.held, arrived).reshape(self.count, -1, self.lanes)
@@ -591,7 +592,7 @@
     grad_image, sums = waiting((list(grad_image), sums), early)
     group_sum = GroupSum(sums)
     group_sum.over_dp()
-    group_sum.over_next(late[:1])
+    group_sum.over_next(late[:2])
     grad_band = {0: grad_image[0]}
     send(grad_image, order, grad_band)
     arrived = [grad_band[offset] for offset in order]
@@ -599,11 +600,11 @@
     grad_band = [grad_band[offset] for offset in range(owners)]
     again = waiting(fields, early[:1])
     output = rows_inside(to_cells(me, scaled.T, image_band, again))
-    group_sum.scatter(late[1:] + arrived[:1])
-    group_sum.gather(arrived[1:3])
+    group_sum.scatter(late[2:])
+    group_sum.gather(arrived[:2])
     group_sum.quarter, output = lax.optimization_barrier((group_sum.quarter, output))
-    group_sum.gather_next(arrived[3:6])
-    half, other = group_sum.gather_dp(arrived[6:])
+    group_sum.gather_next(arrived[2:4])
+    half, other = group_sum.gather_dp(arrived[4:])
     grad_fields = rows_inside(to_cells(me, plain.T, grad_band, cotangent))
     place = lax.axis_index("space")
     here = jnp.stack([lax.axis_index("dp"), place % 2, place // 2]).astype(jnp.int32)

time: 191 us -> 191 us (level)
  waiting for transfers between devices: 45.7 us -> 49.4 us
  starting transfers between devices: 88.1 us -> 84.9 us
    ppermute x38, waiting for transfers between devices: 45.7 us -> 49.4 us  [swap_with(): return lax.ppermute(values, axis, pairs)]
    ppermute x38, starting transfers between devices: 88.1 us -> 84.9 us  [swap_with(): return lax.ppermute(values, axis, pairs)]
    unnamed x67 -> x73, local copies, waits for them, and re-layouts: 4.6 us -> 4.04 us
  transfers between devices with their start and end apart: 38 -> 38, of which waited for: 14 -> 16; matrix products, arithmetic and copies ran while one was open for 7% -> 7% of each run, Pallas kernels for 17% -> 17%
where the time goes in v12:
time: 191 us; the launch traced here: 190 us
  starting transfers between devices  84.9 us (44%)
  waiting for transfers between devices  49.4 us (26%)
  Pallas kernels  36.2 us (19%)
  local copies, waits for them, and re-layouts  15.5 us (8%)
  other arithmetic  2.59 us (1%)
    ppermute x38, starting transfers between devices, swap_with(): return lax.ppermute(values, axis, pairs)  84.9 us
    ppermute x38, waiting for transfers between devices, swap_with(): return lax.ppermute(values, axis, pairs)  49.4 us
    pallas_call x1, Pallas kernels, backward_mid(): pl.pallas_call(functools.partial(backward_kernel, size_of_block, len(band...  12.9 us
    pallas_call x1, Pallas kernels, forward_mid(): pl.pallas_call(functools.partial(forward_kernel, len(bands)), grid_spec=p...  7.65 us
    pallas_call x2, Pallas kernels, to_cells(): pl.pallas_call(to_cells_kernel, grid_spec=pltpu.PrefetchScalarGridSpec(nu...  6.17 us
    pallas_call x2, local copies, waits for them, and re-layouts, to_cells(): pl.pallas_call(to_cells_kernel, grid_spec=pltpu.PrefetchScalarGridSpec(nu...  6.13 us
    pallas_call x2, Pallas kernels, to_modes(): pl.pallas_call(to_modes_kernel, grid_spec=pltpu.PrefetchScalarGridSpec(nu...  4.79 us
    unnamed x73, local copies, waits for them, and re-layouts  4.04 us
  transfers between devices with their start and end apart: 38, of which 16 were waited for; matrix products, arithmetic and copies ran while one was open for 7% of the time, Pallas kernels for 17%

profile of v12, /device:TPU:0, one launch (start us, length us, event | category | flops | bytes accessed | tf_op | source)
XLA Modules:
  0.0 189.8 jit_solution(14224546482488826666)
XLA Ops:
  5.0 3.0 %collective-permute-start = (bf16[128,768]{1,0:T(8,128)(2,1)}, bf16[128,768]{1,0:T(8,128)(2,1)S(1)}, u32[]{:S(2)}, u32[]{:S(2)}) collective-permute-start(bf16[128,768]{1,0:T(8,128)(2,1)} %get-tuple-element.98), channel_id=1, source_target_pairs={{0,2},{2,0},{4,6},{6,4},{8,10},{10,8},{12,14},{14,12},{1,3},{3,1},... | collective-permute-start | bytes 589832 | tf_op jit(solution)/shard_map/ppermute | solution.py:413
  9.6 3.0 %collective-permute-start.3 = (bf16[128,768]{1,0:T(8,128)(2,1)}, bf16[128,768]{1,0:T(8,128)(2,1)S(1)}, u32[]{:S(2)}, u32[]{:S(2)}) collective-permute-start(bf16[128,768]{1,0:T(8,128)(2,1)} %get-tuple-element.101), channel_id=1, source_target_pairs={{0,8},{2,10},{4,12},{6,14},{8,0},{10,2},{12,4},{14,6},{1,9},{3,11}... | collective-permute-start | bytes 589832 | tf_op jit(solution)/shard_map/ppermute | solution.py:413
  13.8 3.6 %collective-permute-start.5 = (bf16[128,768]{1,0:T(8,128)(2,1)}, bf16[128,768]{1,0:T(8,128)(2,1)S(1)}, u32[]{:S(2)}, u32[]{:S(2)}) collective-permute-start(bf16[128,768]{1,0:T(8,128)(2,1)} %get-tuple-element.103), channel_id=1, source_target_pairs={{0,12},{2,14},{4,8},{6,10},{8,4},{10,6},{12,0},{14,2},{1,13},{3,15... | collective-permute-start | bytes 589832 | tf_op jit(solution)/shard_map/ppermute | solution.py:413
  17.4 6.2 %collective-permute-done.1.refs_2_ = bf16[128,768]{1,0:T(8,128)(2,1)S(1)} collective-permute-done((bf16[128,768]{1,0:T(8,128)(2,1)}, bf16[128,768]{1,0:T(8,128)(2,1)S(1)}, u32[]{:S(2)}, u32[]{:S(2)}) %collective-permute-start.1) | collective-permute-done | bytes 196640 | tf_op jit(solution)/shard_map/ppermute | solution.py:413
  33.2 4.5 %collective-permute-start.9 = (bf16[128,768]{1,0:T(8,128)(2,1)}, bf16[128,768]{1,0:T(8,128)(2,1)S(1)}, u32[]{:S(2)}, u32[]{:S(2)}) collective-permute-start(bf16[128,768]{1,0:T(8,128)(2,1)} %get-tuple-element.110), channel_id=1, source_target_pairs={{0,6},{2,4},{4,2},{6,0},{8,14},{10,12},{12,10},{14,8},{1,7},{3,5},... | collective-permute-start | bytes 589832 | tf_op jit(solution)/shard_map/ppermute | solution.py:413
  37.7 3.2 %collective-permute-done.4.refs_5_ = bf16[128,768]{1,0:T(8,128)(2,1)S(1)} collective-permute-done((bf16[128,768]{1,0:T(8,128)(2,1)}, bf16[128,768]{1,0:T(8,128)(2,1)S(1)}, u32[]{:S(2)}, u32[]{:S(2)}) %collective-permute-start.4) | collective-permute-done | bytes 196640 | tf_op jit(solution)/shard_map/ppermute | solution.py:413
  41.6 12.6 %collective-permute-start.11 = (bf16[128,768]{1,0:T(8,128)(2,1)}, bf16[128,768]{1,0:T(8,128)(2,1)}, u32[]{:S(2)}, u32[]{:S(2)}) collective-permute-start(bf16[128,768]{1,0:T(8,128)(2,1)} %get-tuple-element.112), channel_id=1, source_target_pairs={{0,10},{2,8},{4,14},{6,12},{8,2},{10,0},{12,6},{14,4},{1,11},{3,9}... | collective-permute-start | bytes 589832 | tf_op jit(solution)/shard_map/ppermute | solution.py:413
  54.3 7.7 %mix_forward.1 = (bf16[128,768]{1,0:T(8,128)(2,1)}, bf16[128,768]{1,0:T(8,128)(2,1)}, bf16[128,768]{1,0:T(8,128)(2,1)}, bf16[128,768]{1,0:T(8,128)(2,1)}, bf16[1...) custom-call(s32[1]{0:T(128)} %bitcast.me_ref, ...), custom_call_target="tpu_custom_call" | custom-call | flops 2415919104 | bytes 17301504 | tf_op jit(solution)/shard_map/mix_forward/pallas_call | solution.py:340
  62.7 4.7 %collective-permute-start.13 = (bf16[128,768]{1,0:T(8,128)(2,1)S(1)}, bf16[128,768]{1,0:T(8,128)(2,1)}, u32[]{:S(2)}, u32[]{:S(2)}) collective-permute-start(bf16[128,768]{1,0:T(8,128)(2,1)S(1)} %copy-done.27), channel_id=1, source_target_pairs={{0,14},{2,12},{4,10},{6,8},{8,6},{10,4},{12,2},{14,0},{1,15},{3,13... | collective-permute-start | bytes 589832 | tf_op jit(solution)/shard_map/ppermute | solution.py:413
  67.4 8.8 %collective-permute-start.14 = (bf16[128,768]{1,0:T(8,128)(2,1)}, bf16[128,768]{1,0:T(8,128)(2,1)S(1)}, u32[]{:S(2)}, u32[]{:S(2)}) collective-permute-start(bf16[128,768]{1,0:T(8,128)(2,1)} %get-tuple-element.135), channel_id=1, source_target_pairs={{0,8},{2,10},{4,12},{6,14},{8,0},{10,2},{12,4},{14,6},{1,9},{3,11}... | collective-permute-start | bytes 589832 | tf_op jit(solution)/shard_map/ppermute | solution.py:413
  76.9 4.1 %collective-permute-start.16 = (bf16[128,768]{1,0:T(8,128)(2,1)}, bf16[128,768]{1,0:T(8,128)(2,1)S(1)}, u32[]{:S(2)}, u32[]{:S(2)}) collective-permute-start(bf16[128,768]{1,0:T(8,128)(2,1)} %get-tuple-element.137), channel_id=1, source_target_pairs={{0,10},{2,8},{4,14},{6,12},{8,2},{10,0},{12,6},{14,4},{1,11},{3,9}... | collective-permute-start | bytes 589832 | tf_op jit(solution)/shard_map/ppermute | solution.py:413
  81.1 12.9 %mix_backward.1 = (bf16[128,768]{1,0:T(8,128)(2,1)}, bf16[128,768]{1,0:T(8,128)(2,1)}, bf16[128,768]{1,0:T(8,128)(2,1)}, bf16[128,768]{1,0:T(8,128)(2,1)}, bf16[...) custom-call(s32[1]{0:T(128)} %bitcast.me_ref, ...), custom_call_target="tpu_custom_call" | custom-call | flops 4831838208 | bytes 17301504 | tf_op jit(solution)/shard_map/mix_backward/pallas_call | solution.py:378
  94.5 3.4 %collective-permute-done.16.refs_5_ = bf16[128,768]{1,0:T(8,128)(2,1)S(1)} collective-permute-done((bf16[128,768]{1,0:T(8,128)(2,1)}, bf16[128,768]{1,0:T(8,128)(2,1)S(1)}, u32[]{:S(2)}, u32[]{:S(2)}) %collective-permute-start.16) | collective-permute-done | bytes 196640 | tf_op jit(solution)/shard_map/ppermute | solution.py:413
  99.3 7.9 %collective-permute-start.18 = (bf16[128,768]{1,0:T(8,128)(2,1)S(1)}, bf16[128,768]{1,0:T(8,128)(2,1)}, u32[]{:S(2)}, u32[]{:S(2)}) collective-permute-start(bf16[128,768]{1,0:T(8,128)(2,1)S(1)} %copy-done.24), channel_id=1, source_target_pairs={{0,6},{2,4},{4,2},{6,0},{8,14},{10,12},{12,10},{14,8},{1,7},{3,5},... | collective-permute-start | bytes 589832 | tf_op jit(solution)/shard_map/ppermute | solution.py:413
  107.3 3.4 %collective-permute-start.19 = (bf16[128,768]{1,0:T(8,128)(2,1)S(1)}, bf16[128,768]{1,0:T(8,128)(2,1)}, u32[]{:S(2)}, u32[]{:S(2)}) collective-permute-start(bf16[128,768]{1,0:T(8,128)(2,1)S(1)} %copy-done.23), channel_id=1, source_target_pairs={{0,12},{2,14},{4,8},{6,10},{8,4},{10,6},{12,0},{14,2},{1,13},{3,15... | collective-permute-start | bytes 589832 | tf_op jit(solution)/shard_map/ppermute | solution.py:413
  112.9 7.4 %collective-permute-done.19.refs_6_ = bf16[128,768]{1,0:T(8,128)(2,1)} collective-permute-done((bf16[128,768]{1,0:T(8,128)(2,1)S(1)}, bf16[128,768]{1,0:T(8,128)(2,1)}, u32[]{:S(2)}, u32[]{:S(2)}) %collective-permute-start.19) | collective-permute-done | bytes 196640 | tf_op jit(solution)/shard_map/ppermute | solution.py:413
  123.6 8.8 %collective-permute-done.20 = bf16[128,768]{1,0:T(8,128)(2,1)} collective-permute-done((bf16[128,768]{1,0:T(8,128)(2,1)S(1)}, bf16[128,768]{1,0:T(8,128)(2,1)}, u32[]{:S(2)}, u32[]{:S(2)}) %collective-permute-start.20) | collective-permute-done | bytes 196640 | tf_op jit(solution)/shard_map/ppermute | solution.py:413
  136.1 3.7 %collective-permute-start.23 = (bf16[32,768]{1,0:T(8,128)(2,1)S(1)}, bf16[32,768]{1,0:T(8,128)(2,1)S(1)}, u32[]{:S(2)}, u32[]{:S(2)}) collective-permute-start(bf16[32,768]{1,0:T(8,128)(2,1)S(1)} %get-tuple-element.164), channel_id=1, source_target_pairs={{0,4},{2,6},{4,0},{6,2},{8,12},{10,14},{12,8},{14,10},{1,5},{3,7},... | collective-permute-start | bytes 147464 | tf_op jit(solution)/shard_map/ppermute | solution.py:413
  145.7 5.3 %collective-permute-done.26.refs_4_ = bf16[128,768]{1,0:T(8,128)(2,1)S(1)} collective-permute-done((bf16[128,768]{1,0:T(8,128)(2,1)}, bf16[128,768]{1,0:T(8,128)(2,1)S(1)}, u32[]{:S(2)}, u32[]{:S(2)}) %collective-permute-start.26) | collective-permute-done | bytes 196640 | tf_op jit(solution)/shard_map/ppermute | solution.py:413
  151.0 4.5 %collective-permute-done.27.refs_2_ = bf16[128,768]{1,0:T(8,128)(2,1)S(1)} collective-permute-done((bf16[128,768]{1,0:T(8,128)(2,1)}, bf16[128,768]{1,0:T(8,128)(2,1)S(1)}, u32[]{:S(2)}, u32[]{:S(2)}) %collective-permute-start.27) | collective-permute-done | bytes 196640 | tf_op jit(solution)/shard_map/ppermute | solution.py:413
  161.8 3.2 %to_cells.2 = bf16[4,2,180,768]{3,2,1,0:T(8,128)(2,1)S(1)} custom-call(s32[1]{0:T(128)} %bitcast.me_ref, bf16[180,128]{1,0:T(8,128)(2,1)S(1)} %copy-done.3, bf16[4,2,180,768]{3,2,1,0:T(8,128)(2,1)S(1)} %copy.23.base_ref, bf16[128,768]{1,0:T(8,128)(2,1)} %get-tuple-element.149.refs_0_, bf16[128,768]{1,0:T(8,128)(2,1)} %collective-permute-done.21.refs_1_, ...), custom_call_target="tpu_custom_call" | custom-call | flops 283115520 | bytes 5996544 | tf_op jit(solution)/shard_map/to_cells/pallas_call | solution.py:182
  165.1 3.1 %copy.30 = bf16[4,2,180,768]{3,1,2,0:T(2,128)(2,1)} copy(bf16[4,2,180,768]{3,2,1,0:T(8,128)(2,1)S(1)} %to_cells.2) | data formatting | bytes 4423680 | tf_op jit(solution)/shard_map/to_cells/pallas_call | solution.py:182
  177.9 3.0 %collective-permute-done.35.refs_7_ = bf16[128,768]{1,0:T(8,128)(2,1)S(1)} collective-permute-done((bf16[128,768]{1,0:T(8,128)(2,1)S(1)}, bf16[128,768]{1,0:T(8,128)(2,1)S(1)}, u32[]{:S(2)}, u32[]{:S(2)}) %collective-permute-start.35) | collective-permute-done | bytes 196640 | tf_op jit(solution)/shard_map/ppermute | solution.py:413
  184.6 3.1 %copy.26 = bf16[4,2,180,768]{3,1,2,0:T(2,128)(2,1)} copy(bf16[4,2,180,768]{3,2,1,0:T(8,128)(2,1)S(1)} %to_cells.3) | data formatting | bytes 4423680 | tf_op jit(solution)/shard_map/to_cells/pallas_call | solution.py:182
  (152 shorter events, 57.5 us)
Async XLA Ops:
  8.0 15.7 %collective-permute-start.1 = (bf16[128,768]{1,0:T(8,128)(2,1)}, bf16[128,768]{1,0:T(8,128)(2,1)S(1)}, u32[]{:S(2)}, u32[]{:S(2)}) collective-permute-start(bf16[128,768]{1,0:T(8,128)(2,1)} %get-tuple-element.99), channel_id=1, source_target_pairs={{0,4},{2,6},{4,0},{6,2},{8,12},{10,14},{12,8},{14,10},{1,5},{3,7},... | collective-permute-start | bytes 589832 | tf_op jit(solution)/shard_map/ppermute | solution.py:413
  9.6 22.3 %collective-permute-start.2 = (bf16[128,768]{1,0:T(8,128)(2,1)}, bf16[128,768]{1,0:T(8,128)(2,1)S(1)}, u32[]{:S(2)}, u32[]{:S(2)}) collective-permute-start(bf16[128,768]{1,0:T(8,128)(2,1)} %get-tuple-element.100), channel_id=1, source_target_pairs={{0,6},{2,4},{4,2},{6,0},{8,14},{10,12},{12,10},{14,8},{1,7},{3,5},... | collective-permute-start | bytes 589832 | tf_op jit(solution)/shard_map/ppermute | solution.py:413
  9.6 23.0 %collective-permute-start.3 = (bf16[128,768]{1,0:T(8,128)(2,1)}, bf16[128,768]{1,0:T(8,128)(2,1)S(1)}, u32[]{:S(2)}, u32[]{:S(2)}) collective-permute-start(bf16[128,768]{1,0:T(8,128)(2,1)} %get-tuple-element.101), channel_id=1, source_target_pairs={{0,8},{2,10},{4,12},{6,14},{8,0},{10,2},{12,4},{14,6},{1,9},{3,11}... | collective-permute-start | bytes 589832 | tf_op jit(solution)/shard_map/ppermute | solution.py:413
  12.5 28.4 %collective-permute-start.4 = (bf16[128,768]{1,0:T(8,128)(2,1)}, bf16[128,768]{1,0:T(8,128)(2,1)S(1)}, u32[]{:S(2)}, u32[]{:S(2)}) collective-permute-start(bf16[128,768]{1,0:T(8,128)(2,1)} %get-tuple-element.102), channel_id=1, source_target_pairs={{0,10},{2,8},{4,14},{6,12},{8,2},{10,0},{12,6},{14,4},{1,11},{3,9}... | collective-permute-start | bytes 589832 | tf_op jit(solution)/shard_map/ppermute | solution.py:413
  13.8 27.7 %collective-permute-start.5 = (bf16[128,768]{1,0:T(8,128)(2,1)}, bf16[128,768]{1,0:T(8,128)(2,1)S(1)}, u32[]{:S(2)}, u32[]{:S(2)}) collective-permute-start(bf16[128,768]{1,0:T(8,128)(2,1)} %get-tuple-element.103), channel_id=1, source_target_pairs={{0,12},{2,14},{4,8},{6,10},{8,4},{10,6},{12,0},{14,2},{1,13},{3,15... | collective-permute-start | bytes 589832 | tf_op jit(solution)/shard_map/ppermute | solution.py:413
  23.7 30.5 %collective-permute-start.6 = (bf16[128,768]{1,0:T(8,128)(2,1)}, bf16[128,768]{1,0:T(8,128)(2,1)}, u32[]{:S(2)}, u32[]{:S(2)}) collective-permute-start(bf16[128,768]{1,0:T(8,128)(2,1)} %get-tuple-element.104), channel_id=1, source_target_pairs={{0,14},{2,12},{4,10},{6,8},{8,6},{10,4},{12,2},{14,0},{1,15},{3,13... | collective-permute-start | bytes 589832 | tf_op jit(solution)/shard_map/ppermute | solution.py:413
  32.5 30.0 %collective-permute-start.8 = (bf16[128,768]{1,0:T(8,128)(2,1)}, bf16[128,768]{1,0:T(8,128)(2,1)S(1)}, u32[]{:S(2)}, u32[]{:S(2)}) collective-permute-start(bf16[128,768]{1,0:T(8,128)(2,1)} %get-tuple-element.109), channel_id=1, source_target_pairs={{0,4},{2,6},{4,0},{6,2},{8,12},{10,14},{12,8},{14,10},{1,5},{3,7},... | collective-permute-start | bytes 589832 | tf_op jit(solution)/shard_map/ppermute | solution.py:413
  33.2 29.5 %collective-permute-start.9 = (bf16[128,768]{1,0:T(8,128)(2,1)}, bf16[128,768]{1,0:T(8,128)(2,1)S(1)}, u32[]{:S(2)}, u32[]{:S(2)}) collective-permute-start(bf16[128,768]{1,0:T(8,128)(2,1)} %get-tuple-element.110), channel_id=1, source_target_pairs={{0,6},{2,4},{4,2},{6,0},{8,14},{10,12},{12,10},{14,8},{1,7},{3,5},... | collective-permute-start | bytes 589832 | tf_op jit(solution)/shard_map/ppermute | solution.py:413
  41.0 26.4 %collective-permute-start.10 = (bf16[128,768]{1,0:T(8,128)(2,1)}, bf16[128,768]{1,0:T(8,128)(2,1)S(1)}, u32[]{:S(2)}, u32[]{:S(2)}) collective-permute-start(bf16[128,768]{1,0:T(8,128)(2,1)} %get-tuple-element.111), channel_id=1, source_target_pairs={{0,8},{2,10},{4,12},{6,14},{8,0},{10,2},{12,4},{14,6},{1,9},{3,11}... | collective-permute-start | bytes 589832 | tf_op jit(solution)/shard_map/ppermute | solution.py:413
  41.6 35.3 %collective-permute-start.11 = (bf16[128,768]{1,0:T(8,128)(2,1)}, bf16[128,768]{1,0:T(8,128)(2,1)}, u32[]{:S(2)}, u32[]{:S(2)}) collective-permute-start(bf16[128,768]{1,0:T(8,128)(2,1)} %get-tuple-element.112), channel_id=1, source_target_pairs={{0,10},{2,8},{4,14},{6,12},{8,2},{10,0},{12,6},{14,4},{1,11},{3,9}... | collective-permute-start | bytes 589832 | tf_op jit(solution)/shard_map/ppermute | solution.py:413
  61.9 15.0 %collective-permute-start.7 = (bf16[128,768]{1,0:T(8,128)(2,1)}, bf16[128,768]{1,0:T(8,128)(2,1)}, u32[]{:S(2)}, u32[]{:S(2)}) collective-permute-start(bf16[128,768]{1,0:T(8,128)(2,1)} %get-tuple-element.123), channel_id=1, source_target_pairs={{0,2},{2,0},{4,6},{6,4},{8,10},{10,8},{12,14},{14,12},{1,3},{3,1},... | collective-permute-start | bytes 589832 | tf_op jit(solution)/shard_map/ppermute | solution.py:413
  62.5 18.5 %collective-permute-start.12 = (bf16[128,768]{1,0:T(8,128)(2,1)S(1)}, bf16[128,768]{1,0:T(8,128)(2,1)}, u32[]{:S(2)}, u32[]{:S(2)}) collective-permute-start(bf16[128,768]{1,0:T(8,128)(2,1)S(1)} %copy-done.29), channel_id=1, source_target_pairs={{0,12},{2,14},{4,8},{6,10},{8,4},{10,6},{12,0},{14,2},{1,13},{3,15... | collective-permute-start | bytes 589832 | tf_op jit(solution)/shard_map/ppermute | solution.py:413
  62.7 18.3 %collective-permute-start.13 = (bf16[128,768]{1,0:T(8,128)(2,1)S(1)}, bf16[128,768]{1,0:T(8,128)(2,1)}, u32[]{:S(2)}, u32[]{:S(2)}) collective-permute-start(bf16[128,768]{1,0:T(8,128)(2,1)S(1)} %copy-done.27), channel_id=1, source_target_pairs={{0,14},{2,12},{4,10},{6,8},{8,6},{10,4},{12,2},{14,0},{1,15},{3,13... | collective-permute-start | bytes 589832 | tf_op jit(solution)/shard_map/ppermute | solution.py:413
  67.4 27.1 %collective-permute-start.14 = (bf16[128,768]{1,0:T(8,128)(2,1)}, bf16[128,768]{1,0:T(8,128)(2,1)S(1)}, u32[]{:S(2)}, u32[]{:S(2)}) collective-permute-start(bf16[128,768]{1,0:T(8,128)(2,1)} %get-tuple-element.135), channel_id=1, source_target_pairs={{0,8},{2,10},{4,12},{6,14},{8,0},{10,2},{12,4},{14,6},{1,9},{3,11}... | collective-permute-start | bytes 589832 | tf_op jit(solution)/shard_map/ppermute | solution.py:413
  76.9 17.6 %collective-permute-start.15 = (bf16[128,768]{1,0:T(8,128)(2,1)}, bf16[128,768]{1,0:T(8,128)(2,1)S(1)}, u32[]{:S(2)}, u32[]{:S(2)}) collective-permute-start(bf16[128,768]{1,0:T(8,128)(2,1)} %get-tuple-element.136), channel_id=1, source_target_pairs={{0,4},{2,6},{4,0},{6,2},{8,12},{10,14},{12,8},{14,10},{1,5},{3,7},... | collective-permute-start | bytes 589832 | tf_op jit(solution)/shard_map/ppermute | solution.py:413
  76.9 21.1 %collective-permute-start.16 = (bf16[128,768]{1,0:T(8,128)(2,1)}, bf16[128,768]{1,0:T(8,128)(2,1)S(1)}, u32[]{:S(2)}, u32[]{:S(2)}) collective-permute-start(bf16[128,768]{1,0:T(8,128)(2,1)} %get-tuple-element.137), channel_id=1, source_target_pairs={{0,10},{2,8},{4,14},{6,12},{8,2},{10,0},{12,6},{14,4},{1,11},{3,9}... | collective-permute-start | bytes 589832 | tf_op jit(solution)/shard_map/ppermute | solution.py:413
  99.3 13.5 %collective-permute-start.18 = (bf16[128,768]{1,0:T(8,128)(2,1)S(1)}, bf16[128,768]{1,0:T(8,128)(2,1)}, u32[]{:S(2)}, u32[]{:S(2)}) collective-permute-start(bf16[128,768]{1,0:T(8,128)(2,1)S(1)} %copy-done.24), channel_id=1, source_target_pairs={{0,6},{2,4},{4,2},{6,0},{8,14},{10,12},{12,10},{14,8},{1,7},{3,5},... | collective-permute-start | bytes 589832 | tf_op jit(solution)/shard_map/ppermute | solution.py:413
  107.3 13.0 %collective-permute-start.19 = (bf16[128,768]{1,0:T(8,128)(2,1)S(1)}, bf16[128,768]{1,0:T(8,128)(2,1)}, u32[]{:S(2)}, u32[]{:S(2)}) collective-permute-start(bf16[128,768]{1,0:T(8,128)(2,1)S(1)} %copy-done.23), channel_id=1, source_target_pairs={{0,12},{2,14},{4,8},{6,10},{8,4},{10,6},{12,0},{14,2},{1,13},{3,15... | collective-permute-start | bytes 589832 | tf_op jit(solution)/shard_map/ppermute | solution.py:413
  121.8 13.5 %collective-permute-start.21 = (bf16[128,768]{1,0:T(8,128)(2,1)}, bf16[128,768]{1,0:T(8,128)(2,1)}, u32[]{:S(2)}, u32[]{:S(2)}) collective-permute-start(bf16[128,768]{1,0:T(8,128)(2,1)} %get-tuple-element.142), channel_id=1, source_target_pairs={{0,2},{2,0},{4,6},{6,4},{8,10},{10,8},{12,14},{14,12},{1,3},{3,1},... | collective-permute-start | bytes 589832 | tf_op jit(solution)/shard_map/ppermute | solution.py:413
  122.4 13.0 %collective-permute-start.22 = (bf16[128,768]{1,0:T(8,128)(2,1)}, bf16[128,768]{1,0:T(8,128)(2,1)}, u32[]{:S(2)}, u32[]{:S(2)}) collective-permute-start(bf16[128,768]{1,0:T(8,128)(2,1)} %get-tuple-element.143), channel_id=1, source_target_pairs={{0,14},{2,12},{4,10},{6,8},{8,6},{10,4},{12,2},{14,0},{1,15},{3,13... | collective-permute-start | bytes 589832 | tf_op jit(solution)/shard_map/ppermute | solution.py:413
  139.8 15.7 %collective-permute-start.27 = (bf16[128,768]{1,0:T(8,128)(2,1)}, bf16[128,768]{1,0:T(8,128)(2,1)S(1)}, u32[]{:S(2)}, u32[]{:S(2)}) collective-permute-start(bf16[128,768]{1,0:T(8,128)(2,1)} %get-tuple-element.146), channel_id=1, source_target_pairs={{0,4},{2,6},{4,0},{6,2},{8,12},{10,14},{12,8},{14,10},{1,5},{3,7},... | collective-permute-start | bytes 589832 | tf_op jit(solution)/shard_map/ppermute | solution.py:413
  141.6 26.5 %collective-permute-start.32 = (bf16[128,768]{1,0:T(8,128)(2,1)}, bf16[128,768]{1,0:T(8,128)(2,1)S(1)}, u32[]{:S(2)}, u32[]{:S(2)}) collective-permute-start(bf16[128,768]{1,0:T(8,128)(2,1)} %get-tuple-element.153), channel_id=1, source_target_pairs={{0,6},{2,4},{4,2},{6,0},{8,14},{10,12},{12,10},{14,8},{1,7},{3,5},... | collective-permute-start | bytes 589832 | tf_op jit(solution)/shard_map/ppermute | solution.py:413
  142.8 25.4 %collective-permute-start.33 = (bf16[128,768]{1,0:T(8,128)(2,1)}, bf16[128,768]{1,0:T(8,128)(2,1)S(1)}, u32[]{:S(2)}, u32[]{:S(2)}) collective-permute-start(bf16[128,768]{1,0:T(8,128)(2,1)} %get-tuple-element.154), channel_id=1, source_target_pairs={{0,10},{2,8},{4,14},{6,12},{8,2},{10,0},{12,6},{14,4},{1,11},{3,9}... | collective-permute-start | bytes 589832 | tf_op jit(solution)/shard_map/ppermute | solution.py:413
  155.5 12.6 %collective-permute-start.30 = (bf16[32,768]{1,0:T(8,128)(2,1)S(1)}, bf16[32,768]{1,0:T(8,128)(2,1)S(1)}, u32[]{:S(2)}, u32[]{:S(2)}) collective-permute-start(bf16[32,768]{1,0:T(8,128)(2,1)S(1)} %fusion.3), channel_id=1, source_target_pairs={{0,12},{2,14},{4,8},{6,10},{8,4},{10,6},{12,0},{14,2},{1,13},{3,15... | collective-permute-start | bytes 147464 | tf_op jit(solution)/shard_map/ppermute | solution.py:413
  (50 other events, 494.4 us)

commit v13 on v12

--- a/solution.py
+++ b/solution.py
@@ -13,7 +13,7 @@
 
 KW = 64
 shrink_level = 0.05
-FIRST = 4
+FIRST = 5
 HELD = 3
 MIB = 1024 * 1024
 
@@ -600,11 +600,11 @@
     grad_band = [grad_band[offset] for offset in range(owners)]
     again = waiting(fields, early[:1])
     output = rows_inside(to_cells(me, scaled.T, image_band, again))
-    group_sum.scatter(late[2:])
-    group_sum.gather(arrived[:2])
+    group_sum.scatter(late[2:] + arrived[:1])
+    group_sum.gather(arrived[1:3])
     group_sum.quarter, output = lax.optimization_barrier((group_sum.quarter, output))
-    group_sum.gather_next(arrived[2:4])
-    half, other = group_sum.gather_dp(arrived[4:])
+    group_sum.gather_next(arrived[3:5])
+    half, other = group_sum.gather_dp(arrived[5:])
     grad_fields = rows_inside(to_cells(me, plain.T, grad_band, cotangent))
     place = lax.axis_index("space")
     here = jnp.stack([lax.axis_index("dp"), place % 2, place // 2]).astype(jnp.int32)

time: 191 us -> 192 us (level)
  starting transfers between devices: 84.9 us -> 88.9 us
  waiting for transfers between devices: 49.4 us -> 46.6 us
    ppermute x38, starting transfers between devices: 84.9 us -> 88.9 us  [swap_with(): return lax.ppermute(values, axis, pairs)]
    ppermute x38, waiting for transfers between devices: 49.4 us -> 46.6 us  [swap_with(): return lax.ppermute(values, axis, pairs)]
    unnamed x73 -> x69, local copies, waits for them, and re-layouts: 4.04 us -> 4.67 us
  transfers between devices with their start and end apart: 38 -> 38, of which waited for: 16 -> 11; matrix products, arithmetic and copies ran while one was open for 7% -> 7% of each run, Pallas kernels for 17% -> 17%
where the time goes in v13:
time: 192 us
  starting transfers between devices  88.9 us (46%)
  waiting for transfers between devices  46.6 us (24%)
  Pallas kernels  36.3 us (19%)
  local copies, waits for them, and re-layouts  16.1 us (8%)
  other arithmetic  2.59 us (1%)
    ppermute x38, starting transfers between devices, swap_with(): return lax.ppermute(values, axis, pairs)  88.9 us
    ppermute x38, waiting for transfers between devices, swap_with(): return lax.ppermute(values, axis, pairs)  46.6 us
    pallas_call x1, Pallas kernels, backward_mid(): pl.pallas_call(functools.partial(backward_kernel, size_of_block, len(band...  12.9 us
    pallas_call x1, Pallas kernels, forward_mid(): pl.pallas_call(functools.partial(forward_kernel, len(bands)), grid_spec=p...  7.66 us
    pallas_call x2, Pallas kernels, to_cells(): pl.pallas_call(to_cells_kernel, grid_spec=pltpu.PrefetchScalarGridSpec(nu...  6.17 us
    pallas_call x2, local copies, waits for them, and re-layouts, to_cells(): pl.pallas_call(to_cells_kernel, grid_spec=pltpu.PrefetchScalarGridSpec(nu...  6.13 us
    pallas_call x2, Pallas kernels, to_modes(): pl.pallas_call(to_modes_kernel, grid_spec=pltpu.PrefetchScalarGridSpec(nu...  4.79 us
    unnamed x69, local copies, waits for them, and re-layouts  4.67 us
  transfers between devices with their start and end apart: 38, of which 11 were waited for; matrix products, arithmetic and copies ran while one was open for 7% of the time, Pallas kernels for 17%

profile of v13, /device:TPU:0, one launch (start us, length us, event | category | flops | bytes accessed | tf_op | source)
XLA Modules:
  0.0 191.7 jit_solution(17765318351974086923)
XLA Ops:
  13.8 3.6 %collective-permute-start.5 = (bf16[128,768]{1,0:T(8,128)(2,1)}, bf16[128,768]{1,0:T(8,128)(2,1)S(1)}, u32[]{:S(2)}, u32[]{:S(2)}) collective-permute-start(bf16[128,768]{1,0:T(8,128)(2,1)} %get-tuple-element.102), channel_id=1, source_target_pairs={{0,12},{2,14},{4,8},{6,10},{8,4},{10,6},{12,0},{14,2},{1,13},{3,15... | collective-permute-start | bytes 589832 | tf_op jit(solution)/shard_map/ppermute | solution.py:413
  17.4 6.2 %collective-permute-done.1.refs_2_ = bf16[128,768]{1,0:T(8,128)(2,1)S(1)} collective-permute-done((bf16[128,768]{1,0:T(8,128)(2,1)}, bf16[128,768]{1,0:T(8,128)(2,1)S(1)}, u32[]{:S(2)}, u32[]{:S(2)}) %collective-permute-start.1) | collective-permute-done | bytes 196640 | tf_op jit(solution)/shard_map/ppermute | solution.py:413
  33.2 4.5 %collective-permute-start.9 = (bf16[128,768]{1,0:T(8,128)(2,1)}, bf16[128,768]{1,0:T(8,128)(2,1)S(1)}, u32[]{:S(2)}, u32[]{:S(2)}) collective-permute-start(bf16[128,768]{1,0:T(8,128)(2,1)} %get-tuple-element.109), channel_id=1, source_target_pairs={{0,6},{2,4},{4,2},{6,0},{8,14},{10,12},{12,10},{14,8},{1,7},{3,5},... | collective-permute-start | bytes 589832 | tf_op jit(solution)/shard_map/ppermute | solution.py:413
  37.7 3.2 %collective-permute-done.4.refs_5_ = bf16[128,768]{1,0:T(8,128)(2,1)S(1)} collective-permute-done((bf16[128,768]{1,0:T(8,128)(2,1)}, bf16[128,768]{1,0:T(8,128)(2,1)S(1)}, u32[]{:S(2)}, u32[]{:S(2)}) %collective-permute-start.4) | collective-permute-done | bytes 196640 | tf_op jit(solution)/shard_map/ppermute | solution.py:413
  41.6 14.7 %collective-permute-start.11 = (bf16[128,768]{1,0:T(8,128)(2,1)}, bf16[128,768]{1,0:T(8,128)(2,1)}, u32[]{:S(2)}, u32[]{:S(2)}) collective-permute-start(bf16[128,768]{1,0:T(8,128)(2,1)} %get-tuple-element.111), channel_id=1, source_target_pairs={{0,10},{2,8},{4,14},{6,12},{8,2},{10,0},{12,6},{14,4},{1,11},{3,9}... | collective-permute-start | bytes 589832 | tf_op jit(solution)/shard_map/ppermute | solution.py:413
  56.9 7.7 %mix_forward.1 = (bf16[128,768]{1,0:T(8,128)(2,1)}, bf16[128,768]{1,0:T(8,128)(2,1)}, bf16[128,768]{1,0:T(8,128)(2,1)}, bf16[128,768]{1,0:T(8,128)(2,1)}, bf16[1...) custom-call(s32[1]{0:T(128)} %bitcast.me_ref, ...), custom_call_target="tpu_custom_call" | custom-call | flops 2415919104 | bytes 17301504 | tf_op jit(solution)/shard_map/mix_forward/pallas_call | solution.py:340
  64.7 4.8 %collective-permute-start.13 = (bf16[128,768]{1,0:T(8,128)(2,1)S(1)}, bf16[128,768]{1,0:T(8,128)(2,1)}, u32[]{:S(2)}, u32[]{:S(2)}) collective-permute-start(bf16[128,768]{1,0:T(8,128)(2,1)S(1)} %copy-done.25), channel_id=1, source_target_pairs={{0,14},{2,12},{4,10},{6,8},{8,6},{10,4},{12,2},{14,0},{1,15},{3,13... | collective-permute-start | bytes 589832 | tf_op jit(solution)/shard_map/ppermute | solution.py:413
  69.5 8.8 %collective-permute-start.14 = (bf16[128,768]{1,0:T(8,128)(2,1)}, bf16[128,768]{1,0:T(8,128)(2,1)S(1)}, u32[]{:S(2)}, u32[]{:S(2)}) collective-permute-start(bf16[128,768]{1,0:T(8,128)(2,1)} %get-tuple-element.133), channel_id=1, source_target_pairs={{0,8},{2,10},{4,12},{6,14},{8,0},{10,2},{12,4},{14,6},{1,9},{3,11}... | collective-permute-start | bytes 589832 | tf_op jit(solution)/shard_map/ppermute | solution.py:413
  78.3 9.7 %collective-permute-start.16 = (bf16[128,768]{1,0:T(8,128)(2,1)}, bf16[128,768]{1,0:T(8,128)(2,1)S(1)}, u32[]{:S(2)}, u32[]{:S(2)}) collective-permute-start(bf16[128,768]{1,0:T(8,128)(2,1)} %get-tuple-element.135), channel_id=1, source_target_pairs={{0,10},{2,8},{4,14},{6,12},{8,2},{10,0},{12,6},{14,4},{1,11},{3,9}... | collective-permute-start | bytes 589832 | tf_op jit(solution)/shard_map/ppermute | solution.py:413
  88.1 12.9 %mix_backward.1 = (bf16[128,768]{1,0:T(8,128)(2,1)}, bf16[128,768]{1,0:T(8,128)(2,1)}, bf16[128,768]{1,0:T(8,128)(2,1)}, bf16[128,768]{1,0:T(8,128)(2,1)}, bf16[...) custom-call(s32[1]{0:T(128)} %bitcast.me_ref, ...), custom_call_target="tpu_custom_call" | custom-call | flops 4831838208 | bytes 17301504 | tf_op jit(solution)/shard_map/mix_backward/pallas_call | solution.py:378
  103.0 4.3 %collective-permute-start.18 = (bf16[128,768]{1,0:T(8,128)(2,1)S(1)}, bf16[128,768]{1,0:T(8,128)(2,1)}, u32[]{:S(2)}, u32[]{:S(2)}) collective-permute-start(bf16[128,768]{1,0:T(8,128)(2,1)S(1)} %copy-done.22), channel_id=1, source_target_pairs={{0,6},{2,4},{4,2},{6,0},{8,14},{10,12},{12,10},{14,8},{1,7},{3,5},... | collective-permute-start | bytes 589832 | tf_op jit(solution)/shard_map/ppermute | solution.py:413
  112.9 5.4 %collective-permute-done.19.refs_6_ = bf16[128,768]{1,0:T(8,128)(2,1)} collective-permute-done((bf16[128,768]{1,0:T(8,128)(2,1)S(1)}, bf16[128,768]{1,0:T(8,128)(2,1)}, u32[]{:S(2)}, u32[]{:S(2)}) %collective-permute-start.19) | collective-permute-done | bytes 196640 | tf_op jit(solution)/shard_map/ppermute | solution.py:413
  118.3 3.6 %collective-permute-start.20 = (bf16[128,768]{1,0:T(8,128)(2,1)S(1)}, bf16[128,768]{1,0:T(8,128)(2,1)}, u32[]{:S(2)}, u32[]{:S(2)}) collective-permute-start(bf16[128,768]{1,0:T(8,128)(2,1)S(1)} %fusion), channel_id=1, source_target_pairs={{0,2},{2,0},{4,6},{6,4},{8,10},{10,8},{12,14},{14,12},{1,3},{3,1},... | collective-permute-start | bytes 589832 | tf_op jit(solution)/shard_map/ppermute | solution.py:413
  123.5 7.4 %collective-permute-done.20 = bf16[128,768]{1,0:T(8,128)(2,1)} collective-permute-done((bf16[128,768]{1,0:T(8,128)(2,1)S(1)}, bf16[128,768]{1,0:T(8,128)(2,1)}, u32[]{:S(2)}, u32[]{:S(2)}) %collective-permute-start.20) | collective-permute-done | bytes 196640 | tf_op jit(solution)/shard_map/ppermute | solution.py:413
  131.9 3.2 %collective-permute-done.21.refs_1_ = bf16[128,768]{1,0:T(8,128)(2,1)} collective-permute-done((bf16[128,768]{1,0:T(8,128)(2,1)}, bf16[128,768]{1,0:T(8,128)(2,1)}, u32[]{:S(2)}, u32[]{:S(2)}) %collective-permute-start.21) | collective-permute-done | bytes 196640 | tf_op jit(solution)/shard_map/ppermute | solution.py:413
  135.1 5.1 %collective-permute-done.23.refs_4_ = bf16[128,768]{1,0:T(8,128)(2,1)} collective-permute-done((bf16[128,768]{1,0:T(8,128)(2,1)}, bf16[128,768]{1,0:T(8,128)(2,1)}, u32[]{:S(2)}, u32[]{:S(2)}) %collective-permute-start.23) | collective-permute-done | bytes 196640 | tf_op jit(solution)/shard_map/ppermute | solution.py:413
  145.1 3.7 %collective-permute-start.28 = (bf16[128,768]{1,0:T(8,128)(2,1)}, bf16[128,768]{1,0:T(8,128)(2,1)S(1)}, u32[]{:S(2)}, u32[]{:S(2)}) collective-permute-start(bf16[128,768]{1,0:T(8,128)(2,1)} %get-tuple-element.145), channel_id=1, source_target_pairs={{0,10},{2,8},{4,14},{6,12},{8,2},{10,0},{12,6},{14,4},{1,11},{3,9}... | collective-permute-start | bytes 589832 | tf_op jit(solution)/shard_map/ppermute | solution.py:413
  150.4 5.7 %collective-permute-done.27.refs_2_ = bf16[128,768]{1,0:T(8,128)(2,1)S(1)} collective-permute-done((bf16[128,768]{1,0:T(8,128)(2,1)}, bf16[128,768]{1,0:T(8,128)(2,1)S(1)}, u32[]{:S(2)}, u32[]{:S(2)}) %collective-permute-start.27) | collective-permute-done | bytes 196640 | tf_op jit(solution)/shard_map/ppermute | solution.py:413
  158.2 3.4 %collective-permute-start.31 = (bf16[32,768]{1,0:T(8,128)(2,1)S(1)}, bf16[32,768]{1,0:T(8,128)(2,1)S(1)}, u32[]{:S(2)}, u32[]{:S(2)}) collective-permute-start(bf16[32,768]{1,0:T(8,128)(2,1)S(1)} %fusion.3), channel_id=1, source_target_pairs={{0,12},{2,14},{4,8},{6,10},{8,4},{10,6},{12,0},{14,2},{1,13},{3,15... | collective-permute-start | bytes 147464 | tf_op jit(solution)/shard_map/ppermute | solution.py:413
  164.5 3.2 %to_cells.2 = bf16[4,2,180,768]{3,2,1,0:T(8,128)(2,1)S(1)} custom-call(s32[1]{0:T(128)} %bitcast.me_ref, bf16[180,128]{1,0:T(8,128)(2,1)S(1)} %copy-done.3, bf16[4,2,180,768]{3,2,1,0:T(8,128)(2,1)S(1)} %copy.23.base_ref, bf16[128,768]{1,0:T(8,128)(2,1)} %get-tuple-element.148.refs_0_, bf16[128,768]{1,0:T(8,128)(2,1)} %collective-permute-done.21.refs_1_, ...), custom_call_target="tpu_custom_call" | custom-call | flops 283115520 | bytes 5996544 | tf_op jit(solution)/shard_map/to_cells/pallas_call | solution.py:182
  167.8 3.1 %copy.30 = bf16[4,2,180,768]{3,1,2,0:T(2,128)(2,1)} copy(bf16[4,2,180,768]{3,2,1,0:T(8,128)(2,1)S(1)} %to_cells.2) | data formatting | bytes 4423680 | tf_op jit(solution)/shard_map/to_cells/pallas_call | solution.py:182
  173.4 3.8 %collective-permute-start.35 = (bf16[128,768]{1,0:T(8,128)(2,1)S(1)}, bf16[128,768]{1,0:T(8,128)(2,1)S(1)}, u32[]{:S(2)}, u32[]{:S(2)}) collective-permute-start(bf16[128,768]{1,0:T(8,128)(2,1)S(1)} %copy-done.19), channel_id=1, source_target_pairs={{0,14},{2,12},{4,10},{6,8},{8,6},{10,4},{12,2},{14,0},{1,15},{3,13... | collective-permute-start | bytes 589832 | tf_op jit(solution)/shard_map/ppermute | solution.py:413
  178.5 4.2 %collective-permute-done.32.refs_1_ = bf16[128,768]{1,0:T(8,128)(2,1)S(1)} collective-permute-done((bf16[128,768]{1,0:T(8,128)(2,1)S(1)}, bf16[128,768]{1,0:T(8,128)(2,1)S(1)}, u32[]{:S(2)}, u32[]{:S(2)}) %collective-permute-start.32) | collective-permute-done | bytes 196640 | tf_op jit(solution)/shard_map/ppermute | solution.py:413
  186.4 3.1 %copy.26 = bf16[4,2,180,768]{3,1,2,0:T(2,128)(2,1)} copy(bf16[4,2,180,768]{3,2,1,0:T(8,128)(2,1)S(1)} %to_cells.3) | data formatting | bytes 4423680 | tf_op jit(solution)/shard_map/to_cells/pallas_call | solution.py:182
  (148 shorter events, 55.2 us)
Async XLA Ops:
  8.0 15.7 %collective-permute-start.1 = (bf16[128,768]{1,0:T(8,128)(2,1)}, bf16[128,768]{1,0:T(8,128)(2,1)S(1)}, u32[]{:S(2)}, u32[]{:S(2)}) collective-permute-start(bf16[128,768]{1,0:T(8,128)(2,1)} %get-tuple-element.98), channel_id=1, source_target_pairs={{0,4},{2,6},{4,0},{6,2},{8,12},{10,14},{12,8},{14,10},{1,5},{3,7},... | collective-permute-start | bytes 589832 | tf_op jit(solution)/shard_map/ppermute | solution.py:413
  9.6 22.3 %collective-permute-start.2 = (bf16[128,768]{1,0:T(8,128)(2,1)}, bf16[128,768]{1,0:T(8,128)(2,1)S(1)}, u32[]{:S(2)}, u32[]{:S(2)}) collective-permute-start(bf16[128,768]{1,0:T(8,128)(2,1)} %get-tuple-element.99), channel_id=1, source_target_pairs={{0,6},{2,4},{4,2},{6,0},{8,14},{10,12},{12,10},{14,8},{1,7},{3,5},... | collective-permute-start | bytes 589832 | tf_op jit(solution)/shard_map/ppermute | solution.py:413
  9.6 23.0 %collective-permute-start.3 = (bf16[128,768]{1,0:T(8,128)(2,1)}, bf16[128,768]{1,0:T(8,128)(2,1)S(1)}, u32[]{:S(2)}, u32[]{:S(2)}) collective-permute-start(bf16[128,768]{1,0:T(8,128)(2,1)} %get-tuple-element.100), channel_id=1, source_target_pairs={{0,8},{2,10},{4,12},{6,14},{8,0},{10,2},{12,4},{14,6},{1,9},{3,11}... | collective-permute-start | bytes 589832 | tf_op jit(solution)/shard_map/ppermute | solution.py:413
  12.5 28.4 %collective-permute-start.4 = (bf16[128,768]{1,0:T(8,128)(2,1)}, bf16[128,768]{1,0:T(8,128)(2,1)S(1)}, u32[]{:S(2)}, u32[]{:S(2)}) collective-permute-start(bf16[128,768]{1,0:T(8,128)(2,1)} %get-tuple-element.101), channel_id=1, source_target_pairs={{0,10},{2,8},{4,14},{6,12},{8,2},{10,0},{12,6},{14,4},{1,11},{3,9}... | collective-permute-start | bytes 589832 | tf_op jit(solution)/shard_map/ppermute | solution.py:413
  13.8 27.7 %collective-permute-start.5 = (bf16[128,768]{1,0:T(8,128)(2,1)}, bf16[128,768]{1,0:T(8,128)(2,1)S(1)}, u32[]{:S(2)}, u32[]{:S(2)}) collective-permute-start(bf16[128,768]{1,0:T(8,128)(2,1)} %get-tuple-element.102), channel_id=1, source_target_pairs={{0,12},{2,14},{4,8},{6,10},{8,4},{10,6},{12,0},{14,2},{1,13},{3,15... | collective-permute-start | bytes 589832 | tf_op jit(solution)/shard_map/ppermute | solution.py:413
  23.7 32.6 %collective-permute-start.6 = (bf16[128,768]{1,0:T(8,128)(2,1)}, bf16[128,768]{1,0:T(8,128)(2,1)}, u32[]{:S(2)}, u32[]{:S(2)}) collective-permute-start(bf16[128,768]{1,0:T(8,128)(2,1)} %get-tuple-element.103), channel_id=1, source_target_pairs={{0,14},{2,12},{4,10},{6,8},{8,6},{10,4},{12,2},{14,0},{1,15},{3,13... | collective-permute-start | bytes 589832 | tf_op jit(solution)/shard_map/ppermute | solution.py:413
  32.5 32.1 %collective-permute-start.8 = (bf16[128,768]{1,0:T(8,128)(2,1)}, bf16[128,768]{1,0:T(8,128)(2,1)S(1)}, u32[]{:S(2)}, u32[]{:S(2)}) collective-permute-start(bf16[128,768]{1,0:T(8,128)(2,1)} %get-tuple-element.108), channel_id=1, source_target_pairs={{0,4},{2,6},{4,0},{6,2},{8,12},{10,14},{12,8},{14,10},{1,5},{3,7},... | collective-permute-start | bytes 589832 | tf_op jit(solution)/shard_map/ppermute | solution.py:413
  33.2 31.5 %collective-permute-start.9 = (bf16[128,768]{1,0:T(8,128)(2,1)}, bf16[128,768]{1,0:T(8,128)(2,1)S(1)}, u32[]{:S(2)}, u32[]{:S(2)}) collective-permute-start(bf16[128,768]{1,0:T(8,128)(2,1)} %get-tuple-element.109), channel_id=1, source_target_pairs={{0,6},{2,4},{4,2},{6,0},{8,14},{10,12},{12,10},{14,8},{1,7},{3,5},... | collective-permute-start | bytes 589832 | tf_op jit(solution)/shard_map/ppermute | solution.py:413
  41.0 28.5 %collective-permute-start.10 = (bf16[128,768]{1,0:T(8,128)(2,1)}, bf16[128,768]{1,0:T(8,128)(2,1)S(1)}, u32[]{:S(2)}, u32[]{:S(2)}) collective-permute-start(bf16[128,768]{1,0:T(8,128)(2,1)} %get-tuple-element.110), channel_id=1, source_target_pairs={{0,8},{2,10},{4,12},{6,14},{8,0},{10,2},{12,4},{14,6},{1,9},{3,11}... | collective-permute-start | bytes 589832 | tf_op jit(solution)/shard_map/ppermute | solution.py:413
  41.6 36.7 %collective-permute-start.11 = (bf16[128,768]{1,0:T(8,128)(2,1)}, bf16[128,768]{1,0:T(8,128)(2,1)}, u32[]{:S(2)}, u32[]{:S(2)}) collective-permute-start(bf16[128,768]{1,0:T(8,128)(2,1)} %get-tuple-element.111), channel_id=1, source_target_pairs={{0,10},{2,8},{4,14},{6,12},{8,2},{10,0},{12,6},{14,4},{1,11},{3,9}... | collective-permute-start | bytes 589832 | tf_op jit(solution)/shard_map/ppermute | solution.py:413
  56.3 22.0 %collective-permute-start.12 = (bf16[128,768]{1,0:T(8,128)(2,1)}, bf16[128,768]{1,0:T(8,128)(2,1)}, u32[]{:S(2)}, u32[]{:S(2)}) collective-permute-start(bf16[128,768]{1,0:T(8,128)(2,1)} %get-tuple-element.112), channel_id=1, source_target_pairs={{0,12},{2,14},{4,8},{6,10},{8,4},{10,6},{12,0},{14,2},{1,13},{3,15... | collective-permute-start | bytes 589832 | tf_op jit(solution)/shard_map/ppermute | solution.py:413
  64.6 23.4 %collective-permute-start.7 = (bf16[128,768]{1,0:T(8,128)(2,1)S(1)}, bf16[128,768]{1,0:T(8,128)(2,1)}, u32[]{:S(2)}, u32[]{:S(2)}) collective-permute-start(bf16[128,768]{1,0:T(8,128)(2,1)S(1)} %copy-done.27), channel_id=1, source_target_pairs={{0,2},{2,0},{4,6},{6,4},{8,10},{10,8},{12,14},{14,12},{1,3},{3,1},... | collective-permute-start | bytes 589832 | tf_op jit(solution)/shard_map/ppermute | solution.py:413
  64.7 23.3 %collective-permute-start.13 = (bf16[128,768]{1,0:T(8,128)(2,1)S(1)}, bf16[128,768]{1,0:T(8,128)(2,1)}, u32[]{:S(2)}, u32[]{:S(2)}) collective-permute-start(bf16[128,768]{1,0:T(8,128)(2,1)S(1)} %copy-done.25), channel_id=1, source_target_pairs={{0,14},{2,12},{4,10},{6,8},{8,6},{10,4},{12,2},{14,0},{1,15},{3,13... | collective-permute-start | bytes 589832 | tf_op jit(solution)/shard_map/ppermute | solution.py:413
  69.5 31.4 %collective-permute-start.14 = (bf16[128,768]{1,0:T(8,128)(2,1)}, bf16[128,768]{1,0:T(8,128)(2,1)S(1)}, u32[]{:S(2)}, u32[]{:S(2)}) collective-permute-start(bf16[128,768]{1,0:T(8,128)(2,1)} %get-tuple-element.133), channel_id=1, source_target_pairs={{0,8},{2,10},{4,12},{6,14},{8,0},{10,2},{12,4},{14,6},{1,9},{3,11}... | collective-permute-start | bytes 589832 | tf_op jit(solution)/shard_map/ppermute | solution.py:413
  78.3 22.7 %collective-permute-start.15 = (bf16[128,768]{1,0:T(8,128)(2,1)}, bf16[128,768]{1,0:T(8,128)(2,1)S(1)}, u32[]{:S(2)}, u32[]{:S(2)}) collective-permute-start(bf16[128,768]{1,0:T(8,128)(2,1)} %get-tuple-element.134), channel_id=1, source_target_pairs={{0,4},{2,6},{4,0},{6,2},{8,12},{10,14},{12,8},{14,10},{1,5},{3,7},... | collective-permute-start | bytes 589832 | tf_op jit(solution)/shard_map/ppermute | solution.py:413
  78.3 22.7 %collective-permute-start.16 = (bf16[128,768]{1,0:T(8,128)(2,1)}, bf16[128,768]{1,0:T(8,128)(2,1)S(1)}, u32[]{:S(2)}, u32[]{:S(2)}) collective-permute-start(bf16[128,768]{1,0:T(8,128)(2,1)} %get-tuple-element.135), channel_id=1, source_target_pairs={{0,10},{2,8},{4,14},{6,12},{8,2},{10,0},{12,6},{14,4},{1,11},{3,9}... | collective-permute-start | bytes 589832 | tf_op jit(solution)/shard_map/ppermute | solution.py:413
  118.3 12.7 %collective-permute-start.20 = (bf16[128,768]{1,0:T(8,128)(2,1)S(1)}, bf16[128,768]{1,0:T(8,128)(2,1)}, u32[]{:S(2)}, u32[]{:S(2)}) collective-permute-start(bf16[128,768]{1,0:T(8,128)(2,1)S(1)} %fusion), channel_id=1, source_target_pairs={{0,2},{2,0},{4,6},{6,4},{8,10},{10,8},{12,14},{14,12},{1,3},{3,1},... | collective-permute-start | bytes 589832 | tf_op jit(solution)/shard_map/ppermute | solution.py:413
  121.9 13.2 %collective-permute-start.21 = (bf16[128,768]{1,0:T(8,128)(2,1)}, bf16[128,768]{1,0:T(8,128)(2,1)}, u32[]{:S(2)}, u32[]{:S(2)}) collective-permute-start(bf16[128,768]{1,0:T(8,128)(2,1)} %get-tuple-element.140), channel_id=1, source_target_pairs={{0,2},{2,0},{4,6},{6,4},{8,10},{10,8},{12,14},{14,12},{1,3},{3,1},... | collective-permute-start | bytes 589832 | tf_op jit(solution)/shard_map/ppermute | solution.py:413
  122.0 13.1 %collective-permute-start.22 = (bf16[128,768]{1,0:T(8,128)(2,1)}, bf16[128,768]{1,0:T(8,128)(2,1)}, u32[]{:S(2)}, u32[]{:S(2)}) collective-permute-start(bf16[128,768]{1,0:T(8,128)(2,1)} %get-tuple-element.141), channel_id=1, source_target_pairs={{0,14},{2,12},{4,10},{6,8},{8,6},{10,4},{12,2},{14,0},{1,15},{3,13... | collective-permute-start | bytes 589832 | tf_op jit(solution)/shard_map/ppermute | solution.py:413
  123.5 16.7 %collective-permute-start.23 = (bf16[128,768]{1,0:T(8,128)(2,1)}, bf16[128,768]{1,0:T(8,128)(2,1)}, u32[]{:S(2)}, u32[]{:S(2)}) collective-permute-start(bf16[128,768]{1,0:T(8,128)(2,1)} %get-tuple-element.142), channel_id=1, source_target_pairs={{0,8},{2,10},{4,12},{6,14},{8,0},{10,2},{12,4},{14,6},{1,9},{3,11}... | collective-permute-start | bytes 589832 | tf_op jit(solution)/shard_map/ppermute | solution.py:413
  145.1 13.1 %collective-permute-start.28 = (bf16[128,768]{1,0:T(8,128)(2,1)}, bf16[128,768]{1,0:T(8,128)(2,1)S(1)}, u32[]{:S(2)}, u32[]{:S(2)}) collective-permute-start(bf16[128,768]{1,0:T(8,128)(2,1)} %get-tuple-element.145), channel_id=1, source_target_pairs={{0,10},{2,8},{4,14},{6,12},{8,2},{10,0},{12,6},{14,4},{1,11},{3,9}... | collective-permute-start | bytes 589832 | tf_op jit(solution)/shard_map/ppermute | solution.py:413
  148.8 22.1 %collective-permute-start.33 = (bf16[128,768]{1,0:T(8,128)(2,1)}, bf16[128,768]{1,0:T(8,128)(2,1)S(1)}, u32[]{:S(2)}, u32[]{:S(2)}) collective-permute-start(bf16[128,768]{1,0:T(8,128)(2,1)} %get-tuple-element.152), channel_id=1, source_target_pairs={{0,6},{2,4},{4,2},{6,0},{8,14},{10,12},{12,10},{14,8},{1,7},{3,5},... | collective-permute-start | bytes 589832 | tf_op jit(solution)/shard_map/ppermute | solution.py:413
  148.9 22.0 %collective-permute-start.34 = (bf16[128,768]{1,0:T(8,128)(2,1)}, bf16[128,768]{1,0:T(8,128)(2,1)S(1)}, u32[]{:S(2)}, u32[]{:S(2)}) collective-permute-start(bf16[128,768]{1,0:T(8,128)(2,1)} %get-tuple-element.153), channel_id=1, source_target_pairs={{0,12},{2,14},{4,8},{6,10},{8,4},{10,6},{12,0},{14,2},{1,13},{3,15... | collective-permute-start | bytes 589832 | tf_op jit(solution)/shard_map/ppermute | solution.py:413
  158.2 12.6 %collective-permute-start.31 = (bf16[32,768]{1,0:T(8,128)(2,1)S(1)}, bf16[32,768]{1,0:T(8,128)(2,1)S(1)}, u32[]{:S(2)}, u32[]{:S(2)}) collective-permute-start(bf16[32,768]{1,0:T(8,128)(2,1)S(1)} %fusion.3), channel_id=1, source_target_pairs={{0,12},{2,14},{4,8},{6,10},{8,4},{10,6},{12,0},{14,2},{1,13},{3,15... | collective-permute-start | bytes 147464 | tf_op jit(solution)/shard_map/ppermute | solution.py:413
  (48 other events, 478.7 us)

commit v14 on v13

--- a/solution.py
+++ b/solution.py
@@ -114,6 +114,10 @@
     return [pltpu.with_memory_space_constraint(array, pltpu.HBM) for array in arrays]
 
 
+def with_offsets(refs):
+    return [((len(refs) - place) % len(refs), ref) for place, ref in enumerate(refs)]
+
+
 def to_modes_kernel(me_ref, table_ref, cells_ref, *refs):
     modes_refs, held_ref = refs[:-1], refs[-1]
     rows = cells_ref.shape[1]
@@ -121,7 +125,7 @@
     for row in range(rows):
         spectrum = product_of(table_ref[...], cells_ref[0, row])
         held_ref[row] = spectrum.astype(jnp.bfloat16)
-        for offset, modes_ref in enumerate(modes_refs):
+        for offset, modes_ref in with_offsets(modes_refs):
             modes_ref[pl.ds(row * share, share)] = held_ref[row, place_of(me_ref, offset, share)]
 
 
@@ -161,7 +165,7 @@
         if len(modes_refs) == 1:
             spectrum = modes_refs[0][:, run].reshape(held_ref.shape[1:])
         else:
-            for offset, modes_ref in enumerate(modes_refs):
+            for offset, modes_ref in with_offsets(modes_refs):
                 held_ref[row, place_of(me_ref, offset, share)] = modes_ref[run]
             spectrum = held_ref[row]
         image = product_of(table_ref[...], spectrum)
@@ -216,7 +220,7 @@
     samples, size, width = band_ref.shape
     part, half = size // len(bands_refs), size // 2
     for sample in range(samples):
-        for offset, bands_ref in enumerate(bands_refs):
+        for offset, bands_ref in with_offsets(bands_refs):
             place = place_of(me_ref, offset, part)
             band_ref[sample, place] = bands_ref[pl.ds(sample * part, part)]
         mixed = product_of(table_ref[...], band_ref[sample]).astype(jnp.bfloat16)
@@ -240,7 +244,7 @@
             bands_refs[0][:, run] = bands.reshape(lead, size // lead, width)
         else:
             band_ref[sample] = bands
-            for offset, bands_ref in enumerate(bands_refs):
+            for offset, bands_ref in with_offsets(bands_refs):
                 place = place_of(me_ref, offset, part)
                 bands_ref[pl.ds(sample * part, part)] = band_ref[sample, place]
 
@@ -524,9 +528,15 @@
 
     order = mixed_order(owners)
 
+    def place(offset):
+        return (owners - offset) % owners
+
     def send(blocks, offsets, taken):
         for offset in offsets:
-            taken[offset] = swap_with(blocks[offset], "space", offset)
+            taken[offset] = swap_with(blocks[place(offset)], "space", offset)
+
+    def listed(taken):
+        return [taken[place(at)] for at in range(owners)]
 
     def send_all(spectrum):
         spectrum = spectrum.reshape(samples, rows, owners, 2 * modes, channels)
@@ -574,16 +584,17 @@
 
     gathered, cot_gathered = {0: spectrum[0]}, {0: cot_spec[0]}
     send(spectrum, order, gathered)
-    gathered = [gathered[offset] for offset in range(owners)]
+    gathered = listed(gathered)
     image, state = forward_mid(me, lat, lat.T, gathered, w1, b1, w2, b2)
     cot_spec, image = list(cot_spec), list(image)
-    send(cot_spec, order[:FIRST], cot_gathered)
+    falling = range(owners - 1, 0, -1)
+    send(cot_spec, falling[:FIRST], cot_gathered)
     cot_spec, image = waiting((cot_spec, image), [image[0]])
-    send(cot_spec, order[FIRST:], cot_gathered)
+    send(cot_spec, falling[FIRST:], cot_gathered)
 
     image_band = {0: image[0]}
     send(image, order, image_band)
-    cot_gathered = [cot_gathered[offset] for offset in range(owners)]
+    cot_gathered = listed(cot_gathered)
     grad_image, sums = backward_mid(
         me, lat, lat.T, cot_gathered, w1, b1, w2, b2, state, count
     )
@@ -596,8 +607,8 @@
     grad_band = {0: grad_image[0]}
     send(grad_image, order, grad_band)
     arrived = [grad_band[offset] for offset in order]
-    image_band = [image_band[offset] for offset in range(owners)]
-    grad_band = [grad_band[offset] for offset in range(owners)]
+    image_band = listed(image_band)
+    grad_band = listed(grad_band)
     again = waiting(fields, early[:1])
     output = rows_inside(to_cells(me, scaled.T, image_band, again))
     group_sum.scatter(late[2:] + arrived[:1])
@@ -605,12 +616,10 @@
     group_sum.quarter, output = lax.optimization_barrier((group_sum.quarter, output))
     group_sum.gather_next(arrived[3:5])
     half, other = group_sum.gather_dp(arrived[5:])
+    near = lax.axis_index("space")
+    here = jnp.stack([lax.axis_index("dp"), near % 2, near // 2]).astype(jnp.int32)
+    grads = finish_sums(here, half, other, factor, w_first.shape, b_first.shape)
     grad_fields = rows_inside(to_cells(me, plain.T, grad_band, cotangent))
-    place = lax.axis_index("space")
-    here = jnp.stack([lax.axis_index("dp"), place % 2, place // 2]).astype(jnp.int32)
-    grads = finish_sums(
-        here, half, other, factor, w_first.shape, b_first.shape
-    )
     return (rows_outside(output), rows_outside(grad_fields)) + tuple(grads)
 
 

time: 192 us -> 196 us (1.021)
  waiting for transfers between devices: 46.6 us -> 55.3 us
  starting transfers between devices: 88.9 us -> 83.5 us
    ppermute x38, waiting for transfers between devices: 46.6 us -> 55.3 us  [swap_with(): return lax.ppermute(values, axis, pairs)]
    ppermute x38, starting transfers between devices: 88.9 us -> 83.5 us  [swap_with(): return lax.ppermute(values, axis, pairs)]
  transfers between devices with their start and end apart: 38 -> 38, of which waited for: 11 -> 14; matrix products, arithmetic and copies ran while one was open for 7% -> 7% of each run, Pallas kernels for 17% -> 16%
where the time goes in v14:
time: 196 us; the launch traced here: 195 us
  starting transfers between devices  83.5 us (43%)
  waiting for transfers between devices  55.3 us (28%)
  Pallas kernels  36.3 us (19%)
  local copies, waits for them, and re-layouts  16.1 us (8%)
  other arithmetic  2.59 us (1%)
    ppermute x38, starting transfers between devices, swap_with(): return lax.ppermute(values, axis, pairs)  83.5 us
    ppermute x38, waiting for transfers between devices, swap_with(): return lax.ppermute(values, axis, pairs)  55.3 us
    pallas_call x1, Pallas kernels, backward_mid(): pl.pallas_call(functools.partial(backward_kernel, size_of_block, len(band...  12.9 us
    pallas_call x1, Pallas kernels, forward_mid(): pl.pallas_call(functools.partial(forward_kernel, len(bands)), grid_spec=p...  7.66 us
    pallas_call x2, Pallas kernels, to_cells(): pl.pallas_call(to_cells_kernel, grid_spec=pltpu.PrefetchScalarGridSpec(nu...  6.21 us
    pallas_call x2, local copies, waits for them, and re-layouts, to_cells(): pl.pallas_call(to_cells_kernel, grid_spec=pltpu.PrefetchScalarGridSpec(nu...  6.13 us
    pallas_call x2, Pallas kernels, to_modes(): pl.pallas_call(to_modes_kernel, grid_spec=pltpu.PrefetchScalarGridSpec(nu...  4.82 us
    unnamed x69, local copies, waits for them, and re-layouts  4.68 us
  transfers between devices with their start and end apart: 38, of which 14 were waited for; matrix products, arithmetic and copies ran while one was open for 7% of the time, Pallas kernels for 16%

profile of v14, /device:TPU:0, one launch (start us, length us, event | category | flops | bytes accessed | tf_op | source)
XLA Modules:
  0.0 195.0 jit_solution(13557373837589682393)
XLA Ops:
  2.6 2.4 %to_modes.2 = (bf16[128,768]{1,0:T(8,128)(2,1)}, bf16[128,768]{1,0:T(8,128)(2,1)}, bf16[128,768]{1,0:T(8,128)(2,1)}, bf16[128,768]{1,0:T(8,128)(2,1)}, bf16[128,...) custom-call(s32[1]{0:T(128)} %bitcast.me_ref, ...), custom_call_target="tpu_custom_call" | custom-call | flops 283115520 | bytes 3784704 | tf_op jit(solution)/shard_map/to_modes/pallas_call | solution.py:136
  5.0 6.0 %collective-permute-start = (bf16[128,768]{1,0:T(8,128)(2,1)}, bf16[128,768]{1,0:T(8,128)(2,1)S(1)}, u32[]{:S(2)}, u32[]{:S(2)}) collective-permute-start(bf16[128,768]{1,0:T(8,128)(2,1)} %get-tuple-element.97), channel_id=1, source_target_pairs={{0,14},{2,12},{4,10},{6,8},{8,6},{10,4},{12,2},{14,0},{1,15},{3,13... | collective-permute-start | bytes 589832 | tf_op jit(solution)/shard_map/ppermute | solution.py:417
  17.1 17.6 %collective-permute-start.5 = (bf16[128,768]{1,0:T(8,128)(2,1)}, bf16[128,768]{1,0:T(8,128)(2,1)S(1)}, u32[]{:S(2)}, u32[]{:S(2)}) collective-permute-start(bf16[128,768]{1,0:T(8,128)(2,1)} %get-tuple-element.102), channel_id=1, source_target_pairs={{0,4},{2,6},{4,0},{6,2},{8,12},{10,14},{12,8},{14,10},{1,5},{3,7},... | collective-permute-start | bytes 589832 | tf_op jit(solution)/shard_map/ppermute | solution.py:417
  38.6 2.6 %spread_weights.1 = (bf16[2,768,768]{2,1,0:T(8,128)(2,1)}, bf16[2,768,768]{2,1,0:T(8,128)(2,1)}) custom-call(bf16[2,8,96,96]{3,2,1,0:T(8,128)(2,1)S(1)} %copy-done.4, bf16[2,8,96,96]{3,2,1,0:T(8,128)(2,1)S(1)} %copy-done.5), custom_call_target="tpu_custom_call" | custom-call | flops 226492416 | bytes 4718592 | tf_op jit(solution)/shard_map/spread_weights/pallas_call | solution.py:83
  41.2 2.5 %to_modes.3 = (bf16[128,768]{1,0:T(8,128)(2,1)}, bf16[128,768]{1,0:T(8,128)(2,1)}, bf16[128,768]{1,0:T(8,128)(2,1)}, bf16[128,768]{1,0:T(8,128)(2,1)}, bf16[128,...) custom-call(s32[1]{0:T(128)} %bitcast.me_ref, ...), custom_call_target="tpu_custom_call" | custom-call | flops 283115520 | bytes 3784704 | tf_op jit(solution)/shard_map/to_modes/pallas_call | solution.py:136
  48.8 2.4 %collective-permute-start.9 = (bf16[128,768]{1,0:T(8,128)(2,1)}, bf16[128,768]{1,0:T(8,128)(2,1)S(1)}, u32[]{:S(2)}, u32[]{:S(2)}) collective-permute-start(bf16[128,768]{1,0:T(8,128)(2,1)} %get-tuple-element.109), channel_id=1, source_target_pairs={{0,10},{2,8},{4,14},{6,12},{8,2},{10,0},{12,6},{14,4},{1,11},{3,9}... | collective-permute-start | bytes 589832 | tf_op jit(solution)/shard_map/ppermute | solution.py:417
  54.1 7.7 %mix_forward.1 = (bf16[128,768]{1,0:T(8,128)(2,1)}, bf16[128,768]{1,0:T(8,128)(2,1)}, bf16[128,768]{1,0:T(8,128)(2,1)}, bf16[128,768]{1,0:T(8,128)(2,1)}, bf16[1...) custom-call(s32[1]{0:T(128)} %bitcast.me_ref, ...), custom_call_target="tpu_custom_call" | custom-call | flops 2415919104 | bytes 17301504 | tf_op jit(solution)/shard_map/mix_forward/pallas_call | solution.py:344
  61.8 9.6 %collective-permute-start.12 = (bf16[128,768]{1,0:T(8,128)(2,1)S(1)}, bf16[128,768]{1,0:T(8,128)(2,1)}, u32[]{:S(2)}, u32[]{:S(2)}) collective-permute-start(bf16[128,768]{1,0:T(8,128)(2,1)S(1)} %copy-done.27), channel_id=1, source_target_pairs={{0,4},{2,6},{4,0},{6,2},{8,12},{10,14},{12,8},{14,10},{1,5},{3,7},... | collective-permute-start | bytes 589832 | tf_op jit(solution)/shard_map/ppermute | solution.py:417
  71.5 7.7 %collective-permute-done.9.refs_3_ = bf16[128,768]{1,0:T(8,128)(2,1)S(1)} collective-permute-done((bf16[128,768]{1,0:T(8,128)(2,1)}, bf16[128,768]{1,0:T(8,128)(2,1)S(1)}, u32[]{:S(2)}, u32[]{:S(2)}) %collective-permute-start.9) | collective-permute-done | bytes 196640 | tf_op jit(solution)/shard_map/ppermute | solution.py:417
  81.7 8.5 %collective-permute-start.16 = (bf16[128,768]{1,0:T(8,128)(2,1)}, bf16[128,768]{1,0:T(8,128)(2,1)S(1)}, u32[]{:S(2)}, u32[]{:S(2)}) collective-permute-start(bf16[128,768]{1,0:T(8,128)(2,1)} %get-tuple-element.135), channel_id=1, source_target_pairs={{0,10},{2,8},{4,14},{6,12},{8,2},{10,0},{12,6},{14,4},{1,11},{3,9}... | collective-permute-start | bytes 589832 | tf_op jit(solution)/shard_map/ppermute | solution.py:417
  90.2 12.9 %mix_backward.1 = (bf16[128,768]{1,0:T(8,128)(2,1)}, bf16[128,768]{1,0:T(8,128)(2,1)}, bf16[128,768]{1,0:T(8,128)(2,1)}, bf16[128,768]{1,0:T(8,128)(2,1)}, bf16[...) custom-call(s32[1]{0:T(128)} %bitcast.me_ref, ...), custom_call_target="tpu_custom_call" | custom-call | flops 4831838208 | bytes 17301504 | tf_op jit(solution)/shard_map/mix_backward/pallas_call | solution.py:382
  108.9 8.7 %collective-permute-done.18.refs_5_ = bf16[128,768]{1,0:T(8,128)(2,1)} collective-permute-done((bf16[128,768]{1,0:T(8,128)(2,1)S(1)}, bf16[128,768]{1,0:T(8,128)(2,1)}, u32[]{:S(2)}, u32[]{:S(2)}) %collective-permute-start.18) | collective-permute-done | bytes 196640 | tf_op jit(solution)/shard_map/ppermute | solution.py:417
  123.0 6.1 %collective-permute-done.20 = bf16[128,768]{1,0:T(8,128)(2,1)} collective-permute-done((bf16[128,768]{1,0:T(8,128)(2,1)S(1)}, bf16[128,768]{1,0:T(8,128)(2,1)}, u32[]{:S(2)}, u32[]{:S(2)}) %collective-permute-start.20) | collective-permute-done | bytes 196640 | tf_op jit(solution)/shard_map/ppermute | solution.py:417
  132.0 7.4 %collective-permute-done.23.refs_4_ = bf16[128,768]{1,0:T(8,128)(2,1)} collective-permute-done((bf16[128,768]{1,0:T(8,128)(2,1)}, bf16[128,768]{1,0:T(8,128)(2,1)}, u32[]{:S(2)}, u32[]{:S(2)}) %collective-permute-start.23) | collective-permute-done | bytes 196640 | tf_op jit(solution)/shard_map/ppermute | solution.py:417
  141.4 2.6 %collective-permute-start.24 = (bf16[32,768]{1,0:T(8,128)(2,1)S(1)}, bf16[32,768]{1,0:T(8,128)(2,1)S(1)}, u32[]{:S(2)}, u32[]{:S(2)}) collective-permute-start(bf16[32,768]{1,0:T(8,128)(2,1)S(1)} %get-tuple-element.162), channel_id=1, source_target_pairs={{0,4},{2,6},{4,0},{6,2},{8,12},{10,14},{12,8},{14,10},{1,5},{3,7},... | collective-permute-start | bytes 147464 | tf_op jit(solution)/shard_map/ppermute | solution.py:417
  149.8 5.8 %collective-permute-done.27.refs_6_ = bf16[128,768]{1,0:T(8,128)(2,1)S(1)} collective-permute-done((bf16[128,768]{1,0:T(8,128)(2,1)}, bf16[128,768]{1,0:T(8,128)(2,1)S(1)}, u32[]{:S(2)}, u32[]{:S(2)}) %collective-permute-start.27) | collective-permute-done | bytes 196640 | tf_op jit(solution)/shard_map/ppermute | solution.py:417
  155.6 6.6 %collective-permute-done.28.refs_3_ = bf16[128,768]{1,0:T(8,128)(2,1)S(1)} collective-permute-done((bf16[128,768]{1,0:T(8,128)(2,1)}, bf16[128,768]{1,0:T(8,128)(2,1)S(1)}, u32[]{:S(2)}, u32[]{:S(2)}) %collective-permute-start.28) | collective-permute-done | bytes 196640 | tf_op jit(solution)/shard_map/ppermute | solution.py:417
  164.1 2.6 %collective-permute-start.29 = (bf16[32,768]{1,0:T(8,128)(2,1)S(1)}, bf16[32,768]{1,0:T(8,128)(2,1)S(1)}, u32[]{:S(2)}, u32[]{:S(2)}) collective-permute-start(bf16[32,768]{1,0:T(8,128)(2,1)S(1)} %fusion.3), channel_id=1, source_target_pairs={{0,4},{2,6},{4,0},{6,2},{8,12},{10,14},{12,8},{14,10},{1,5},{3,7},... | collective-permute-start | bytes 147464 | tf_op jit(solution)/shard_map/ppermute | solution.py:417
  168.6 3.2 %to_cells.2 = bf16[4,2,180,768]{3,2,1,0:T(8,128)(2,1)S(1)} custom-call(s32[1]{0:T(128)} %bitcast.me_ref, bf16[180,128]{1,0:T(8,128)(2,1)S(1)} %copy-done.3, bf16[4,2,180,768]{3,2,1,0:T(8,128)(2,1)S(1)} %copy.23.base_ref, bf16[128,768]{1,0:T(8,128)(2,1)} %get-tuple-element.148.refs_0_, bf16[128,768]{1,0:T(8,128)(2,1)} %collective-permute-done.22.refs_1_, ...), custom_call_target="tpu_custom_call" | custom-call | flops 283115520 | bytes 5996544 | tf_op jit(solution)/shard_map/to_cells/pallas_call | solution.py:186
  171.8 3.1 %copy.30 = bf16[4,2,180,768]{3,1,2,0:T(2,128)(2,1)} copy(bf16[4,2,180,768]{3,2,1,0:T(8,128)(2,1)S(1)} %to_cells.2) | data formatting | bytes 4423680 | tf_op jit(solution)/shard_map/to_cells/pallas_call | solution.py:186
  175.8 2.5 %collective-permute-start.32 = (bf16[128,768]{1,0:T(8,128)(2,1)S(1)}, bf16[128,768]{1,0:T(8,128)(2,1)S(1)}, u32[]{:S(2)}, u32[]{:S(2)}) collective-permute-start(bf16[128,768]{1,0:T(8,128)(2,1)S(1)} %copy-done.20), channel_id=1, source_target_pairs={{0,14},{2,12},{4,10},{6,8},{8,6},{10,4},{12,2},{14,0},{1,15},{3,13... | collective-permute-start | bytes 589832 | tf_op jit(solution)/shard_map/ppermute | solution.py:417
  180.8 3.5 %collective-permute-done.32.refs_1_ = bf16[128,768]{1,0:T(8,128)(2,1)S(1)} collective-permute-done((bf16[128,768]{1,0:T(8,128)(2,1)S(1)}, bf16[128,768]{1,0:T(8,128)(2,1)S(1)}, u32[]{:S(2)}, u32[]{:S(2)}) %collective-permute-start.32) | collective-permute-done | bytes 196640 | tf_op jit(solution)/shard_map/ppermute | solution.py:417
  186.8 3.0 %to_cells.3 = bf16[4,2,180,768]{3,2,1,0:T(8,128)(2,1)S(1)} custom-call(s32[1]{0:T(128)} %bitcast.me_ref, bf16[180,128]{1,0:T(8,128)(2,1)S(1)} %copy-done.2, bf16[4,2,180,768]{3,2,1,0:T(8,128)(2,1)S(1)} %copy.22.cells_ref.base_ref, bf16[128,768]{1,0:T(8,128)(2,1)} %get-tuple-element.150.refs_0_, bf16[128,768]{1,0:T(8,128)(2,1)} %copy-done.15, ...), custom_call_target="tpu_custom_call" | custom-call | flops 283115520 | bytes 5996544 | tf_op jit(solution)/shard_map/to_cells/pallas_call | solution.py:186
  189.8 3.1 %copy.26 = bf16[4,2,180,768]{3,1,2,0:T(2,128)(2,1)} copy(bf16[4,2,180,768]{3,2,1,0:T(8,128)(2,1)S(1)} %to_cells.3) | data formatting | bytes 4423680 | tf_op jit(solution)/shard_map/to_cells/pallas_call | solution.py:186
  (148 shorter events, 56.0 us)
Async XLA Ops:
  11.0 23.7 %collective-permute-start.1 = (bf16[128,768]{1,0:T(8,128)(2,1)}, bf16[128,768]{1,0:T(8,128)(2,1)S(1)}, u32[]{:S(2)}, u32[]{:S(2)}) collective-permute-start(bf16[128,768]{1,0:T(8,128)(2,1)} %get-tuple-element.98), channel_id=1, source_target_pairs={{0,12},{2,14},{4,8},{6,10},{8,4},{10,6},{12,0},{14,2},{1,13},{3,15... | collective-permute-start | bytes 589832 | tf_op jit(solution)/shard_map/ppermute | solution.py:417
  11.2 32.4 %collective-permute-start.2 = (bf16[128,768]{1,0:T(8,128)(2,1)}, bf16[128,768]{1,0:T(8,128)(2,1)S(1)}, u32[]{:S(2)}, u32[]{:S(2)}) collective-permute-start(bf16[128,768]{1,0:T(8,128)(2,1)} %get-tuple-element.99), channel_id=1, source_target_pairs={{0,10},{2,8},{4,14},{6,12},{8,2},{10,0},{12,6},{14,4},{1,11},{3,9}... | collective-permute-start | bytes 589832 | tf_op jit(solution)/shard_map/ppermute | solution.py:417
  12.0 34.7 %collective-permute-start.3 = (bf16[128,768]{1,0:T(8,128)(2,1)}, bf16[128,768]{1,0:T(8,128)(2,1)S(1)}, u32[]{:S(2)}, u32[]{:S(2)}) collective-permute-start(bf16[128,768]{1,0:T(8,128)(2,1)} %get-tuple-element.100), channel_id=1, source_target_pairs={{0,8},{2,10},{4,12},{6,14},{8,0},{10,2},{12,4},{14,6},{1,9},{3,11}... | collective-permute-start | bytes 589832 | tf_op jit(solution)/shard_map/ppermute | solution.py:417
  14.0 34.8 %collective-permute-start.4 = (bf16[128,768]{1,0:T(8,128)(2,1)}, bf16[128,768]{1,0:T(8,128)(2,1)S(1)}, u32[]{:S(2)}, u32[]{:S(2)}) collective-permute-start(bf16[128,768]{1,0:T(8,128)(2,1)} %get-tuple-element.101), channel_id=1, source_target_pairs={{0,6},{2,4},{4,2},{6,0},{8,14},{10,12},{12,10},{14,8},{1,7},{3,5},... | collective-permute-start | bytes 589832 | tf_op jit(solution)/shard_map/ppermute | solution.py:417
  17.1 34.1 %collective-permute-start.5 = (bf16[128,768]{1,0:T(8,128)(2,1)}, bf16[128,768]{1,0:T(8,128)(2,1)S(1)}, u32[]{:S(2)}, u32[]{:S(2)}) collective-permute-start(bf16[128,768]{1,0:T(8,128)(2,1)} %get-tuple-element.102), channel_id=1, source_target_pairs={{0,4},{2,6},{4,0},{6,2},{8,12},{10,14},{12,8},{14,10},{1,5},{3,7},... | collective-permute-start | bytes 589832 | tf_op jit(solution)/shard_map/ppermute | solution.py:417
  34.7 17.9 %collective-permute-start.6 = (bf16[128,768]{1,0:T(8,128)(2,1)}, bf16[128,768]{1,0:T(8,128)(2,1)}, u32[]{:S(2)}, u32[]{:S(2)}) collective-permute-start(bf16[128,768]{1,0:T(8,128)(2,1)} %get-tuple-element.103), channel_id=1, source_target_pairs={{0,2},{2,0},{4,6},{6,4},{8,10},{10,8},{12,14},{14,12},{1,3},{3,1},... | collective-permute-start | bytes 589832 | tf_op jit(solution)/shard_map/ppermute | solution.py:417
  44.3 17.5 %collective-permute-start.7 = (bf16[128,768]{1,0:T(8,128)(2,1)}, bf16[128,768]{1,0:T(8,128)(2,1)S(1)}, u32[]{:S(2)}, u32[]{:S(2)}) collective-permute-start(bf16[128,768]{1,0:T(8,128)(2,1)} %get-tuple-element.107), channel_id=1, source_target_pairs={{0,14},{2,12},{4,10},{6,8},{8,6},{10,4},{12,2},{14,0},{1,15},{3,13... | collective-permute-start | bytes 589832 | tf_op jit(solution)/shard_map/ppermute | solution.py:417
  47.4 24.0 %collective-permute-start.8 = (bf16[128,768]{1,0:T(8,128)(2,1)}, bf16[128,768]{1,0:T(8,128)(2,1)S(1)}, u32[]{:S(2)}, u32[]{:S(2)}) collective-permute-start(bf16[128,768]{1,0:T(8,128)(2,1)} %get-tuple-element.108), channel_id=1, source_target_pairs={{0,12},{2,14},{4,8},{6,10},{8,4},{10,6},{12,0},{14,2},{1,13},{3,15... | collective-permute-start | bytes 589832 | tf_op jit(solution)/shard_map/ppermute | solution.py:417
  48.8 30.3 %collective-permute-start.9 = (bf16[128,768]{1,0:T(8,128)(2,1)}, bf16[128,768]{1,0:T(8,128)(2,1)S(1)}, u32[]{:S(2)}, u32[]{:S(2)}) collective-permute-start(bf16[128,768]{1,0:T(8,128)(2,1)} %get-tuple-element.109), channel_id=1, source_target_pairs={{0,10},{2,8},{4,14},{6,12},{8,2},{10,0},{12,6},{14,4},{1,11},{3,9}... | collective-permute-start | bytes 589832 | tf_op jit(solution)/shard_map/ppermute | solution.py:417
  51.2 29.1 %collective-permute-start.10 = (bf16[128,768]{1,0:T(8,128)(2,1)}, bf16[128,768]{1,0:T(8,128)(2,1)}, u32[]{:S(2)}, u32[]{:S(2)}) collective-permute-start(bf16[128,768]{1,0:T(8,128)(2,1)} %get-tuple-element.110), channel_id=1, source_target_pairs={{0,8},{2,10},{4,12},{6,14},{8,0},{10,2},{12,4},{14,6},{1,9},{3,11}... | collective-permute-start | bytes 589832 | tf_op jit(solution)/shard_map/ppermute | solution.py:417
  52.7 29.0 %collective-permute-start.11 = (bf16[128,768]{1,0:T(8,128)(2,1)}, bf16[128,768]{1,0:T(8,128)(2,1)}, u32[]{:S(2)}, u32[]{:S(2)}) collective-permute-start(bf16[128,768]{1,0:T(8,128)(2,1)} %get-tuple-element.111), channel_id=1, source_target_pairs={{0,6},{2,4},{4,2},{6,0},{8,14},{10,12},{12,10},{14,8},{1,7},{3,5},... | collective-permute-start | bytes 589832 | tf_op jit(solution)/shard_map/ppermute | solution.py:417
  61.8 28.4 %collective-permute-start.12 = (bf16[128,768]{1,0:T(8,128)(2,1)S(1)}, bf16[128,768]{1,0:T(8,128)(2,1)}, u32[]{:S(2)}, u32[]{:S(2)}) collective-permute-start(bf16[128,768]{1,0:T(8,128)(2,1)S(1)} %copy-done.27), channel_id=1, source_target_pairs={{0,4},{2,6},{4,0},{6,2},{8,12},{10,14},{12,8},{14,10},{1,5},{3,7},... | collective-permute-start | bytes 589832 | tf_op jit(solution)/shard_map/ppermute | solution.py:417
  71.4 18.8 %collective-permute-start.13 = (bf16[128,768]{1,0:T(8,128)(2,1)S(1)}, bf16[128,768]{1,0:T(8,128)(2,1)}, u32[]{:S(2)}, u32[]{:S(2)}) collective-permute-start(bf16[128,768]{1,0:T(8,128)(2,1)S(1)} %copy-done.25), channel_id=1, source_target_pairs={{0,2},{2,0},{4,6},{6,4},{8,10},{10,8},{12,14},{14,12},{1,3},{3,1},... | collective-permute-start | bytes 589832 | tf_op jit(solution)/shard_map/ppermute | solution.py:417
  79.1 24.0 %collective-permute-start.14 = (bf16[128,768]{1,0:T(8,128)(2,1)}, bf16[128,768]{1,0:T(8,128)(2,1)S(1)}, u32[]{:S(2)}, u32[]{:S(2)}) collective-permute-start(bf16[128,768]{1,0:T(8,128)(2,1)} %get-tuple-element.133), channel_id=1, source_target_pairs={{0,8},{2,10},{4,12},{6,14},{8,0},{10,2},{12,4},{14,6},{1,9},{3,11}... | collective-permute-start | bytes 589832 | tf_op jit(solution)/shard_map/ppermute | solution.py:417
  80.3 22.8 %collective-permute-start.15 = (bf16[128,768]{1,0:T(8,128)(2,1)}, bf16[128,768]{1,0:T(8,128)(2,1)S(1)}, u32[]{:S(2)}, u32[]{:S(2)}) collective-permute-start(bf16[128,768]{1,0:T(8,128)(2,1)} %get-tuple-element.134), channel_id=1, source_target_pairs={{0,4},{2,6},{4,0},{6,2},{8,12},{10,14},{12,8},{14,10},{1,5},{3,7},... | collective-permute-start | bytes 589832 | tf_op jit(solution)/shard_map/ppermute | solution.py:417
  81.7 21.4 %collective-permute-start.16 = (bf16[128,768]{1,0:T(8,128)(2,1)}, bf16[128,768]{1,0:T(8,128)(2,1)S(1)}, u32[]{:S(2)}, u32[]{:S(2)}) collective-permute-start(bf16[128,768]{1,0:T(8,128)(2,1)} %get-tuple-element.135), channel_id=1, source_target_pairs={{0,10},{2,8},{4,14},{6,12},{8,2},{10,0},{12,6},{14,4},{1,11},{3,9}... | collective-permute-start | bytes 589832 | tf_op jit(solution)/shard_map/ppermute | solution.py:417
  105.1 12.5 %collective-permute-start.18 = (bf16[128,768]{1,0:T(8,128)(2,1)S(1)}, bf16[128,768]{1,0:T(8,128)(2,1)}, u32[]{:S(2)}, u32[]{:S(2)}) collective-permute-start(bf16[128,768]{1,0:T(8,128)(2,1)S(1)} %copy-done.22), channel_id=1, source_target_pairs={{0,6},{2,4},{4,2},{6,0},{8,14},{10,12},{12,10},{14,8},{1,7},{3,5},... | collective-permute-start | bytes 589832 | tf_op jit(solution)/shard_map/ppermute | solution.py:417
  105.2 12.4 %collective-permute-start.19 = (bf16[128,768]{1,0:T(8,128)(2,1)S(1)}, bf16[128,768]{1,0:T(8,128)(2,1)}, u32[]{:S(2)}, u32[]{:S(2)}) collective-permute-start(bf16[128,768]{1,0:T(8,128)(2,1)S(1)} %copy-done.21), channel_id=1, source_target_pairs={{0,12},{2,14},{4,8},{6,10},{8,4},{10,6},{12,0},{14,2},{1,13},{3,15... | collective-permute-start | bytes 589832 | tf_op jit(solution)/shard_map/ppermute | solution.py:417
  118.2 13.8 %collective-permute-start.21 = (bf16[128,768]{1,0:T(8,128)(2,1)}, bf16[128,768]{1,0:T(8,128)(2,1)}, u32[]{:S(2)}, u32[]{:S(2)}) collective-permute-start(bf16[128,768]{1,0:T(8,128)(2,1)} %get-tuple-element.140), channel_id=1, source_target_pairs={{0,2},{2,0},{4,6},{6,4},{8,10},{10,8},{12,14},{14,12},{1,3},{3,1},... | collective-permute-start | bytes 589832 | tf_op jit(solution)/shard_map/ppermute | solution.py:417
  121.6 17.8 %collective-permute-start.23 = (bf16[128,768]{1,0:T(8,128)(2,1)}, bf16[128,768]{1,0:T(8,128)(2,1)}, u32[]{:S(2)}, u32[]{:S(2)}) collective-permute-start(bf16[128,768]{1,0:T(8,128)(2,1)} %get-tuple-element.142), channel_id=1, source_target_pairs={{0,8},{2,10},{4,12},{6,14},{8,0},{10,2},{12,4},{14,6},{1,9},{3,11}... | collective-permute-start | bytes 589832 | tf_op jit(solution)/shard_map/ppermute | solution.py:417
  144.0 18.3 %collective-permute-start.28 = (bf16[128,768]{1,0:T(8,128)(2,1)}, bf16[128,768]{1,0:T(8,128)(2,1)S(1)}, u32[]{:S(2)}, u32[]{:S(2)}) collective-permute-start(bf16[128,768]{1,0:T(8,128)(2,1)} %get-tuple-element.145), channel_id=1, source_target_pairs={{0,10},{2,8},{4,14},{6,12},{8,2},{10,0},{12,6},{14,4},{1,11},{3,9}... | collective-permute-start | bytes 589832 | tf_op jit(solution)/shard_map/ppermute | solution.py:417
  146.2 28.8 %collective-permute-start.33 = (bf16[128,768]{1,0:T(8,128)(2,1)}, bf16[128,768]{1,0:T(8,128)(2,1)S(1)}, u32[]{:S(2)}, u32[]{:S(2)}) collective-permute-start(bf16[128,768]{1,0:T(8,128)(2,1)} %get-tuple-element.152), channel_id=1, source_target_pairs={{0,12},{2,14},{4,8},{6,10},{8,4},{10,6},{12,0},{14,2},{1,13},{3,15... | collective-permute-start | bytes 589832 | tf_op jit(solution)/shard_map/ppermute | solution.py:417
  148.4 26.5 %collective-permute-start.34 = (bf16[128,768]{1,0:T(8,128)(2,1)}, bf16[128,768]{1,0:T(8,128)(2,1)S(1)}, u32[]{:S(2)}, u32[]{:S(2)}) collective-permute-start(bf16[128,768]{1,0:T(8,128)(2,1)} %get-tuple-element.153), channel_id=1, source_target_pairs={{0,6},{2,4},{4,2},{6,0},{8,14},{10,12},{12,10},{14,8},{1,7},{3,5},... | collective-permute-start | bytes 589832 | tf_op jit(solution)/shard_map/ppermute | solution.py:417
  162.3 12.6 %collective-permute-start.31 = (bf16[32,768]{1,0:T(8,128)(2,1)S(1)}, bf16[32,768]{1,0:T(8,128)(2,1)S(1)}, u32[]{:S(2)}, u32[]{:S(2)}) collective-permute-start(bf16[32,768]{1,0:T(8,128)(2,1)S(1)} %fusion.3), channel_id=1, source_target_pairs={{0,12},{2,14},{4,8},{6,10},{8,4},{10,6},{12,0},{14,2},{1,13},{3,15... | collective-permute-start | bytes 147464 | tf_op jit(solution)/shard_map/ppermute | solution.py:417
  (48 other events, 466.7 us)

commit v15 on v14

--- a/solution.py
+++ b/solution.py
@@ -14,7 +14,7 @@
 KW = 64
 shrink_level = 0.05
 FIRST = 5
-HELD = 3
+HELD = 5
 MIB = 1024 * 1024
 
 
@@ -603,7 +603,7 @@
     grad_image, sums = waiting((list(grad_image), sums), early)
     group_sum = GroupSum(sums)
     group_sum.over_dp()
-    group_sum.over_next(late[:2])
+    group_sum.over_next(late[:1])
     grad_band = {0: grad_image[0]}
     send(grad_image, order, grad_band)
     arrived = [grad_band[offset] for offset in order]
@@ -611,11 +611,11 @@
     grad_band = listed(grad_band)
     again = waiting(fields, early[:1])
     output = rows_inside(to_cells(me, scaled.T, image_band, again))
-    group_sum.scatter(late[2:] + arrived[:1])
+    group_sum.scatter(late[1:] + arrived[:1])
     group_sum.gather(arrived[1:3])
     group_sum.quarter, output = lax.optimization_barrier((group_sum.quarter, output))
-    group_sum.gather_next(arrived[3:5])
-    half, other = group_sum.gather_dp(arrived[5:])
+    group_sum.gather_next(arrived[3:6])
+    half, other = group_sum.gather_dp(arrived[6:])
     near = lax.axis_index("space")
     here = jnp.stack([lax.axis_index("dp"), near % 2, near // 2]).astype(jnp.int32)
     grads = finish_sums(here, half, other, factor, w_first.shape, b_first.shape)

time: 196 us -> 189 us (0.964)
  waiting for transfers between devices: 55.3 us -> 50.9 us
    ppermute x38, waiting for transfers between devices: 55.3 us -> 50.9 us  [swap_with(): return lax.ppermute(values, axis, pairs)]
    unnamed x69 -> x65, local copies, waits for them, and re-layouts: 4.68 us -> 4.02 us
  transfers between devices with their start and end apart: 38 -> 38, of which waited for: 14 -> 14; matrix products, arithmetic and copies ran while one was open for 7% -> 7% of each run, Pallas kernels for 16% -> 17%
where the time goes in v15:
time: 189 us; the launch traced here: 188 us
  starting transfers between devices  82 us (43%)
  waiting for transfers between devices  50.9 us (27%)
  Pallas kernels  36.1 us (19%)
  local copies, waits for them, and re-layouts  15.6 us (8%)
  other arithmetic  2.58 us (1%)
    ppermute x38, starting transfers between devices, swap_with(): return lax.ppermute(values, axis, pairs)  82 us
    ppermute x38, waiting for transfers between devices, swap_with(): return lax.ppermute(values, axis, pairs)  50.9 us
    pallas_call x1, Pallas kernels, backward_mid(): pl.pallas_call(functools.partial(backward_kernel, size_of_block, len(band...  12.8 us
    pallas_call x1, Pallas kernels, forward_mid(): pl.pallas_call(functools.partial(forward_kernel, len(bands)), grid_spec=p...  7.6 us
    pallas_call x2, Pallas kernels, to_cells(): pl.pallas_call(to_cells_kernel, grid_spec=pltpu.PrefetchScalarGridSpec(nu...  6.19 us
    pallas_call x2, local copies, waits for them, and re-layouts, to_cells(): pl.pallas_call(to_cells_kernel, grid_spec=pltpu.PrefetchScalarGridSpec(nu...  6.13 us
    pallas_call x2, Pallas kernels, to_modes(): pl.pallas_call(to_modes_kernel, grid_spec=pltpu.PrefetchScalarGridSpec(nu...  4.82 us
    unnamed x65, local copies, waits for them, and re-layouts  4.02 us
  transfers between devices with their start and end apart: 38, of which 14 were waited for; matrix products, arithmetic and copies ran while one was open for 7% of the time, Pallas kernels for 17%

profile of v15, /device:TPU:0, one launch (start us, length us, event | category | flops | bytes accessed | tf_op | source)
XLA Modules:
  0.0 188.3 jit_solution(10973276385937798316)
XLA Ops:
  5.0 6.0 %collective-permute-start = (bf16[128,768]{1,0:T(8,128)(2,1)}, bf16[128,768]{1,0:T(8,128)(2,1)S(1)}, u32[]{:S(2)}, u32[]{:S(2)}) collective-permute-start(bf16[128,768]{1,0:T(8,128)(2,1)} %get-tuple-element.97), channel_id=1, source_target_pairs={{0,14},{2,12},{4,10},{6,8},{8,6},{10,4},{12,2},{14,0},{1,15},{3,13... | collective-permute-start | bytes 589832 | tf_op jit(solution)/shard_map/ppermute | solution.py:417
  17.1 17.6 %collective-permute-start.5 = (bf16[128,768]{1,0:T(8,128)(2,1)}, bf16[128,768]{1,0:T(8,128)(2,1)}, u32[]{:S(2)}, u32[]{:S(2)}) collective-permute-start(bf16[128,768]{1,0:T(8,128)(2,1)} %get-tuple-element.102), channel_id=1, source_target_pairs={{0,4},{2,6},{4,0},{6,2},{8,12},{10,14},{12,8},{14,10},{1,5},{3,7},... | collective-permute-start | bytes 589832 | tf_op jit(solution)/shard_map/ppermute | solution.py:417
  38.6 2.6 %spread_weights.1 = (bf16[2,768,768]{2,1,0:T(8,128)(2,1)}, bf16[2,768,768]{2,1,0:T(8,128)(2,1)}) custom-call(bf16[2,8,96,96]{3,2,1,0:T(8,128)(2,1)S(1)} %copy-done.4, bf16[2,8,96,96]{3,2,1,0:T(8,128)(2,1)S(1)} %copy-done.5), custom_call_target="tpu_custom_call" | custom-call | flops 226492416 | bytes 4718592 | tf_op jit(solution)/shard_map/spread_weights/pallas_call | solution.py:83
  41.2 2.5 %to_modes.3 = (bf16[128,768]{1,0:T(8,128)(2,1)}, bf16[128,768]{1,0:T(8,128)(2,1)}, bf16[128,768]{1,0:T(8,128)(2,1)}, bf16[128,768]{1,0:T(8,128)(2,1)}, bf16[128,...) custom-call(s32[1]{0:T(128)} %bitcast.me_ref, ...), custom_call_target="tpu_custom_call" | custom-call | flops 283115520 | bytes 3784704 | tf_op jit(solution)/shard_map/to_modes/pallas_call | solution.py:136
  54.1 7.6 %mix_forward.1 = (bf16[128,768]{1,0:T(8,128)(2,1)}, bf16[128,768]{1,0:T(8,128)(2,1)}, bf16[128,768]{1,0:T(8,128)(2,1)}, bf16[128,768]{1,0:T(8,128)(2,1)}, bf16[1...) custom-call(s32[1]{0:T(128)} %bitcast.me_ref, ...), custom_call_target="tpu_custom_call" | custom-call | flops 2415919104 | bytes 17301504 | tf_op jit(solution)/shard_map/mix_forward/pallas_call | solution.py:344
  61.7 9.7 %collective-permute-start.12 = (bf16[128,768]{1,0:T(8,128)(2,1)}, bf16[128,768]{1,0:T(8,128)(2,1)}, u32[]{:S(2)}, u32[]{:S(2)}) collective-permute-start(bf16[128,768]{1,0:T(8,128)(2,1)} %get-tuple-element.122), channel_id=1, source_target_pairs={{0,4},{2,6},{4,0},{6,2},{8,12},{10,14},{12,8},{14,10},{1,5},{3,7},... | collective-permute-start | bytes 589832 | tf_op jit(solution)/shard_map/ppermute | solution.py:417
  71.5 7.7 %collective-permute-done.9.refs_3_ = bf16[128,768]{1,0:T(8,128)(2,1)S(1)} collective-permute-done((bf16[128,768]{1,0:T(8,128)(2,1)}, bf16[128,768]{1,0:T(8,128)(2,1)S(1)}, u32[]{:S(2)}, u32[]{:S(2)}) %collective-permute-start.9) | collective-permute-done | bytes 196640 | tf_op jit(solution)/shard_map/ppermute | solution.py:417
  81.7 8.5 %collective-permute-start.16 = (bf16[128,768]{1,0:T(8,128)(2,1)}, bf16[128,768]{1,0:T(8,128)(2,1)S(1)}, u32[]{:S(2)}, u32[]{:S(2)}) collective-permute-start(bf16[128,768]{1,0:T(8,128)(2,1)} %get-tuple-element.135), channel_id=1, source_target_pairs={{0,10},{2,8},{4,14},{6,12},{8,2},{10,0},{12,6},{14,4},{1,11},{3,9}... | collective-permute-start | bytes 589832 | tf_op jit(solution)/shard_map/ppermute | solution.py:417
  92.1 12.8 %mix_backward.1 = (bf16[128,768]{1,0:T(8,128)(2,1)}, bf16[128,768]{1,0:T(8,128)(2,1)}, bf16[128,768]{1,0:T(8,128)(2,1)}, bf16[128,768]{1,0:T(8,128)(2,1)}, bf16[...) custom-call(s32[1]{0:T(128)} %bitcast.me_ref, ...), custom_call_target="tpu_custom_call" | custom-call | flops 4831838208 | bytes 17301504 | tf_op jit(solution)/shard_map/mix_backward/pallas_call | solution.py:382
  104.9 3.5 %collective-permute-done.17.refs_5_ = bf16[128,768]{1,0:T(8,128)(2,1)S(1)} collective-permute-done((bf16[128,768]{1,0:T(8,128)(2,1)}, bf16[128,768]{1,0:T(8,128)(2,1)S(1)}, u32[]{:S(2)}, u32[]{:S(2)}) %collective-permute-start.17) | collective-permute-done | bytes 196640 | tf_op jit(solution)/shard_map/ppermute | solution.py:417
  113.8 3.6 %collective-permute-done.20.refs_7_ = bf16[128,768]{1,0:T(8,128)(2,1)} collective-permute-done((bf16[128,768]{1,0:T(8,128)(2,1)S(1)}, bf16[128,768]{1,0:T(8,128)(2,1)}, u32[]{:S(2)}, u32[]{:S(2)}) %collective-permute-start.20) | collective-permute-done | bytes 196640 | tf_op jit(solution)/shard_map/ppermute | solution.py:417
  117.7 2.8 %collective-permute-start.22 = (bf16[128,768]{1,0:T(8,128)(2,1)}, bf16[128,768]{1,0:T(8,128)(2,1)}, u32[]{:S(2)}, u32[]{:S(2)}) collective-permute-start(bf16[128,768]{1,0:T(8,128)(2,1)} %get-tuple-element.141), channel_id=1, source_target_pairs={{0,14},{2,12},{4,10},{6,8},{8,6},{10,4},{12,2},{14,0},{1,15},{3,13... | collective-permute-start | bytes 589832 | tf_op jit(solution)/shard_map/ppermute | solution.py:417
  120.5 7.3 %collective-permute-done.21 = bf16[128,768]{1,0:T(8,128)(2,1)} collective-permute-done((bf16[128,768]{1,0:T(8,128)(2,1)S(1)}, bf16[128,768]{1,0:T(8,128)(2,1)}, u32[]{:S(2)}, u32[]{:S(2)}) %collective-permute-start.21) | collective-permute-done | bytes 196640 | tf_op jit(solution)/shard_map/ppermute | solution.py:417
  128.8 9.4 %collective-permute-done.23.refs_4_ = bf16[128,768]{1,0:T(8,128)(2,1)} collective-permute-done((bf16[128,768]{1,0:T(8,128)(2,1)}, bf16[128,768]{1,0:T(8,128)(2,1)}, u32[]{:S(2)}, u32[]{:S(2)}) %collective-permute-start.23) | collective-permute-done | bytes 196640 | tf_op jit(solution)/shard_map/ppermute | solution.py:417
  139.0 3.7 %collective-permute-start.24 = (bf16[32,768]{1,0:T(8,128)(2,1)S(1)}, bf16[32,768]{1,0:T(8,128)(2,1)S(1)}, u32[]{:S(2)}, u32[]{:S(2)}) collective-permute-start(bf16[32,768]{1,0:T(8,128)(2,1)S(1)} %get-tuple-element.162), channel_id=1, source_target_pairs={{0,4},{2,6},{4,0},{6,2},{8,12},{10,14},{12,8},{14,10},{1,5},{3,7},... | collective-permute-start | bytes 147464 | tf_op jit(solution)/shard_map/ppermute | solution.py:417
  146.9 4.9 %collective-permute-done.27.refs_6_ = bf16[128,768]{1,0:T(8,128)(2,1)S(1)} collective-permute-done((bf16[128,768]{1,0:T(8,128)(2,1)}, bf16[128,768]{1,0:T(8,128)(2,1)S(1)}, u32[]{:S(2)}, u32[]{:S(2)}) %collective-permute-start.27) | collective-permute-done | bytes 196640 | tf_op jit(solution)/shard_map/ppermute | solution.py:417
  151.8 3.0 %collective-permute-done.28.refs_3_ = bf16[128,768]{1,0:T(8,128)(2,1)S(1)} collective-permute-done((bf16[128,768]{1,0:T(8,128)(2,1)}, bf16[128,768]{1,0:T(8,128)(2,1)S(1)}, u32[]{:S(2)}, u32[]{:S(2)}) %collective-permute-start.28) | collective-permute-done | bytes 196640 | tf_op jit(solution)/shard_map/ppermute | solution.py:417
  155.5 3.1 %collective-permute-start.33 = (bf16[128,768]{1,0:T(8,128)(2,1)}, bf16[128,768]{1,0:T(8,128)(2,1)S(1)}, u32[]{:S(2)}, u32[]{:S(2)}) collective-permute-start(bf16[128,768]{1,0:T(8,128)(2,1)} %get-tuple-element.152), channel_id=1, source_target_pairs={{0,12},{2,14},{4,8},{6,10},{8,4},{10,6},{12,0},{14,2},{1,13},{3,15... | collective-permute-start | bytes 589832 | tf_op jit(solution)/shard_map/ppermute | solution.py:417
  164.0 3.2 %to_cells.2 = bf16[4,2,180,768]{3,2,1,0:T(8,128)(2,1)S(1)} custom-call(s32[1]{0:T(128)} %bitcast.me_ref, bf16[180,128]{1,0:T(8,128)(2,1)S(1)} %copy-done.3, bf16[4,2,180,768]{3,2,1,0:T(8,128)(2,1)S(1)} %copy.23.base_ref, bf16[128,768]{1,0:T(8,128)(2,1)} %get-tuple-element.148.refs_0_, bf16[128,768]{1,0:T(8,128)(2,1)} %collective-permute-done.22.refs_1_, ...), custom_call_target="tpu_custom_call" | custom-call | flops 283115520 | bytes 5996544 | tf_op jit(solution)/shard_map/to_cells/pallas_call | solution.py:186
  167.3 3.1 %copy.30 = bf16[4,2,180,768]{3,1,2,0:T(2,128)(2,1)} copy(bf16[4,2,180,768]{3,2,1,0:T(8,128)(2,1)S(1)} %to_cells.2) | data formatting | bytes 4423680 | tf_op jit(solution)/shard_map/to_cells/pallas_call | solution.py:186
  170.9 3.4 %collective-permute-start.32 = (bf16[128,768]{1,0:T(8,128)(2,1)S(1)}, bf16[128,768]{1,0:T(8,128)(2,1)S(1)}, u32[]{:S(2)}, u32[]{:S(2)}) collective-permute-start(bf16[128,768]{1,0:T(8,128)(2,1)S(1)} %copy-done.21), channel_id=1, source_target_pairs={{0,14},{2,12},{4,10},{6,8},{8,6},{10,4},{12,2},{14,0},{1,15},{3,13... | collective-permute-start | bytes 589832 | tf_op jit(solution)/shard_map/ppermute | solution.py:417
  176.2 3.2 %collective-permute-done.32.refs_1_ = bf16[128,768]{1,0:T(8,128)(2,1)S(1)} collective-permute-done((bf16[128,768]{1,0:T(8,128)(2,1)S(1)}, bf16[128,768]{1,0:T(8,128)(2,1)S(1)}, u32[]{:S(2)}, u32[]{:S(2)}) %collective-permute-start.32) | collective-permute-done | bytes 196640 | tf_op jit(solution)/shard_map/ppermute | solution.py:417
  180.1 3.0 %to_cells.3 = bf16[4,2,180,768]{3,2,1,0:T(8,128)(2,1)S(1)} custom-call(s32[1]{0:T(128)} %bitcast.me_ref, bf16[180,128]{1,0:T(8,128)(2,1)S(1)} %copy-done.2, bf16[4,2,180,768]{3,2,1,0:T(8,128)(2,1)S(1)} %copy.22.cells_ref.base_ref, bf16[128,768]{1,0:T(8,128)(2,1)} %get-tuple-element.150.refs_0_, bf16[128,768]{1,0:T(8,128)(2,1)} %copy-done.18, ...), custom_call_target="tpu_custom_call" | custom-call | flops 283115520 | bytes 5996544 | tf_op jit(solution)/shard_map/to_cells/pallas_call | solution.py:186
  183.1 3.1 %copy.26 = bf16[4,2,180,768]{3,1,2,0:T(2,128)(2,1)} copy(bf16[4,2,180,768]{3,2,1,0:T(8,128)(2,1)S(1)} %to_cells.3) | data formatting | bytes 4423680 | tf_op jit(solution)/shard_map/to_cells/pallas_call | solution.py:186
  (144 shorter events, 52.1 us)
Async XLA Ops:
  5.0 12.1 %collective-permute-start = (bf16[128,768]{1,0:T(8,128)(2,1)}, bf16[128,768]{1,0:T(8,128)(2,1)S(1)}, u32[]{:S(2)}, u32[]{:S(2)}) collective-permute-start(bf16[128,768]{1,0:T(8,128)(2,1)} %get-tuple-element.97), channel_id=1, source_target_pairs={{0,14},{2,12},{4,10},{6,8},{8,6},{10,4},{12,2},{14,0},{1,15},{3,13... | collective-permute-start | bytes 589832 | tf_op jit(solution)/shard_map/ppermute | solution.py:417
  11.0 23.7 %collective-permute-start.1 = (bf16[128,768]{1,0:T(8,128)(2,1)}, bf16[128,768]{1,0:T(8,128)(2,1)S(1)}, u32[]{:S(2)}, u32[]{:S(2)}) collective-permute-start(bf16[128,768]{1,0:T(8,128)(2,1)} %get-tuple-element.98), channel_id=1, source_target_pairs={{0,12},{2,14},{4,8},{6,10},{8,4},{10,6},{12,0},{14,2},{1,13},{3,15... | collective-permute-start | bytes 589832 | tf_op jit(solution)/shard_map/ppermute | solution.py:417
  11.2 32.4 %collective-permute-start.2 = (bf16[128,768]{1,0:T(8,128)(2,1)}, bf16[128,768]{1,0:T(8,128)(2,1)S(1)}, u32[]{:S(2)}, u32[]{:S(2)}) collective-permute-start(bf16[128,768]{1,0:T(8,128)(2,1)} %get-tuple-element.99), channel_id=1, source_target_pairs={{0,10},{2,8},{4,14},{6,12},{8,2},{10,0},{12,6},{14,4},{1,11},{3,9}... | collective-permute-start | bytes 589832 | tf_op jit(solution)/shard_map/ppermute | solution.py:417
  12.0 34.7 %collective-permute-start.3 = (bf16[128,768]{1,0:T(8,128)(2,1)}, bf16[128,768]{1,0:T(8,128)(2,1)S(1)}, u32[]{:S(2)}, u32[]{:S(2)}) collective-permute-start(bf16[128,768]{1,0:T(8,128)(2,1)} %get-tuple-element.100), channel_id=1, source_target_pairs={{0,8},{2,10},{4,12},{6,14},{8,0},{10,2},{12,4},{14,6},{1,9},{3,11}... | collective-permute-start | bytes 589832 | tf_op jit(solution)/shard_map/ppermute | solution.py:417
  14.0 34.7 %collective-permute-start.4 = (bf16[128,768]{1,0:T(8,128)(2,1)}, bf16[128,768]{1,0:T(8,128)(2,1)S(1)}, u32[]{:S(2)}, u32[]{:S(2)}) collective-permute-start(bf16[128,768]{1,0:T(8,128)(2,1)} %get-tuple-element.101), channel_id=1, source_target_pairs={{0,6},{2,4},{4,2},{6,0},{8,14},{10,12},{12,10},{14,8},{1,7},{3,5},... | collective-permute-start | bytes 589832 | tf_op jit(solution)/shard_map/ppermute | solution.py:417
  17.1 34.1 %collective-permute-start.5 = (bf16[128,768]{1,0:T(8,128)(2,1)}, bf16[128,768]{1,0:T(8,128)(2,1)}, u32[]{:S(2)}, u32[]{:S(2)}) collective-permute-start(bf16[128,768]{1,0:T(8,128)(2,1)} %get-tuple-element.102), channel_id=1, source_target_pairs={{0,4},{2,6},{4,0},{6,2},{8,12},{10,14},{12,8},{14,10},{1,5},{3,7},... | collective-permute-start | bytes 589832 | tf_op jit(solution)/shard_map/ppermute | solution.py:417
  34.7 17.9 %collective-permute-start.6 = (bf16[128,768]{1,0:T(8,128)(2,1)}, bf16[128,768]{1,0:T(8,128)(2,1)}, u32[]{:S(2)}, u32[]{:S(2)}) collective-permute-start(bf16[128,768]{1,0:T(8,128)(2,1)} %get-tuple-element.103), channel_id=1, source_target_pairs={{0,2},{2,0},{4,6},{6,4},{8,10},{10,8},{12,14},{14,12},{1,3},{3,1},... | collective-permute-start | bytes 589832 | tf_op jit(solution)/shard_map/ppermute | solution.py:417
  44.3 17.4 %collective-permute-start.7 = (bf16[128,768]{1,0:T(8,128)(2,1)}, bf16[128,768]{1,0:T(8,128)(2,1)S(1)}, u32[]{:S(2)}, u32[]{:S(2)}) collective-permute-start(bf16[128,768]{1,0:T(8,128)(2,1)} %get-tuple-element.107), channel_id=1, source_target_pairs={{0,14},{2,12},{4,10},{6,8},{8,6},{10,4},{12,2},{14,0},{1,15},{3,13... | collective-permute-start | bytes 589832 | tf_op jit(solution)/shard_map/ppermute | solution.py:417
  47.3 24.0 %collective-permute-start.8 = (bf16[128,768]{1,0:T(8,128)(2,1)}, bf16[128,768]{1,0:T(8,128)(2,1)S(1)}, u32[]{:S(2)}, u32[]{:S(2)}) collective-permute-start(bf16[128,768]{1,0:T(8,128)(2,1)} %get-tuple-element.108), channel_id=1, source_target_pairs={{0,12},{2,14},{4,8},{6,10},{8,4},{10,6},{12,0},{14,2},{1,13},{3,15... | collective-permute-start | bytes 589832 | tf_op jit(solution)/shard_map/ppermute | solution.py:417
  48.8 30.4 %collective-permute-start.9 = (bf16[128,768]{1,0:T(8,128)(2,1)}, bf16[128,768]{1,0:T(8,128)(2,1)S(1)}, u32[]{:S(2)}, u32[]{:S(2)}) collective-permute-start(bf16[128,768]{1,0:T(8,128)(2,1)} %get-tuple-element.109), channel_id=1, source_target_pairs={{0,10},{2,8},{4,14},{6,12},{8,2},{10,0},{12,6},{14,4},{1,11},{3,9}... | collective-permute-start | bytes 589832 | tf_op jit(solution)/shard_map/ppermute | solution.py:417
  51.2 29.2 %collective-permute-start.10 = (bf16[128,768]{1,0:T(8,128)(2,1)}, bf16[128,768]{1,0:T(8,128)(2,1)}, u32[]{:S(2)}, u32[]{:S(2)}) collective-permute-start(bf16[128,768]{1,0:T(8,128)(2,1)} %get-tuple-element.110), channel_id=1, source_target_pairs={{0,8},{2,10},{4,12},{6,14},{8,0},{10,2},{12,4},{14,6},{1,9},{3,11}... | collective-permute-start | bytes 589832 | tf_op jit(solution)/shard_map/ppermute | solution.py:417
  52.6 29.0 %collective-permute-start.11 = (bf16[128,768]{1,0:T(8,128)(2,1)}, bf16[128,768]{1,0:T(8,128)(2,1)}, u32[]{:S(2)}, u32[]{:S(2)}) collective-permute-start(bf16[128,768]{1,0:T(8,128)(2,1)} %get-tuple-element.111), channel_id=1, source_target_pairs={{0,6},{2,4},{4,2},{6,0},{8,14},{10,12},{12,10},{14,8},{1,7},{3,5},... | collective-permute-start | bytes 589832 | tf_op jit(solution)/shard_map/ppermute | solution.py:417
  61.7 28.5 %collective-permute-start.12 = (bf16[128,768]{1,0:T(8,128)(2,1)}, bf16[128,768]{1,0:T(8,128)(2,1)}, u32[]{:S(2)}, u32[]{:S(2)}) collective-permute-start(bf16[128,768]{1,0:T(8,128)(2,1)} %get-tuple-element.122), channel_id=1, source_target_pairs={{0,4},{2,6},{4,0},{6,2},{8,12},{10,14},{12,8},{14,10},{1,5},{3,7},... | collective-permute-start | bytes 589832 | tf_op jit(solution)/shard_map/ppermute | solution.py:417
  71.4 18.8 %collective-permute-start.13 = (bf16[128,768]{1,0:T(8,128)(2,1)S(1)}, bf16[128,768]{1,0:T(8,128)(2,1)}, u32[]{:S(2)}, u32[]{:S(2)}) collective-permute-start(bf16[128,768]{1,0:T(8,128)(2,1)S(1)} %copy-done.26), channel_id=1, source_target_pairs={{0,2},{2,0},{4,6},{6,4},{8,10},{10,8},{12,14},{14,12},{1,3},{3,1},... | collective-permute-start | bytes 589832 | tf_op jit(solution)/shard_map/ppermute | solution.py:417
  79.1 25.8 %collective-permute-start.14 = (bf16[128,768]{1,0:T(8,128)(2,1)}, bf16[128,768]{1,0:T(8,128)(2,1)S(1)}, u32[]{:S(2)}, u32[]{:S(2)}) collective-permute-start(bf16[128,768]{1,0:T(8,128)(2,1)} %get-tuple-element.133), channel_id=1, source_target_pairs={{0,8},{2,10},{4,12},{6,14},{8,0},{10,2},{12,4},{14,6},{1,9},{3,11}... | collective-permute-start | bytes 589832 | tf_op jit(solution)/shard_map/ppermute | solution.py:417
  80.4 24.6 %collective-permute-start.15 = (bf16[128,768]{1,0:T(8,128)(2,1)}, bf16[128,768]{1,0:T(8,128)(2,1)S(1)}, u32[]{:S(2)}, u32[]{:S(2)}) collective-permute-start(bf16[128,768]{1,0:T(8,128)(2,1)} %get-tuple-element.134), channel_id=1, source_target_pairs={{0,4},{2,6},{4,0},{6,2},{8,12},{10,14},{12,8},{14,10},{1,5},{3,7},... | collective-permute-start | bytes 589832 | tf_op jit(solution)/shard_map/ppermute | solution.py:417
  81.7 23.2 %collective-permute-start.16 = (bf16[128,768]{1,0:T(8,128)(2,1)}, bf16[128,768]{1,0:T(8,128)(2,1)S(1)}, u32[]{:S(2)}, u32[]{:S(2)}) collective-permute-start(bf16[128,768]{1,0:T(8,128)(2,1)} %get-tuple-element.135), channel_id=1, source_target_pairs={{0,10},{2,8},{4,14},{6,12},{8,2},{10,0},{12,6},{14,4},{1,11},{3,9}... | collective-permute-start | bytes 589832 | tf_op jit(solution)/shard_map/ppermute | solution.py:417
  90.2 18.3 %collective-permute-start.17 = (bf16[128,768]{1,0:T(8,128)(2,1)}, bf16[128,768]{1,0:T(8,128)(2,1)S(1)}, u32[]{:S(2)}, u32[]{:S(2)}) collective-permute-start(bf16[128,768]{1,0:T(8,128)(2,1)} %get-tuple-element.136), channel_id=1, source_target_pairs={{0,6},{2,4},{4,2},{6,0},{8,14},{10,12},{12,10},{14,8},{1,7},{3,5},... | collective-permute-start | bytes 589832 | tf_op jit(solution)/shard_map/ppermute | solution.py:417
  90.2 18.3 %collective-permute-start.18 = (bf16[128,768]{1,0:T(8,128)(2,1)}, bf16[128,768]{1,0:T(8,128)(2,1)S(1)}, u32[]{:S(2)}, u32[]{:S(2)}) collective-permute-start(bf16[128,768]{1,0:T(8,128)(2,1)} %get-tuple-element.137), channel_id=1, source_target_pairs={{0,12},{2,14},{4,8},{6,10},{8,4},{10,6},{12,0},{14,2},{1,13},{3,15... | collective-permute-start | bytes 589832 | tf_op jit(solution)/shard_map/ppermute | solution.py:417
  120.5 17.7 %collective-permute-start.23 = (bf16[128,768]{1,0:T(8,128)(2,1)}, bf16[128,768]{1,0:T(8,128)(2,1)}, u32[]{:S(2)}, u32[]{:S(2)}) collective-permute-start(bf16[128,768]{1,0:T(8,128)(2,1)} %get-tuple-element.142), channel_id=1, source_target_pairs={{0,8},{2,10},{4,12},{6,14},{8,0},{10,2},{12,4},{14,6},{1,9},{3,11}... | collective-permute-start | bytes 589832 | tf_op jit(solution)/shard_map/ppermute | solution.py:417
  142.7 12.0 %collective-permute-start.28 = (bf16[128,768]{1,0:T(8,128)(2,1)}, bf16[128,768]{1,0:T(8,128)(2,1)S(1)}, u32[]{:S(2)}, u32[]{:S(2)}) collective-permute-start(bf16[128,768]{1,0:T(8,128)(2,1)} %get-tuple-element.145), channel_id=1, source_target_pairs={{0,10},{2,8},{4,14},{6,12},{8,2},{10,0},{12,6},{14,4},{1,11},{3,9}... | collective-permute-start | bytes 589832 | tf_op jit(solution)/shard_map/ppermute | solution.py:417
  155.5 14.8 %collective-permute-start.33 = (bf16[128,768]{1,0:T(8,128)(2,1)}, bf16[128,768]{1,0:T(8,128)(2,1)S(1)}, u32[]{:S(2)}, u32[]{:S(2)}) collective-permute-start(bf16[128,768]{1,0:T(8,128)(2,1)} %get-tuple-element.152), channel_id=1, source_target_pairs={{0,12},{2,14},{4,8},{6,10},{8,4},{10,6},{12,0},{14,2},{1,13},{3,15... | collective-permute-start | bytes 589832 | tf_op jit(solution)/shard_map/ppermute | solution.py:417
  158.6 11.8 %collective-permute-start.34 = (bf16[128,768]{1,0:T(8,128)(2,1)}, bf16[128,768]{1,0:T(8,128)(2,1)S(1)}, u32[]{:S(2)}, u32[]{:S(2)}) collective-permute-start(bf16[128,768]{1,0:T(8,128)(2,1)} %get-tuple-element.153), channel_id=1, source_target_pairs={{0,6},{2,4},{4,2},{6,0},{8,14},{10,12},{12,10},{14,8},{1,7},{3,5},... | collective-permute-start | bytes 589832 | tf_op jit(solution)/shard_map/ppermute | solution.py:417
  158.6 11.8 %collective-permute-start.35 = (bf16[128,768]{1,0:T(8,128)(2,1)}, bf16[128,768]{1,0:T(8,128)(2,1)S(1)}, u32[]{:S(2)}, u32[]{:S(2)}) collective-permute-start(bf16[128,768]{1,0:T(8,128)(2,1)} %get-tuple-element.154), channel_id=1, source_target_pairs={{0,2},{2,0},{4,6},{6,4},{8,10},{10,8},{12,14},{14,12},{1,3},{3,1},... | collective-permute-start | bytes 589832 | tf_op jit(solution)/shard_map/ppermute | solution.py:417
  (46 other events, 442.3 us)

commit v16 on v15

--- a/solution.py
+++ b/solution.py
@@ -426,10 +426,9 @@
     near = [offset for offset in (2, 3, 1) if offset < size // 2]
     near += list(range(4, size // 2))
     order = []
-    while far or near:
-        order += far[:1] + near[:1]
-        far, near = far[1:], near[1:]
-    return order
+    for place, offset in enumerate(far):
+        order += [offset] + near[place : place + 1] * (place < len(near) - 1)
+    return order + near[-1:]
 
 
 def pick(pair, side):
@@ -583,11 +582,13 @@
         return (output, grad_fields) + tuple(grads)
 
     gathered, cot_gathered = {0: spectrum[0]}, {0: cot_spec[0]}
-    send(spectrum, order, gathered)
+    falling = range(owners - 1, 0, -1)
+    send(spectrum, falling[:FIRST], gathered)
+    spectrum = waiting(list(spectrum), [cot_spec[0], w1, w2])
+    send(spectrum, falling[FIRST:], gathered)
     gathered = listed(gathered)
     image, state = forward_mid(me, lat, lat.T, gathered, w1, b1, w2, b2)
     cot_spec, image = list(cot_spec), list(image)
-    falling = range(owners - 1, 0, -1)
     send(cot_spec, falling[:FIRST], cot_gathered)
     cot_spec, image = waiting((cot_spec, image), [image[0]])
     send(cot_spec, falling[FIRST:], cot_gathered)

time: 189 us -> 189 us (level)
  waiting for transfers between devices: 50.9 us -> 55.1 us
  starting transfers between devices: 82 us -> 79.1 us
    ppermute x38, waiting for transfers between devices: 50.9 us -> 55.1 us  [swap_with(): return lax.ppermute(values, axis, pairs)]
    ppermute x38, starting transfers between devices: 82 us -> 79.1 us  [swap_with(): return lax.ppermute(values, axis, pairs)]
  transfers between devices with their start and end apart: 38 -> 38, of which waited for: 14 -> 17; matrix products, arithmetic and copies ran while one was open for 7% -> 6% of each run, Pallas kernels for 17% -> 17%
where the time goes in v16:
time: 189 us; the launch traced here: 188 us
  starting transfers between devices  79.1 us (42%)
  waiting for transfers between devices  55.1 us (29%)
  Pallas kernels  36.1 us (19%)
  local copies, waits for them, and re-layouts  14.2 us (8%)
  other arithmetic  2.58 us (1%)
    ppermute x38, starting transfers between devices, swap_with(): return lax.ppermute(values, axis, pairs)  79.1 us
    ppermute x38, waiting for transfers between devices, swap_with(): return lax.ppermute(values, axis, pairs)  55.1 us
    pallas_call x1, Pallas kernels, backward_mid(): pl.pallas_call(functools.partial(backward_kernel, size_of_block, len(band...  12.8 us
    pallas_call x1, Pallas kernels, forward_mid(): pl.pallas_call(functools.partial(forward_kernel, len(bands)), grid_spec=p...  7.51 us
    pallas_call x2, Pallas kernels, to_cells(): pl.pallas_call(to_cells_kernel, grid_spec=pltpu.PrefetchScalarGridSpec(nu...  6.21 us
    pallas_call x2, local copies, waits for them, and re-layouts, to_cells(): pl.pallas_call(to_cells_kernel, grid_spec=pltpu.PrefetchScalarGridSpec(nu...  6.13 us
    pallas_call x2, Pallas kernels, to_modes(): pl.pallas_call(to_modes_kernel, grid_spec=pltpu.PrefetchScalarGridSpec(nu...  4.83 us
    unnamed x65, local copies, waits for them, and re-layouts  4.45 us
  transfers between devices with their start and end apart: 38, of which 17 were waited for; matrix products, arithmetic and copies ran while one was open for 6% of the time, Pallas kernels for 17%

profile of v16, /device:TPU:0, one launch (start us, length us, event | category | flops | bytes accessed | tf_op | source)
XLA Modules:
  0.0 188.1 jit_solution(10220080343320777204)
XLA Ops:
  5.0 6.1 %collective-permute-start = (bf16[128,768]{1,0:T(8,128)(2,1)}, bf16[128,768]{1,0:T(8,128)(2,1)S(1)}, u32[]{:S(2)}, u32[]{:S(2)}) collective-permute-start(bf16[128,768]{1,0:T(8,128)(2,1)} %get-tuple-element.99), channel_id=1, source_target_pairs={{0,14},{2,12},{4,10},{6,8},{8,6},{10,4},{12,2},{14,0},{1,15},{3,13... | collective-permute-start | bytes 589832 | tf_op jit(solution)/shard_map/ppermute | solution.py:417
  21.8 13.0 %collective-permute-start.5 = (bf16[128,768]{1,0:T(8,128)(2,1)}, bf16[128,768]{1,0:T(8,128)(2,1)}, u32[]{:S(2)}, u32[]{:S(2)}) collective-permute-start(bf16[128,768]{1,0:T(8,128)(2,1)} %get-tuple-element.108), channel_id=1, source_target_pairs={{0,4},{2,6},{4,0},{6,2},{8,12},{10,14},{12,8},{14,10},{1,5},{3,7},... | collective-permute-start | bytes 589832 | tf_op jit(solution)/shard_map/ppermute | solution.py:417
  37.2 4.6 %collective-permute-done.2.refs_3_ = bf16[128,768]{1,0:T(8,128)(2,1)S(1)} collective-permute-done((bf16[128,768]{1,0:T(8,128)(2,1)}, bf16[128,768]{1,0:T(8,128)(2,1)S(1)}, u32[]{:S(2)}, u32[]{:S(2)}) %collective-permute-start.2) | collective-permute-done | bytes 196640 | tf_op jit(solution)/shard_map/ppermute | solution.py:417
  41.8 3.4 %collective-permute-start.7 = (bf16[128,768]{1,0:T(8,128)(2,1)}, bf16[128,768]{1,0:T(8,128)(2,1)S(1)}, u32[]{:S(2)}, u32[]{:S(2)}) collective-permute-start(bf16[128,768]{1,0:T(8,128)(2,1)} %get-tuple-element.111), channel_id=1, source_target_pairs={{0,14},{2,12},{4,10},{6,8},{8,6},{10,4},{12,2},{14,0},{1,15},{3,13... | collective-permute-start | bytes 589832 | tf_op jit(solution)/shard_map/ppermute | solution.py:417
  45.2 2.9 %collective-permute-done.3.refs_4_ = bf16[128,768]{1,0:T(8,128)(2,1)S(1)} collective-permute-done((bf16[128,768]{1,0:T(8,128)(2,1)}, bf16[128,768]{1,0:T(8,128)(2,1)S(1)}, u32[]{:S(2)}, u32[]{:S(2)}) %collective-permute-start.3) | collective-permute-done | bytes 196640 | tf_op jit(solution)/shard_map/ppermute | solution.py:417
  56.8 7.5 %mix_forward.1 = (bf16[128,768]{1,0:T(8,128)(2,1)}, bf16[128,768]{1,0:T(8,128)(2,1)}, bf16[128,768]{1,0:T(8,128)(2,1)}, bf16[128,768]{1,0:T(8,128)(2,1)}, bf16[1...) custom-call(s32[1]{0:T(128)} %bitcast.me_ref, ...), custom_call_target="tpu_custom_call" | custom-call | flops 2415919104 | bytes 17301504 | tf_op jit(solution)/shard_map/mix_forward/pallas_call | solution.py:344
  64.4 5.1 %collective-permute-start.12 = (bf16[128,768]{1,0:T(8,128)(2,1)S(1)}, bf16[128,768]{1,0:T(8,128)(2,1)}, u32[]{:S(2)}, u32[]{:S(2)}) collective-permute-start(bf16[128,768]{1,0:T(8,128)(2,1)S(1)} %copy-done.25), channel_id=1, source_target_pairs={{0,4},{2,6},{4,0},{6,2},{8,12},{10,14},{12,8},{14,10},{1,5},{3,7},... | collective-permute-start | bytes 589832 | tf_op jit(solution)/shard_map/ppermute | solution.py:417
  71.1 5.6 %collective-permute-done.9.refs_3_ = bf16[128,768]{1,0:T(8,128)(2,1)} collective-permute-done((bf16[128,768]{1,0:T(8,128)(2,1)}, bf16[128,768]{1,0:T(8,128)(2,1)}, u32[]{:S(2)}, u32[]{:S(2)}) %collective-permute-start.9) | collective-permute-done | bytes 196640 | tf_op jit(solution)/shard_map/ppermute | solution.py:417
  76.7 8.4 %collective-permute-done.10.refs_4_ = bf16[128,768]{1,0:T(8,128)(2,1)} collective-permute-done((bf16[128,768]{1,0:T(8,128)(2,1)}, bf16[128,768]{1,0:T(8,128)(2,1)}, u32[]{:S(2)}, u32[]{:S(2)}) %collective-permute-start.10) | collective-permute-done | bytes 196640 | tf_op jit(solution)/shard_map/ppermute | solution.py:417
  85.1 3.1 %collective-permute-start.16 = (bf16[128,768]{1,0:T(8,128)(2,1)}, bf16[128,768]{1,0:T(8,128)(2,1)S(1)}, u32[]{:S(2)}, u32[]{:S(2)}) collective-permute-start(bf16[128,768]{1,0:T(8,128)(2,1)} %get-tuple-element.139), channel_id=1, source_target_pairs={{0,10},{2,8},{4,14},{6,12},{8,2},{10,0},{12,6},{14,4},{1,11},{3,9}... | collective-permute-start | bytes 589832 | tf_op jit(solution)/shard_map/ppermute | solution.py:417
  90.4 12.8 %mix_backward.1 = (bf16[128,768]{1,0:T(8,128)(2,1)}, bf16[128,768]{1,0:T(8,128)(2,1)}, bf16[128,768]{1,0:T(8,128)(2,1)}, bf16[128,768]{1,0:T(8,128)(2,1)}, bf16[...) custom-call(s32[1]{0:T(128)} %bitcast.me_ref, ...), custom_call_target="tpu_custom_call" | custom-call | flops 4831838208 | bytes 17301504 | tf_op jit(solution)/shard_map/mix_backward/pallas_call | solution.py:382
  105.2 4.7 %collective-permute-start.20 = (bf16[128,768]{1,0:T(8,128)(2,1)S(1)}, bf16[128,768]{1,0:T(8,128)(2,1)}, u32[]{:S(2)}, u32[]{:S(2)}) collective-permute-start(bf16[128,768]{1,0:T(8,128)(2,1)S(1)} %copy-done.23), channel_id=1, source_target_pairs={{0,14},{2,12},{4,10},{6,8},{8,6},{10,4},{12,2},{14,0},{1,15},{3,13... | collective-permute-start | bytes 589832 | tf_op jit(solution)/shard_map/ppermute | solution.py:417
  111.3 4.2 %collective-permute-done.20.refs_1_ = bf16[128,768]{1,0:T(8,128)(2,1)} collective-permute-done((bf16[128,768]{1,0:T(8,128)(2,1)S(1)}, bf16[128,768]{1,0:T(8,128)(2,1)}, u32[]{:S(2)}, u32[]{:S(2)}) %collective-permute-start.20) | collective-permute-done | bytes 196640 | tf_op jit(solution)/shard_map/ppermute | solution.py:417
  115.5 2.8 %collective-permute-start.21 = (bf16[128,768]{1,0:T(8,128)(2,1)S(1)}, bf16[128,768]{1,0:T(8,128)(2,1)}, u32[]{:S(2)}, u32[]{:S(2)}) collective-permute-start(bf16[128,768]{1,0:T(8,128)(2,1)S(1)} %fusion), channel_id=1, source_target_pairs={{0,2},{2,0},{4,6},{6,4},{8,10},{10,8},{12,14},{14,12},{1,3},{3,1},... | collective-permute-start | bytes 589832 | tf_op jit(solution)/shard_map/ppermute | solution.py:417
  118.5 4.1 %collective-permute-start.23 = (bf16[128,768]{1,0:T(8,128)(2,1)}, bf16[128,768]{1,0:T(8,128)(2,1)}, u32[]{:S(2)}, u32[]{:S(2)}) collective-permute-start(bf16[128,768]{1,0:T(8,128)(2,1)} %get-tuple-element.146), channel_id=1, source_target_pairs={{0,8},{2,10},{4,12},{6,14},{8,0},{10,2},{12,4},{14,6},{1,9},{3,11}... | collective-permute-start | bytes 589832 | tf_op jit(solution)/shard_map/ppermute | solution.py:417
  127.3 3.9 %collective-permute-done.23.refs_4_ = bf16[128,768]{1,0:T(8,128)(2,1)} collective-permute-done((bf16[128,768]{1,0:T(8,128)(2,1)}, bf16[128,768]{1,0:T(8,128)(2,1)}, u32[]{:S(2)}, u32[]{:S(2)}) %collective-permute-start.23) | collective-permute-done | bytes 196640 | tf_op jit(solution)/shard_map/ppermute | solution.py:417
  141.1 4.7 %collective-permute-done.27.refs_6_ = bf16[128,768]{1,0:T(8,128)(2,1)S(1)} collective-permute-done((bf16[128,768]{1,0:T(8,128)(2,1)}, bf16[128,768]{1,0:T(8,128)(2,1)S(1)}, u32[]{:S(2)}, u32[]{:S(2)}) %collective-permute-start.27) | collective-permute-done | bytes 196640 | tf_op jit(solution)/shard_map/ppermute | solution.py:417
  153.6 2.9 %collective-permute-start.30 = (bf16[32,768]{1,0:T(8,128)(2,1)S(1)}, bf16[32,768]{1,0:T(8,128)(2,1)S(1)}, u32[]{:S(2)}, u32[]{:S(2)}) collective-permute-start(bf16[32,768]{1,0:T(8,128)(2,1)S(1)} %fusion.3), channel_id=1, source_target_pairs={{0,8},{2,10},{4,12},{6,14},{8,0},{10,2},{12,4},{14,6},{1,9},{3,11}... | collective-permute-start | bytes 147464 | tf_op jit(solution)/shard_map/ppermute | solution.py:417
  159.9 3.2 %to_cells.2 = bf16[4,2,180,768]{3,2,1,0:T(8,128)(2,1)S(1)} custom-call(s32[1]{0:T(128)} %bitcast.me_ref, bf16[180,128]{1,0:T(8,128)(2,1)S(1)} %copy-done.3, bf16[4,2,180,768]{3,2,1,0:T(8,128)(2,1)S(1)} %copy.23.base_ref, bf16[128,768]{1,0:T(8,128)(2,1)} %get-tuple-element.152.refs_0_, bf16[128,768]{1,0:T(8,128)(2,1)} %collective-permute-done.20.refs_1_, ...), custom_call_target="tpu_custom_call" | custom-call | flops 283115520 | bytes 5996544 | tf_op jit(solution)/shard_map/to_cells/pallas_call | solution.py:186
  163.2 3.1 %copy.30 = bf16[4,2,180,768]{3,1,2,0:T(2,128)(2,1)} copy(bf16[4,2,180,768]{3,2,1,0:T(8,128)(2,1)S(1)} %to_cells.2) | data formatting | bytes 4423680 | tf_op jit(solution)/shard_map/to_cells/pallas_call | solution.py:186
  166.2 3.4 %collective-permute-done.30 = bf16[32,768]{1,0:T(8,128)(2,1)S(1)} collective-permute-done((bf16[32,768]{1,0:T(8,128)(2,1)S(1)}, bf16[32,768]{1,0:T(8,128)(2,1)S(1)}, u32[]{:S(2)}, u32[]{:S(2)}) %collective-permute-start.30) | collective-permute-done | bytes 49184 | tf_op jit(solution)/shard_map/ppermute | solution.py:417
  171.9 5.2 %collective-permute-done.36 = bf16[4,32,768]{2,1,0:T(8,128)(2,1)S(1)} collective-permute-done((bf16[4,32,768]{2,1,0:T(8,128)(2,1)S(1)}, bf16[4,32,768]{2,1,0:T(8,128)(2,1)S(1)}, u32[]{:S(2)}, u32[]{:S(2)}) %collective-permute-start.36) | collective-permute-done | bytes 196640 | tf_op jit(solution)/shard_map/ppermute | solution.py:417
  179.8 3.0 %to_cells.3 = bf16[4,2,180,768]{3,2,1,0:T(8,128)(2,1)S(1)} custom-call(s32[1]{0:T(128)} %bitcast.me_ref, bf16[180,128]{1,0:T(8,128)(2,1)S(1)} %copy-done.2, bf16[4,2,180,768]{3,2,1,0:T(8,128)(2,1)S(1)} %copy.22.cells_ref.base_ref, bf16[128,768]{1,0:T(8,128)(2,1)} %get-tuple-element.154.refs_0_, bf16[128,768]{1,0:T(8,128)(2,1)} %copy-done.16, ...), custom_call_target="tpu_custom_call" | custom-call | flops 283115520 | bytes 5996544 | tf_op jit(solution)/shard_map/to_cells/pallas_call | solution.py:186
  182.9 3.1 %copy.26 = bf16[4,2,180,768]{3,1,2,0:T(2,128)(2,1)} copy(bf16[4,2,180,768]{3,2,1,0:T(8,128)(2,1)S(1)} %to_cells.3) | data formatting | bytes 4423680 | tf_op jit(solution)/shard_map/to_cells/pallas_call | solution.py:186
  (144 shorter events, 66.3 us)
Async XLA Ops:
  5.0 16.7 %collective-permute-start = (bf16[128,768]{1,0:T(8,128)(2,1)}, bf16[128,768]{1,0:T(8,128)(2,1)S(1)}, u32[]{:S(2)}, u32[]{:S(2)}) collective-permute-start(bf16[128,768]{1,0:T(8,128)(2,1)} %get-tuple-element.99), channel_id=1, source_target_pairs={{0,14},{2,12},{4,10},{6,8},{8,6},{10,4},{12,2},{14,0},{1,15},{3,13... | collective-permute-start | bytes 589832 | tf_op jit(solution)/shard_map/ppermute | solution.py:417
  11.1 23.7 %collective-permute-start.1 = (bf16[128,768]{1,0:T(8,128)(2,1)}, bf16[128,768]{1,0:T(8,128)(2,1)S(1)}, u32[]{:S(2)}, u32[]{:S(2)}) collective-permute-start(bf16[128,768]{1,0:T(8,128)(2,1)} %get-tuple-element.100), channel_id=1, source_target_pairs={{0,12},{2,14},{4,8},{6,10},{8,4},{10,6},{12,0},{14,2},{1,13},{3,15... | collective-permute-start | bytes 589832 | tf_op jit(solution)/shard_map/ppermute | solution.py:417
  11.3 30.5 %collective-permute-start.2 = (bf16[128,768]{1,0:T(8,128)(2,1)}, bf16[128,768]{1,0:T(8,128)(2,1)S(1)}, u32[]{:S(2)}, u32[]{:S(2)}) collective-permute-start(bf16[128,768]{1,0:T(8,128)(2,1)} %get-tuple-element.101), channel_id=1, source_target_pairs={{0,10},{2,8},{4,14},{6,12},{8,2},{10,0},{12,6},{14,4},{1,11},{3,9}... | collective-permute-start | bytes 589832 | tf_op jit(solution)/shard_map/ppermute | solution.py:417
  12.0 36.1 %collective-permute-start.3 = (bf16[128,768]{1,0:T(8,128)(2,1)}, bf16[128,768]{1,0:T(8,128)(2,1)S(1)}, u32[]{:S(2)}, u32[]{:S(2)}) collective-permute-start(bf16[128,768]{1,0:T(8,128)(2,1)} %get-tuple-element.102), channel_id=1, source_target_pairs={{0,8},{2,10},{4,12},{6,14},{8,0},{10,2},{12,4},{14,6},{1,9},{3,11}... | collective-permute-start | bytes 589832 | tf_op jit(solution)/shard_map/ppermute | solution.py:417
  14.1 37.2 %collective-permute-start.4 = (bf16[128,768]{1,0:T(8,128)(2,1)}, bf16[128,768]{1,0:T(8,128)(2,1)}, u32[]{:S(2)}, u32[]{:S(2)}) collective-permute-start(bf16[128,768]{1,0:T(8,128)(2,1)} %get-tuple-element.103), channel_id=1, source_target_pairs={{0,6},{2,4},{4,2},{6,0},{8,14},{10,12},{12,10},{14,8},{1,7},{3,5},... | collective-permute-start | bytes 589832 | tf_op jit(solution)/shard_map/ppermute | solution.py:417
  21.8 31.4 %collective-permute-start.5 = (bf16[128,768]{1,0:T(8,128)(2,1)}, bf16[128,768]{1,0:T(8,128)(2,1)}, u32[]{:S(2)}, u32[]{:S(2)}) collective-permute-start(bf16[128,768]{1,0:T(8,128)(2,1)} %get-tuple-element.108), channel_id=1, source_target_pairs={{0,4},{2,6},{4,0},{6,2},{8,12},{10,14},{12,8},{14,10},{1,5},{3,7},... | collective-permute-start | bytes 589832 | tf_op jit(solution)/shard_map/ppermute | solution.py:417
  35.5 18.7 %collective-permute-start.6 = (bf16[128,768]{1,0:T(8,128)(2,1)}, bf16[128,768]{1,0:T(8,128)(2,1)}, u32[]{:S(2)}, u32[]{:S(2)}) collective-permute-start(bf16[128,768]{1,0:T(8,128)(2,1)} %get-tuple-element.109), channel_id=1, source_target_pairs={{0,2},{2,0},{4,6},{6,4},{8,10},{10,8},{12,14},{14,12},{1,3},{3,1},... | collective-permute-start | bytes 589832 | tf_op jit(solution)/shard_map/ppermute | solution.py:417
  41.8 22.5 %collective-permute-start.7 = (bf16[128,768]{1,0:T(8,128)(2,1)}, bf16[128,768]{1,0:T(8,128)(2,1)S(1)}, u32[]{:S(2)}, u32[]{:S(2)}) collective-permute-start(bf16[128,768]{1,0:T(8,128)(2,1)} %get-tuple-element.111), channel_id=1, source_target_pairs={{0,14},{2,12},{4,10},{6,8},{8,6},{10,4},{12,2},{14,0},{1,15},{3,13... | collective-permute-start | bytes 589832 | tf_op jit(solution)/shard_map/ppermute | solution.py:417
  48.8 20.7 %collective-permute-start.8 = (bf16[128,768]{1,0:T(8,128)(2,1)}, bf16[128,768]{1,0:T(8,128)(2,1)S(1)}, u32[]{:S(2)}, u32[]{:S(2)}) collective-permute-start(bf16[128,768]{1,0:T(8,128)(2,1)} %get-tuple-element.112), channel_id=1, source_target_pairs={{0,12},{2,14},{4,8},{6,10},{8,4},{10,6},{12,0},{14,2},{1,13},{3,15... | collective-permute-start | bytes 589832 | tf_op jit(solution)/shard_map/ppermute | solution.py:417
  51.3 25.4 %collective-permute-start.9 = (bf16[128,768]{1,0:T(8,128)(2,1)}, bf16[128,768]{1,0:T(8,128)(2,1)}, u32[]{:S(2)}, u32[]{:S(2)}) collective-permute-start(bf16[128,768]{1,0:T(8,128)(2,1)} %get-tuple-element.113), channel_id=1, source_target_pairs={{0,10},{2,8},{4,14},{6,12},{8,2},{10,0},{12,6},{14,4},{1,11},{3,9}... | collective-permute-start | bytes 589832 | tf_op jit(solution)/shard_map/ppermute | solution.py:417
  53.2 31.9 %collective-permute-start.10 = (bf16[128,768]{1,0:T(8,128)(2,1)}, bf16[128,768]{1,0:T(8,128)(2,1)}, u32[]{:S(2)}, u32[]{:S(2)}) collective-permute-start(bf16[128,768]{1,0:T(8,128)(2,1)} %get-tuple-element.114), channel_id=1, source_target_pairs={{0,8},{2,10},{4,12},{6,14},{8,0},{10,2},{12,4},{14,6},{1,9},{3,11}... | collective-permute-start | bytes 589832 | tf_op jit(solution)/shard_map/ppermute | solution.py:417
  54.2 30.9 %collective-permute-start.11 = (bf16[128,768]{1,0:T(8,128)(2,1)}, bf16[128,768]{1,0:T(8,128)(2,1)}, u32[]{:S(2)}, u32[]{:S(2)}) collective-permute-start(bf16[128,768]{1,0:T(8,128)(2,1)} %get-tuple-element.115), channel_id=1, source_target_pairs={{0,6},{2,4},{4,2},{6,0},{8,14},{10,12},{12,10},{14,8},{1,7},{3,5},... | collective-permute-start | bytes 589832 | tf_op jit(solution)/shard_map/ppermute | solution.py:417
  64.4 23.8 %collective-permute-start.12 = (bf16[128,768]{1,0:T(8,128)(2,1)S(1)}, bf16[128,768]{1,0:T(8,128)(2,1)}, u32[]{:S(2)}, u32[]{:S(2)}) collective-permute-start(bf16[128,768]{1,0:T(8,128)(2,1)S(1)} %copy-done.25), channel_id=1, source_target_pairs={{0,4},{2,6},{4,0},{6,2},{8,12},{10,14},{12,8},{14,10},{1,5},{3,7},... | collective-permute-start | bytes 589832 | tf_op jit(solution)/shard_map/ppermute | solution.py:417
  69.5 19.5 %collective-permute-start.13 = (bf16[128,768]{1,0:T(8,128)(2,1)S(1)}, bf16[128,768]{1,0:T(8,128)(2,1)}, u32[]{:S(2)}, u32[]{:S(2)}) collective-permute-start(bf16[128,768]{1,0:T(8,128)(2,1)S(1)} %copy-done.24), channel_id=1, source_target_pairs={{0,2},{2,0},{4,6},{6,4},{8,10},{10,8},{12,14},{14,12},{1,3},{3,1},... | collective-permute-start | bytes 589832 | tf_op jit(solution)/shard_map/ppermute | solution.py:417
  76.7 26.5 %collective-permute-start.14 = (bf16[128,768]{1,0:T(8,128)(2,1)}, bf16[128,768]{1,0:T(8,128)(2,1)S(1)}, u32[]{:S(2)}, u32[]{:S(2)}) collective-permute-start(bf16[128,768]{1,0:T(8,128)(2,1)} %get-tuple-element.137), channel_id=1, source_target_pairs={{0,8},{2,10},{4,12},{6,14},{8,0},{10,2},{12,4},{14,6},{1,9},{3,11}... | collective-permute-start | bytes 589832 | tf_op jit(solution)/shard_map/ppermute | solution.py:417
  85.1 18.1 %collective-permute-start.15 = (bf16[128,768]{1,0:T(8,128)(2,1)}, bf16[128,768]{1,0:T(8,128)(2,1)S(1)}, u32[]{:S(2)}, u32[]{:S(2)}) collective-permute-start(bf16[128,768]{1,0:T(8,128)(2,1)} %get-tuple-element.138), channel_id=1, source_target_pairs={{0,4},{2,6},{4,0},{6,2},{8,12},{10,14},{12,8},{14,10},{1,5},{3,7},... | collective-permute-start | bytes 589832 | tf_op jit(solution)/shard_map/ppermute | solution.py:417
  85.1 18.1 %collective-permute-start.16 = (bf16[128,768]{1,0:T(8,128)(2,1)}, bf16[128,768]{1,0:T(8,128)(2,1)S(1)}, u32[]{:S(2)}, u32[]{:S(2)}) collective-permute-start(bf16[128,768]{1,0:T(8,128)(2,1)} %get-tuple-element.139), channel_id=1, source_target_pairs={{0,10},{2,8},{4,14},{6,12},{8,2},{10,0},{12,6},{14,4},{1,11},{3,9}... | collective-permute-start | bytes 589832 | tf_op jit(solution)/shard_map/ppermute | solution.py:417
  88.2 15.0 %collective-permute-start.17 = (bf16[128,768]{1,0:T(8,128)(2,1)}, bf16[128,768]{1,0:T(8,128)(2,1)S(1)}, u32[]{:S(2)}, u32[]{:S(2)}) collective-permute-start(bf16[128,768]{1,0:T(8,128)(2,1)} %get-tuple-element.140), channel_id=1, source_target_pairs={{0,6},{2,4},{4,2},{6,0},{8,14},{10,12},{12,10},{14,8},{1,7},{3,5},... | collective-permute-start | bytes 589832 | tf_op jit(solution)/shard_map/ppermute | solution.py:417
  89.0 14.4 %collective-permute-start.18 = (bf16[128,768]{1,0:T(8,128)(2,1)}, bf16[128,768]{1,0:T(8,128)(2,1)S(1)}, u32[]{:S(2)}, u32[]{:S(2)}) collective-permute-start(bf16[128,768]{1,0:T(8,128)(2,1)} %get-tuple-element.141), channel_id=1, source_target_pairs={{0,12},{2,14},{4,8},{6,10},{8,4},{10,6},{12,0},{14,2},{1,13},{3,15... | collective-permute-start | bytes 589832 | tf_op jit(solution)/shard_map/ppermute | solution.py:417
  149.2 20.5 %collective-permute-start.32 = (bf16[128,768]{1,0:T(8,128)(2,1)}, bf16[128,768]{1,0:T(8,128)(2,1)S(1)}, u32[]{:S(2)}, u32[]{:S(2)}) collective-permute-start(bf16[128,768]{1,0:T(8,128)(2,1)} %get-tuple-element.155), channel_id=1, source_target_pairs={{0,14},{2,12},{4,10},{6,8},{8,6},{10,4},{12,2},{14,0},{1,15},{3,13... | collective-permute-start | bytes 589832 | tf_op jit(solution)/shard_map/ppermute | solution.py:417
  151.7 18.0 %collective-permute-start.33 = (bf16[128,768]{1,0:T(8,128)(2,1)}, bf16[128,768]{1,0:T(8,128)(2,1)S(1)}, u32[]{:S(2)}, u32[]{:S(2)}) collective-permute-start(bf16[128,768]{1,0:T(8,128)(2,1)} %get-tuple-element.156), channel_id=1, source_target_pairs={{0,12},{2,14},{4,8},{6,10},{8,4},{10,6},{12,0},{14,2},{1,13},{3,15... | collective-permute-start | bytes 589832 | tf_op jit(solution)/shard_map/ppermute | solution.py:417
  153.6 16.2 %collective-permute-start.34 = (bf16[128,768]{1,0:T(8,128)(2,1)}, bf16[128,768]{1,0:T(8,128)(2,1)S(1)}, u32[]{:S(2)}, u32[]{:S(2)}) collective-permute-start(bf16[128,768]{1,0:T(8,128)(2,1)} %get-tuple-element.157), channel_id=1, source_target_pairs={{0,6},{2,4},{4,2},{6,0},{8,14},{10,12},{12,10},{14,8},{1,7},{3,5},... | collective-permute-start | bytes 589832 | tf_op jit(solution)/shard_map/ppermute | solution.py:417
  153.6 16.1 %collective-permute-start.30 = (bf16[32,768]{1,0:T(8,128)(2,1)S(1)}, bf16[32,768]{1,0:T(8,128)(2,1)S(1)}, u32[]{:S(2)}, u32[]{:S(2)}) collective-permute-start(bf16[32,768]{1,0:T(8,128)(2,1)S(1)} %fusion.3), channel_id=1, source_target_pairs={{0,8},{2,10},{4,12},{6,14},{8,0},{10,2},{12,4},{14,6},{1,9},{3,11}... | collective-permute-start | bytes 147464 | tf_op jit(solution)/shard_map/ppermute | solution.py:417
  156.5 13.2 %collective-permute-start.29 = (bf16[32,768]{1,0:T(8,128)(2,1)S(1)}, bf16[32,768]{1,0:T(8,128)(2,1)S(1)}, u32[]{:S(2)}, u32[]{:S(2)}) collective-permute-start(bf16[32,768]{1,0:T(8,128)(2,1)S(1)} %fusion.3), channel_id=1, source_target_pairs={{0,4},{2,6},{4,0},{6,2},{8,12},{10,14},{12,8},{14,10},{1,5},{3,7},... | collective-permute-start | bytes 147464 | tf_op jit(solution)/shard_map/ppermute | solution.py:417
  (46 other events, 515.3 us)

commit v17 on v16

--- a/solution.py
+++ b/solution.py
@@ -615,8 +615,8 @@
     group_sum.scatter(late[1:] + arrived[:1])
     group_sum.gather(arrived[1:3])
     group_sum.quarter, output = lax.optimization_barrier((group_sum.quarter, output))
-    group_sum.gather_next(arrived[3:6])
-    half, other = group_sum.gather_dp(arrived[6:])
+    group_sum.gather_next(arrived[3:5])
+    half, other = group_sum.gather_dp(arrived[5:])
     near = lax.axis_index("space")
     here = jnp.stack([lax.axis_index("dp"), near % 2, near // 2]).astype(jnp.int32)
     grads = finish_sums(here, half, other, factor, w_first.shape, b_first.shape)

time: 189 us -> 187 us (0.989)
  starting transfers between devices: 79.1 us -> 76.6 us
    ppermute x38, starting transfers between devices: 79.1 us -> 76.6 us  [swap_with(): return lax.ppermute(values, axis, pairs)]
    unnamed x65 -> x67, local copies, waits for them, and re-layouts: 4.45 us -> 4.41 us
  transfers between devices with their start and end apart: 38 -> 38, of which waited for: 17 -> 16; matrix products, arithmetic and copies ran while one was open for 6% -> 6% of each run, Pallas kernels for 17% -> 17%
where the time goes in v17:
time: 187 us
  starting transfers between devices  76.6 us (41%)
  waiting for transfers between devices  56.1 us (30%)
  Pallas kernels  36.1 us (19%)
  local copies, waits for them, and re-layouts  14.2 us (8%)
  other arithmetic  2.59 us (1%)
    ppermute x38, starting transfers between devices, swap_with(): return lax.ppermute(values, axis, pairs)  76.6 us
    ppermute x38, waiting for transfers between devices, swap_with(): return lax.ppermute(values, axis, pairs)  56.1 us
    pallas_call x1, Pallas kernels, backward_mid(): pl.pallas_call(functools.partial(backward_kernel, size_of_block, len(band...  12.8 us
    pallas_call x1, Pallas kernels, forward_mid(): pl.pallas_call(functools.partial(forward_kernel, len(bands)), grid_spec=p...  7.52 us
    pallas_call x2, Pallas kernels, to_cells(): pl.pallas_call(to_cells_kernel, grid_spec=pltpu.PrefetchScalarGridSpec(nu...  6.21 us
    pallas_call x2, local copies, waits for them, and re-layouts, to_cells(): pl.pallas_call(to_cells_kernel, grid_spec=pltpu.PrefetchScalarGridSpec(nu...  6.13 us
    pallas_call x2, Pallas kernels, to_modes(): pl.pallas_call(to_modes_kernel, grid_spec=pltpu.PrefetchScalarGridSpec(nu...  4.83 us
    unnamed x67, local copies, waits for them, and re-layouts  4.41 us
  transfers between devices with their start and end apart: 38, of which 16 were waited for; matrix products, arithmetic and copies ran while one was open for 6% of the time, Pallas kernels for 17%

profile of v17, /device:TPU:0, one launch (start us, length us, event | category | flops | bytes accessed | tf_op | source)
XLA Modules:
  0.0 186.6 jit_solution(10385891629822803274)
XLA Ops:
  5.0 6.1 %collective-permute-start = (bf16[128,768]{1,0:T(8,128)(2,1)}, bf16[128,768]{1,0:T(8,128)(2,1)S(1)}, u32[]{:S(2)}, u32[]{:S(2)}) collective-permute-start(bf16[128,768]{1,0:T(8,128)(2,1)} %get-tuple-element.99), channel_id=1, source_target_pairs={{0,14},{2,12},{4,10},{6,8},{8,6},{10,4},{12,2},{14,0},{1,15},{3,13... | collective-permute-start | bytes 589832 | tf_op jit(solution)/shard_map/ppermute | solution.py:417
  21.8 13.0 %collective-permute-start.5 = (bf16[128,768]{1,0:T(8,128)(2,1)}, bf16[128,768]{1,0:T(8,128)(2,1)}, u32[]{:S(2)}, u32[]{:S(2)}) collective-permute-start(bf16[128,768]{1,0:T(8,128)(2,1)} %get-tuple-element.108), channel_id=1, source_target_pairs={{0,4},{2,6},{4,0},{6,2},{8,12},{10,14},{12,8},{14,10},{1,5},{3,7},... | collective-permute-start | bytes 589832 | tf_op jit(solution)/shard_map/ppermute | solution.py:417
  37.2 4.6 %collective-permute-done.2.refs_3_ = bf16[128,768]{1,0:T(8,128)(2,1)S(1)} collective-permute-done((bf16[128,768]{1,0:T(8,128)(2,1)}, bf16[128,768]{1,0:T(8,128)(2,1)S(1)}, u32[]{:S(2)}, u32[]{:S(2)}) %collective-permute-start.2) | collective-permute-done | bytes 196640 | tf_op jit(solution)/shard_map/ppermute | solution.py:417
  41.8 3.4 %collective-permute-start.7 = (bf16[128,768]{1,0:T(8,128)(2,1)}, bf16[128,768]{1,0:T(8,128)(2,1)S(1)}, u32[]{:S(2)}, u32[]{:S(2)}) collective-permute-start(bf16[128,768]{1,0:T(8,128)(2,1)} %get-tuple-element.111), channel_id=1, source_target_pairs={{0,14},{2,12},{4,10},{6,8},{8,6},{10,4},{12,2},{14,0},{1,15},{3,13... | collective-permute-start | bytes 589832 | tf_op jit(solution)/shard_map/ppermute | solution.py:417
  45.2 2.9 %collective-permute-done.3.refs_4_ = bf16[128,768]{1,0:T(8,128)(2,1)S(1)} collective-permute-done((bf16[128,768]{1,0:T(8,128)(2,1)}, bf16[128,768]{1,0:T(8,128)(2,1)S(1)}, u32[]{:S(2)}, u32[]{:S(2)}) %collective-permute-start.3) | collective-permute-done | bytes 196640 | tf_op jit(solution)/shard_map/ppermute | solution.py:417
  56.8 7.5 %mix_forward.1 = (bf16[128,768]{1,0:T(8,128)(2,1)}, bf16[128,768]{1,0:T(8,128)(2,1)}, bf16[128,768]{1,0:T(8,128)(2,1)}, bf16[128,768]{1,0:T(8,128)(2,1)}, bf16[1...) custom-call(s32[1]{0:T(128)} %bitcast.me_ref, ...), custom_call_target="tpu_custom_call" | custom-call | flops 2415919104 | bytes 17301504 | tf_op jit(solution)/shard_map/mix_forward/pallas_call | solution.py:344
  64.4 5.1 %collective-permute-start.12 = (bf16[128,768]{1,0:T(8,128)(2,1)S(1)}, bf16[128,768]{1,0:T(8,128)(2,1)}, u32[]{:S(2)}, u32[]{:S(2)}) collective-permute-start(bf16[128,768]{1,0:T(8,128)(2,1)S(1)} %copy-done.26), channel_id=1, source_target_pairs={{0,4},{2,6},{4,0},{6,2},{8,12},{10,14},{12,8},{14,10},{1,5},{3,7},... | collective-permute-start | bytes 589832 | tf_op jit(solution)/shard_map/ppermute | solution.py:417
  71.1 5.6 %collective-permute-done.9.refs_3_ = bf16[128,768]{1,0:T(8,128)(2,1)} collective-permute-done((bf16[128,768]{1,0:T(8,128)(2,1)}, bf16[128,768]{1,0:T(8,128)(2,1)}, u32[]{:S(2)}, u32[]{:S(2)}) %collective-permute-start.9) | collective-permute-done | bytes 196640 | tf_op jit(solution)/shard_map/ppermute | solution.py:417
  76.6 8.4 %collective-permute-done.10.refs_4_ = bf16[128,768]{1,0:T(8,128)(2,1)} collective-permute-done((bf16[128,768]{1,0:T(8,128)(2,1)}, bf16[128,768]{1,0:T(8,128)(2,1)}, u32[]{:S(2)}, u32[]{:S(2)}) %collective-permute-start.10) | collective-permute-done | bytes 196640 | tf_op jit(solution)/shard_map/ppermute | solution.py:417
  85.0 3.1 %collective-permute-start.16 = (bf16[128,768]{1,0:T(8,128)(2,1)}, bf16[128,768]{1,0:T(8,128)(2,1)S(1)}, u32[]{:S(2)}, u32[]{:S(2)}) collective-permute-start(bf16[128,768]{1,0:T(8,128)(2,1)} %get-tuple-element.139), channel_id=1, source_target_pairs={{0,10},{2,8},{4,14},{6,12},{8,2},{10,0},{12,6},{14,4},{1,11},{3,9}... | collective-permute-start | bytes 589832 | tf_op jit(solution)/shard_map/ppermute | solution.py:417
  90.3 12.8 %mix_backward.1 = (bf16[128,768]{1,0:T(8,128)(2,1)}, bf16[128,768]{1,0:T(8,128)(2,1)}, bf16[128,768]{1,0:T(8,128)(2,1)}, bf16[128,768]{1,0:T(8,128)(2,1)}, bf16[...) custom-call(s32[1]{0:T(128)} %bitcast.me_ref, ...), custom_call_target="tpu_custom_call" | custom-call | flops 4831838208 | bytes 17301504 | tf_op jit(solution)/shard_map/mix_backward/pallas_call | solution.py:382
  105.1 4.7 %collective-permute-start.20 = (bf16[128,768]{1,0:T(8,128)(2,1)S(1)}, bf16[128,768]{1,0:T(8,128)(2,1)}, u32[]{:S(2)}, u32[]{:S(2)}) collective-permute-start(bf16[128,768]{1,0:T(8,128)(2,1)S(1)} %copy-done.24), channel_id=1, source_target_pairs={{0,14},{2,12},{4,10},{6,8},{8,6},{10,4},{12,2},{14,0},{1,15},{3,13... | collective-permute-start | bytes 589832 | tf_op jit(solution)/shard_map/ppermute | solution.py:417
  111.3 4.2 %collective-permute-done.20.refs_1_ = bf16[128,768]{1,0:T(8,128)(2,1)} collective-permute-done((bf16[128,768]{1,0:T(8,128)(2,1)S(1)}, bf16[128,768]{1,0:T(8,128)(2,1)}, u32[]{:S(2)}, u32[]{:S(2)}) %collective-permute-start.20) | collective-permute-done | bytes 196640 | tf_op jit(solution)/shard_map/ppermute | solution.py:417
  115.5 2.8 %collective-permute-start.21 = (bf16[128,768]{1,0:T(8,128)(2,1)S(1)}, bf16[128,768]{1,0:T(8,128)(2,1)}, u32[]{:S(2)}, u32[]{:S(2)}) collective-permute-start(bf16[128,768]{1,0:T(8,128)(2,1)S(1)} %fusion), channel_id=1, source_target_pairs={{0,2},{2,0},{4,6},{6,4},{8,10},{10,8},{12,14},{14,12},{1,3},{3,1},... | collective-permute-start | bytes 589832 | tf_op jit(solution)/shard_map/ppermute | solution.py:417
  118.5 4.1 %collective-permute-start.23 = (bf16[128,768]{1,0:T(8,128)(2,1)}, bf16[128,768]{1,0:T(8,128)(2,1)}, u32[]{:S(2)}, u32[]{:S(2)}) collective-permute-start(bf16[128,768]{1,0:T(8,128)(2,1)} %get-tuple-element.146), channel_id=1, source_target_pairs={{0,8},{2,10},{4,12},{6,14},{8,0},{10,2},{12,4},{14,6},{1,9},{3,11}... | collective-permute-start | bytes 589832 | tf_op jit(solution)/shard_map/ppermute | solution.py:417
  127.3 3.9 %collective-permute-done.23.refs_4_ = bf16[128,768]{1,0:T(8,128)(2,1)} collective-permute-done((bf16[128,768]{1,0:T(8,128)(2,1)}, bf16[128,768]{1,0:T(8,128)(2,1)}, u32[]{:S(2)}, u32[]{:S(2)}) %collective-permute-start.23) | collective-permute-done | bytes 196640 | tf_op jit(solution)/shard_map/ppermute | solution.py:417
  132.9 2.8 %collective-permute-start.24 = (bf16[32,768]{1,0:T(8,128)(2,1)S(1)}, bf16[32,768]{1,0:T(8,128)(2,1)S(1)}, u32[]{:S(2)}, u32[]{:S(2)}) collective-permute-start(bf16[32,768]{1,0:T(8,128)(2,1)S(1)} %get-tuple-element.166), channel_id=1, source_target_pairs={{0,4},{2,6},{4,0},{6,2},{8,12},{10,14},{12,8},{14,10},{1,5},{3,7},... | collective-permute-start | bytes 147464 | tf_op jit(solution)/shard_map/ppermute | solution.py:417
  141.1 7.3 %collective-permute-done.27.refs_6_ = bf16[128,768]{1,0:T(8,128)(2,1)S(1)} collective-permute-done((bf16[128,768]{1,0:T(8,128)(2,1)}, bf16[128,768]{1,0:T(8,128)(2,1)S(1)}, u32[]{:S(2)}, u32[]{:S(2)}) %collective-permute-start.27) | collective-permute-done | bytes 196640 | tf_op jit(solution)/shard_map/ppermute | solution.py:417
  148.3 5.7 %collective-permute-done.28.refs_3_ = bf16[128,768]{1,0:T(8,128)(2,1)S(1)} collective-permute-done((bf16[128,768]{1,0:T(8,128)(2,1)}, bf16[128,768]{1,0:T(8,128)(2,1)S(1)}, u32[]{:S(2)}, u32[]{:S(2)}) %collective-permute-start.28) | collective-permute-done | bytes 196640 | tf_op jit(solution)/shard_map/ppermute | solution.py:417
  160.3 3.2 %to_cells.2 = bf16[4,2,180,768]{3,2,1,0:T(8,128)(2,1)S(1)} custom-call(s32[1]{0:T(128)} %bitcast.me_ref, bf16[180,128]{1,0:T(8,128)(2,1)S(1)} %copy-done.3, bf16[4,2,180,768]{3,2,1,0:T(8,128)(2,1)S(1)} %copy.23.base_ref, bf16[128,768]{1,0:T(8,128)(2,1)} %get-tuple-element.152.refs_0_, bf16[128,768]{1,0:T(8,128)(2,1)} %collective-permute-done.20.refs_1_, ...), custom_call_target="tpu_custom_call" | custom-call | flops 283115520 | bytes 5996544 | tf_op jit(solution)/shard_map/to_cells/pallas_call | solution.py:186
  163.6 3.1 %copy.30 = bf16[4,2,180,768]{3,1,2,0:T(2,128)(2,1)} copy(bf16[4,2,180,768]{3,2,1,0:T(8,128)(2,1)S(1)} %to_cells.2) | data formatting | bytes 4423680 | tf_op jit(solution)/shard_map/to_cells/pallas_call | solution.py:186
  172.5 3.3 %collective-permute-done.32.refs_1_ = bf16[128,768]{1,0:T(8,128)(2,1)S(1)} collective-permute-done((bf16[128,768]{1,0:T(8,128)(2,1)S(1)}, bf16[128,768]{1,0:T(8,128)(2,1)S(1)}, u32[]{:S(2)}, u32[]{:S(2)}) %collective-permute-start.32) | collective-permute-done | bytes 196640 | tf_op jit(solution)/shard_map/ppermute | solution.py:417
  178.4 3.0 %to_cells.3 = bf16[4,2,180,768]{3,2,1,0:T(8,128)(2,1)S(1)} custom-call(s32[1]{0:T(128)} %bitcast.me_ref, bf16[180,128]{1,0:T(8,128)(2,1)S(1)} %copy-done.2, bf16[4,2,180,768]{3,2,1,0:T(8,128)(2,1)S(1)} %copy.22.cells_ref.base_ref, bf16[128,768]{1,0:T(8,128)(2,1)} %get-tuple-element.154.refs_0_, bf16[128,768]{1,0:T(8,128)(2,1)} %copy-done.18, ...), custom_call_target="tpu_custom_call" | custom-call | flops 283115520 | bytes 5996544 | tf_op jit(solution)/shard_map/to_cells/pallas_call | solution.py:186
  181.4 3.1 %copy.26 = bf16[4,2,180,768]{3,1,2,0:T(2,128)(2,1)} copy(bf16[4,2,180,768]{3,2,1,0:T(8,128)(2,1)S(1)} %to_cells.3) | data formatting | bytes 4423680 | tf_op jit(solution)/shard_map/to_cells/pallas_call | solution.py:186
  (146 shorter events, 62.1 us)
Async XLA Ops:
  5.0 16.8 %collective-permute-start = (bf16[128,768]{1,0:T(8,128)(2,1)}, bf16[128,768]{1,0:T(8,128)(2,1)S(1)}, u32[]{:S(2)}, u32[]{:S(2)}) collective-permute-start(bf16[128,768]{1,0:T(8,128)(2,1)} %get-tuple-element.99), channel_id=1, source_target_pairs={{0,14},{2,12},{4,10},{6,8},{8,6},{10,4},{12,2},{14,0},{1,15},{3,13... | collective-permute-start | bytes 589832 | tf_op jit(solution)/shard_map/ppermute | solution.py:417
  11.1 23.7 %collective-permute-start.1 = (bf16[128,768]{1,0:T(8,128)(2,1)}, bf16[128,768]{1,0:T(8,128)(2,1)S(1)}, u32[]{:S(2)}, u32[]{:S(2)}) collective-permute-start(bf16[128,768]{1,0:T(8,128)(2,1)} %get-tuple-element.100), channel_id=1, source_target_pairs={{0,12},{2,14},{4,8},{6,10},{8,4},{10,6},{12,0},{14,2},{1,13},{3,15... | collective-permute-start | bytes 589832 | tf_op jit(solution)/shard_map/ppermute | solution.py:417
  11.3 30.5 %collective-permute-start.2 = (bf16[128,768]{1,0:T(8,128)(2,1)}, bf16[128,768]{1,0:T(8,128)(2,1)S(1)}, u32[]{:S(2)}, u32[]{:S(2)}) collective-permute-start(bf16[128,768]{1,0:T(8,128)(2,1)} %get-tuple-element.101), channel_id=1, source_target_pairs={{0,10},{2,8},{4,14},{6,12},{8,2},{10,0},{12,6},{14,4},{1,11},{3,9}... | collective-permute-start | bytes 589832 | tf_op jit(solution)/shard_map/ppermute | solution.py:417
  12.0 36.1 %collective-permute-start.3 = (bf16[128,768]{1,0:T(8,128)(2,1)}, bf16[128,768]{1,0:T(8,128)(2,1)S(1)}, u32[]{:S(2)}, u32[]{:S(2)}) collective-permute-start(bf16[128,768]{1,0:T(8,128)(2,1)} %get-tuple-element.102), channel_id=1, source_target_pairs={{0,8},{2,10},{4,12},{6,14},{8,0},{10,2},{12,4},{14,6},{1,9},{3,11}... | collective-permute-start | bytes 589832 | tf_op jit(solution)/shard_map/ppermute | solution.py:417
  14.1 37.2 %collective-permute-start.4 = (bf16[128,768]{1,0:T(8,128)(2,1)}, bf16[128,768]{1,0:T(8,128)(2,1)}, u32[]{:S(2)}, u32[]{:S(2)}) collective-permute-start(bf16[128,768]{1,0:T(8,128)(2,1)} %get-tuple-element.103), channel_id=1, source_target_pairs={{0,6},{2,4},{4,2},{6,0},{8,14},{10,12},{12,10},{14,8},{1,7},{3,5},... | collective-permute-start | bytes 589832 | tf_op jit(solution)/shard_map/ppermute | solution.py:417
  21.8 31.4 %collective-permute-start.5 = (bf16[128,768]{1,0:T(8,128)(2,1)}, bf16[128,768]{1,0:T(8,128)(2,1)}, u32[]{:S(2)}, u32[]{:S(2)}) collective-permute-start(bf16[128,768]{1,0:T(8,128)(2,1)} %get-tuple-element.108), channel_id=1, source_target_pairs={{0,4},{2,6},{4,0},{6,2},{8,12},{10,14},{12,8},{14,10},{1,5},{3,7},... | collective-permute-start | bytes 589832 | tf_op jit(solution)/shard_map/ppermute | solution.py:417
  35.5 18.7 %collective-permute-start.6 = (bf16[128,768]{1,0:T(8,128)(2,1)}, bf16[128,768]{1,0:T(8,128)(2,1)}, u32[]{:S(2)}, u32[]{:S(2)}) collective-permute-start(bf16[128,768]{1,0:T(8,128)(2,1)} %get-tuple-element.109), channel_id=1, source_target_pairs={{0,2},{2,0},{4,6},{6,4},{8,10},{10,8},{12,14},{14,12},{1,3},{3,1},... | collective-permute-start | bytes 589832 | tf_op jit(solution)/shard_map/ppermute | solution.py:417
  41.8 22.5 %collective-permute-start.7 = (bf16[128,768]{1,0:T(8,128)(2,1)}, bf16[128,768]{1,0:T(8,128)(2,1)S(1)}, u32[]{:S(2)}, u32[]{:S(2)}) collective-permute-start(bf16[128,768]{1,0:T(8,128)(2,1)} %get-tuple-element.111), channel_id=1, source_target_pairs={{0,14},{2,12},{4,10},{6,8},{8,6},{10,4},{12,2},{14,0},{1,15},{3,13... | collective-permute-start | bytes 589832 | tf_op jit(solution)/shard_map/ppermute | solution.py:417
  48.8 20.7 %collective-permute-start.8 = (bf16[128,768]{1,0:T(8,128)(2,1)}, bf16[128,768]{1,0:T(8,128)(2,1)S(1)}, u32[]{:S(2)}, u32[]{:S(2)}) collective-permute-start(bf16[128,768]{1,0:T(8,128)(2,1)} %get-tuple-element.112), channel_id=1, source_target_pairs={{0,12},{2,14},{4,8},{6,10},{8,4},{10,6},{12,0},{14,2},{1,13},{3,15... | collective-permute-start | bytes 589832 | tf_op jit(solution)/shard_map/ppermute | solution.py:417
  51.3 25.4 %collective-permute-start.9 = (bf16[128,768]{1,0:T(8,128)(2,1)}, bf16[128,768]{1,0:T(8,128)(2,1)}, u32[]{:S(2)}, u32[]{:S(2)}) collective-permute-start(bf16[128,768]{1,0:T(8,128)(2,1)} %get-tuple-element.113), channel_id=1, source_target_pairs={{0,10},{2,8},{4,14},{6,12},{8,2},{10,0},{12,6},{14,4},{1,11},{3,9}... | collective-permute-start | bytes 589832 | tf_op jit(solution)/shard_map/ppermute | solution.py:417
  53.2 31.9 %collective-permute-start.10 = (bf16[128,768]{1,0:T(8,128)(2,1)}, bf16[128,768]{1,0:T(8,128)(2,1)}, u32[]{:S(2)}, u32[]{:S(2)}) collective-permute-start(bf16[128,768]{1,0:T(8,128)(2,1)} %get-tuple-element.114), channel_id=1, source_target_pairs={{0,8},{2,10},{4,12},{6,14},{8,0},{10,2},{12,4},{14,6},{1,9},{3,11}... | collective-permute-start | bytes 589832 | tf_op jit(solution)/shard_map/ppermute | solution.py:417
  54.2 30.9 %collective-permute-start.11 = (bf16[128,768]{1,0:T(8,128)(2,1)}, bf16[128,768]{1,0:T(8,128)(2,1)}, u32[]{:S(2)}, u32[]{:S(2)}) collective-permute-start(bf16[128,768]{1,0:T(8,128)(2,1)} %get-tuple-element.115), channel_id=1, source_target_pairs={{0,6},{2,4},{4,2},{6,0},{8,14},{10,12},{12,10},{14,8},{1,7},{3,5},... | collective-permute-start | bytes 589832 | tf_op jit(solution)/shard_map/ppermute | solution.py:417
  64.4 23.8 %collective-permute-start.12 = (bf16[128,768]{1,0:T(8,128)(2,1)S(1)}, bf16[128,768]{1,0:T(8,128)(2,1)}, u32[]{:S(2)}, u32[]{:S(2)}) collective-permute-start(bf16[128,768]{1,0:T(8,128)(2,1)S(1)} %copy-done.26), channel_id=1, source_target_pairs={{0,4},{2,6},{4,0},{6,2},{8,12},{10,14},{12,8},{14,10},{1,5},{3,7},... | collective-permute-start | bytes 589832 | tf_op jit(solution)/shard_map/ppermute | solution.py:417
  69.5 19.5 %collective-permute-start.13 = (bf16[128,768]{1,0:T(8,128)(2,1)S(1)}, bf16[128,768]{1,0:T(8,128)(2,1)}, u32[]{:S(2)}, u32[]{:S(2)}) collective-permute-start(bf16[128,768]{1,0:T(8,128)(2,1)S(1)} %copy-done.25), channel_id=1, source_target_pairs={{0,2},{2,0},{4,6},{6,4},{8,10},{10,8},{12,14},{14,12},{1,3},{3,1},... | collective-permute-start | bytes 589832 | tf_op jit(solution)/shard_map/ppermute | solution.py:417
  76.6 26.5 %collective-permute-start.14 = (bf16[128,768]{1,0:T(8,128)(2,1)}, bf16[128,768]{1,0:T(8,128)(2,1)S(1)}, u32[]{:S(2)}, u32[]{:S(2)}) collective-permute-start(bf16[128,768]{1,0:T(8,128)(2,1)} %get-tuple-element.137), channel_id=1, source_target_pairs={{0,8},{2,10},{4,12},{6,14},{8,0},{10,2},{12,4},{14,6},{1,9},{3,11}... | collective-permute-start | bytes 589832 | tf_op jit(solution)/shard_map/ppermute | solution.py:417
  85.0 18.1 %collective-permute-start.15 = (bf16[128,768]{1,0:T(8,128)(2,1)}, bf16[128,768]{1,0:T(8,128)(2,1)S(1)}, u32[]{:S(2)}, u32[]{:S(2)}) collective-permute-start(bf16[128,768]{1,0:T(8,128)(2,1)} %get-tuple-element.138), channel_id=1, source_target_pairs={{0,4},{2,6},{4,0},{6,2},{8,12},{10,14},{12,8},{14,10},{1,5},{3,7},... | collective-permute-start | bytes 589832 | tf_op jit(solution)/shard_map/ppermute | solution.py:417
  85.0 18.1 %collective-permute-start.16 = (bf16[128,768]{1,0:T(8,128)(2,1)}, bf16[128,768]{1,0:T(8,128)(2,1)S(1)}, u32[]{:S(2)}, u32[]{:S(2)}) collective-permute-start(bf16[128,768]{1,0:T(8,128)(2,1)} %get-tuple-element.139), channel_id=1, source_target_pairs={{0,10},{2,8},{4,14},{6,12},{8,2},{10,0},{12,6},{14,4},{1,11},{3,9}... | collective-permute-start | bytes 589832 | tf_op jit(solution)/shard_map/ppermute | solution.py:417
  88.2 15.0 %collective-permute-start.17 = (bf16[128,768]{1,0:T(8,128)(2,1)}, bf16[128,768]{1,0:T(8,128)(2,1)S(1)}, u32[]{:S(2)}, u32[]{:S(2)}) collective-permute-start(bf16[128,768]{1,0:T(8,128)(2,1)} %get-tuple-element.140), channel_id=1, source_target_pairs={{0,6},{2,4},{4,2},{6,0},{8,14},{10,12},{12,10},{14,8},{1,7},{3,5},... | collective-permute-start | bytes 589832 | tf_op jit(solution)/shard_map/ppermute | solution.py:417
  89.0 14.4 %collective-permute-start.18 = (bf16[128,768]{1,0:T(8,128)(2,1)}, bf16[128,768]{1,0:T(8,128)(2,1)S(1)}, u32[]{:S(2)}, u32[]{:S(2)}) collective-permute-start(bf16[128,768]{1,0:T(8,128)(2,1)} %get-tuple-element.141), channel_id=1, source_target_pairs={{0,12},{2,14},{4,8},{6,10},{8,4},{10,6},{12,0},{14,2},{1,13},{3,15... | collective-permute-start | bytes 589832 | tf_op jit(solution)/shard_map/ppermute | solution.py:417
  118.5 12.7 %collective-permute-start.23 = (bf16[128,768]{1,0:T(8,128)(2,1)}, bf16[128,768]{1,0:T(8,128)(2,1)}, u32[]{:S(2)}, u32[]{:S(2)}) collective-permute-start(bf16[128,768]{1,0:T(8,128)(2,1)} %get-tuple-element.146), channel_id=1, source_target_pairs={{0,8},{2,10},{4,12},{6,14},{8,0},{10,2},{12,4},{14,6},{1,9},{3,11}... | collective-permute-start | bytes 589832 | tf_op jit(solution)/shard_map/ppermute | solution.py:417
  135.7 12.7 %collective-permute-start.27 = (bf16[128,768]{1,0:T(8,128)(2,1)}, bf16[128,768]{1,0:T(8,128)(2,1)S(1)}, u32[]{:S(2)}, u32[]{:S(2)}) collective-permute-start(bf16[128,768]{1,0:T(8,128)(2,1)} %get-tuple-element.148), channel_id=1, source_target_pairs={{0,4},{2,6},{4,0},{6,2},{8,12},{10,14},{12,8},{14,10},{1,5},{3,7},... | collective-permute-start | bytes 589832 | tf_op jit(solution)/shard_map/ppermute | solution.py:417
  135.7 18.3 %collective-permute-start.28 = (bf16[128,768]{1,0:T(8,128)(2,1)}, bf16[128,768]{1,0:T(8,128)(2,1)S(1)}, u32[]{:S(2)}, u32[]{:S(2)}) collective-permute-start(bf16[128,768]{1,0:T(8,128)(2,1)} %get-tuple-element.149), channel_id=1, source_target_pairs={{0,10},{2,8},{4,14},{6,12},{8,2},{10,0},{12,6},{14,4},{1,11},{3,9}... | collective-permute-start | bytes 589832 | tf_op jit(solution)/shard_map/ppermute | solution.py:417
  138.4 28.3 %collective-permute-start.33 = (bf16[128,768]{1,0:T(8,128)(2,1)}, bf16[128,768]{1,0:T(8,128)(2,1)S(1)}, u32[]{:S(2)}, u32[]{:S(2)}) collective-permute-start(bf16[128,768]{1,0:T(8,128)(2,1)} %get-tuple-element.156), channel_id=1, source_target_pairs={{0,12},{2,14},{4,8},{6,10},{8,4},{10,6},{12,0},{14,2},{1,13},{3,15... | collective-permute-start | bytes 589832 | tf_op jit(solution)/shard_map/ppermute | solution.py:417
  140.0 26.7 %collective-permute-start.34 = (bf16[128,768]{1,0:T(8,128)(2,1)}, bf16[128,768]{1,0:T(8,128)(2,1)S(1)}, u32[]{:S(2)}, u32[]{:S(2)}) collective-permute-start(bf16[128,768]{1,0:T(8,128)(2,1)} %get-tuple-element.157), channel_id=1, source_target_pairs={{0,6},{2,4},{4,2},{6,0},{8,14},{10,12},{12,10},{14,8},{1,7},{3,5},... | collective-permute-start | bytes 589832 | tf_op jit(solution)/shard_map/ppermute | solution.py:417
  (47 other events, 501.6 us)

commit v18 on v17

--- a/solution.py
+++ b/solution.py
@@ -614,8 +614,8 @@
     output = rows_inside(to_cells(me, scaled.T, image_band, again))
     group_sum.scatter(late[1:] + arrived[:1])
     group_sum.gather(arrived[1:3])
-    group_sum.quarter, output = lax.optimization_barrier((group_sum.quarter, output))
     group_sum.gather_next(arrived[3:5])
+    group_sum.half, output = lax.optimization_barrier((group_sum.half, output))
     half, other = group_sum.gather_dp(arrived[5:])
     near = lax.axis_index("space")
     here = jnp.stack([lax.axis_index("dp"), near % 2, near // 2]).astype(jnp.int32)

time: 187 us -> 183 us (0.979)
  waiting for transfers between devices: 56.1 us -> 50.7 us
    ppermute x38, waiting for transfers between devices: 56.1 us -> 50.7 us  [swap_with(): return lax.ppermute(values, axis, pairs)]
    unnamed x67 -> x63, local copies, waits for them, and re-layouts: 4.41 us -> 4.41 us
where the time goes in v18:
time: 183 us; the launch traced here: 182 us
  starting transfers between devices  77.3 us (42%)
  waiting for transfers between devices  50.7 us (28%)
  Pallas kernels  36.1 us (20%)
  local copies, waits for them, and re-layouts  14.1 us (8%)
  other arithmetic  2.58 us (1%)
    ppermute x38, starting transfers between devices, swap_with(): return lax.ppermute(values, axis, pairs)  77.3 us
    ppermute x38, waiting for transfers between devices, swap_with(): return lax.ppermute(values, axis, pairs)  50.7 us
    pallas_call x1, Pallas kernels, backward_mid(): pl.pallas_call(functools.partial(backward_kernel, size_of_block, len(band...  12.7 us
    pallas_call x1, Pallas kernels, forward_mid(): pl.pallas_call(functools.partial(forward_kernel, len(bands)), grid_spec=p...  7.51 us
    pallas_call x2, Pallas kernels, to_cells(): pl.pallas_call(to_cells_kernel, grid_spec=pltpu.PrefetchScalarGridSpec(nu...  6.21 us
    pallas_call x2, local copies, waits for them, and re-layouts, to_cells(): pl.pallas_call(to_cells_kernel, grid_spec=pltpu.PrefetchScalarGridSpec(nu...  6.13 us
    pallas_call x2, Pallas kernels, to_modes(): pl.pallas_call(to_modes_kernel, grid_spec=pltpu.PrefetchScalarGridSpec(nu...  4.83 us
    unnamed x63, local copies, waits for them, and re-layouts  4.41 us
  transfers between devices with their start and end apart: 38, of which 16 were waited for; matrix products, arithmetic and copies ran while one was open for 6% of the time, Pallas kernels for 17%

profile of v18, /device:TPU:0, one launch (start us, length us, event | category | flops | bytes accessed | tf_op | source)
XLA Modules:
  0.0 182.0 jit_solution(15678859485998606639)
XLA Ops:
  5.0 6.1 %collective-permute-start = (bf16[128,768]{1,0:T(8,128)(2,1)}, bf16[128,768]{1,0:T(8,128)(2,1)S(1)}, u32[]{:S(2)}, u32[]{:S(2)}) collective-permute-start(bf16[128,768]{1,0:T(8,128)(2,1)} %get-tuple-element.99), channel_id=1, source_target_pairs={{0,14},{2,12},{4,10},{6,8},{8,6},{10,4},{12,2},{14,0},{1,15},{3,13... | collective-permute-start | bytes 589832 | tf_op jit(solution)/shard_map/ppermute | solution.py:417
  21.8 13.0 %collective-permute-start.5 = (bf16[128,768]{1,0:T(8,128)(2,1)}, bf16[128,768]{1,0:T(8,128)(2,1)}, u32[]{:S(2)}, u32[]{:S(2)}) collective-permute-start(bf16[128,768]{1,0:T(8,128)(2,1)} %get-tuple-element.108), channel_id=1, source_target_pairs={{0,4},{2,6},{4,0},{6,2},{8,12},{10,14},{12,8},{14,10},{1,5},{3,7},... | collective-permute-start | bytes 589832 | tf_op jit(solution)/shard_map/ppermute | solution.py:417
  37.2 4.6 %collective-permute-done.2.refs_3_ = bf16[128,768]{1,0:T(8,128)(2,1)S(1)} collective-permute-done((bf16[128,768]{1,0:T(8,128)(2,1)}, bf16[128,768]{1,0:T(8,128)(2,1)S(1)}, u32[]{:S(2)}, u32[]{:S(2)}) %collective-permute-start.2) | collective-permute-done | bytes 196640 | tf_op jit(solution)/shard_map/ppermute | solution.py:417
  41.8 3.4 %collective-permute-start.7 = (bf16[128,768]{1,0:T(8,128)(2,1)}, bf16[128,768]{1,0:T(8,128)(2,1)S(1)}, u32[]{:S(2)}, u32[]{:S(2)}) collective-permute-start(bf16[128,768]{1,0:T(8,128)(2,1)} %get-tuple-element.111), channel_id=1, source_target_pairs={{0,14},{2,12},{4,10},{6,8},{8,6},{10,4},{12,2},{14,0},{1,15},{3,13... | collective-permute-start | bytes 589832 | tf_op jit(solution)/shard_map/ppermute | solution.py:417
  45.2 2.9 %collective-permute-done.3.refs_4_ = bf16[128,768]{1,0:T(8,128)(2,1)S(1)} collective-permute-done((bf16[128,768]{1,0:T(8,128)(2,1)}, bf16[128,768]{1,0:T(8,128)(2,1)S(1)}, u32[]{:S(2)}, u32[]{:S(2)}) %collective-permute-start.3) | collective-permute-done | bytes 196640 | tf_op jit(solution)/shard_map/ppermute | solution.py:417
  56.8 7.5 %mix_forward.1 = (bf16[128,768]{1,0:T(8,128)(2,1)}, bf16[128,768]{1,0:T(8,128)(2,1)}, bf16[128,768]{1,0:T(8,128)(2,1)}, bf16[128,768]{1,0:T(8,128)(2,1)}, bf16[1...) custom-call(s32[1]{0:T(128)} %bitcast.me_ref, ...), custom_call_target="tpu_custom_call" | custom-call | flops 2415919104 | bytes 17301504 | tf_op jit(solution)/shard_map/mix_forward/pallas_call | solution.py:344
  64.4 5.1 %collective-permute-start.12 = (bf16[128,768]{1,0:T(8,128)(2,1)S(1)}, bf16[128,768]{1,0:T(8,128)(2,1)}, u32[]{:S(2)}, u32[]{:S(2)}) collective-permute-start(bf16[128,768]{1,0:T(8,128)(2,1)S(1)} %copy-done.24), channel_id=1, source_target_pairs={{0,4},{2,6},{4,0},{6,2},{8,12},{10,14},{12,8},{14,10},{1,5},{3,7},... | collective-permute-start | bytes 589832 | tf_op jit(solution)/shard_map/ppermute | solution.py:417
  71.1 5.6 %collective-permute-done.9.refs_3_ = bf16[128,768]{1,0:T(8,128)(2,1)} collective-permute-done((bf16[128,768]{1,0:T(8,128)(2,1)}, bf16[128,768]{1,0:T(8,128)(2,1)}, u32[]{:S(2)}, u32[]{:S(2)}) %collective-permute-start.9) | collective-permute-done | bytes 196640 | tf_op jit(solution)/shard_map/ppermute | solution.py:417
  76.6 8.4 %collective-permute-done.10.refs_4_ = bf16[128,768]{1,0:T(8,128)(2,1)} collective-permute-done((bf16[128,768]{1,0:T(8,128)(2,1)}, bf16[128,768]{1,0:T(8,128)(2,1)}, u32[]{:S(2)}, u32[]{:S(2)}) %collective-permute-start.10) | collective-permute-done | bytes 196640 | tf_op jit(solution)/shard_map/ppermute | solution.py:417
  85.0 3.1 %collective-permute-start.16 = (bf16[128,768]{1,0:T(8,128)(2,1)}, bf16[128,768]{1,0:T(8,128)(2,1)S(1)}, u32[]{:S(2)}, u32[]{:S(2)}) collective-permute-start(bf16[128,768]{1,0:T(8,128)(2,1)} %get-tuple-element.139), channel_id=1, source_target_pairs={{0,10},{2,8},{4,14},{6,12},{8,2},{10,0},{12,6},{14,4},{1,11},{3,9}... | collective-permute-start | bytes 589832 | tf_op jit(solution)/shard_map/ppermute | solution.py:417
  90.3 12.7 %mix_backward.1 = (bf16[128,768]{1,0:T(8,128)(2,1)}, bf16[128,768]{1,0:T(8,128)(2,1)}, bf16[128,768]{1,0:T(8,128)(2,1)}, bf16[128,768]{1,0:T(8,128)(2,1)}, bf16[...) custom-call(s32[1]{0:T(128)} %bitcast.me_ref, ...), custom_call_target="tpu_custom_call" | custom-call | flops 4831838208 | bytes 17301504 | tf_op jit(solution)/shard_map/mix_backward/pallas_call | solution.py:382
  105.1 4.7 %collective-permute-start.20 = (bf16[128,768]{1,0:T(8,128)(2,1)S(1)}, bf16[128,768]{1,0:T(8,128)(2,1)}, u32[]{:S(2)}, u32[]{:S(2)}) collective-permute-start(bf16[128,768]{1,0:T(8,128)(2,1)S(1)} %copy-done.22), channel_id=1, source_target_pairs={{0,14},{2,12},{4,10},{6,8},{8,6},{10,4},{12,2},{14,0},{1,15},{3,13... | collective-permute-start | bytes 589832 | tf_op jit(solution)/shard_map/ppermute | solution.py:417
  111.3 4.2 %collective-permute-done.20.refs_1_ = bf16[128,768]{1,0:T(8,128)(2,1)} collective-permute-done((bf16[128,768]{1,0:T(8,128)(2,1)S(1)}, bf16[128,768]{1,0:T(8,128)(2,1)}, u32[]{:S(2)}, u32[]{:S(2)}) %collective-permute-start.20) | collective-permute-done | bytes 196640 | tf_op jit(solution)/shard_map/ppermute | solution.py:417
  115.5 2.9 %collective-permute-start.21 = (bf16[128,768]{1,0:T(8,128)(2,1)S(1)}, bf16[128,768]{1,0:T(8,128)(2,1)}, u32[]{:S(2)}, u32[]{:S(2)}) collective-permute-start(bf16[128,768]{1,0:T(8,128)(2,1)S(1)} %fusion), channel_id=1, source_target_pairs={{0,2},{2,0},{4,6},{6,4},{8,10},{10,8},{12,14},{14,12},{1,3},{3,1},... | collective-permute-start | bytes 589832 | tf_op jit(solution)/shard_map/ppermute | solution.py:417
  118.5 4.1 %collective-permute-start.23 = (bf16[128,768]{1,0:T(8,128)(2,1)}, bf16[128,768]{1,0:T(8,128)(2,1)}, u32[]{:S(2)}, u32[]{:S(2)}) collective-permute-start(bf16[128,768]{1,0:T(8,128)(2,1)} %get-tuple-element.146), channel_id=1, source_target_pairs={{0,8},{2,10},{4,12},{6,14},{8,0},{10,2},{12,4},{14,6},{1,9},{3,11}... | collective-permute-start | bytes 589832 | tf_op jit(solution)/shard_map/ppermute | solution.py:417
  127.3 3.9 %collective-permute-done.23.refs_4_ = bf16[128,768]{1,0:T(8,128)(2,1)} collective-permute-done((bf16[128,768]{1,0:T(8,128)(2,1)}, bf16[128,768]{1,0:T(8,128)(2,1)}, u32[]{:S(2)}, u32[]{:S(2)}) %collective-permute-start.23) | collective-permute-done | bytes 196640 | tf_op jit(solution)/shard_map/ppermute | solution.py:417
  132.9 2.7 %collective-permute-start.24 = (bf16[32,768]{1,0:T(8,128)(2,1)S(1)}, bf16[32,768]{1,0:T(8,128)(2,1)S(1)}, u32[]{:S(2)}, u32[]{:S(2)}) collective-permute-start(bf16[32,768]{1,0:T(8,128)(2,1)S(1)} %get-tuple-element.166), channel_id=1, source_target_pairs={{0,4},{2,6},{4,0},{6,2},{8,12},{10,14},{12,8},{14,10},{1,5},{3,7},... | collective-permute-start | bytes 147464 | tf_op jit(solution)/shard_map/ppermute | solution.py:417
  141.1 5.8 %collective-permute-done.27.refs_6_ = bf16[128,768]{1,0:T(8,128)(2,1)S(1)} collective-permute-done((bf16[128,768]{1,0:T(8,128)(2,1)}, bf16[128,768]{1,0:T(8,128)(2,1)S(1)}, u32[]{:S(2)}, u32[]{:S(2)}) %collective-permute-start.27) | collective-permute-done | bytes 196640 | tf_op jit(solution)/shard_map/ppermute | solution.py:417
  147.0 2.9 %collective-permute-done.28.refs_3_ = bf16[128,768]{1,0:T(8,128)(2,1)S(1)} collective-permute-done((bf16[128,768]{1,0:T(8,128)(2,1)}, bf16[128,768]{1,0:T(8,128)(2,1)S(1)}, u32[]{:S(2)}, u32[]{:S(2)}) %collective-permute-start.28) | collective-permute-done | bytes 196640 | tf_op jit(solution)/shard_map/ppermute | solution.py:417
  151.5 2.7 %collective-permute-start.29 = (bf16[32,768]{1,0:T(8,128)(2,1)S(1)}, bf16[32,768]{1,0:T(8,128)(2,1)S(1)}, u32[]{:S(2)}, u32[]{:S(2)}) collective-permute-start(bf16[32,768]{1,0:T(8,128)(2,1)S(1)} %fusion.3), channel_id=1, source_target_pairs={{0,4},{2,6},{4,0},{6,2},{8,12},{10,14},{12,8},{14,10},{1,5},{3,7},... | collective-permute-start | bytes 147464 | tf_op jit(solution)/shard_map/ppermute | solution.py:417
  165.9 3.2 %to_cells.2 = bf16[4,2,180,768]{3,2,1,0:T(8,128)(2,1)S(1)} custom-call(s32[1]{0:T(128)} %bitcast.me_ref, bf16[180,128]{1,0:T(8,128)(2,1)S(1)} %copy-done.3, bf16[4,2,180,768]{3,2,1,0:T(8,128)(2,1)S(1)} %copy.23.base_ref, bf16[128,768]{1,0:T(8,128)(2,1)} %get-tuple-element.155.refs_0_, bf16[128,768]{1,0:T(8,128)(2,1)} %collective-permute-done.20.refs_1_, ...), custom_call_target="tpu_custom_call" | custom-call | flops 283115520 | bytes 5996544 | tf_op jit(solution)/shard_map/to_cells/pallas_call | solution.py:186
  169.1 3.1 %copy.30 = bf16[4,2,180,768]{3,1,2,0:T(2,128)(2,1)} copy(bf16[4,2,180,768]{3,2,1,0:T(8,128)(2,1)S(1)} %to_cells.2) | data formatting | bytes 4423680 | tf_op jit(solution)/shard_map/to_cells/pallas_call | solution.py:186
  173.7 3.0 %to_cells.3 = bf16[4,2,180,768]{3,2,1,0:T(8,128)(2,1)S(1)} custom-call(s32[1]{0:T(128)} %bitcast.me_ref, bf16[180,128]{1,0:T(8,128)(2,1)S(1)} %copy-done.2, bf16[4,2,180,768]{3,2,1,0:T(8,128)(2,1)S(1)} %copy.22.cells_ref.base_ref, bf16[128,768]{1,0:T(8,128)(2,1)} %get-tuple-element.157.refs_0_, bf16[128,768]{1,0:T(8,128)(2,1)} %copy-done.18, ...), custom_call_target="tpu_custom_call" | custom-call | flops 283115520 | bytes 5996544 | tf_op jit(solution)/shard_map/to_cells/pallas_call | solution.py:186
  176.7 3.1 %copy.26 = bf16[4,2,180,768]{3,1,2,0:T(2,128)(2,1)} copy(bf16[4,2,180,768]{3,2,1,0:T(8,128)(2,1)S(1)} %to_cells.3) | data formatting | bytes 4423680 | tf_op jit(solution)/shard_map/to_cells/pallas_call | solution.py:186
  (142 shorter events, 62.3 us)
Async XLA Ops:
  5.0 16.8 %collective-permute-start = (bf16[128,768]{1,0:T(8,128)(2,1)}, bf16[128,768]{1,0:T(8,128)(2,1)S(1)}, u32[]{:S(2)}, u32[]{:S(2)}) collective-permute-start(bf16[128,768]{1,0:T(8,128)(2,1)} %get-tuple-element.99), channel_id=1, source_target_pairs={{0,14},{2,12},{4,10},{6,8},{8,6},{10,4},{12,2},{14,0},{1,15},{3,13... | collective-permute-start | bytes 589832 | tf_op jit(solution)/shard_map/ppermute | solution.py:417
  11.1 23.7 %collective-permute-start.1 = (bf16[128,768]{1,0:T(8,128)(2,1)}, bf16[128,768]{1,0:T(8,128)(2,1)S(1)}, u32[]{:S(2)}, u32[]{:S(2)}) collective-permute-start(bf16[128,768]{1,0:T(8,128)(2,1)} %get-tuple-element.100), channel_id=1, source_target_pairs={{0,12},{2,14},{4,8},{6,10},{8,4},{10,6},{12,0},{14,2},{1,13},{3,15... | collective-permute-start | bytes 589832 | tf_op jit(solution)/shard_map/ppermute | solution.py:417
  11.3 30.5 %collective-permute-start.2 = (bf16[128,768]{1,0:T(8,128)(2,1)}, bf16[128,768]{1,0:T(8,128)(2,1)S(1)}, u32[]{:S(2)}, u32[]{:S(2)}) collective-permute-start(bf16[128,768]{1,0:T(8,128)(2,1)} %get-tuple-element.101), channel_id=1, source_target_pairs={{0,10},{2,8},{4,14},{6,12},{8,2},{10,0},{12,6},{14,4},{1,11},{3,9}... | collective-permute-start | bytes 589832 | tf_op jit(solution)/shard_map/ppermute | solution.py:417
  12.0 36.1 %collective-permute-start.3 = (bf16[128,768]{1,0:T(8,128)(2,1)}, bf16[128,768]{1,0:T(8,128)(2,1)S(1)}, u32[]{:S(2)}, u32[]{:S(2)}) collective-permute-start(bf16[128,768]{1,0:T(8,128)(2,1)} %get-tuple-element.102), channel_id=1, source_target_pairs={{0,8},{2,10},{4,12},{6,14},{8,0},{10,2},{12,4},{14,6},{1,9},{3,11}... | collective-permute-start | bytes 589832 | tf_op jit(solution)/shard_map/ppermute | solution.py:417
  14.1 37.2 %collective-permute-start.4 = (bf16[128,768]{1,0:T(8,128)(2,1)}, bf16[128,768]{1,0:T(8,128)(2,1)}, u32[]{:S(2)}, u32[]{:S(2)}) collective-permute-start(bf16[128,768]{1,0:T(8,128)(2,1)} %get-tuple-element.103), channel_id=1, source_target_pairs={{0,6},{2,4},{4,2},{6,0},{8,14},{10,12},{12,10},{14,8},{1,7},{3,5},... | collective-permute-start | bytes 589832 | tf_op jit(solution)/shard_map/ppermute | solution.py:417
  21.8 31.4 %collective-permute-start.5 = (bf16[128,768]{1,0:T(8,128)(2,1)}, bf16[128,768]{1,0:T(8,128)(2,1)}, u32[]{:S(2)}, u32[]{:S(2)}) collective-permute-start(bf16[128,768]{1,0:T(8,128)(2,1)} %get-tuple-element.108), channel_id=1, source_target_pairs={{0,4},{2,6},{4,0},{6,2},{8,12},{10,14},{12,8},{14,10},{1,5},{3,7},... | collective-permute-start | bytes 589832 | tf_op jit(solution)/shard_map/ppermute | solution.py:417
  35.5 18.7 %collective-permute-start.6 = (bf16[128,768]{1,0:T(8,128)(2,1)}, bf16[128,768]{1,0:T(8,128)(2,1)}, u32[]{:S(2)}, u32[]{:S(2)}) collective-permute-start(bf16[128,768]{1,0:T(8,128)(2,1)} %get-tuple-element.109), channel_id=1, source_target_pairs={{0,2},{2,0},{4,6},{6,4},{8,10},{10,8},{12,14},{14,12},{1,3},{3,1},... | collective-permute-start | bytes 589832 | tf_op jit(solution)/shard_map/ppermute | solution.py:417
  41.8 22.5 %collective-permute-start.7 = (bf16[128,768]{1,0:T(8,128)(2,1)}, bf16[128,768]{1,0:T(8,128)(2,1)S(1)}, u32[]{:S(2)}, u32[]{:S(2)}) collective-permute-start(bf16[128,768]{1,0:T(8,128)(2,1)} %get-tuple-element.111), channel_id=1, source_target_pairs={{0,14},{2,12},{4,10},{6,8},{8,6},{10,4},{12,2},{14,0},{1,15},{3,13... | collective-permute-start | bytes 589832 | tf_op jit(solution)/shard_map/ppermute | solution.py:417
  48.8 20.7 %collective-permute-start.8 = (bf16[128,768]{1,0:T(8,128)(2,1)}, bf16[128,768]{1,0:T(8,128)(2,1)S(1)}, u32[]{:S(2)}, u32[]{:S(2)}) collective-permute-start(bf16[128,768]{1,0:T(8,128)(2,1)} %get-tuple-element.112), channel_id=1, source_target_pairs={{0,12},{2,14},{4,8},{6,10},{8,4},{10,6},{12,0},{14,2},{1,13},{3,15... | collective-permute-start | bytes 589832 | tf_op jit(solution)/shard_map/ppermute | solution.py:417
  51.3 25.4 %collective-permute-start.9 = (bf16[128,768]{1,0:T(8,128)(2,1)}, bf16[128,768]{1,0:T(8,128)(2,1)}, u32[]{:S(2)}, u32[]{:S(2)}) collective-permute-start(bf16[128,768]{1,0:T(8,128)(2,1)} %get-tuple-element.113), channel_id=1, source_target_pairs={{0,10},{2,8},{4,14},{6,12},{8,2},{10,0},{12,6},{14,4},{1,11},{3,9}... | collective-permute-start | bytes 589832 | tf_op jit(solution)/shard_map/ppermute | solution.py:417
  53.2 31.9 %collective-permute-start.10 = (bf16[128,768]{1,0:T(8,128)(2,1)}, bf16[128,768]{1,0:T(8,128)(2,1)}, u32[]{:S(2)}, u32[]{:S(2)}) collective-permute-start(bf16[128,768]{1,0:T(8,128)(2,1)} %get-tuple-element.114), channel_id=1, source_target_pairs={{0,8},{2,10},{4,12},{6,14},{8,0},{10,2},{12,4},{14,6},{1,9},{3,11}... | collective-permute-start | bytes 589832 | tf_op jit(solution)/shard_map/ppermute | solution.py:417
  54.2 30.9 %collective-permute-start.11 = (bf16[128,768]{1,0:T(8,128)(2,1)}, bf16[128,768]{1,0:T(8,128)(2,1)}, u32[]{:S(2)}, u32[]{:S(2)}) collective-permute-start(bf16[128,768]{1,0:T(8,128)(2,1)} %get-tuple-element.115), channel_id=1, source_target_pairs={{0,6},{2,4},{4,2},{6,0},{8,14},{10,12},{12,10},{14,8},{1,7},{3,5},... | collective-permute-start | bytes 589832 | tf_op jit(solution)/shard_map/ppermute | solution.py:417
  64.4 23.8 %collective-permute-start.12 = (bf16[128,768]{1,0:T(8,128)(2,1)S(1)}, bf16[128,768]{1,0:T(8,128)(2,1)}, u32[]{:S(2)}, u32[]{:S(2)}) collective-permute-start(bf16[128,768]{1,0:T(8,128)(2,1)S(1)} %copy-done.24), channel_id=1, source_target_pairs={{0,4},{2,6},{4,0},{6,2},{8,12},{10,14},{12,8},{14,10},{1,5},{3,7},... | collective-permute-start | bytes 589832 | tf_op jit(solution)/shard_map/ppermute | solution.py:417
  69.5 19.5 %collective-permute-start.13 = (bf16[128,768]{1,0:T(8,128)(2,1)S(1)}, bf16[128,768]{1,0:T(8,128)(2,1)}, u32[]{:S(2)}, u32[]{:S(2)}) collective-permute-start(bf16[128,768]{1,0:T(8,128)(2,1)S(1)} %copy-done.23), channel_id=1, source_target_pairs={{0,2},{2,0},{4,6},{6,4},{8,10},{10,8},{12,14},{14,12},{1,3},{3,1},... | collective-permute-start | bytes 589832 | tf_op jit(solution)/shard_map/ppermute | solution.py:417
  76.6 26.5 %collective-permute-start.14 = (bf16[128,768]{1,0:T(8,128)(2,1)}, bf16[128,768]{1,0:T(8,128)(2,1)S(1)}, u32[]{:S(2)}, u32[]{:S(2)}) collective-permute-start(bf16[128,768]{1,0:T(8,128)(2,1)} %get-tuple-element.137), channel_id=1, source_target_pairs={{0,8},{2,10},{4,12},{6,14},{8,0},{10,2},{12,4},{14,6},{1,9},{3,11}... | collective-permute-start | bytes 589832 | tf_op jit(solution)/shard_map/ppermute | solution.py:417
  85.0 18.1 %collective-permute-start.15 = (bf16[128,768]{1,0:T(8,128)(2,1)}, bf16[128,768]{1,0:T(8,128)(2,1)S(1)}, u32[]{:S(2)}, u32[]{:S(2)}) collective-permute-start(bf16[128,768]{1,0:T(8,128)(2,1)} %get-tuple-element.138), channel_id=1, source_target_pairs={{0,4},{2,6},{4,0},{6,2},{8,12},{10,14},{12,8},{14,10},{1,5},{3,7},... | collective-permute-start | bytes 589832 | tf_op jit(solution)/shard_map/ppermute | solution.py:417
  85.0 18.1 %collective-permute-start.16 = (bf16[128,768]{1,0:T(8,128)(2,1)}, bf16[128,768]{1,0:T(8,128)(2,1)S(1)}, u32[]{:S(2)}, u32[]{:S(2)}) collective-permute-start(bf16[128,768]{1,0:T(8,128)(2,1)} %get-tuple-element.139), channel_id=1, source_target_pairs={{0,10},{2,8},{4,14},{6,12},{8,2},{10,0},{12,6},{14,4},{1,11},{3,9}... | collective-permute-start | bytes 589832 | tf_op jit(solution)/shard_map/ppermute | solution.py:417
  88.1 15.0 %collective-permute-start.17 = (bf16[128,768]{1,0:T(8,128)(2,1)}, bf16[128,768]{1,0:T(8,128)(2,1)S(1)}, u32[]{:S(2)}, u32[]{:S(2)}) collective-permute-start(bf16[128,768]{1,0:T(8,128)(2,1)} %get-tuple-element.140), channel_id=1, source_target_pairs={{0,6},{2,4},{4,2},{6,0},{8,14},{10,12},{12,10},{14,8},{1,7},{3,5},... | collective-permute-start | bytes 589832 | tf_op jit(solution)/shard_map/ppermute | solution.py:417
  89.0 14.4 %collective-permute-start.18 = (bf16[128,768]{1,0:T(8,128)(2,1)}, bf16[128,768]{1,0:T(8,128)(2,1)S(1)}, u32[]{:S(2)}, u32[]{:S(2)}) collective-permute-start(bf16[128,768]{1,0:T(8,128)(2,1)} %get-tuple-element.141), channel_id=1, source_target_pairs={{0,12},{2,14},{4,8},{6,10},{8,4},{10,6},{12,0},{14,2},{1,13},{3,15... | collective-permute-start | bytes 589832 | tf_op jit(solution)/shard_map/ppermute | solution.py:417
  118.5 12.7 %collective-permute-start.23 = (bf16[128,768]{1,0:T(8,128)(2,1)}, bf16[128,768]{1,0:T(8,128)(2,1)}, u32[]{:S(2)}, u32[]{:S(2)}) collective-permute-start(bf16[128,768]{1,0:T(8,128)(2,1)} %get-tuple-element.146), channel_id=1, source_target_pairs={{0,8},{2,10},{4,12},{6,14},{8,0},{10,2},{12,4},{14,6},{1,9},{3,11}... | collective-permute-start | bytes 589832 | tf_op jit(solution)/shard_map/ppermute | solution.py:417
  135.7 14.1 %collective-permute-start.28 = (bf16[128,768]{1,0:T(8,128)(2,1)}, bf16[128,768]{1,0:T(8,128)(2,1)S(1)}, u32[]{:S(2)}, u32[]{:S(2)}) collective-permute-start(bf16[128,768]{1,0:T(8,128)(2,1)} %get-tuple-element.149), channel_id=1, source_target_pairs={{0,10},{2,8},{4,14},{6,12},{8,2},{10,0},{12,6},{14,4},{1,11},{3,9}... | collective-permute-start | bytes 589832 | tf_op jit(solution)/shard_map/ppermute | solution.py:417
  138.4 21.3 %collective-permute-start.32 = (bf16[128,768]{1,0:T(8,128)(2,1)}, bf16[128,768]{1,0:T(8,128)(2,1)S(1)}, u32[]{:S(2)}, u32[]{:S(2)}) collective-permute-start(bf16[128,768]{1,0:T(8,128)(2,1)} %get-tuple-element.151), channel_id=1, source_target_pairs={{0,6},{2,4},{4,2},{6,0},{8,14},{10,12},{12,10},{14,8},{1,7},{3,5},... | collective-permute-start | bytes 589832 | tf_op jit(solution)/shard_map/ppermute | solution.py:417
  139.2 20.5 %collective-permute-start.33 = (bf16[128,768]{1,0:T(8,128)(2,1)}, bf16[128,768]{1,0:T(8,128)(2,1)S(1)}, u32[]{:S(2)}, u32[]{:S(2)}) collective-permute-start(bf16[128,768]{1,0:T(8,128)(2,1)} %get-tuple-element.152), channel_id=1, source_target_pairs={{0,12},{2,14},{4,8},{6,10},{8,4},{10,6},{12,0},{14,2},{1,13},{3,15... | collective-permute-start | bytes 589832 | tf_op jit(solution)/shard_map/ppermute | solution.py:417
  159.7 12.5 %collective-permute-start.34 = (bf16[4,32,768]{2,1,0:T(8,128)(2,1)S(1)}, bf16[4,32,768]{2,1,0:T(8,128)(2,1)S(1)}, u32[]{:S(2)}, u32[]{:S(2)}) collective-permute-start(bf16[4,32,768]{2,1,0:T(8,128)(2,1)S(1)} %pad_maximum_fusion.1), channel_id=1, source_target_pairs={{0,2},{2,0},{4,6},{6,4},{8,10},{10,8},{12,14},{14,12},{1,3},{3,1},... | collective-permute-start | bytes 589832 | tf_op jit(solution)/shard_map/ppermute | solution.py:417
  (45 other events, 473.1 us)

commit v19 on v18

--- a/solution.py
+++ b/solution.py
@@ -604,13 +604,14 @@
     grad_image, sums = waiting((list(grad_image), sums), early)
     group_sum = GroupSum(sums)
     group_sum.over_dp()
+    again = with_layout_constraint(waiting(fields, early[:1]), Layout(major_to_minor=(0, 1, 2, 3)))
+    group_sum.held, again = lax.optimization_barrier((group_sum.held, again))
     group_sum.over_next(late[:1])
     grad_band = {0: grad_image[0]}
     send(grad_image, order, grad_band)
     arrived = [grad_band[offset] for offset in order]
     image_band = listed(image_band)
     grad_band = listed(grad_band)
-    again = waiting(fields, early[:1])
     output = rows_inside(to_cells(me, scaled.T, image_band, again))
     group_sum.scatter(late[1:] + arrived[:1])
     group_sum.gather(arrived[1:3])

time: 183 us -> 189 us (1.033)
  starting transfers between devices: 77.3 us -> 87.9 us
  waiting for transfers between devices: 50.7 us -> 41.7 us
  local copies, waits for them, and re-layouts: 14.1 us -> 18.2 us
    ppermute x38, starting transfers between devices: 77.3 us -> 87.9 us  [swap_with(): return lax.ppermute(values, axis, pairs)]
    ppermute x38, waiting for transfers between devices: 50.7 us -> 41.7 us  [swap_with(): return lax.ppermute(values, axis, pairs)]
    unnamed x63 -> x75, local copies, waits for them, and re-layouts: 4.41 us -> 7.06 us
  transfers between devices with their start and end apart: 38 -> 38, of which waited for: 16 -> 12; matrix products, arithmetic and copies ran while one was open for 6% -> 7% of each run, Pallas kernels for 17% -> 14%
where the time goes in v19:
time: 189 us; the launch traced here: 188 us
  starting transfers between devices  87.9 us (47%)
  waiting for transfers between devices  41.7 us (22%)
  Pallas kernels  35.9 us (19%)
  local copies, waits for them, and re-layouts  18.2 us (10%)
  other arithmetic  3.22 us (2%)
    ppermute x38, starting transfers between devices, swap_with(): return lax.ppermute(values, axis, pairs)  87.9 us
    ppermute x38, waiting for transfers between devices, swap_with(): return lax.ppermute(values, axis, pairs)  41.7 us
    pallas_call x1, Pallas kernels, backward_mid(): pl.pallas_call(functools.partial(backward_kernel, size_of_block, len(band...  12.8 us
    pallas_call x1, Pallas kernels, forward_mid(): pl.pallas_call(functools.partial(forward_kernel, len(bands)), grid_spec=p...  7.56 us
    unnamed x75, local copies, waits for them, and re-layouts  7.06 us
    pallas_call x2, local copies, waits for them, and re-layouts, to_cells(): pl.pallas_call(to_cells_kernel, grid_spec=pltpu.PrefetchScalarGridSpec(nu...  6.13 us
    pallas_call x2, Pallas kernels, to_cells(): pl.pallas_call(to_cells_kernel, grid_spec=pltpu.PrefetchScalarGridSpec(nu...  5.98 us
    pallas_call x2, Pallas kernels, to_modes(): pl.pallas_call(to_modes_kernel, grid_spec=pltpu.PrefetchScalarGridSpec(nu...  4.81 us
  transfers between devices with their start and end apart: 38, of which 12 were waited for; matrix products, arithmetic and copies ran while one was open for 7% of the time, Pallas kernels for 14%

profile of v19, /device:TPU:0, one launch (start us, length us, event | category | flops | bytes accessed | tf_op | source)
XLA Modules:
  0.0 188.1 jit_solution(16361740078574741989)
XLA Ops:
  11.2 3.1 %collective-permute-start.5 = (bf16[128,768]{1,0:T(8,128)(2,1)S(1)}, bf16[128,768]{1,0:T(8,128)(2,1)S(1)}, u32[]{:S(2)}, u32[]{:S(2)}) collective-permute-start(bf16[128,768]{1,0:T(8,128)(2,1)S(1)} %copy-done.36), channel_id=1, source_target_pairs={{0,4},{2,6},{4,0},{6,2},{8,12},{10,14},{12,8},{14,10},{1,5},{3,7},... | collective-permute-start | bytes 589832 | tf_op jit(solution)/shard_map/ppermute | solution.py:417
  24.1 8.6 %collective-permute-start.4 = (bf16[128,768]{1,0:T(8,128)(2,1)S(1)}, bf16[128,768]{1,0:T(8,128)(2,1)}, u32[]{:S(2)}, u32[]{:S(2)}) collective-permute-start(bf16[128,768]{1,0:T(8,128)(2,1)S(1)} %copy-done.29), channel_id=1, source_target_pairs={{0,6},{2,4},{4,2},{6,0},{8,14},{10,12},{12,10},{14,8},{1,7},{3,5},... | collective-permute-start | bytes 589832 | tf_op jit(solution)/shard_map/ppermute | solution.py:417
  33.0 11.4 %collective-permute-start.10 = (bf16[128,768]{1,0:T(8,128)(2,1)}, bf16[128,768]{1,0:T(8,128)(2,1)S(1)}, u32[]{:S(2)}, u32[]{:S(2)}) collective-permute-start(bf16[128,768]{1,0:T(8,128)(2,1)} %get-tuple-element.116), channel_id=1, source_target_pairs={{0,8},{2,10},{4,12},{6,14},{8,0},{10,2},{12,4},{14,6},{1,9},{3,11}... | collective-permute-start | bytes 589832 | tf_op jit(solution)/shard_map/ppermute | solution.py:417
  45.0 4.8 %collective-permute-start.11 = (bf16[128,768]{1,0:T(8,128)(2,1)}, bf16[128,768]{1,0:T(8,128)(2,1)S(1)}, u32[]{:S(2)}, u32[]{:S(2)}) collective-permute-start(bf16[128,768]{1,0:T(8,128)(2,1)} %get-tuple-element.117), channel_id=1, source_target_pairs={{0,6},{2,4},{4,2},{6,0},{8,14},{10,12},{12,10},{14,8},{1,7},{3,5},... | collective-permute-start | bytes 589832 | tf_op jit(solution)/shard_map/ppermute | solution.py:417
  49.8 4.3 %collective-permute-done.2.refs_3_ = bf16[128,768]{1,0:T(8,128)(2,1)} collective-permute-done((bf16[128,768]{1,0:T(8,128)(2,1)}, bf16[128,768]{1,0:T(8,128)(2,1)}, u32[]{:S(2)}, u32[]{:S(2)}) %collective-permute-start.2) | collective-permute-done | bytes 196640 | tf_op jit(solution)/shard_map/ppermute | solution.py:417
  54.0 3.2 %collective-permute-start.7 = (bf16[128,768]{1,0:T(8,128)(2,1)}, bf16[128,768]{1,0:T(8,128)(2,1)}, u32[]{:S(2)}, u32[]{:S(2)}) collective-permute-start(bf16[128,768]{1,0:T(8,128)(2,1)} %get-tuple-element.113), channel_id=1, source_target_pairs={{0,14},{2,12},{4,10},{6,8},{8,6},{10,4},{12,2},{14,0},{1,15},{3,13... | collective-permute-start | bytes 589832 | tf_op jit(solution)/shard_map/ppermute | solution.py:417
  57.2 9.2 %collective-permute-done.3.refs_4_ = bf16[128,768]{1,0:T(8,128)(2,1)} collective-permute-done((bf16[128,768]{1,0:T(8,128)(2,1)}, bf16[128,768]{1,0:T(8,128)(2,1)}, u32[]{:S(2)}, u32[]{:S(2)}) %collective-permute-start.3) | collective-permute-done | bytes 196640 | tf_op jit(solution)/shard_map/ppermute | solution.py:417
  66.6 7.6 %mix_forward.1 = (bf16[128,768]{1,0:T(8,128)(2,1)}, bf16[128,768]{1,0:T(8,128)(2,1)}, bf16[128,768]{1,0:T(8,128)(2,1)}, bf16[128,768]{1,0:T(8,128)(2,1)}, bf16[1...) custom-call(s32[1]{0:T(128)} %bitcast.me_ref, ...), custom_call_target="tpu_custom_call" | custom-call | flops 2415919104 | bytes 17301504 | tf_op jit(solution)/shard_map/mix_forward/pallas_call | solution.py:344
  74.2 4.4 %collective-permute-start.12 = (bf16[128,768]{1,0:T(8,128)(2,1)S(1)}, bf16[128,768]{1,0:T(8,128)(2,1)}, u32[]{:S(2)}, u32[]{:S(2)}) collective-permute-start(bf16[128,768]{1,0:T(8,128)(2,1)S(1)} %copy-done.26), channel_id=1, source_target_pairs={{0,4},{2,6},{4,0},{6,2},{8,12},{10,14},{12,8},{14,10},{1,5},{3,7},... | collective-permute-start | bytes 589832 | tf_op jit(solution)/shard_map/ppermute | solution.py:417
  81.6 6.0 %collective-permute-start.15 = (bf16[128,768]{1,0:T(8,128)(2,1)}, bf16[128,768]{1,0:T(8,128)(2,1)S(1)}, u32[]{:S(2)}, u32[]{:S(2)}) collective-permute-start(bf16[128,768]{1,0:T(8,128)(2,1)} %get-tuple-element.140), channel_id=1, source_target_pairs={{0,4},{2,6},{4,0},{6,2},{8,12},{10,14},{12,8},{14,10},{1,5},{3,7},... | collective-permute-start | bytes 589832 | tf_op jit(solution)/shard_map/ppermute | solution.py:417
  87.6 4.4 %collective-permute-done.9.refs_3_ = bf16[128,768]{1,0:T(8,128)(2,1)} collective-permute-done((bf16[128,768]{1,0:T(8,128)(2,1)}, bf16[128,768]{1,0:T(8,128)(2,1)}, u32[]{:S(2)}, u32[]{:S(2)}) %collective-permute-start.9) | collective-permute-done | bytes 196640 | tf_op jit(solution)/shard_map/ppermute | solution.py:417
  92.0 4.9 %collective-permute-start.17 = (bf16[128,768]{1,0:T(8,128)(2,1)}, bf16[128,768]{1,0:T(8,128)(2,1)S(1)}, u32[]{:S(2)}, u32[]{:S(2)}) collective-permute-start(bf16[128,768]{1,0:T(8,128)(2,1)} %get-tuple-element.142), channel_id=1, source_target_pairs={{0,6},{2,4},{4,2},{6,0},{8,14},{10,12},{12,10},{14,8},{1,7},{3,5},... | collective-permute-start | bytes 589832 | tf_op jit(solution)/shard_map/ppermute | solution.py:417
  97.3 12.8 %mix_backward.1 = (bf16[128,768]{1,0:T(8,128)(2,1)}, bf16[128,768]{1,0:T(8,128)(2,1)}, bf16[128,768]{1,0:T(8,128)(2,1)}, bf16[128,768]{1,0:T(8,128)(2,1)}, bf16[...) custom-call(s32[1]{0:T(128)} %bitcast.me_ref, ...), custom_call_target="tpu_custom_call" | custom-call | flops 4831838208 | bytes 17301504 | tf_op jit(solution)/shard_map/mix_backward/pallas_call | solution.py:382
  112.1 3.9 %collective-permute-start.20 = (bf16[128,768]{1,0:T(8,128)(2,1)S(1)}, bf16[128,768]{1,0:T(8,128)(2,1)}, u32[]{:S(2)}, u32[]{:S(2)}) collective-permute-start(bf16[128,768]{1,0:T(8,128)(2,1)S(1)} %copy-done.24), channel_id=1, source_target_pairs={{0,14},{2,12},{4,10},{6,8},{8,6},{10,4},{12,2},{14,0},{1,15},{3,13... | collective-permute-start | bytes 589832 | tf_op jit(solution)/shard_map/ppermute | solution.py:417
  116.0 3.3 %copy.23.base_ref = bf16[4,2,180,768]{3,2,1,0:T(8,128)(2,1)} copy(bf16[4,2,180,768]{3,1,2,0:T(2,128)(2,1)} %param.13) | data formatting | bytes 4423680 | tf_op jit(solution)/shard_map/optimization_barrier | solution.py:421
  124.4 4.6 %collective-permute-start.23 = (bf16[128,768]{1,0:T(8,128)(2,1)}, bf16[128,768]{1,0:T(8,128)(2,1)}, u32[]{:S(2)}, u32[]{:S(2)}) collective-permute-start(bf16[128,768]{1,0:T(8,128)(2,1)} %get-tuple-element.150), channel_id=1, source_target_pairs={{0,8},{2,10},{4,12},{6,14},{8,0},{10,2},{12,4},{14,6},{1,9},{3,11}... | collective-permute-start | bytes 589832 | tf_op jit(solution)/shard_map/ppermute | solution.py:417
  133.1 4.6 %collective-permute-done.23.refs_4_ = bf16[128,768]{1,0:T(8,128)(2,1)} collective-permute-done((bf16[128,768]{1,0:T(8,128)(2,1)}, bf16[128,768]{1,0:T(8,128)(2,1)}, u32[]{:S(2)}, u32[]{:S(2)}) %collective-permute-start.23) | collective-permute-done | bytes 196640 | tf_op jit(solution)/shard_map/ppermute | solution.py:417
  148.4 4.4 %collective-permute-done.27.refs_6_ = bf16[128,768]{1,0:T(8,128)(2,1)S(1)} collective-permute-done((bf16[128,768]{1,0:T(8,128)(2,1)}, bf16[128,768]{1,0:T(8,128)(2,1)S(1)}, u32[]{:S(2)}, u32[]{:S(2)}) %collective-permute-start.27) | collective-permute-done | bytes 196640 | tf_op jit(solution)/shard_map/ppermute | solution.py:417
  152.8 3.4 %collective-permute-done.28.refs_3_ = bf16[128,768]{1,0:T(8,128)(2,1)S(1)} collective-permute-done((bf16[128,768]{1,0:T(8,128)(2,1)}, bf16[128,768]{1,0:T(8,128)(2,1)S(1)}, u32[]{:S(2)}, u32[]{:S(2)}) %collective-permute-start.28) | collective-permute-done | bytes 196640 | tf_op jit(solution)/shard_map/ppermute | solution.py:417
  162.2 4.1 %collective-permute-done.30 = bf16[32,768]{1,0:T(8,128)(2,1)S(1)} collective-permute-done((bf16[32,768]{1,0:T(8,128)(2,1)S(1)}, bf16[32,768]{1,0:T(8,128)(2,1)S(1)}, u32[]{:S(2)}, u32[]{:S(2)}) %collective-permute-start.30) | collective-permute-done | bytes 49184 | tf_op jit(solution)/shard_map/ppermute | solution.py:417
  172.1 3.0 %to_cells.2 = bf16[4,2,180,768]{3,2,1,0:T(8,128)(2,1)S(1)} custom-call(s32[1]{0:T(128)} %bitcast.me_ref, bf16[180,128]{1,0:T(8,128)(2,1)S(1)} %copy-done.4, bf16[4,2,180,768]{3,2,1,0:T(8,128)(2,1)S(1)} %copy-done, bf16[128,768]{1,0:T(8,128)(2,1)} %get-tuple-element.159.refs_0_, bf16[128,768]{1,0:T(8,128)(2,1)} %collective-permute-done.20.refs_1_, ...), custom_call_target="tpu_custom_call" | custom-call | flops 283115520 | bytes 5996544 | tf_op jit(solution)/shard_map/to_cells/pallas_call | solution.py:186
  175.2 3.1 %copy.30 = bf16[4,2,180,768]{3,1,2,0:T(2,128)(2,1)} copy(bf16[4,2,180,768]{3,2,1,0:T(8,128)(2,1)S(1)} %to_cells.2) | data formatting | bytes 4423680 | tf_op jit(solution)/shard_map/to_cells/pallas_call | solution.py:186
  179.8 3.0 %to_cells.3 = bf16[4,2,180,768]{3,2,1,0:T(8,128)(2,1)S(1)} custom-call(s32[1]{0:T(128)} %bitcast.me_ref, bf16[180,128]{1,0:T(8,128)(2,1)S(1)} %copy-done.3, bf16[4,2,180,768]{3,2,1,0:T(8,128)(2,1)S(1)} %copy.22.cells_ref.base_ref, bf16[128,768]{1,0:T(8,128)(2,1)} %get-tuple-element.161.refs_0_, bf16[128,768]{1,0:T(8,128)(2,1)} %copy-done.20, ...), custom_call_target="tpu_custom_call" | custom-call | flops 283115520 | bytes 5996544 | tf_op jit(solution)/shard_map/to_cells/pallas_call | solution.py:186
  182.8 3.1 %copy.26 = bf16[4,2,180,768]{3,1,2,0:T(2,128)(2,1)} copy(bf16[4,2,180,768]{3,2,1,0:T(8,128)(2,1)S(1)} %to_cells.3) | data formatting | bytes 4423680 | tf_op jit(solution)/shard_map/to_cells/pallas_call | solution.py:186
  (154 shorter events, 62.0 us)
Async XLA Ops:
  15.8 17.2 %collective-permute-start = (bf16[128,768]{1,0:T(8,128)(2,1)S(1)}, bf16[128,768]{1,0:T(8,128)(2,1)S(1)}, u32[]{:S(2)}, u32[]{:S(2)}) collective-permute-start(bf16[128,768]{1,0:T(8,128)(2,1)S(1)} %copy-done.34), channel_id=1, source_target_pairs={{0,14},{2,12},{4,10},{6,8},{8,6},{10,4},{12,2},{14,0},{1,15},{3,13... | collective-permute-start | bytes 589832 | tf_op jit(solution)/shard_map/ppermute | solution.py:417
  18.2 26.1 %collective-permute-start.1 = (bf16[128,768]{1,0:T(8,128)(2,1)}, bf16[128,768]{1,0:T(8,128)(2,1)S(1)}, u32[]{:S(2)}, u32[]{:S(2)}) collective-permute-start(bf16[128,768]{1,0:T(8,128)(2,1)} %get-tuple-element.102), channel_id=1, source_target_pairs={{0,12},{2,14},{4,8},{6,10},{8,4},{10,6},{12,0},{14,2},{1,13},{3,15... | collective-permute-start | bytes 589832 | tf_op jit(solution)/shard_map/ppermute | solution.py:417
  19.6 34.5 %collective-permute-start.2 = (bf16[128,768]{1,0:T(8,128)(2,1)}, bf16[128,768]{1,0:T(8,128)(2,1)}, u32[]{:S(2)}, u32[]{:S(2)}) collective-permute-start(bf16[128,768]{1,0:T(8,128)(2,1)} %get-tuple-element.103), channel_id=1, source_target_pairs={{0,10},{2,8},{4,14},{6,12},{8,2},{10,0},{12,6},{14,4},{1,11},{3,9}... | collective-permute-start | bytes 589832 | tf_op jit(solution)/shard_map/ppermute | solution.py:417
  21.3 45.2 %collective-permute-start.3 = (bf16[128,768]{1,0:T(8,128)(2,1)}, bf16[128,768]{1,0:T(8,128)(2,1)}, u32[]{:S(2)}, u32[]{:S(2)}) collective-permute-start(bf16[128,768]{1,0:T(8,128)(2,1)} %get-tuple-element.104), channel_id=1, source_target_pairs={{0,8},{2,10},{4,12},{6,14},{8,0},{10,2},{12,4},{14,6},{1,9},{3,11}... | collective-permute-start | bytes 589832 | tf_op jit(solution)/shard_map/ppermute | solution.py:417
  24.1 42.3 %collective-permute-start.4 = (bf16[128,768]{1,0:T(8,128)(2,1)S(1)}, bf16[128,768]{1,0:T(8,128)(2,1)}, u32[]{:S(2)}, u32[]{:S(2)}) collective-permute-start(bf16[128,768]{1,0:T(8,128)(2,1)S(1)} %copy-done.29), channel_id=1, source_target_pairs={{0,6},{2,4},{4,2},{6,0},{8,14},{10,12},{12,10},{14,8},{1,7},{3,5},... | collective-permute-start | bytes 589832 | tf_op jit(solution)/shard_map/ppermute | solution.py:417
  33.0 41.2 %collective-permute-start.10 = (bf16[128,768]{1,0:T(8,128)(2,1)}, bf16[128,768]{1,0:T(8,128)(2,1)S(1)}, u32[]{:S(2)}, u32[]{:S(2)}) collective-permute-start(bf16[128,768]{1,0:T(8,128)(2,1)} %get-tuple-element.116), channel_id=1, source_target_pairs={{0,8},{2,10},{4,12},{6,14},{8,0},{10,2},{12,4},{14,6},{1,9},{3,11}... | collective-permute-start | bytes 589832 | tf_op jit(solution)/shard_map/ppermute | solution.py:417
  45.0 33.6 %collective-permute-start.11 = (bf16[128,768]{1,0:T(8,128)(2,1)}, bf16[128,768]{1,0:T(8,128)(2,1)S(1)}, u32[]{:S(2)}, u32[]{:S(2)}) collective-permute-start(bf16[128,768]{1,0:T(8,128)(2,1)} %get-tuple-element.117), channel_id=1, source_target_pairs={{0,6},{2,4},{4,2},{6,0},{8,14},{10,12},{12,10},{14,8},{1,7},{3,5},... | collective-permute-start | bytes 589832 | tf_op jit(solution)/shard_map/ppermute | solution.py:417
  54.0 26.0 %collective-permute-start.7 = (bf16[128,768]{1,0:T(8,128)(2,1)}, bf16[128,768]{1,0:T(8,128)(2,1)}, u32[]{:S(2)}, u32[]{:S(2)}) collective-permute-start(bf16[128,768]{1,0:T(8,128)(2,1)} %get-tuple-element.113), channel_id=1, source_target_pairs={{0,14},{2,12},{4,10},{6,8},{8,6},{10,4},{12,2},{14,0},{1,15},{3,13... | collective-permute-start | bytes 589832 | tf_op jit(solution)/shard_map/ppermute | solution.py:417
  66.5 15.1 %collective-permute-start.8 = (bf16[128,768]{1,0:T(8,128)(2,1)}, bf16[128,768]{1,0:T(8,128)(2,1)}, u32[]{:S(2)}, u32[]{:S(2)}) collective-permute-start(bf16[128,768]{1,0:T(8,128)(2,1)} %get-tuple-element.114), channel_id=1, source_target_pairs={{0,12},{2,14},{4,8},{6,10},{8,4},{10,6},{12,0},{14,2},{1,13},{3,15... | collective-permute-start | bytes 589832 | tf_op jit(solution)/shard_map/ppermute | solution.py:417
  66.5 25.5 %collective-permute-start.9 = (bf16[128,768]{1,0:T(8,128)(2,1)}, bf16[128,768]{1,0:T(8,128)(2,1)}, u32[]{:S(2)}, u32[]{:S(2)}) collective-permute-start(bf16[128,768]{1,0:T(8,128)(2,1)} %get-tuple-element.115), channel_id=1, source_target_pairs={{0,10},{2,8},{4,14},{6,12},{8,2},{10,0},{12,6},{14,4},{1,11},{3,9}... | collective-permute-start | bytes 589832 | tf_op jit(solution)/shard_map/ppermute | solution.py:417
  74.2 17.8 %collective-permute-start.12 = (bf16[128,768]{1,0:T(8,128)(2,1)S(1)}, bf16[128,768]{1,0:T(8,128)(2,1)}, u32[]{:S(2)}, u32[]{:S(2)}) collective-permute-start(bf16[128,768]{1,0:T(8,128)(2,1)S(1)} %copy-done.26), channel_id=1, source_target_pairs={{0,4},{2,6},{4,0},{6,2},{8,12},{10,14},{12,8},{14,10},{1,5},{3,7},... | collective-permute-start | bytes 589832 | tf_op jit(solution)/shard_map/ppermute | solution.py:417
  78.6 18.3 %collective-permute-start.13 = (bf16[128,768]{1,0:T(8,128)(2,1)S(1)}, bf16[128,768]{1,0:T(8,128)(2,1)}, u32[]{:S(2)}, u32[]{:S(2)}) collective-permute-start(bf16[128,768]{1,0:T(8,128)(2,1)S(1)} %copy-done.25), channel_id=1, source_target_pairs={{0,2},{2,0},{4,6},{6,4},{8,10},{10,8},{12,14},{14,12},{1,3},{3,1},... | collective-permute-start | bytes 589832 | tf_op jit(solution)/shard_map/ppermute | solution.py:417
  80.0 30.1 %collective-permute-start.14 = (bf16[128,768]{1,0:T(8,128)(2,1)}, bf16[128,768]{1,0:T(8,128)(2,1)S(1)}, u32[]{:S(2)}, u32[]{:S(2)}) collective-permute-start(bf16[128,768]{1,0:T(8,128)(2,1)} %get-tuple-element.139), channel_id=1, source_target_pairs={{0,8},{2,10},{4,12},{6,14},{8,0},{10,2},{12,4},{14,6},{1,9},{3,11}... | collective-permute-start | bytes 589832 | tf_op jit(solution)/shard_map/ppermute | solution.py:417
  81.6 28.5 %collective-permute-start.15 = (bf16[128,768]{1,0:T(8,128)(2,1)}, bf16[128,768]{1,0:T(8,128)(2,1)S(1)}, u32[]{:S(2)}, u32[]{:S(2)}) collective-permute-start(bf16[128,768]{1,0:T(8,128)(2,1)} %get-tuple-element.140), channel_id=1, source_target_pairs={{0,4},{2,6},{4,0},{6,2},{8,12},{10,14},{12,8},{14,10},{1,5},{3,7},... | collective-permute-start | bytes 589832 | tf_op jit(solution)/shard_map/ppermute | solution.py:417
  92.0 18.1 %collective-permute-start.16 = (bf16[128,768]{1,0:T(8,128)(2,1)}, bf16[128,768]{1,0:T(8,128)(2,1)S(1)}, u32[]{:S(2)}, u32[]{:S(2)}) collective-permute-start(bf16[128,768]{1,0:T(8,128)(2,1)} %get-tuple-element.141), channel_id=1, source_target_pairs={{0,10},{2,8},{4,14},{6,12},{8,2},{10,0},{12,6},{14,4},{1,11},{3,9}... | collective-permute-start | bytes 589832 | tf_op jit(solution)/shard_map/ppermute | solution.py:417
  92.0 18.1 %collective-permute-start.17 = (bf16[128,768]{1,0:T(8,128)(2,1)}, bf16[128,768]{1,0:T(8,128)(2,1)S(1)}, u32[]{:S(2)}, u32[]{:S(2)}) collective-permute-start(bf16[128,768]{1,0:T(8,128)(2,1)} %get-tuple-element.142), channel_id=1, source_target_pairs={{0,6},{2,4},{4,2},{6,0},{8,14},{10,12},{12,10},{14,8},{1,7},{3,5},... | collective-permute-start | bytes 589832 | tf_op jit(solution)/shard_map/ppermute | solution.py:417
  96.9 13.3 %collective-permute-start.18 = (bf16[128,768]{1,0:T(8,128)(2,1)}, bf16[128,768]{1,0:T(8,128)(2,1)S(1)}, u32[]{:S(2)}, u32[]{:S(2)}) collective-permute-start(bf16[128,768]{1,0:T(8,128)(2,1)} %get-tuple-element.143), channel_id=1, source_target_pairs={{0,12},{2,14},{4,8},{6,10},{8,4},{10,6},{12,0},{14,2},{1,13},{3,15... | collective-permute-start | bytes 589832 | tf_op jit(solution)/shard_map/ppermute | solution.py:417
  124.4 13.3 %collective-permute-start.23 = (bf16[128,768]{1,0:T(8,128)(2,1)}, bf16[128,768]{1,0:T(8,128)(2,1)}, u32[]{:S(2)}, u32[]{:S(2)}) collective-permute-start(bf16[128,768]{1,0:T(8,128)(2,1)} %get-tuple-element.150), channel_id=1, source_target_pairs={{0,8},{2,10},{4,12},{6,14},{8,0},{10,2},{12,4},{14,6},{1,9},{3,11}... | collective-permute-start | bytes 589832 | tf_op jit(solution)/shard_map/ppermute | solution.py:417
  142.2 10.6 %collective-permute-start.27 = (bf16[128,768]{1,0:T(8,128)(2,1)}, bf16[128,768]{1,0:T(8,128)(2,1)S(1)}, u32[]{:S(2)}, u32[]{:S(2)}) collective-permute-start(bf16[128,768]{1,0:T(8,128)(2,1)} %get-tuple-element.152), channel_id=1, source_target_pairs={{0,4},{2,6},{4,0},{6,2},{8,12},{10,14},{12,8},{14,10},{1,5},{3,7},... | collective-permute-start | bytes 589832 | tf_op jit(solution)/shard_map/ppermute | solution.py:417
  142.2 14.0 %collective-permute-start.28 = (bf16[128,768]{1,0:T(8,128)(2,1)}, bf16[128,768]{1,0:T(8,128)(2,1)S(1)}, u32[]{:S(2)}, u32[]{:S(2)}) collective-permute-start(bf16[128,768]{1,0:T(8,128)(2,1)} %get-tuple-element.153), channel_id=1, source_target_pairs={{0,10},{2,8},{4,14},{6,12},{8,2},{10,0},{12,6},{14,4},{1,11},{3,9}... | collective-permute-start | bytes 589832 | tf_op jit(solution)/shard_map/ppermute | solution.py:417
  144.5 21.7 %collective-permute-start.32 = (bf16[128,768]{1,0:T(8,128)(2,1)}, bf16[128,768]{1,0:T(8,128)(2,1)S(1)}, u32[]{:S(2)}, u32[]{:S(2)}) collective-permute-start(bf16[128,768]{1,0:T(8,128)(2,1)} %get-tuple-element.155), channel_id=1, source_target_pairs={{0,6},{2,4},{4,2},{6,0},{8,14},{10,12},{12,10},{14,8},{1,7},{3,5},... | collective-permute-start | bytes 589832 | tf_op jit(solution)/shard_map/ppermute | solution.py:417
  145.1 21.1 %collective-permute-start.33 = (bf16[128,768]{1,0:T(8,128)(2,1)}, bf16[128,768]{1,0:T(8,128)(2,1)S(1)}, u32[]{:S(2)}, u32[]{:S(2)}) collective-permute-start(bf16[128,768]{1,0:T(8,128)(2,1)} %get-tuple-element.156), channel_id=1, source_target_pairs={{0,12},{2,14},{4,8},{6,10},{8,4},{10,6},{12,0},{14,2},{1,13},{3,15... | collective-permute-start | bytes 589832 | tf_op jit(solution)/shard_map/ppermute | solution.py:417
  166.3 11.9 %collective-permute-start.34 = (bf16[4,32,768]{2,1,0:T(8,128)(2,1)S(1)}, bf16[4,32,768]{2,1,0:T(8,128)(2,1)S(1)}, u32[]{:S(2)}, u32[]{:S(2)}) collective-permute-start(bf16[4,32,768]{2,1,0:T(8,128)(2,1)S(1)} %pad_maximum_fusion.1), channel_id=1, source_target_pairs={{0,2},{2,0},{4,6},{6,4},{8,10},{10,8},{12,14},{14,12},{1,3},{3,1},... | collective-permute-start | bytes 589832 | tf_op jit(solution)/shard_map/ppermute | solution.py:417
  167.5 10.8 %collective-permute-start.35 = (bf16[128,768]{1,0:T(8,128)(2,1)}, bf16[128,768]{1,0:T(8,128)(2,1)S(1)}, u32[]{:S(2)}, u32[]{:S(2)}) collective-permute-start(bf16[128,768]{1,0:T(8,128)(2,1)} %get-tuple-element.162), channel_id=1, source_target_pairs={{0,14},{2,12},{4,10},{6,8},{8,6},{10,4},{12,2},{14,0},{1,15},{3,13... | collective-permute-start | bytes 589832 | tf_op jit(solution)/shard_map/ppermute | solution.py:417
  (51 other events, 566.5 us)

commit v20 on v18

--- a/solution.py
+++ b/solution.py
@@ -604,7 +604,7 @@
     grad_image, sums = waiting((list(grad_image), sums), early)
     group_sum = GroupSum(sums)
     group_sum.over_dp()
-    group_sum.over_next(late[:1])
+    group_sum.over_next(early)
     grad_band = {0: grad_image[0]}
     send(grad_image, order, grad_band)
     arrived = [grad_band[offset] for offset in order]
@@ -612,7 +612,7 @@
     grad_band = listed(grad_band)
     again = waiting(fields, early[:1])
     output = rows_inside(to_cells(me, scaled.T, image_band, again))
-    group_sum.scatter(late[1:] + arrived[:1])
+    group_sum.scatter(late + arrived[:1])
     group_sum.gather(arrived[1:3])
     group_sum.gather_next(arrived[3:5])
     group_sum.half, output = lax.optimization_barrier((group_sum.half, output))

time: 183 us -> 182 us (level)
  starting transfers between devices: 77.3 us -> 73.1 us
  waiting for transfers between devices: 50.7 us -> 54.2 us
    ppermute x38, starting transfers between devices: 77.3 us -> 73.1 us  [swap_with(): return lax.ppermute(values, axis, pairs)]
    ppermute x38, waiting for transfers between devices: 50.7 us -> 54.2 us  [swap_with(): return lax.ppermute(values, axis, pairs)]
    unnamed x63 -> x65, local copies, waits for them, and re-layouts: 4.41 us -> 5.01 us
  transfers between devices with their start and end apart: 38 -> 38, of which waited for: 16 -> 16; matrix products, arithmetic and copies ran while one was open for 6% -> 5% of each run, Pallas kernels for 17% -> 17%
where the time goes in v20:
time: 182 us
  starting transfers between devices  73.1 us (40%)
  waiting for transfers between devices  54.2 us (30%)
  Pallas kernels  36 us (20%)
  local copies, waits for them, and re-layouts  14.8 us (8%)
  other arithmetic  2.59 us (1%)
    ppermute x38, starting transfers between devices, swap_with(): return lax.ppermute(values, axis, pairs)  73.1 us
    ppermute x38, waiting for transfers between devices, swap_with(): return lax.ppermute(values, axis, pairs)  54.2 us
    pallas_call x1, Pallas kernels, backward_mid(): pl.pallas_call(functools.partial(backward_kernel, size_of_block, len(band...  12.7 us
    pallas_call x1, Pallas kernels, forward_mid(): pl.pallas_call(functools.partial(forward_kernel, len(bands)), grid_spec=p...  7.52 us
    pallas_call x2, Pallas kernels, to_cells(): pl.pallas_call(to_cells_kernel, grid_spec=pltpu.PrefetchScalarGridSpec(nu...  6.21 us
    pallas_call x2, local copies, waits for them, and re-layouts, to_cells(): pl.pallas_call(to_cells_kernel, grid_spec=pltpu.PrefetchScalarGridSpec(nu...  6.13 us
    unnamed x65, local copies, waits for them, and re-layouts  5.01 us
    pallas_call x2, Pallas kernels, to_modes(): pl.pallas_call(to_modes_kernel, grid_spec=pltpu.PrefetchScalarGridSpec(nu...  4.8 us
  transfers between devices with their start and end apart: 38, of which 16 were waited for; matrix products, arithmetic and copies ran while one was open for 5% of the time, Pallas kernels for 17%

profile of v20, /device:TPU:0, one launch (start us, length us, event | category | flops | bytes accessed | tf_op | source)
XLA Modules:
  0.0 181.8 jit_solution(16851414146462697924)
XLA Ops:
  5.0 6.1 %collective-permute-start = (bf16[128,768]{1,0:T(8,128)(2,1)}, bf16[128,768]{1,0:T(8,128)(2,1)S(1)}, u32[]{:S(2)}, u32[]{:S(2)}) collective-permute-start(bf16[128,768]{1,0:T(8,128)(2,1)} %get-tuple-element.99), channel_id=1, source_target_pairs={{0,14},{2,12},{4,10},{6,8},{8,6},{10,4},{12,2},{14,0},{1,15},{3,13... | collective-permute-start | bytes 589832 | tf_op jit(solution)/shard_map/ppermute | solution.py:417
  21.7 13.1 %collective-permute-start.5 = (bf16[128,768]{1,0:T(8,128)(2,1)}, bf16[128,768]{1,0:T(8,128)(2,1)}, u32[]{:S(2)}, u32[]{:S(2)}) collective-permute-start(bf16[128,768]{1,0:T(8,128)(2,1)} %get-tuple-element.108), channel_id=1, source_target_pairs={{0,4},{2,6},{4,0},{6,2},{8,12},{10,14},{12,8},{14,10},{1,5},{3,7},... | collective-permute-start | bytes 589832 | tf_op jit(solution)/shard_map/ppermute | solution.py:417
  37.2 4.6 %collective-permute-done.2.refs_3_ = bf16[128,768]{1,0:T(8,128)(2,1)S(1)} collective-permute-done((bf16[128,768]{1,0:T(8,128)(2,1)}, bf16[128,768]{1,0:T(8,128)(2,1)S(1)}, u32[]{:S(2)}, u32[]{:S(2)}) %collective-permute-start.2) | collective-permute-done | bytes 196640 | tf_op jit(solution)/shard_map/ppermute | solution.py:417
  41.8 3.4 %collective-permute-start.7 = (bf16[128,768]{1,0:T(8,128)(2,1)}, bf16[128,768]{1,0:T(8,128)(2,1)S(1)}, u32[]{:S(2)}, u32[]{:S(2)}) collective-permute-start(bf16[128,768]{1,0:T(8,128)(2,1)} %get-tuple-element.111), channel_id=1, source_target_pairs={{0,14},{2,12},{4,10},{6,8},{8,6},{10,4},{12,2},{14,0},{1,15},{3,13... | collective-permute-start | bytes 589832 | tf_op jit(solution)/shard_map/ppermute | solution.py:417
  45.2 2.9 %collective-permute-done.3.refs_4_ = bf16[128,768]{1,0:T(8,128)(2,1)S(1)} collective-permute-done((bf16[128,768]{1,0:T(8,128)(2,1)}, bf16[128,768]{1,0:T(8,128)(2,1)S(1)}, u32[]{:S(2)}, u32[]{:S(2)}) %collective-permute-start.3) | collective-permute-done | bytes 196640 | tf_op jit(solution)/shard_map/ppermute | solution.py:417
  56.8 7.5 %mix_forward.1 = (bf16[128,768]{1,0:T(8,128)(2,1)}, bf16[128,768]{1,0:T(8,128)(2,1)}, bf16[128,768]{1,0:T(8,128)(2,1)}, bf16[128,768]{1,0:T(8,128)(2,1)}, bf16[1...) custom-call(s32[1]{0:T(128)} %bitcast.me_ref, ...), custom_call_target="tpu_custom_call" | custom-call | flops 2415919104 | bytes 17301504 | tf_op jit(solution)/shard_map/mix_forward/pallas_call | solution.py:344
  64.4 5.1 %collective-permute-start.12 = (bf16[128,768]{1,0:T(8,128)(2,1)S(1)}, bf16[128,768]{1,0:T(8,128)(2,1)}, u32[]{:S(2)}, u32[]{:S(2)}) collective-permute-start(bf16[128,768]{1,0:T(8,128)(2,1)S(1)} %copy-done.23), channel_id=1, source_target_pairs={{0,4},{2,6},{4,0},{6,2},{8,12},{10,14},{12,8},{14,10},{1,5},{3,7},... | collective-permute-start | bytes 589832 | tf_op jit(solution)/shard_map/ppermute | solution.py:417
  71.1 5.5 %collective-permute-done.9.refs_3_ = bf16[128,768]{1,0:T(8,128)(2,1)S(1)} collective-permute-done((bf16[128,768]{1,0:T(8,128)(2,1)}, bf16[128,768]{1,0:T(8,128)(2,1)S(1)}, u32[]{:S(2)}, u32[]{:S(2)}) %collective-permute-start.9) | collective-permute-done | bytes 196640 | tf_op jit(solution)/shard_map/ppermute | solution.py:417
  76.5 8.5 %collective-permute-done.10.refs_4_ = bf16[128,768]{1,0:T(8,128)(2,1)} collective-permute-done((bf16[128,768]{1,0:T(8,128)(2,1)}, bf16[128,768]{1,0:T(8,128)(2,1)}, u32[]{:S(2)}, u32[]{:S(2)}) %collective-permute-start.10) | collective-permute-done | bytes 196640 | tf_op jit(solution)/shard_map/ppermute | solution.py:417
  85.0 3.1 %collective-permute-start.16 = (bf16[128,768]{1,0:T(8,128)(2,1)}, bf16[128,768]{1,0:T(8,128)(2,1)S(1)}, u32[]{:S(2)}, u32[]{:S(2)}) collective-permute-start(bf16[128,768]{1,0:T(8,128)(2,1)} %get-tuple-element.139), channel_id=1, source_target_pairs={{0,10},{2,8},{4,14},{6,12},{8,2},{10,0},{12,6},{14,4},{1,11},{3,9}... | collective-permute-start | bytes 589832 | tf_op jit(solution)/shard_map/ppermute | solution.py:417
  90.3 12.7 %mix_backward.1 = (bf16[128,768]{1,0:T(8,128)(2,1)}, bf16[128,768]{1,0:T(8,128)(2,1)}, bf16[128,768]{1,0:T(8,128)(2,1)}, bf16[128,768]{1,0:T(8,128)(2,1)}, bf16[...) custom-call(s32[1]{0:T(128)} %bitcast.me_ref, ...), custom_call_target="tpu_custom_call" | custom-call | flops 4831838208 | bytes 17301504 | tf_op jit(solution)/shard_map/mix_backward/pallas_call | solution.py:382
  109.0 3.0 %collective-permute-start.20 = (bf16[128,768]{1,0:T(8,128)(2,1)S(1)}, bf16[128,768]{1,0:T(8,128)(2,1)}, u32[]{:S(2)}, u32[]{:S(2)}) collective-permute-start(bf16[128,768]{1,0:T(8,128)(2,1)S(1)} %fusion), channel_id=1, source_target_pairs={{0,2},{2,0},{4,6},{6,4},{8,10},{10,8},{12,14},{14,12},{1,3},{3,1},... | collective-permute-start | bytes 589832 | tf_op jit(solution)/shard_map/ppermute | solution.py:417
  115.7 5.8 %collective-permute-done.20 = bf16[128,768]{1,0:T(8,128)(2,1)} collective-permute-done((bf16[128,768]{1,0:T(8,128)(2,1)S(1)}, bf16[128,768]{1,0:T(8,128)(2,1)}, u32[]{:S(2)}, u32[]{:S(2)}) %collective-permute-start.20) | collective-permute-done | bytes 196640 | tf_op jit(solution)/shard_map/ppermute | solution.py:417
  122.8 2.9 %collective-permute-done.22.refs_7_ = bf16[128,768]{1,0:T(8,128)(2,1)} collective-permute-done((bf16[128,768]{1,0:T(8,128)(2,1)}, bf16[128,768]{1,0:T(8,128)(2,1)}, u32[]{:S(2)}, u32[]{:S(2)}) %collective-permute-start.22) | collective-permute-done | bytes 196640 | tf_op jit(solution)/shard_map/ppermute | solution.py:417
  125.7 5.9 %collective-permute-done.23.refs_4_ = bf16[128,768]{1,0:T(8,128)(2,1)} collective-permute-done((bf16[128,768]{1,0:T(8,128)(2,1)}, bf16[128,768]{1,0:T(8,128)(2,1)}, u32[]{:S(2)}, u32[]{:S(2)}) %collective-permute-start.23) | collective-permute-done | bytes 196640 | tf_op jit(solution)/shard_map/ppermute | solution.py:417
  136.2 2.7 %collective-permute-start.28 = (bf16[128,768]{1,0:T(8,128)(2,1)}, bf16[128,768]{1,0:T(8,128)(2,1)S(1)}, u32[]{:S(2)}, u32[]{:S(2)}) collective-permute-start(bf16[128,768]{1,0:T(8,128)(2,1)} %get-tuple-element.149), channel_id=1, source_target_pairs={{0,10},{2,8},{4,14},{6,12},{8,2},{10,0},{12,6},{14,4},{1,11},{3,9}... | collective-permute-start | bytes 589832 | tf_op jit(solution)/shard_map/ppermute | solution.py:417
  142.0 5.4 %collective-permute-done.27.refs_6_ = bf16[128,768]{1,0:T(8,128)(2,1)S(1)} collective-permute-done((bf16[128,768]{1,0:T(8,128)(2,1)}, bf16[128,768]{1,0:T(8,128)(2,1)S(1)}, u32[]{:S(2)}, u32[]{:S(2)}) %collective-permute-start.27) | collective-permute-done | bytes 196640 | tf_op jit(solution)/shard_map/ppermute | solution.py:417
  147.4 2.8 %collective-permute-done.28.refs_3_ = bf16[128,768]{1,0:T(8,128)(2,1)S(1)} collective-permute-done((bf16[128,768]{1,0:T(8,128)(2,1)}, bf16[128,768]{1,0:T(8,128)(2,1)S(1)}, u32[]{:S(2)}, u32[]{:S(2)}) %collective-permute-start.28) | collective-permute-done | bytes 196640 | tf_op jit(solution)/shard_map/ppermute | solution.py:417
  154.6 3.8 %collective-permute-done.31 = bf16[32,768]{1,0:T(8,128)(2,1)S(1)} collective-permute-done((bf16[32,768]{1,0:T(8,128)(2,1)S(1)}, bf16[32,768]{1,0:T(8,128)(2,1)S(1)}, u32[]{:S(2)}, u32[]{:S(2)}) %collective-permute-start.31) | collective-permute-done | bytes 49184 | tf_op jit(solution)/shard_map/ppermute | solution.py:417
  161.0 2.9 %collective-permute-start.35 = (bf16[128,768]{1,0:T(8,128)(2,1)}, bf16[128,768]{1,0:T(8,128)(2,1)S(1)}, u32[]{:S(2)}, u32[]{:S(2)}) collective-permute-start(bf16[128,768]{1,0:T(8,128)(2,1)} %get-tuple-element.158), channel_id=1, source_target_pairs={{0,14},{2,12},{4,10},{6,8},{8,6},{10,4},{12,2},{14,0},{1,15},{3,13... | collective-permute-start | bytes 589832 | tf_op jit(solution)/shard_map/ppermute | solution.py:417
  166.4 3.2 %to_cells.2 = bf16[4,2,180,768]{3,2,1,0:T(8,128)(2,1)S(1)} custom-call(s32[1]{0:T(128)} %bitcast.me_ref, bf16[180,128]{1,0:T(8,128)(2,1)S(1)} %copy-done.3, bf16[4,2,180,768]{3,2,1,0:T(8,128)(2,1)S(1)} %copy.23.base_ref, bf16[128,768]{1,0:T(8,128)(2,1)} %get-tuple-element.155.refs_0_, bf16[128,768]{1,0:T(8,128)(2,1)} %collective-permute-done.21.refs_1_, ...), custom_call_target="tpu_custom_call" | custom-call | flops 283115520 | bytes 5996544 | tf_op jit(solution)/shard_map/to_cells/pallas_call | solution.py:186
  169.6 3.1 %copy.30 = bf16[4,2,180,768]{3,1,2,0:T(2,128)(2,1)} copy(bf16[4,2,180,768]{3,2,1,0:T(8,128)(2,1)S(1)} %to_cells.2) | data formatting | bytes 4423680 | tf_op jit(solution)/shard_map/to_cells/pallas_call | solution.py:186
  173.5 3.0 %to_cells.3 = bf16[4,2,180,768]{3,2,1,0:T(8,128)(2,1)S(1)} custom-call(s32[1]{0:T(128)} %bitcast.me_ref, bf16[180,128]{1,0:T(8,128)(2,1)S(1)} %copy-done.2, bf16[4,2,180,768]{3,2,1,0:T(8,128)(2,1)S(1)} %copy.22.cells_ref.base_ref, bf16[128,768]{1,0:T(8,128)(2,1)} %get-tuple-element.157.refs_0_, bf16[128,768]{1,0:T(8,128)(2,1)} %copy-done.18, ...), custom_call_target="tpu_custom_call" | custom-call | flops 283115520 | bytes 5996544 | tf_op jit(solution)/shard_map/to_cells/pallas_call | solution.py:186
  176.5 3.1 %copy.26 = bf16[4,2,180,768]{3,1,2,0:T(2,128)(2,1)} copy(bf16[4,2,180,768]{3,2,1,0:T(8,128)(2,1)S(1)} %to_cells.3) | data formatting | bytes 4423680 | tf_op jit(solution)/shard_map/to_cells/pallas_call | solution.py:186
  (144 shorter events, 60.8 us)
Async XLA Ops:
  5.0 16.7 %collective-permute-start = (bf16[128,768]{1,0:T(8,128)(2,1)}, bf16[128,768]{1,0:T(8,128)(2,1)S(1)}, u32[]{:S(2)}, u32[]{:S(2)}) collective-permute-start(bf16[128,768]{1,0:T(8,128)(2,1)} %get-tuple-element.99), channel_id=1, source_target_pairs={{0,14},{2,12},{4,10},{6,8},{8,6},{10,4},{12,2},{14,0},{1,15},{3,13... | collective-permute-start | bytes 589832 | tf_op jit(solution)/shard_map/ppermute | solution.py:417
  11.1 23.7 %collective-permute-start.1 = (bf16[128,768]{1,0:T(8,128)(2,1)}, bf16[128,768]{1,0:T(8,128)(2,1)S(1)}, u32[]{:S(2)}, u32[]{:S(2)}) collective-permute-start(bf16[128,768]{1,0:T(8,128)(2,1)} %get-tuple-element.100), channel_id=1, source_target_pairs={{0,12},{2,14},{4,8},{6,10},{8,4},{10,6},{12,0},{14,2},{1,13},{3,15... | collective-permute-start | bytes 589832 | tf_op jit(solution)/shard_map/ppermute | solution.py:417
  11.3 30.5 %collective-permute-start.2 = (bf16[128,768]{1,0:T(8,128)(2,1)}, bf16[128,768]{1,0:T(8,128)(2,1)S(1)}, u32[]{:S(2)}, u32[]{:S(2)}) collective-permute-start(bf16[128,768]{1,0:T(8,128)(2,1)} %get-tuple-element.101), channel_id=1, source_target_pairs={{0,10},{2,8},{4,14},{6,12},{8,2},{10,0},{12,6},{14,4},{1,11},{3,9}... | collective-permute-start | bytes 589832 | tf_op jit(solution)/shard_map/ppermute | solution.py:417
  12.0 36.1 %collective-permute-start.3 = (bf16[128,768]{1,0:T(8,128)(2,1)}, bf16[128,768]{1,0:T(8,128)(2,1)S(1)}, u32[]{:S(2)}, u32[]{:S(2)}) collective-permute-start(bf16[128,768]{1,0:T(8,128)(2,1)} %get-tuple-element.102), channel_id=1, source_target_pairs={{0,8},{2,10},{4,12},{6,14},{8,0},{10,2},{12,4},{14,6},{1,9},{3,11}... | collective-permute-start | bytes 589832 | tf_op jit(solution)/shard_map/ppermute | solution.py:417
  14.1 37.2 %collective-permute-start.4 = (bf16[128,768]{1,0:T(8,128)(2,1)}, bf16[128,768]{1,0:T(8,128)(2,1)S(1)}, u32[]{:S(2)}, u32[]{:S(2)}) collective-permute-start(bf16[128,768]{1,0:T(8,128)(2,1)} %get-tuple-element.103), channel_id=1, source_target_pairs={{0,6},{2,4},{4,2},{6,0},{8,14},{10,12},{12,10},{14,8},{1,7},{3,5},... | collective-permute-start | bytes 589832 | tf_op jit(solution)/shard_map/ppermute | solution.py:417
  21.7 31.4 %collective-permute-start.5 = (bf16[128,768]{1,0:T(8,128)(2,1)}, bf16[128,768]{1,0:T(8,128)(2,1)}, u32[]{:S(2)}, u32[]{:S(2)}) collective-permute-start(bf16[128,768]{1,0:T(8,128)(2,1)} %get-tuple-element.108), channel_id=1, source_target_pairs={{0,4},{2,6},{4,0},{6,2},{8,12},{10,14},{12,8},{14,10},{1,5},{3,7},... | collective-permute-start | bytes 589832 | tf_op jit(solution)/shard_map/ppermute | solution.py:417
  35.5 19.4 %collective-permute-start.6 = (bf16[128,768]{1,0:T(8,128)(2,1)}, bf16[128,768]{1,0:T(8,128)(2,1)}, u32[]{:S(2)}, u32[]{:S(2)}) collective-permute-start(bf16[128,768]{1,0:T(8,128)(2,1)} %get-tuple-element.109), channel_id=1, source_target_pairs={{0,2},{2,0},{4,6},{6,4},{8,10},{10,8},{12,14},{14,12},{1,3},{3,1},... | collective-permute-start | bytes 589832 | tf_op jit(solution)/shard_map/ppermute | solution.py:417
  41.8 22.5 %collective-permute-start.7 = (bf16[128,768]{1,0:T(8,128)(2,1)}, bf16[128,768]{1,0:T(8,128)(2,1)S(1)}, u32[]{:S(2)}, u32[]{:S(2)}) collective-permute-start(bf16[128,768]{1,0:T(8,128)(2,1)} %get-tuple-element.111), channel_id=1, source_target_pairs={{0,14},{2,12},{4,10},{6,8},{8,6},{10,4},{12,2},{14,0},{1,15},{3,13... | collective-permute-start | bytes 589832 | tf_op jit(solution)/shard_map/ppermute | solution.py:417
  48.8 20.7 %collective-permute-start.8 = (bf16[128,768]{1,0:T(8,128)(2,1)}, bf16[128,768]{1,0:T(8,128)(2,1)S(1)}, u32[]{:S(2)}, u32[]{:S(2)}) collective-permute-start(bf16[128,768]{1,0:T(8,128)(2,1)} %get-tuple-element.112), channel_id=1, source_target_pairs={{0,12},{2,14},{4,8},{6,10},{8,4},{10,6},{12,0},{14,2},{1,13},{3,15... | collective-permute-start | bytes 589832 | tf_op jit(solution)/shard_map/ppermute | solution.py:417
  51.9 24.6 %collective-permute-start.9 = (bf16[128,768]{1,0:T(8,128)(2,1)}, bf16[128,768]{1,0:T(8,128)(2,1)S(1)}, u32[]{:S(2)}, u32[]{:S(2)}) collective-permute-start(bf16[128,768]{1,0:T(8,128)(2,1)} %get-tuple-element.113), channel_id=1, source_target_pairs={{0,10},{2,8},{4,14},{6,12},{8,2},{10,0},{12,6},{14,4},{1,11},{3,9}... | collective-permute-start | bytes 589832 | tf_op jit(solution)/shard_map/ppermute | solution.py:417
  53.1 31.9 %collective-permute-start.10 = (bf16[128,768]{1,0:T(8,128)(2,1)}, bf16[128,768]{1,0:T(8,128)(2,1)}, u32[]{:S(2)}, u32[]{:S(2)}) collective-permute-start(bf16[128,768]{1,0:T(8,128)(2,1)} %get-tuple-element.114), channel_id=1, source_target_pairs={{0,8},{2,10},{4,12},{6,14},{8,0},{10,2},{12,4},{14,6},{1,9},{3,11}... | collective-permute-start | bytes 589832 | tf_op jit(solution)/shard_map/ppermute | solution.py:417
  54.8 30.2 %collective-permute-start.11 = (bf16[128,768]{1,0:T(8,128)(2,1)}, bf16[128,768]{1,0:T(8,128)(2,1)}, u32[]{:S(2)}, u32[]{:S(2)}) collective-permute-start(bf16[128,768]{1,0:T(8,128)(2,1)} %get-tuple-element.115), channel_id=1, source_target_pairs={{0,6},{2,4},{4,2},{6,0},{8,14},{10,12},{12,10},{14,8},{1,7},{3,5},... | collective-permute-start | bytes 589832 | tf_op jit(solution)/shard_map/ppermute | solution.py:417
  64.4 23.8 %collective-permute-start.12 = (bf16[128,768]{1,0:T(8,128)(2,1)S(1)}, bf16[128,768]{1,0:T(8,128)(2,1)}, u32[]{:S(2)}, u32[]{:S(2)}) collective-permute-start(bf16[128,768]{1,0:T(8,128)(2,1)S(1)} %copy-done.23), channel_id=1, source_target_pairs={{0,4},{2,6},{4,0},{6,2},{8,12},{10,14},{12,8},{14,10},{1,5},{3,7},... | collective-permute-start | bytes 589832 | tf_op jit(solution)/shard_map/ppermute | solution.py:417
  69.5 19.5 %collective-permute-start.13 = (bf16[128,768]{1,0:T(8,128)(2,1)S(1)}, bf16[128,768]{1,0:T(8,128)(2,1)}, u32[]{:S(2)}, u32[]{:S(2)}) collective-permute-start(bf16[128,768]{1,0:T(8,128)(2,1)S(1)} %copy-done.22), channel_id=1, source_target_pairs={{0,2},{2,0},{4,6},{6,4},{8,10},{10,8},{12,14},{14,12},{1,3},{3,1},... | collective-permute-start | bytes 589832 | tf_op jit(solution)/shard_map/ppermute | solution.py:417
  76.5 26.5 %collective-permute-start.14 = (bf16[128,768]{1,0:T(8,128)(2,1)}, bf16[128,768]{1,0:T(8,128)(2,1)S(1)}, u32[]{:S(2)}, u32[]{:S(2)}) collective-permute-start(bf16[128,768]{1,0:T(8,128)(2,1)} %get-tuple-element.137), channel_id=1, source_target_pairs={{0,8},{2,10},{4,12},{6,14},{8,0},{10,2},{12,4},{14,6},{1,9},{3,11}... | collective-permute-start | bytes 589832 | tf_op jit(solution)/shard_map/ppermute | solution.py:417
  85.0 18.1 %collective-permute-start.15 = (bf16[128,768]{1,0:T(8,128)(2,1)}, bf16[128,768]{1,0:T(8,128)(2,1)S(1)}, u32[]{:S(2)}, u32[]{:S(2)}) collective-permute-start(bf16[128,768]{1,0:T(8,128)(2,1)} %get-tuple-element.138), channel_id=1, source_target_pairs={{0,4},{2,6},{4,0},{6,2},{8,12},{10,14},{12,8},{14,10},{1,5},{3,7},... | collective-permute-start | bytes 589832 | tf_op jit(solution)/shard_map/ppermute | solution.py:417
  85.0 18.1 %collective-permute-start.16 = (bf16[128,768]{1,0:T(8,128)(2,1)}, bf16[128,768]{1,0:T(8,128)(2,1)S(1)}, u32[]{:S(2)}, u32[]{:S(2)}) collective-permute-start(bf16[128,768]{1,0:T(8,128)(2,1)} %get-tuple-element.139), channel_id=1, source_target_pairs={{0,10},{2,8},{4,14},{6,12},{8,2},{10,0},{12,6},{14,4},{1,11},{3,9}... | collective-permute-start | bytes 589832 | tf_op jit(solution)/shard_map/ppermute | solution.py:417
  88.1 15.0 %collective-permute-start.17 = (bf16[128,768]{1,0:T(8,128)(2,1)}, bf16[128,768]{1,0:T(8,128)(2,1)S(1)}, u32[]{:S(2)}, u32[]{:S(2)}) collective-permute-start(bf16[128,768]{1,0:T(8,128)(2,1)} %get-tuple-element.140), channel_id=1, source_target_pairs={{0,6},{2,4},{4,2},{6,0},{8,14},{10,12},{12,10},{14,8},{1,7},{3,5},... | collective-permute-start | bytes 589832 | tf_op jit(solution)/shard_map/ppermute | solution.py:417
  89.0 14.4 %collective-permute-start.18 = (bf16[128,768]{1,0:T(8,128)(2,1)}, bf16[128,768]{1,0:T(8,128)(2,1)S(1)}, u32[]{:S(2)}, u32[]{:S(2)}) collective-permute-start(bf16[128,768]{1,0:T(8,128)(2,1)} %get-tuple-element.141), channel_id=1, source_target_pairs={{0,12},{2,14},{4,8},{6,10},{8,4},{10,6},{12,0},{14,2},{1,13},{3,15... | collective-permute-start | bytes 589832 | tf_op jit(solution)/shard_map/ppermute | solution.py:417
  115.7 16.0 %collective-permute-start.23 = (bf16[128,768]{1,0:T(8,128)(2,1)}, bf16[128,768]{1,0:T(8,128)(2,1)}, u32[]{:S(2)}, u32[]{:S(2)}) collective-permute-start(bf16[128,768]{1,0:T(8,128)(2,1)} %get-tuple-element.146), channel_id=1, source_target_pairs={{0,8},{2,10},{4,12},{6,14},{8,0},{10,2},{12,4},{14,6},{1,9},{3,11}... | collective-permute-start | bytes 589832 | tf_op jit(solution)/shard_map/ppermute | solution.py:417
  136.2 14.0 %collective-permute-start.28 = (bf16[128,768]{1,0:T(8,128)(2,1)}, bf16[128,768]{1,0:T(8,128)(2,1)S(1)}, u32[]{:S(2)}, u32[]{:S(2)}) collective-permute-start(bf16[128,768]{1,0:T(8,128)(2,1)} %get-tuple-element.149), channel_id=1, source_target_pairs={{0,10},{2,8},{4,14},{6,12},{8,2},{10,0},{12,6},{14,4},{1,11},{3,9}... | collective-permute-start | bytes 589832 | tf_op jit(solution)/shard_map/ppermute | solution.py:417
  138.8 21.2 %collective-permute-start.32 = (bf16[128,768]{1,0:T(8,128)(2,1)}, bf16[128,768]{1,0:T(8,128)(2,1)S(1)}, u32[]{:S(2)}, u32[]{:S(2)}) collective-permute-start(bf16[128,768]{1,0:T(8,128)(2,1)} %get-tuple-element.151), channel_id=1, source_target_pairs={{0,6},{2,4},{4,2},{6,0},{8,14},{10,12},{12,10},{14,8},{1,7},{3,5},... | collective-permute-start | bytes 589832 | tf_op jit(solution)/shard_map/ppermute | solution.py:417
  139.8 20.3 %collective-permute-start.33 = (bf16[128,768]{1,0:T(8,128)(2,1)}, bf16[128,768]{1,0:T(8,128)(2,1)S(1)}, u32[]{:S(2)}, u32[]{:S(2)}) collective-permute-start(bf16[128,768]{1,0:T(8,128)(2,1)} %get-tuple-element.152), channel_id=1, source_target_pairs={{0,12},{2,14},{4,8},{6,10},{8,4},{10,6},{12,0},{14,2},{1,13},{3,15... | collective-permute-start | bytes 589832 | tf_op jit(solution)/shard_map/ppermute | solution.py:417
  160.1 12.6 %collective-permute-start.34 = (bf16[4,32,768]{2,1,0:T(8,128)(2,1)S(1)}, bf16[4,32,768]{2,1,0:T(8,128)(2,1)S(1)}, u32[]{:S(2)}, u32[]{:S(2)}) collective-permute-start(bf16[4,32,768]{2,1,0:T(8,128)(2,1)S(1)} %pad_maximum_fusion.1), channel_id=1, source_target_pairs={{0,2},{2,0},{4,6},{6,4},{8,10},{10,8},{12,14},{14,12},{1,3},{3,1},... | collective-permute-start | bytes 589832 | tf_op jit(solution)/shard_map/ppermute | solution.py:417
  (46 other events, 476.3 us)
